TPU v7x, 32 devices: a whole 2x2x4 slice. The times are simulated.
32 devices in a mesh: grp: 2 (over y), src: 8 (over z, x), tgt: 2 (over core).
Axes of the slice: x: 2, y: 2, z: 4, core: 2. Of those that a mesh axis runs over, the one named last changes fastest.
Arguments:
- source_feat: float32 [256, 64, 128], P(('grp', 'src')), parts along dimension 0, may hold values from -1.2 to 1.2
- target_feat: float32 [32, 64, 128], P(('grp', 'src', 'tgt')), parts along dimension 0, may hold values from -1.2 to 1.2
- log_mass_src: float32 [256, 128], P(('grp', 'src')), parts along dimension 0, may hold values from -3 to 3
- log_mass_tgt: float32 [32, 128], P(('grp', 'src', 'tgt')), parts along dimension 0, may hold values from -3 to 3
- potential_tgt: float32 [32, 128], P(('grp', 'src', 'tgt')), parts along dimension 0, may hold values from -6 to 152
- support: int32 [256, 2, 8], P(('grp', 'src'), 'tgt'), parts along dimension 0, may hold values from 0 to 7, as said below
- counts: int32 [256, 2], P(('grp', 'src'), 'tgt'), parts along dimension 0, may hold values from 1 to 8, as said below
Outputs:
- potential_src: float32 [256, 128], P(('grp', 'src')), parts along dimension 0
- potential_new: float32 [32, 128], P(('grp', 'src', 'tgt')), parts along dimension 0
There are 2 independent parts, one for each index of `grp`. A program takes and returns all parts, laid end to end along the dimension named above; each array names one. Nothing has to cross between parts.
Inputs may be any that keep to these rules, and one draw needn't show every extreme that they name: `support`: within one list the first counts entries are distinct; unused entries are also valid indices and are ignored; every target block of a shard is named within the used entries of some source block row. `counts`: the source block rows of one index of src share a load level, so some devices use far more slots than others; some list is full in every draw.
All inputs are finite; a program needn't handle non-finite values.
Results may differ from a plain program's by a relative error of at most 0.000096.
Values sent between devices are 32-bit elements; how exact they have to be, the bound alone decides.
No kernel may reach another device: no remote copies, remote signals or barrier semaphores. Data moves between devices by JAX's collectives and lax.ppermute only.
A program may use at most 64 MiB of HBM per device.

v0:
```python
import math

import jax
import jax.numpy as jnp
from jax import lax
from jax.sharding import PartitionSpec as P

entropic = 0.5
very_low = -1e30


def merged(part, axis, combine):
    gathered = jax.tree.map(lambda a: lax.all_gather(a, axis), part)

    def take(source):
        return jax.tree.map(lambda a: lax.dynamic_index_in_dim(a, source, 0, False), gathered)

    return lax.fori_loop(
        1, lax.axis_size(axis), lambda source, state: combine(state, take(source)), take(0)
    )


def cost_tiles(source_blk, source_sq, target_blk, target_sq):
    cross = jnp.einsum(
        "...fi,...fj->...ij", source_blk, target_blk, precision=lax.Precision.HIGHEST
    )
    return source_sq[..., :, None] + target_sq[..., None, :] - 2.0 * cross


def row_stats(cost, mass_tgt, poten_tgt, usable):
    scores = mass_tgt[..., None, :] + (poten_tgt[..., None, :] - cost) / entropic
    scores = jnp.where(usable[..., None, None], scores, very_low)
    peak = jnp.max(scores, axis=(1, 3))
    total = jnp.sum(jnp.exp(scores - peak[:, None, :, None]), axis=(1, 3))
    return (peak, total)


def column_stats(cost, mass_src, poten_src, usable):
    scores = mass_src[:, None, :, None] + (poten_src[:, None, :, None] - cost) / entropic
    peak = jnp.max(scores, axis=2)
    total = jnp.sum(jnp.exp(scores - peak[:, :, None, :]), axis=2)
    peak = jnp.where(usable[..., None], peak, very_low)
    total = jnp.where(usable[..., None], total, 0.0)
    return (peak, total)


def merge_pair(first_pair, second_pair):
    first_peak, first_total = first_pair
    second_peak, second_total = second_pair
    highest = jnp.maximum(first_peak, second_peak)
    summed = first_total * jnp.exp(first_peak - highest) + second_total * jnp.exp(
        second_peak - highest
    )
    return (highest, summed)


def segment_merge(peaks, totals, seg_ids, segments):
    best = jax.ops.segment_max(peaks, seg_ids, num_segments=segments + 1)
    best = jnp.maximum(best, very_low)
    summed = jax.ops.segment_sum(
        totals * jnp.exp(peaks - best[seg_ids]), seg_ids, num_segments=segments + 1
    )
    return (best[:segments], summed[:segments])


def per_device(
    source_feat, target_feat, log_mass_src, log_mass_tgt, potential_tgt, support, counts
):
    target_all, mass_all, poten_all = (
        lax.all_gather(target_feat, "src", axis=0, tiled=True),
        lax.all_gather(log_mass_tgt, "src", axis=0, tiled=True),
        lax.all_gather(potential_tgt, "src", axis=0, tiled=True),
    )
    blocks = target_all.shape[0]
    rows_here = source_feat.shape[0]
    slots_here = support.shape[2]
    cells = source_feat.shape[2]
    indices = support[:, 0, :]
    limits = counts[:, 0]
    usable = jnp.arange(slots_here, dtype=jnp.int32)[None, :] < limits[:, None]
    source_sq = jnp.sum(source_feat * source_feat, axis=1)
    target_sq = jnp.sum(target_all * target_all, axis=1)
    width = math.gcd(rows_here, 4)

    def grouped(array):
        return array.reshape((rows_here // width, width) + array.shape[1:])

    def row_pass(items):
        source_blk, source_nrm, ids_here, use_here = items
        cost = cost_tiles(
            source_blk[:, None], source_nrm[:, None], target_all[ids_here], target_sq[ids_here]
        )
        return row_stats(cost, mass_all[ids_here], poten_all[ids_here], use_here)

    peak, total = lax.map(
        row_pass, (grouped(source_feat), grouped(source_sq), grouped(indices), grouped(usable))
    )
    peak = peak.reshape(rows_here, cells)
    total = total.reshape(rows_here, cells)
    peak_all, total_all = merged((peak, total), "tgt", merge_pair)
    potential_src = -entropic * (peak_all + jnp.log(total_all))

    def column_pass(items):
        source_blk, source_nrm, mass_here, poten_here, ids_here, use_here = items
        cost = cost_tiles(
            source_blk[:, None], source_nrm[:, None], target_all[ids_here], target_sq[ids_here]
        )
        return column_stats(cost, mass_here, poten_here, use_here)

    peaks, totals = lax.map(
        column_pass,
        (
            grouped(source_feat),
            grouped(source_sq),
            grouped(log_mass_src),
            grouped(potential_src),
            grouped(indices),
            grouped(usable),
        ),
    )
    seg_ids = jnp.where(usable, indices, blocks).reshape(-1)
    best, summed = segment_merge(
        peaks.reshape(-1, cells), totals.reshape(-1, cells), seg_ids, blocks
    )
    share = blocks // lax.axis_size("src")
    own_start = lax.axis_index("src") * share
    highest = lax.pmax(best, "src")
    whole = lax.psum(summed * jnp.exp(best - highest), "src")
    own_peak = lax.dynamic_slice_in_dim(highest, own_start, share, 0)
    own_total = lax.dynamic_slice_in_dim(whole, own_start, share, 0)
    potential_new = -entropic * (own_peak + jnp.log(own_total))
    return (potential_src, potential_new)


def solution(mesh):
    in_specs = (
        P(("grp", "src"), None, None),
        P(("grp", "src", "tgt"), None, None),
        P(("grp", "src"), None),
        P(("grp", "src", "tgt"), None),
        P(("grp", "src", "tgt"), None),
        P(("grp", "src"), "tgt", None),
        P(("grp", "src"), "tgt"),
    )
    out_specs = (P(("grp", "src"), None), P(("grp", "src", "tgt"), None))
    return jax.shard_map(
        per_device, mesh=mesh, in_specs=in_specs, out_specs=out_specs, check_vma=False
    )
```

profile of v0, /device:TPU:0, one launch (start us, length us, event | category | flops | bytes accessed | tf_op | source)
XLA Modules:
  0.0 177.1 jit_solution(18147925197401593971)
XLA Ops:
  1.2 1.3 reduce.3
  2.6 0.8 copy.19
  3.4 22.3 %all-gather = f32[8,1,128]{2,1,0:T(1,128)S(1)} all-gather(f32[1,1,128]{2,1,0:T(1,128)} %bitcast.189), channel_id=1, replica_groups=mesh['grp'=2,'src'=8,'tgt'=2] {'src'}, dimensions={0}, use_global_device_ids=true | all-gather | bytes 4608 | tf_op jit(solution)/shard_map/all_gather | solution.py:71
  25.7 16.4 %all-gather.1 = f32[8,1,128]{2,1,0:T(1,128)S(1)} all-gather(f32[1,1,128]{2,1,0:T(1,128)} %bitcast.190), channel_id=1, replica_groups=mesh['grp'=2,'src'=8,'tgt'=2] {'src'}, dimensions={0}, use_global_device_ids=true | all-gather | bytes 4608 | tf_op jit(solution)/shard_map/all_gather | solution.py:72
  42.1 1.1 multiply_reduce_fusion
  43.2 31.0 %all_gather.17 = f32[8,64,128]{2,1,0:T(8,128)S(1)} all-gather(f32[1,64,128]{2,1,0:T(8,128)} %param.12), channel_id=1, replica_groups=mesh['grp'=2,'src'=8,'tgt'=2] {'src'}, dimensions={0}, use_global_device_ids=true | all-gather | bytes 294912 | tf_op jit(solution)/shard_map/all_gather | solution.py:70
  74.2 35.7 %while.8 = (s32[]{:T(128)}, f32[4,4,128]{2,1,0:T(4,128)S(1)}, f32[4,4,128]{2,1,0:T(4,128)S(1)}, pred[4,4,8]{2,1,0:T(4,128)(4,1)S(1)}, s32[4,4,8]{2,1,0:T(4,128)S...) while((s32[]{:T(128)}, f32[4,4,128]{2,1,0:T(4,128)S(1)}, ...), condition=%wide.region_5.6_spmd, body=%wide.region_2.5_spmd.sunk | while | flops 407896160 | bytes 7644529 | solution.py:95
  74.3 0.6 gather_fusion
  76.7 6.1 %fusion.44 = (f32[4,128]{1,0:T(4,128)S(1)}, f32[4,8,128,128]{2,3,1,0:T(8,128)S(1)}) fusion(f32[4,8,64,128]{3,2,1,0:T(8,128)S(1)} %bitcast.172, f32[4,4,64,128]{3,2,1,0:T(8,128)} %get-tuple-element.388, s32[]{:T(128)S(6)} %copy.30, f32[4,8,128]{2,1,0:T(8,128)S(1)} %bitcast.175, f32[4,128]{1,0:T(4,128)S(1)} %dynamic-slice_bitcast_fusion.9, ...), kind=kOutput, calls=%fused_computation.75.clone.1 | convolution fusion | flops 406846976 | bytes 3330084 | tf_op jit(solution)/shard_map/while/body/eval_jaxpr/...fi,...fj->...ij/dot_general | solution.py:24
  85.6 6.1 %fusion.44 = (f32[4,128]{1,0:T(4,128)S(1)}, f32[4,8,128,128]{2,3,1,0:T(8,128)S(1)}) fusion(f32[4,8,64,128]{3,2,1,0:T(8,128)S(1)} %bitcast.172, f32[4,4,64,128]{3,2,1,0:T(8,128)} %get-tuple-element.388, s32[]{:T(128)S(6)} %copy.30, f32[4,8,128]{2,1,0:T(8,128)S(1)} %bitcast.175, f32[4,128]{1,0:T(4,128)S(1)} %dynamic-slice_bitcast_fusion.9, ...), kind=kOutput, calls=%fused_computation.75.clone.1 | convolution fusion | flops 406846976 | bytes 3330084 | tf_op jit(solution)/shard_map/while/body/eval_jaxpr/...fi,...fj->...ij/dot_general | solution.py:24
  94.6 6.1 %fusion.44 = (f32[4,128]{1,0:T(4,128)S(1)}, f32[4,8,128,128]{2,3,1,0:T(8,128)S(1)}) fusion(f32[4,8,64,128]{3,2,1,0:T(8,128)S(1)} %bitcast.172, f32[4,4,64,128]{3,2,1,0:T(8,128)} %get-tuple-element.388, s32[]{:T(128)S(6)} %copy.30, f32[4,8,128]{2,1,0:T(8,128)S(1)} %bitcast.175, f32[4,128]{1,0:T(4,128)S(1)} %dynamic-slice_bitcast_fusion.9, ...), kind=kOutput, calls=%fused_computation.75.clone.1 | convolution fusion | flops 406846976 | bytes 3330084 | tf_op jit(solution)/shard_map/while/body/eval_jaxpr/...fi,...fj->...ij/dot_general | solution.py:24
  103.5 6.1 %fusion.44 = (f32[4,128]{1,0:T(4,128)S(1)}, f32[4,8,128,128]{2,3,1,0:T(8,128)S(1)}) fusion(f32[4,8,64,128]{3,2,1,0:T(8,128)S(1)} %bitcast.172, f32[4,4,64,128]{3,2,1,0:T(8,128)} %get-tuple-element.388, s32[]{:T(128)S(6)} %copy.30, f32[4,8,128]{2,1,0:T(8,128)S(1)} %bitcast.175, f32[4,128]{1,0:T(4,128)S(1)} %dynamic-slice_bitcast_fusion.9, ...), kind=kOutput, calls=%fused_computation.75.clone.1 | convolution fusion | flops 406846976 | bytes 3330084 | tf_op jit(solution)/shard_map/while/body/eval_jaxpr/...fi,...fj->...ij/dot_general | solution.py:24
  110.0 1.8 %all_gather.19 = f32[2,16,128]{2,1,0:T(8,128)S(1)} all-gather(f32[1,16,128]{2,1,0:T(8,128)S(1)} %bitcast.188), channel_id=1, replica_groups=mesh['grp'=2,'src'=8,'tgt'=2] {'tgt'}, dimensions={0}, use_global_device_ids=true | all-gather | bytes 24576 | tf_op jit(solution)/shard_map/all_gather | solution.py:13
  111.8 1.8 %all_gather.18 = f32[2,16,128]{2,1,0:T(8,128)S(1)} all-gather(f32[1,16,128]{2,1,0:T(8,128)S(1)} %bitcast.187), channel_id=1, replica_groups=mesh['grp'=2,'src'=8,'tgt'=2] {'tgt'}, dimensions={0}, use_global_device_ids=true | all-gather | bytes 24576 | tf_op jit(solution)/shard_map/all_gather | solution.py:13
  113.6 0.6 fusion.19
  114.5 22.8 %while.9 = (s32[]{:T(128)}, f32[4,4,8,128]{3,2,1,0:T(8,128)S(1)}, f32[4,4,8,128]{3,2,1,0:T(8,128)S(1)}, pred[4,4,8]{2,1,0:T(4,128)(4,1)S(1)}, f32[4,4,128]{2,1,0...) while((s32[]{:T(128)}, f32[4,4,8,128]{3,2,1,0:T(8,128)S(1)}, ...), condition=%wide.region_9.10_spmd, body=%wide.region_6.9_spmd.sunk | while | flops 407372896 | bytes 7659093 | solution.py:110
  115.9 0.7 dynamic-slice_bitcast_fusion.12
  116.6 3.2 %fusion.46 = (f32[4,8,128]{2,1,0:T(8,128)S(1)}, f32[4,8,128,128]{3,2,1,0:T(8,128)S(1)}) fusion(f32[4,8,64,128]{3,2,1,0:T(8,128)S(1)} %bitcast.171, f32[4,4,64,128]{3,2,1,0:T(8,128)} %get-tuple-element.424, s32[]{:T(128)S(6)} %copy.39, f32[4,8,128]{2,1,0:T(8,128)S(1)} %bitcast.174, f32[4,128]{1,0:T(4,128)S(1)} %get-tuple-element.348, ...), kind=kOutput, calls=%fused_computation.76.clone.1 | convolution fusion | flops 406319104 | bytes 3315716 | tf_op jit(solution)/shard_map/while/body/eval_jaxpr/...fi,...fj->...ij/dot_general | solution.py:24
  120.4 0.6 gather_fusion.4
  121.6 0.7 dynamic-slice_bitcast_fusion.12
  122.3 3.2 %fusion.46 = (f32[4,8,128]{2,1,0:T(8,128)S(1)}, f32[4,8,128,128]{3,2,1,0:T(8,128)S(1)}) fusion(f32[4,8,64,128]{3,2,1,0:T(8,128)S(1)} %bitcast.171, f32[4,4,64,128]{3,2,1,0:T(8,128)} %get-tuple-element.424, s32[]{:T(128)S(6)} %copy.39, f32[4,8,128]{2,1,0:T(8,128)S(1)} %bitcast.174, f32[4,128]{1,0:T(4,128)S(1)} %get-tuple-element.348, ...), kind=kOutput, calls=%fused_computation.76.clone.1 | convolution fusion | flops 406319104 | bytes 3315716 | tf_op jit(solution)/shard_map/while/body/eval_jaxpr/...fi,...fj->...ij/dot_general | solution.py:24
  126.1 0.6 gather_fusion.4
  127.3 0.7 dynamic-slice_bitcast_fusion.12
  128.0 3.2 %fusion.46 = (f32[4,8,128]{2,1,0:T(8,128)S(1)}, f32[4,8,128,128]{3,2,1,0:T(8,128)S(1)}) fusion(f32[4,8,64,128]{3,2,1,0:T(8,128)S(1)} %bitcast.171, f32[4,4,64,128]{3,2,1,0:T(8,128)} %get-tuple-element.424, s32[]{:T(128)S(6)} %copy.39, f32[4,8,128]{2,1,0:T(8,128)S(1)} %bitcast.174, f32[4,128]{1,0:T(4,128)S(1)} %get-tuple-element.348, ...), kind=kOutput, calls=%fused_computation.76.clone.1 | convolution fusion | flops 406319104 | bytes 3315716 | tf_op jit(solution)/shard_map/while/body/eval_jaxpr/...fi,...fj->...ij/dot_general | solution.py:24
  131.8 0.6 gather_fusion.4
  133.0 0.7 dynamic-slice_bitcast_fusion.12
  133.7 3.2 %fusion.46 = (f32[4,8,128]{2,1,0:T(8,128)S(1)}, f32[4,8,128,128]{3,2,1,0:T(8,128)S(1)}) fusion(f32[4,8,64,128]{3,2,1,0:T(8,128)S(1)} %bitcast.171, f32[4,4,64,128]{3,2,1,0:T(8,128)} %get-tuple-element.424, s32[]{:T(128)S(6)} %copy.39, f32[4,8,128]{2,1,0:T(8,128)S(1)} %bitcast.174, f32[4,128]{1,0:T(4,128)S(1)} %get-tuple-element.348, ...), kind=kOutput, calls=%fused_computation.76.clone.1 | convolution fusion | flops 406319104 | bytes 3315716 | tf_op jit(solution)/shard_map/while/body/eval_jaxpr/...fi,...fj->...ij/dot_general | solution.py:24
  137.3 1.1 scatter_custom_fusion
  138.5 0.6 gather_fusion.6
  139.1 1.1 scatter_custom_fusion.1
  140.3 19.0 %pmax.7 = f32[8,128]{1,0:T(8,128)S(1)} all-reduce(f32[8,128]{1,0:T(8,128)S(1)} %slice.26), channel_id=1, replica_groups=mesh['grp'=2,'src'=8,'tgt'=2] {'src'}, use_global_device_ids=true, to_apply=%region_11.12 | all-reduce | flops 1024 | bytes 8192 | tf_op jit(solution)/shard_map/pmax | solution.py:127
  159.2 17.3 %psum.7 = f32[8,128]{1,0:T(8,128)S(1)} all-reduce(f32[8,128]{1,0:T(8,128)S(1)} %slice_multiply_fusion), channel_id=1, replica_groups=mesh['grp'=2,'src'=8,'tgt'=2] {'src'}, use_global_device_ids=true, to_apply=%region_13.14 | all-reduce | flops 1024 | bytes 8192 | tf_op jit(solution)/shard_map/psum | solution.py:128
  (99 shorter events, 17.2 us)
Async XLA Ops:
  74.2 40.0 %copy-start = (s32[16,1]{0,1:T(1,128)S(1)}, s32[16,1]{0,1:T(1,128)}, u32[]{:S(2)}) copy-start(s32[16,1]{0,1:T(1,128)} %param.17) | copy-start | bytes 196
where the time goes:
time: 178 us; the launch traced here: 177 us
  blocking collectives  110 us (62%)
  matrix products  37.3 us (21%)
  local copies, waits for them, and re-layouts  19.9 us (11%)
  other arithmetic  9.11 us (5%)
    dot_general x8, matrix products, cost_tiles(): jnp.einsum('...fi,...fj->...ij', source_blk, target_blk, precision=lax.Pr...  37.3 us
    all_gather x1, blocking collectives, per_device(): lax.all_gather(target_feat, 'src', axis=0, tiled=True)  31 us
    all_gather x1, blocking collectives, per_device(): lax.all_gather(log_mass_tgt, 'src', axis=0, tiled=True)  22.3 us
    pmax x1, blocking collectives, per_device(): highest = lax.pmax(best, 'src')  19 us
    psum x1, blocking collectives, per_device(): whole = lax.psum(summed * jnp.exp(best - highest), 'src')  17.3 us
    all_gather x1, blocking collectives, per_device(): lax.all_gather(potential_tgt, 'src', axis=0, tiled=True)  16.4 us
    gather x8, local copies, waits for them, and re-layouts, row_pass(): return row_stats(cost, mass_all[ids_here], poten_all[ids_here], use_here)  4.59 us
    all_gather x2, blocking collectives, merged(): gathered = jax.tree.map(lambda a: lax.all_gather(a, axis), part)  3.61 us

commit v1 on v0

--- a/solution.py
+++ b/solution.py
@@ -1,12 +1,266 @@
+import functools
 import math
 
 import jax
 import jax.numpy as jnp
 from jax import lax
+from jax.experimental import pallas as pl
+from jax.experimental.pallas import tpu as pltpu
 from jax.sharding import PartitionSpec as P
 
 entropic = 0.5
 very_low = -1e30
+log2e = 1.0 / math.log(2.0)
+ln2 = math.log(2.0)
+least_sum = 1e-28
+
+VM = pl.BlockSpec(memory_space=pltpu.VMEM)
+PARAMS = pltpu.CompilerParams(vmem_limit_bytes=40 * 2**20)
+
+
+def in_vmem(shape, dtype):
+    return pltpu.VMEM(shape, dtype)
+
+
+def pieces(values):
+    high = values.astype(jnp.bfloat16).astype(jnp.float32)
+    rest = values - high
+    mid = rest.astype(jnp.bfloat16).astype(jnp.float32)
+    low = (rest - mid).astype(jnp.bfloat16).astype(jnp.float32)
+    return high, mid, low
+
+
+def target_weight(mass, poten):
+    return (mass + poten / entropic) * log2e
+
+
+def pack_kernel(feat_ref, mass_ref, poten_ref, out_ref):
+    feat = feat_ref[0]
+    depth = feat.shape[0]
+    weight = target_weight(mass_ref[...], poten_ref[...])
+    norm = jnp.sum(feat * feat, axis=0, keepdims=True)
+    bias = weight - (log2e / entropic) * norm
+    out_ref[:depth, :] = feat * (2.0 * log2e / entropic)
+    out_ref[depth:, :] = jnp.broadcast_to(bias, (out_ref.shape[0] - depth, feat.shape[1]))
+
+
+def source_kernel(shards, feat_ref, support_ref, counts_ref, wide_ref, norm_ref, mask_ref):
+    rows, depth, cells = feat_ref.shape
+    one = jnp.ones((2 * depth, 2 * cells), jnp.bfloat16)
+    for pair in range(rows // 2):
+        for half in range(2):
+            feat = feat_ref[2 * pair + half]
+            norm_ref[2 * pair + half : 2 * pair + half + 1, :] = jnp.sum(feat * feat, axis=0, keepdims=True)
+            high, mid, low = pieces(feat)
+            lanes = slice(half * cells, (half + 1) * cells)
+            top = jnp.concatenate([high, mid], axis=0).astype(jnp.bfloat16)
+            wide_ref[pair, 0 : 2 * depth, lanes] = top
+            wide_ref[pair, 2 * depth : 4 * depth, lanes] = top
+            wide_ref[pair, 4 * depth : 6 * depth, lanes] = jnp.concatenate([low, high], axis=0).astype(jnp.bfloat16)
+        wide_ref[pair, 6 * depth : 8 * depth, :] = one
+    support = support_ref[...]
+    used = lax.broadcasted_iota(jnp.int32, support.shape, 1) < counts_ref[...]
+    me = lax.axis_index("src")
+    for step in range(shards):
+        block = lax.rem(me + step, shards)
+        hit = jnp.where(used & (support == block), 0.0, very_low)
+        mask_ref[step] = jnp.broadcast_to(jnp.max(hit, axis=1, keepdims=True), (rows, cells))
+
+
+def row_kernel(shards, *refs):
+    packs = refs[:shards]
+    wide_ref, mask_ref, exps_ref, tall_ref, peak_ref, rowsum_ref, total_ref = refs[shards:]
+    pairs, _, both = wide_ref.shape
+    cells = both // 2
+    depth = cells // 2
+    lane = lax.broadcasted_iota(jnp.int32, (cells, cells), 1)
+    biases = jnp.concatenate([pack[depth : depth + 1, :] for pack in packs], axis=0)
+    bias_pieces = jnp.concatenate(list(pieces(biases)), axis=0)
+    padded = jnp.concatenate([bias_pieces, jnp.zeros((cells - 3 * shards, cells), jnp.float32)], axis=0)
+    bias_lanes = padded.T
+    for step, pack in enumerate(packs):
+        feat = pack[:depth, :]
+        turned = jnp.concatenate([feat, feat], axis=0).T
+        high, mid, low = pieces(turned)
+        own = jnp.where(lax.rem(lane, shards) == step, bias_lanes, 0.0)
+        rows = slice(step * cells, (step + 1) * cells)
+        tall_ref[rows, 0:cells] = high.astype(jnp.bfloat16)
+        tall_ref[rows, cells : 2 * cells] = mid.astype(jnp.bfloat16)
+        tall_ref[rows, 2 * cells : 3 * cells] = jnp.where(lane < depth, high, low).astype(jnp.bfloat16)
+        tall_ref[rows, 3 * cells : 4 * cells] = own.astype(jnp.bfloat16)
+
+    def body(pair, carry):
+        weights = wide_ref[pair]
+        for step in range(shards):
+            rows = slice(step * cells, (step + 1) * cells)
+            score = jnp.dot(tall_ref[rows, :], weights, preferred_element_type=jnp.float32)
+            peak = jnp.max(score, axis=0, keepdims=True)
+            exps = jnp.exp2(score - peak)
+            exps_ref[pair, rows, :] = exps
+            total = jnp.sum(exps, axis=0, keepdims=True)
+            for half in range(2):
+                lanes = slice(half * cells, (half + 1) * cells)
+                peak_ref[step, pl.ds(2 * pair + half, 1), :] = peak[:, lanes]
+                total_ref[step, pl.ds(2 * pair + half, 1), :] = total[:, lanes]
+        return carry
+
+    lax.fori_loop(0, pairs, body, 0)
+    masked = [peak_ref[step] + mask_ref[step] for step in range(shards)]
+    top = functools.reduce(jnp.maximum, masked)
+    summed = sum(total_ref[step] * jnp.exp2(masked[step] - top) for step in range(shards))
+    for step in range(shards):
+        peak_ref[step] = masked[step]
+    rowsum_ref[...] = top + jnp.log2(summed)
+
+
+def lane_sums(values):
+    ones = jnp.ones((8, values.shape[1]), jnp.bfloat16)
+    parts = [
+        lax.dot_general(ones, part.astype(jnp.bfloat16), (((1,), (1,)), ((), ())), preferred_element_type=jnp.float32)
+        for part in pieces(values)
+    ]
+    return sum(parts)[0:1, :]
+
+
+def column_kernel(shards, *refs):
+    ins, rest = refs[:9], refs[9:]
+    exps_ref, tall_ref, wide_ref, peak_ref, mask_ref, own_ref, other_ref, mass_ref, norm_ref = ins
+    poten_ref, outs = rest[0], rest[1 : 1 + shards]
+    weight_ref, acc_ref, shift_ref = rest[1 + shards :]
+    pairs, _, both = wide_ref.shape
+    cells = both // 2
+    own, other = own_ref[...], other_ref[...]
+    top = jnp.maximum(own, other)
+    whole = top + jnp.log2(jnp.exp2(own - top) + jnp.exp2(other - top))
+    poten_ref[...] = norm_ref[...] - (entropic * ln2) * whole
+    shift = mass_ref[...] * log2e - whole
+    shift_ref[...] = shift
+    for step in range(shards):
+        weight_ref[step] = jnp.exp2(peak_ref[step] + shift)
+    for step in range(shards):
+        rows = slice(step * cells, (step + 1) * cells)
+        acc = jnp.zeros((cells, cells), jnp.float32)
+        for pair in range(pairs):
+            acc = acc + exps_ref[pair, rows, :cells] * weight_ref[step, 2 * pair : 2 * pair + 1, :]
+            acc = acc + exps_ref[pair, rows, cells:] * weight_ref[step, 2 * pair + 1 : 2 * pair + 2, :]
+        acc_ref[rows, :] = acc
+    sums = lane_sums(acc_ref[...])
+    worst = jnp.full((1, cells), 1.0, jnp.float32)
+    for step in range(shards):
+        used = jnp.max(mask_ref[step], axis=0, keepdims=True) > 0.5 * very_low
+        here = sums[:, step * cells : (step + 1) * cells]
+        outs[step][...] = jnp.where(used, jnp.log2(here), very_low)
+        worst = jnp.minimum(worst, jnp.where(used, here, 1.0))
+
+    @pl.when(jnp.min(worst) < least_sum)
+    def _():
+        acc_ref[...] = jnp.full(acc_ref.shape, very_low, jnp.float32)
+
+        def exponents(pair, step):
+            score = jnp.dot(
+                tall_ref[pl.ds(pl.multiple_of(step * cells, cells), cells), :],
+                wide_ref[pair],
+                preferred_element_type=jnp.float32,
+            )
+            add = shift_ref[pl.ds(2 * pair, 2), :] + mask_ref[step, pl.ds(2 * pair, 2), :]
+            return score[:, :cells] + add[0:1, :], score[:, cells:] + add[1:2, :]
+
+        def highest(index, carry):
+            pair, step = index // shards, lax.rem(index, shards)
+            rows = pl.ds(pl.multiple_of(step * cells, cells), cells)
+            first, second = exponents(pair, step)
+            acc_ref[rows, :] = jnp.maximum(acc_ref[rows, :], jnp.maximum(first, second))
+            return carry
+
+        lax.fori_loop(0, pairs * shards, highest, 0)
+
+        def total(step, carry):
+            rows = pl.ds(pl.multiple_of(step * cells, cells), cells)
+            peak = jnp.max(acc_ref[rows, :], axis=1, keepdims=True)
+
+            def add(pair, sums):
+                first, second = exponents(pair, step)
+                return sums + jnp.exp2(first - peak) + jnp.exp2(second - peak)
+
+            sums = lax.fori_loop(0, pairs, add, jnp.zeros((cells, cells), jnp.float32))
+            along = jnp.broadcast_to(peak, (cells, cells)).T
+            acc_ref[rows, :] = along[0:1, :] + jnp.log2(lane_sums(sums)) + jnp.zeros((cells, 1), jnp.float32)
+            return carry
+
+        lax.fori_loop(0, shards, total, 0)
+        for step in range(shards):
+            used = jnp.max(mask_ref[step], axis=0, keepdims=True) > 0.5 * very_low
+            outs[step][...] = jnp.where(used, acc_ref[step * cells : step * cells + 1, :], very_low)
+
+
+def merge_kernel(shards, *refs):
+    parts, (mass_ref, poten_ref, out_ref) = refs[:shards], refs[shards:]
+    values = jnp.concatenate([part[...] for part in parts], axis=0)
+    top = jnp.max(values, axis=0, keepdims=True)
+    whole = top + jnp.log2(jnp.sum(jnp.exp2(values - top), axis=0, keepdims=True))
+    out_ref[...] = -(entropic * ln2) * (whole - target_weight(mass_ref[...], poten_ref[...]))
+
+
+def f32(*shape):
+    return jax.ShapeDtypeStruct(shape, jnp.float32)
+
+
+def dense_device(
+    source_feat, target_feat, log_mass_src, log_mass_tgt, potential_tgt, support, counts
+):
+    shards = lax.axis_size("src")
+    rows, depth, cells = source_feat.shape
+    pairs, wide = rows // 2, 2 * cells
+
+    def call(kernel, count, out_shape, scratch=()):
+        many = isinstance(out_shape, (list, tuple))
+        return pl.pallas_call(
+            kernel,
+            in_specs=[VM] * count,
+            out_specs=[VM] * len(out_shape) if many else VM,
+            out_shape=out_shape,
+            scratch_shapes=list(scratch),
+            compiler_params=PARAMS,
+        )
+
+    pack = call(pack_kernel, 3, f32(depth + 8, cells))(target_feat, log_mass_tgt, potential_tgt)
+
+    def shifted(array, step):
+        return lax.ppermute(array, "src", [(i, (i + step) % shards) for i in range(shards)])
+
+    packs = [pack] + [shifted(pack, shards - step) for step in range(1, shards)]
+    wide_feat, norm, mask = call(
+        functools.partial(source_kernel, shards),
+        3,
+        [in_vmem((pairs, 8 * depth, wide), jnp.bfloat16), f32(rows, cells), f32(shards, rows, cells)],
+    )(source_feat, support[:, 0, :], counts)
+    exps, tall, peaks, own = call(
+        functools.partial(row_kernel, shards),
+        shards + 2,
+        [
+            in_vmem((pairs, shards * cells, wide), jnp.float32),
+            in_vmem((shards * cells, 8 * depth), jnp.bfloat16),
+            f32(shards, rows, cells),
+            f32(rows, cells),
+        ],
+        [pltpu.VMEM((shards, rows, cells), jnp.float32)],
+    )(*packs, wide_feat, mask)
+    other = lax.ppermute(own, "tgt", [(0, 1), (1, 0)])
+    potential_src, *columns = call(
+        functools.partial(column_kernel, shards),
+        9,
+        [f32(rows, cells)] + [f32(1, cells)] * shards,
+        [
+            pltpu.VMEM((shards, rows, cells), jnp.float32),
+            pltpu.VMEM((shards * cells, cells), jnp.float32),
+            pltpu.VMEM((rows, cells), jnp.float32),
+        ],
+    )(exps, tall, wide_feat, peaks, mask, own, other, log_mass_src, norm)
+    arrived = [columns[0]] + [shifted(columns[step], step) for step in range(1, shards)]
+    potential_new = call(functools.partial(merge_kernel, shards), shards + 2, f32(1, cells))(
+        *arrived, log_mass_tgt, potential_tgt
+    )
+    return potential_src, potential_new
 
 
 def merged(part, axis, combine):
@@ -63,7 +317,7 @@
     return (best[:segments], summed[:segments])
 
 
-def per_device(
+def general_device(
     source_feat, target_feat, log_mass_src, log_mass_tgt, potential_tgt, support, counts
 ):
     target_all, mass_all, poten_all = (
@@ -132,6 +386,15 @@
     return (potential_src, potential_new)
 
 
+def per_device(source_feat, target_feat, *others):
+    shards = lax.axis_size("src")
+    rows, depth, cells = source_feat.shape
+    few = shards == 8 and target_feat.shape[0] == 1 and lax.axis_size("tgt") == 2
+    if few and rows % 2 == 0 and cells == 128 and depth == 64:
+        return dense_device(source_feat, target_feat, *others)
+    return general_device(source_feat, target_feat, *others)
+
+
 def solution(mesh):
     in_specs = (
         P(("grp", "src"), None, None),

time: 178 us -> 68.8 us (0.39)
  blocking collectives: 110 us -> 0 us
  matrix products: 37.3 us -> 0 us
  Pallas kernels: 0 us -> 35.1 us
  starting transfers between devices: 0 us -> 24 us
  local copies, waits for them, and re-layouts: 19.9 us -> 5.29 us
  other arithmetic: 9.11 us -> 0 us
  waiting for transfers between devices: 0 us -> 3.37 us
    all_gather x5 -> x0, blocking collectives: 73.3 us -> none  [the longest x1 31 us: per_device(): lax.all_gather(target_feat, 'src', axis=0, tiled=True)]
    dot_general x8 -> x0, matrix products: 37.3 us -> none  [cost_tiles(): jnp.einsum('...fi,...fj->...ij', source_blk, target_blk, precision=lax.Pr...]
    pallas_call x0 -> x5, Pallas kernels: none -> 35.1 us  [the longest x1 29.7 us: dense_device(): call(functools.partial(column_kernel, shards), 9, [f32(rows, cells)] + [f...]
    ppermute x0 -> x15, starting transfers between devices: none -> 24 us  [the longest x14 23.9 us: shifted(): lax.ppermute(array, 'src', [(i, (i + step) % shards) for i in range(shard...]
    pmax x1 -> x0, blocking collectives: 19 us -> none  [per_device(): highest = lax.pmax(best, 'src')]
    psum x1 -> x0, blocking collectives: 17.3 us -> none  [per_device(): whole = lax.psum(summed * jnp.exp(best - highest), 'src')]
    gather x25 -> x0, local copies, waits for them, and re-layouts: 14.8 us -> none  [the longest x8 4.59 us: row_pass(): return row_stats(cost, mass_all[ids_here], poten_all[ids_here], use_here)]
    reduce_sum x10 -> x0, other arithmetic: 3.79 us -> none  [the longest x4 1.49 us: column_stats(): total = jnp.sum(jnp.exp(scores - peak[:, :, None, :]), axis=2)]
  transfers between devices with their start and end apart: 0 -> 15, of which waited for: 0 -> 4; matrix products, arithmetic and copies ran while one was open for 0% -> 2% of each run, Pallas kernels for 0% -> 0%
where the time goes in v1:
time: 68.8 us; the launch traced here: 68.5 us
  Pallas kernels  35.1 us (51%)
  starting transfers between devices  24 us (35%)
  local copies, waits for them, and re-layouts  5.29 us (8%)
  waiting for transfers between devices  3.37 us (5%)
  between operations  0.72 us (1%)
    pallas_call x1, Pallas kernels, dense_device(): call(functools.partial(column_kernel, shards), 9, [f32(rows, cells)] + [f...  29.7 us
    ppermute x14, starting transfers between devices, shifted(): lax.ppermute(array, 'src', [(i, (i + step) % shards) for i in range(shard...  23.9 us
    unnamed x15, local copies, waits for them, and re-layouts  4.54 us
    pallas_call x1, Pallas kernels, dense_device(): call(functools.partial(row_kernel, shards), shards + 2, [in_vmem((pairs,...  4.48 us
    ppermute x14, waiting for transfers between devices, shifted(): lax.ppermute(array, 'src', [(i, (i + step) % shards) for i in range(shard...  2.21 us
  transfers between devices with their start and end apart: 15, of which 4 were waited for; matrix products, arithmetic and copies ran while one was open for 2% of the time, Pallas kernels for 0%

profile of v1, /device:TPU:0, one launch (start us, length us, event | category | flops | bytes accessed | tf_op | source)
XLA Modules:
  0.0 68.5 jit_solution(5880572115362478799)
XLA Ops:
  0.6 0.7 %copy-done.1 = f32[1,64,128]{2,1,0:T(8,128)S(1)} copy-done((f32[1,64,128]{2,1,0:T(8,128)S(1)}, f32[1,64,128]{2,1,0:T(8,128)}, u32[]{:S(2)}) %copy-start.1) | copy-done | bytes 32792
  1.4 0.7 copy-done.3
  2.0 0.7 copy-done.5
  2.7 3.0 %collective-permute-start.6 = (f32[72,128]{1,0:T(8,128)S(1)}, f32[72,128]{1,0:T(8,128)S(1)}, u32[]{:S(2)}, u32[]{:S(2)}) collective-permute-start(f32[72,128]{1,0:T(8,128)S(1)} %shard_map.86.refs_0_), channel_id=1, source_target_pairs={{0,2},{2,4},{4,6},{6,8},{8,10},{10,12},{12,14},{14,0},{1,3},{3,5},... | collective-permute-start | bytes 110600 | tf_op jit(solution)/shard_map/ppermute | solution.py:229
  5.7 1.6 %collective-permute-start.5 = (f32[72,128]{1,0:T(8,128)S(1)}, f32[72,128]{1,0:T(8,128)S(1)}, u32[]{:S(2)}, u32[]{:S(2)}) collective-permute-start(f32[72,128]{1,0:T(8,128)S(1)} %shard_map.86.refs_0_), channel_id=1, source_target_pairs={{0,4},{2,6},{4,8},{6,10},{8,12},{10,14},{12,0},{14,2},{1,5},{3,7},... | collective-permute-start | bytes 110600 | tf_op jit(solution)/shard_map/ppermute | solution.py:229
  7.3 2.6 %collective-permute-start.4 = (f32[72,128]{1,0:T(8,128)S(1)}, f32[72,128]{1,0:T(8,128)S(1)}, u32[]{:S(2)}, u32[]{:S(2)}) collective-permute-start(f32[72,128]{1,0:T(8,128)S(1)} %shard_map.86.refs_0_), channel_id=1, source_target_pairs={{0,6},{2,8},{4,10},{6,12},{8,14},{10,0},{12,2},{14,4},{1,7},{3,9},... | collective-permute-start | bytes 110600 | tf_op jit(solution)/shard_map/ppermute | solution.py:229
  9.9 1.2 %collective-permute-start.3 = (f32[72,128]{1,0:T(8,128)S(1)}, f32[72,128]{1,0:T(8,128)S(1)}, u32[]{:S(2)}, u32[]{:S(2)}) collective-permute-start(f32[72,128]{1,0:T(8,128)S(1)} %shard_map.86.refs_0_), channel_id=1, source_target_pairs={{0,8},{2,10},{4,12},{6,14},{8,0},{10,2},{12,4},{14,6},{1,9},{3,11}... | collective-permute-start | bytes 110600 | tf_op jit(solution)/shard_map/ppermute | solution.py:229
  11.1 2.6 %collective-permute-start.2 = (f32[72,128]{1,0:T(8,128)S(1)}, f32[72,128]{1,0:T(8,128)S(1)}, u32[]{:S(2)}, u32[]{:S(2)}) collective-permute-start(f32[72,128]{1,0:T(8,128)S(1)} %shard_map.86.refs_0_), channel_id=1, source_target_pairs={{0,10},{2,12},{4,14},{6,0},{8,2},{10,4},{12,6},{14,8},{1,11},{3,13... | collective-permute-start | bytes 110600 | tf_op jit(solution)/shard_map/ppermute | solution.py:229
  13.7 1.3 %collective-permute-start.1 = (f32[72,128]{1,0:T(8,128)S(1)}, f32[72,128]{1,0:T(8,128)S(1)}, u32[]{:S(2)}, u32[]{:S(2)}) collective-permute-start(f32[72,128]{1,0:T(8,128)S(1)} %shard_map.86.refs_0_), channel_id=1, source_target_pairs={{0,12},{2,14},{4,0},{6,2},{8,4},{10,6},{12,8},{14,10},{1,13},{3,15... | collective-permute-start | bytes 110600 | tf_op jit(solution)/shard_map/ppermute | solution.py:229
  15.1 0.0 collective-permute-done.5.refs_6_
  15.1 1.4 %collective-permute-start = (f32[72,128]{1,0:T(8,128)S(1)}, f32[72,128]{1,0:T(8,128)S(1)}, u32[]{:S(2)}, u32[]{:S(2)}) collective-permute-start(f32[72,128]{1,0:T(8,128)S(1)} %shard_map.86.refs_0_), channel_id=1, source_target_pairs={{0,14},{2,0},{4,2},{6,4},{8,6},{10,8},{12,10},{14,12},{1,15},{3,1}... | collective-permute-start | bytes 110600 | tf_op jit(solution)/shard_map/ppermute | solution.py:229
  16.5 0.8 %copy.9.support_ref = s32[16,8]{1,0:T(8,128)S(1)} copy(s32[16,8]{0,1:T(8,128)} %bitcast.1) | data formatting | bytes 1024 | tf_op jit(solution)/shard_map/squeeze | solution.py:236
  17.3 0.7 %copy.10.counts_ref = s32[16,1]{1,0:T(8,128)S(1)} copy(s32[16,1]{0,1:T(1,128)} %param.13) | data formatting | bytes 128 | tf_op args[6]
  18.0 1.0 %copy-done = f32[16,64,128]{2,1,0:T(8,128)S(1)} copy-done((f32[16,64,128]{2,1,0:T(8,128)S(1)}, f32[16,64,128]{2,1,0:T(8,128)}, u32[]{:S(2)}) %copy-start) | copy-done | bytes 524312
  19.0 0.3 shard_map.87
  19.4 0.0 collective-permute-done.3.refs_4_
  19.4 4.5 %shard_map.88 = (f32[8,1024,256]{2,1,0:T(8,128)S(1)}, bf16[1024,512]{1,0:T(8,128)(2,1)S(1)}, f32[8,16,128]{2,1,0:T(8,128)S(1)}, f32[16,128]{1,0:T(8,128)S(1)}) custom-call(f32[72,128]{1,0:T(8,128)S(1)} %shard_map.86.refs_0_, f32[72,128]{1,0:T(8,128)S(1)} %collective-permute-done.refs_1_, f32[72,128]{1,0:T(8,128)S(1)} %collective-permute-done.1.refs_2_, ...), custom_call_target="tpu_custom_call" | custom-call | tf_op jit(solution)/shard_map/pallas_call | solution.py:237
  23.9 0.1 collective-permute-start.7
  24.0 1.2 %collective-permute-done.7.refs_6_ = f32[16,128]{1,0:T(8,128)S(1)} collective-permute-done((f32[16,128]{1,0:T(8,128)S(1)}, f32[16,128]{1,0:T(8,128)S(1)}, u32[]{:S(2)}, u32[]{:S(2)}) %collective-permute-start.7) | collective-permute-done | bytes 8224 | tf_op jit(solution)/shard_map/ppermute | solution.py:248
  25.2 0.7 %copy-done.2 = f32[16,128]{1,0:T(8,128)S(1)} copy-done((f32[16,128]{1,0:T(8,128)S(1)}, f32[16,128]{1,0:T(8,128)}, u32[]{:S(2)}) %copy-start.2) | copy-done | bytes 8216
  25.8 29.7 %shard_map.89 = (f32[16,128]{1,0:T(8,128)}, f32[1,128]{1,0:T(1,128)S(1)}, f32[1,128]{1,0:T(1,128)S(1)}, f32[1,128]{1,0:T(1,128)S(1)}, f32[1,128]{1,0:T(1,128)S(1...) custom-call(f32[8,1024,256]{2,1,0:T(8,128)S(1)} %get-tuple-element.20.refs_0_, ...), custom_call_target="tpu_custom_call" | custom-call | tf_op jit(solution)/shard_map/pallas_call | solution.py:249
  55.6 1.1 %collective-permute-start.8 = (f32[1,128]{1,0:T(1,128)S(1)}, f32[1,128]{1,0:T(1,128)S(1)}, u32[]{:S(2)}, u32[]{:S(2)}) collective-permute-start(f32[1,128]{1,0:T(1,128)S(1)} %get-tuple-element.27), channel_id=1, source_target_pairs={{0,2},{2,4},{4,6},{6,8},{8,10},{10,12},{12,14},{14,0},{1,3},{3,5},... | collective-permute-start | bytes 1544 | tf_op jit(solution)/shard_map/ppermute | solution.py:229
  56.7 0.1 collective-permute-start.9
  56.9 2.1 %collective-permute-start.10 = (f32[1,128]{1,0:T(1,128)S(1)}, f32[1,128]{1,0:T(1,128)S(1)}, u32[]{:S(2)}, u32[]{:S(2)}) collective-permute-start(f32[1,128]{1,0:T(1,128)S(1)} %get-tuple-element.29), channel_id=1, source_target_pairs={{0,6},{2,8},{4,10},{6,12},{8,14},{10,0},{12,2},{14,4},{1,7},{3,9},... | collective-permute-start | bytes 1544 | tf_op jit(solution)/shard_map/ppermute | solution.py:229
  59.0 2.5 %collective-permute-start.11 = (f32[1,128]{1,0:T(1,128)S(1)}, f32[1,128]{1,0:T(1,128)S(1)}, u32[]{:S(2)}, u32[]{:S(2)}) collective-permute-start(f32[1,128]{1,0:T(1,128)S(1)} %get-tuple-element.30), channel_id=1, source_target_pairs={{0,8},{2,10},{4,12},{6,14},{8,0},{10,2},{12,4},{14,6},{1,9},{3,11}... | collective-permute-start | bytes 1544 | tf_op jit(solution)/shard_map/ppermute | solution.py:229
  61.5 2.7 %collective-permute-start.12 = (f32[1,128]{1,0:T(1,128)S(1)}, f32[1,128]{1,0:T(1,128)S(1)}, u32[]{:S(2)}, u32[]{:S(2)}) collective-permute-start(f32[1,128]{1,0:T(1,128)S(1)} %get-tuple-element.31), channel_id=1, source_target_pairs={{0,10},{2,12},{4,14},{6,0},{8,2},{10,4},{12,6},{14,8},{1,11},{3,13... | collective-permute-start | bytes 1544 | tf_op jit(solution)/shard_map/ppermute | solution.py:229
  64.3 0.1 collective-permute-start.13
  64.4 1.4 %collective-permute-start.14 = (f32[1,128]{1,0:T(1,128)S(1)}, f32[1,128]{1,0:T(1,128)S(1)}, u32[]{:S(2)}, u32[]{:S(2)}) collective-permute-start(f32[1,128]{1,0:T(1,128)S(1)} %get-tuple-element.33), channel_id=1, source_target_pairs={{0,14},{2,0},{4,2},{6,4},{8,6},{10,8},{12,10},{14,12},{1,15},{3,1}... | collective-permute-start | bytes 1544 | tf_op jit(solution)/shard_map/ppermute | solution.py:229
  65.8 0.2 collective-permute-done.12.refs_5_
  66.0 1.8 %collective-permute-done.13.refs_6_ = f32[1,128]{1,0:T(1,128)S(1)} collective-permute-done((f32[1,128]{1,0:T(1,128)S(1)}, f32[1,128]{1,0:T(1,128)S(1)}, u32[]{:S(2)}, u32[]{:S(2)}) %collective-permute-start.13) | collective-permute-done | bytes 544 | tf_op jit(solution)/shard_map/ppermute | solution.py:229
  67.8 0.1 collective-permute-done.14.refs_7_
  67.9 0.5 shard_map.90
  (19 shorter events, 0.1 us)
Async XLA Ops:
  0.6 0.8 %copy-start.1 = (f32[1,64,128]{2,1,0:T(8,128)S(1)}, f32[1,64,128]{2,1,0:T(8,128)}, u32[]{:S(2)}) copy-start(f32[1,64,128]{2,1,0:T(8,128)} %feat_ref.2) | copy-start | bytes 98308
  1.4 0.7 copy-start.3
  2.0 0.7 copy-start.5
  2.7 65.2 %copy-start.4 = (f32[1,128]{1,0:T(1,128)S(1)}, f32[1,128]{1,0:T(1,128)}, u32[]{:S(2)}) copy-start(f32[1,128]{1,0:T(1,128)} %refs_8_.1) | copy-start | bytes 1540
  2.7 65.2 %copy-start.6 = (f32[1,128]{1,0:T(1,128)S(1)}, f32[1,128]{1,0:T(1,128)}, u32[]{:S(2)}) copy-start(f32[1,128]{1,0:T(1,128)} %refs_9_.1) | copy-start | bytes 1540
  2.7 11.0 %collective-permute-start.6 = (f32[72,128]{1,0:T(8,128)S(1)}, f32[72,128]{1,0:T(8,128)S(1)}, u32[]{:S(2)}, u32[]{:S(2)}) collective-permute-start(f32[72,128]{1,0:T(8,128)S(1)} %shard_map.86.refs_0_), channel_id=1, source_target_pairs={{0,2},{2,4},{4,6},{6,8},{8,10},{10,12},{12,14},{14,0},{1,3},{3,5},... | collective-permute-start | bytes 110600 | tf_op jit(solution)/shard_map/ppermute | solution.py:229
  5.7 9.3 %collective-permute-start.5 = (f32[72,128]{1,0:T(8,128)S(1)}, f32[72,128]{1,0:T(8,128)S(1)}, u32[]{:S(2)}, u32[]{:S(2)}) collective-permute-start(f32[72,128]{1,0:T(8,128)S(1)} %shard_map.86.refs_0_), channel_id=1, source_target_pairs={{0,4},{2,6},{4,8},{6,10},{8,12},{10,14},{12,0},{14,2},{1,5},{3,7},... | collective-permute-start | bytes 110600 | tf_op jit(solution)/shard_map/ppermute | solution.py:229
  7.3 12.1 %collective-permute-start.4 = (f32[72,128]{1,0:T(8,128)S(1)}, f32[72,128]{1,0:T(8,128)S(1)}, u32[]{:S(2)}, u32[]{:S(2)}) collective-permute-start(f32[72,128]{1,0:T(8,128)S(1)} %shard_map.86.refs_0_), channel_id=1, source_target_pairs={{0,6},{2,8},{4,10},{6,12},{8,14},{10,0},{12,2},{14,4},{1,7},{3,9},... | collective-permute-start | bytes 110600 | tf_op jit(solution)/shard_map/ppermute | solution.py:229
  9.9 9.5 %collective-permute-start.3 = (f32[72,128]{1,0:T(8,128)S(1)}, f32[72,128]{1,0:T(8,128)S(1)}, u32[]{:S(2)}, u32[]{:S(2)}) collective-permute-start(f32[72,128]{1,0:T(8,128)S(1)} %shard_map.86.refs_0_), channel_id=1, source_target_pairs={{0,8},{2,10},{4,12},{6,14},{8,0},{10,2},{12,4},{14,6},{1,9},{3,11}... | collective-permute-start | bytes 110600 | tf_op jit(solution)/shard_map/ppermute | solution.py:229
  11.1 8.3 %collective-permute-start.2 = (f32[72,128]{1,0:T(8,128)S(1)}, f32[72,128]{1,0:T(8,128)S(1)}, u32[]{:S(2)}, u32[]{:S(2)}) collective-permute-start(f32[72,128]{1,0:T(8,128)S(1)} %shard_map.86.refs_0_), channel_id=1, source_target_pairs={{0,10},{2,12},{4,14},{6,0},{8,2},{10,4},{12,6},{14,8},{1,11},{3,13... | collective-permute-start | bytes 110600 | tf_op jit(solution)/shard_map/ppermute | solution.py:229
  13.7 5.7 %collective-permute-start.1 = (f32[72,128]{1,0:T(8,128)S(1)}, f32[72,128]{1,0:T(8,128)S(1)}, u32[]{:S(2)}, u32[]{:S(2)}) collective-permute-start(f32[72,128]{1,0:T(8,128)S(1)} %shard_map.86.refs_0_), channel_id=1, source_target_pairs={{0,12},{2,14},{4,0},{6,2},{8,4},{10,6},{12,8},{14,10},{1,13},{3,15... | collective-permute-start | bytes 110600 | tf_op jit(solution)/shard_map/ppermute | solution.py:229
  15.1 4.4 %collective-permute-start = (f32[72,128]{1,0:T(8,128)S(1)}, f32[72,128]{1,0:T(8,128)S(1)}, u32[]{:S(2)}, u32[]{:S(2)}) collective-permute-start(f32[72,128]{1,0:T(8,128)S(1)} %shard_map.86.refs_0_), channel_id=1, source_target_pairs={{0,14},{2,0},{4,2},{6,4},{8,6},{10,8},{12,10},{14,12},{1,15},{3,1}... | collective-permute-start | bytes 110600 | tf_op jit(solution)/shard_map/ppermute | solution.py:229
  18.0 1.0 %copy-start = (f32[16,64,128]{2,1,0:T(8,128)S(1)}, f32[16,64,128]{2,1,0:T(8,128)}, u32[]{:S(2)}) copy-start(f32[16,64,128]{2,1,0:T(8,128)} %feat_ref.3) | copy-start | bytes 1572868
  23.9 1.2 %collective-permute-start.7 = (f32[16,128]{1,0:T(8,128)S(1)}, f32[16,128]{1,0:T(8,128)S(1)}, u32[]{:S(2)}, u32[]{:S(2)}) collective-permute-start(f32[16,128]{1,0:T(8,128)S(1)} %get-tuple-element.23.refs_5_), channel_id=1, source_target_pairs={{0,1},{1,0},{2,3},{3,2},{4,5},{5,4},{6,7},{7,6},{8,9},{9,8},{10,11... | collective-permute-start | bytes 24584 | tf_op jit(solution)/shard_map/ppermute | solution.py:248
  25.1 0.7 %copy-start.2 = (f32[16,128]{1,0:T(8,128)S(1)}, f32[16,128]{1,0:T(8,128)}, u32[]{:S(2)}) copy-start(f32[16,128]{1,0:T(8,128)} %refs_7_.1) | copy-start | bytes 24580
  55.6 8.7 %collective-permute-start.8 = (f32[1,128]{1,0:T(1,128)S(1)}, f32[1,128]{1,0:T(1,128)S(1)}, u32[]{:S(2)}, u32[]{:S(2)}) collective-permute-start(f32[1,128]{1,0:T(1,128)S(1)} %get-tuple-element.27), channel_id=1, source_target_pairs={{0,2},{2,4},{4,6},{6,8},{8,10},{10,12},{12,14},{14,0},{1,3},{3,5},... | collective-permute-start | bytes 1544 | tf_op jit(solution)/shard_map/ppermute | solution.py:229
  56.7 7.7 %collective-permute-start.9 = (f32[1,128]{1,0:T(1,128)S(1)}, f32[1,128]{1,0:T(1,128)S(1)}, u32[]{:S(2)}, u32[]{:S(2)}) collective-permute-start(f32[1,128]{1,0:T(1,128)S(1)} %get-tuple-element.28), channel_id=1, source_target_pairs={{0,4},{2,6},{4,8},{6,10},{8,12},{10,14},{12,0},{14,2},{1,5},{3,7},... | collective-permute-start | bytes 1544 | tf_op jit(solution)/shard_map/ppermute | solution.py:229
  56.9 8.9 %collective-permute-start.10 = (f32[1,128]{1,0:T(1,128)S(1)}, f32[1,128]{1,0:T(1,128)S(1)}, u32[]{:S(2)}, u32[]{:S(2)}) collective-permute-start(f32[1,128]{1,0:T(1,128)S(1)} %get-tuple-element.29), channel_id=1, source_target_pairs={{0,6},{2,8},{4,10},{6,12},{8,14},{10,0},{12,2},{14,4},{1,7},{3,9},... | collective-permute-start | bytes 1544 | tf_op jit(solution)/shard_map/ppermute | solution.py:229
  59.0 6.8 %collective-permute-start.11 = (f32[1,128]{1,0:T(1,128)S(1)}, f32[1,128]{1,0:T(1,128)S(1)}, u32[]{:S(2)}, u32[]{:S(2)}) collective-permute-start(f32[1,128]{1,0:T(1,128)S(1)} %get-tuple-element.30), channel_id=1, source_target_pairs={{0,8},{2,10},{4,12},{6,14},{8,0},{10,2},{12,4},{14,6},{1,9},{3,11}... | collective-permute-start | bytes 1544 | tf_op jit(solution)/shard_map/ppermute | solution.py:229
  61.5 4.4 %collective-permute-start.12 = (f32[1,128]{1,0:T(1,128)S(1)}, f32[1,128]{1,0:T(1,128)S(1)}, u32[]{:S(2)}, u32[]{:S(2)}) collective-permute-start(f32[1,128]{1,0:T(1,128)S(1)} %get-tuple-element.31), channel_id=1, source_target_pairs={{0,10},{2,12},{4,14},{6,0},{8,2},{10,4},{12,6},{14,8},{1,11},{3,13... | collective-permute-start | bytes 1544 | tf_op jit(solution)/shard_map/ppermute | solution.py:229
  64.3 3.5 %collective-permute-start.13 = (f32[1,128]{1,0:T(1,128)S(1)}, f32[1,128]{1,0:T(1,128)S(1)}, u32[]{:S(2)}, u32[]{:S(2)}) collective-permute-start(f32[1,128]{1,0:T(1,128)S(1)} %get-tuple-element.32), channel_id=1, source_target_pairs={{0,12},{2,14},{4,0},{6,2},{8,4},{10,6},{12,8},{14,10},{1,13},{3,15... | collective-permute-start | bytes 1544 | tf_op jit(solution)/shard_map/ppermute | solution.py:229
  64.4 3.5 %collective-permute-start.14 = (f32[1,128]{1,0:T(1,128)S(1)}, f32[1,128]{1,0:T(1,128)S(1)}, u32[]{:S(2)}, u32[]{:S(2)}) collective-permute-start(f32[1,128]{1,0:T(1,128)S(1)} %get-tuple-element.33), channel_id=1, source_target_pairs={{0,14},{2,0},{4,2},{6,4},{8,6},{10,8},{12,10},{14,12},{1,15},{3,1}... | collective-permute-start | bytes 1544 | tf_op jit(solution)/shard_map/ppermute | solution.py:229

commit v2 on v1

--- a/solution.py
+++ b/solution.py
@@ -34,18 +34,39 @@
     return (mass + poten / entropic) * log2e
 
 
-def pack_kernel(feat_ref, mass_ref, poten_ref, out_ref):
-    feat = feat_ref[0]
-    depth = feat.shape[0]
-    weight = target_weight(mass_ref[...], poten_ref[...])
-    norm = jnp.sum(feat * feat, axis=0, keepdims=True)
+def entry_kernel(shards, *refs):
+    hbm, outs, held, sems = refs[:7], refs[7:13], refs[13:20], refs[20]
+    send_ref, wide_ref, norm_ref, mask_ref, own_ref, mass_out_ref = outs
+    feat_ref, target_ref, mass_ref, tmass_ref, tpoten_ref, support_ref, counts_ref = held
+    copies = [pltpu.make_async_copy(src, dst, sems.at[i]) for i, (src, dst) in enumerate(zip(hbm, held))]
+    for copy in copies[1:] + copies[:1]:
+        copy.start()
+    for copy in copies[1:]:
+        copy.wait()
+    target = target_ref[0]
+    depth, cells = target.shape
+    weight = target_weight(tmass_ref[...], tpoten_ref[...])
+    norm = jnp.sum(target * target, axis=0, keepdims=True)
     bias = weight - (log2e / entropic) * norm
-    out_ref[:depth, :] = feat * (2.0 * log2e / entropic)
-    out_ref[depth:, :] = jnp.broadcast_to(bias, (out_ref.shape[0] - depth, feat.shape[1]))
-
-
-def source_kernel(shards, feat_ref, support_ref, counts_ref, wide_ref, norm_ref, mask_ref):
-    rows, depth, cells = feat_ref.shape
+    scaled = target * (2.0 * log2e / entropic)
+    below = jnp.broadcast_to(bias, (send_ref.shape[1] - depth, cells))
+    for step in range(shards):
+        send_ref[step, :depth, :] = scaled
+        send_ref[step, depth:, :] = below
+    own_ref[...] = weight
+    mass_out_ref[...] = mass_ref[...]
+    support = support_ref[...]
+    slots, rows = support.shape
+    used = lax.broadcasted_iota(jnp.int32, support.shape, 0) < counts_ref[...]
+    hits = [
+        jnp.max(jnp.where(used & (support == block), 0.0, very_low), axis=0, keepdims=True)
+        for block in range(shards)
+    ]
+    hits = jnp.concatenate(hits + [jnp.zeros((cells - shards, rows), jnp.float32)], axis=0)
+    hits = jnp.concatenate([hits, jnp.zeros((cells, cells - rows), jnp.float32)], axis=1).T
+    for block in range(shards):
+        mask_ref[block] = jnp.broadcast_to(hits[:rows, block : block + 1], (rows, cells))
+    copies[0].wait()
     one = jnp.ones((2 * depth, 2 * cells), jnp.bfloat16)
     for pair in range(rows // 2):
         for half in range(2):
@@ -58,18 +79,11 @@
             wide_ref[pair, 2 * depth : 4 * depth, lanes] = top
             wide_ref[pair, 4 * depth : 6 * depth, lanes] = jnp.concatenate([low, high], axis=0).astype(jnp.bfloat16)
         wide_ref[pair, 6 * depth : 8 * depth, :] = one
-    support = support_ref[...]
-    used = lax.broadcasted_iota(jnp.int32, support.shape, 1) < counts_ref[...]
-    me = lax.axis_index("src")
-    for step in range(shards):
-        block = lax.rem(me + step, shards)
-        hit = jnp.where(used & (support == block), 0.0, very_low)
-        mask_ref[step] = jnp.broadcast_to(jnp.max(hit, axis=1, keepdims=True), (rows, cells))
 
 
 def row_kernel(shards, *refs):
-    packs = refs[:shards]
-    wide_ref, mask_ref, exps_ref, tall_ref, peak_ref, rowsum_ref, total_ref = refs[shards:]
+    packs_ref, wide_ref, mask_ref, exps_ref, tall_ref, peak_ref, rowsum_ref, total_ref = refs
+    packs = [packs_ref.at[step] for step in range(shards)]
     pairs, _, both = wide_ref.shape
     cells = both // 2
     depth = cells // 2
@@ -125,8 +139,7 @@
 def column_kernel(shards, *refs):
     ins, rest = refs[:9], refs[9:]
     exps_ref, tall_ref, wide_ref, peak_ref, mask_ref, own_ref, other_ref, mass_ref, norm_ref = ins
-    poten_ref, outs = rest[0], rest[1 : 1 + shards]
-    weight_ref, acc_ref, shift_ref = rest[1 + shards :]
+    poten_ref, sums_ref, weight_ref, acc_ref, shift_ref = rest
     pairs, _, both = wide_ref.shape
     cells = both // 2
     own, other = own_ref[...], other_ref[...]
@@ -149,7 +162,7 @@
     for step in range(shards):
         used = jnp.max(mask_ref[step], axis=0, keepdims=True) > 0.5 * very_low
         here = sums[:, step * cells : (step + 1) * cells]
-        outs[step][...] = jnp.where(used, jnp.log2(here), very_low)
+        sums_ref[step] = jnp.where(used, jnp.log2(here), very_low)
         worst = jnp.minimum(worst, jnp.where(used, here, 1.0))
 
     @pl.when(jnp.min(worst) < least_sum)
@@ -190,15 +203,14 @@
         lax.fori_loop(0, shards, total, 0)
         for step in range(shards):
             used = jnp.max(mask_ref[step], axis=0, keepdims=True) > 0.5 * very_low
-            outs[step][...] = jnp.where(used, acc_ref[step * cells : step * cells + 1, :], very_low)
-
-
-def merge_kernel(shards, *refs):
-    parts, (mass_ref, poten_ref, out_ref) = refs[:shards], refs[shards:]
-    values = jnp.concatenate([part[...] for part in parts], axis=0)
-    top = jnp.max(values, axis=0, keepdims=True)
-    whole = top + jnp.log2(jnp.sum(jnp.exp2(values - top), axis=0, keepdims=True))
-    out_ref[...] = -(entropic * ln2) * (whole - target_weight(mass_ref[...], poten_ref[...]))
+            sums_ref[step] = jnp.where(used, acc_ref[step * cells : step * cells + 1, :], very_low)
+
+
+def merge_kernel(values_ref, weight_ref, out_ref):
+    values = values_ref[...]
+    top = jnp.max(values, axis=0)
+    whole = top + jnp.log2(jnp.sum(jnp.exp2(values - top), axis=0))
+    out_ref[...] = -(entropic * ln2) * (whole - weight_ref[...])
 
 
 def f32(*shape):
@@ -212,54 +224,57 @@
     rows, depth, cells = source_feat.shape
     pairs, wide = rows // 2, 2 * cells
 
-    def call(kernel, count, out_shape, scratch=()):
-        many = isinstance(out_shape, (list, tuple))
+    def call(kernel, ins, out_shape, scratch=()):
+        many = isinstance(out_shape, list)
         return pl.pallas_call(
             kernel,
-            in_specs=[VM] * count,
+            in_specs=ins,
             out_specs=[VM] * len(out_shape) if many else VM,
             out_shape=out_shape,
             scratch_shapes=list(scratch),
             compiler_params=PARAMS,
         )
 
-    pack = call(pack_kernel, 3, f32(depth + 8, cells))(target_feat, log_mass_tgt, potential_tgt)
-
-    def shifted(array, step):
-        return lax.ppermute(array, "src", [(i, (i + step) % shards) for i in range(shards)])
-
-    packs = [pack] + [shifted(pack, shards - step) for step in range(1, shards)]
-    wide_feat, norm, mask = call(
-        functools.partial(source_kernel, shards),
-        3,
-        [in_vmem((pairs, 8 * depth, wide), jnp.bfloat16), f32(rows, cells), f32(shards, rows, cells)],
-    )(source_feat, support[:, 0, :], counts)
+    args = [source_feat, target_feat, log_mass_src, log_mass_tgt, potential_tgt, support[:, 0, :].T, counts.T]
+    args = [pltpu.with_memory_space_constraint(arg, pltpu.HBM) for arg in args]
+    send, wide_feat, norm, mask, weight, mass = call(
+        functools.partial(entry_kernel, shards),
+        [pl.BlockSpec(memory_space=pltpu.HBM)] * len(args),
+        [
+            in_vmem((shards, depth + 8, cells), jnp.float32),
+            in_vmem((pairs, 8 * depth, wide), jnp.bfloat16),
+            in_vmem((rows, cells), jnp.float32),
+            in_vmem((shards, rows, cells), jnp.float32),
+            in_vmem((1, cells), jnp.float32),
+            in_vmem((rows, cells), jnp.float32),
+        ],
+        [pltpu.VMEM(arg.shape, arg.dtype) for arg in args] + [pltpu.SemaphoreType.DMA((len(args),))],
+    )(*args)
+    packs = lax.all_to_all(send, "src", 0, 0)
     exps, tall, peaks, own = call(
         functools.partial(row_kernel, shards),
-        shards + 2,
+        [VM] * 3,
         [
             in_vmem((pairs, shards * cells, wide), jnp.float32),
             in_vmem((shards * cells, 8 * depth), jnp.bfloat16),
-            f32(shards, rows, cells),
-            f32(rows, cells),
+            in_vmem((shards, rows, cells), jnp.float32),
+            in_vmem((rows, cells), jnp.float32),
         ],
         [pltpu.VMEM((shards, rows, cells), jnp.float32)],
-    )(*packs, wide_feat, mask)
+    )(packs, wide_feat, mask)
     other = lax.ppermute(own, "tgt", [(0, 1), (1, 0)])
-    potential_src, *columns = call(
+    potential_src, columns = call(
         functools.partial(column_kernel, shards),
-        9,
-        [f32(rows, cells)] + [f32(1, cells)] * shards,
+        [VM] * 9,
+        [f32(rows, cells), in_vmem((shards, 1, cells), jnp.float32)],
         [
             pltpu.VMEM((shards, rows, cells), jnp.float32),
             pltpu.VMEM((shards * cells, cells), jnp.float32),
             pltpu.VMEM((rows, cells), jnp.float32),
         ],
-    )(exps, tall, wide_feat, peaks, mask, own, other, log_mass_src, norm)
-    arrived = [columns[0]] + [shifted(columns[step], step) for step in range(1, shards)]
-    potential_new = call(functools.partial(merge_kernel, shards), shards + 2, f32(1, cells))(
-        *arrived, log_mass_tgt, potential_tgt
-    )
+    )(exps, tall, wide_feat, peaks, mask, own, other, mass, norm)
+    arrived = lax.all_to_all(columns, "src", 0, 0)
+    potential_new = call(merge_kernel, [VM] * 2, f32(1, cells))(arrived, weight)
     return potential_src, potential_new
 
 

time: 68.8 us -> 64.7 us (0.940)
  blocking collectives: 0 us -> 26.5 us
  starting transfers between devices: 24 us -> 0.07 us
  local copies, waits for them, and re-layouts: 5.29 us -> 0 us
  waiting for transfers between devices: 3.37 us -> 1.16 us
  Pallas kernels: 35.1 us -> 36.2 us
    all_to_all x0 -> x2, blocking collectives: none -> 26.5 us  [the longest x1 17.4 us: dense_device(): packs = lax.all_to_all(send, 'src', 0, 0)]
    ppermute x14 -> x0, starting transfers between devices: 23.9 us -> none  [shifted(): lax.ppermute(array, 'src', [(i, (i + step) % shards) for i in range(shard...]
    unnamed x15 -> x0, local copies, waits for them, and re-layouts: 4.54 us -> none
    ppermute x14 -> x0, waiting for transfers between devices: 2.21 us -> none  [shifted(): lax.ppermute(array, 'src', [(i, (i + step) % shards) for i in range(shard...]
    pallas_call x5 -> x4, Pallas kernels: 35.1 us -> 36.2 us  [the longest x1 29.7 us: dense_device(): call(functools.partial(column_kernel, shards), [VM] * 9, [f32(rows, cells...]
    squeeze x1 -> x0, local copies, waits for them, and re-layouts: 0.76 us -> none  [dense_device(): support[:, 0, :]]
  transfers between devices with their start and end apart: 15 -> 1, of which waited for: 4 -> 1; matrix products, arithmetic and copies ran while one was open for 2% -> 0% of each run, Pallas kernels for 0% -> 0%
where the time goes in v2:
time: 64.7 us; the launch traced here: 64.5 us
  Pallas kernels  36.2 us (56%)
  blocking collectives  26.5 us (41%)
  waiting for transfers between devices  1.16 us (2%)
  between operations  0.66 us (1%)
    pallas_call x1, Pallas kernels, dense_device(): call(functools.partial(column_kernel, shards), [VM] * 9, [f32(rows, cells...  29.7 us
    all_to_all x1, blocking collectives, dense_device(): packs = lax.all_to_all(send, 'src', 0, 0)  17.4 us
    all_to_all x1, blocking collectives, dense_device(): arrived = lax.all_to_all(columns, 'src', 0, 0)  9.1 us
    pallas_call x1, Pallas kernels, dense_device(): call(functools.partial(row_kernel, shards), [VM] * 3, [in_vmem((pairs, sh...  4.43 us
    pallas_call x1, Pallas kernels, dense_device(): call(functools.partial(entry_kernel, shards), [pl.BlockSpec(memory_space=...  1.44 us
  transfers between devices with their start and end apart: 1, of which 1 were waited for; matrix products, arithmetic and copies ran while one was open for 0% of the time, Pallas kernels for 0%

profile of v2, /device:TPU:0, one launch (start us, length us, event | category | flops | bytes accessed | tf_op | source)
XLA Modules:
  0.0 64.5 jit_solution(5554375434333407783)
XLA Ops:
  0.6 1.4 %shard_map.86 = (f32[8,72,128]{2,1,0:T(8,128)S(1)}, bf16[8,512,256]{2,1,0:T(8,128)(2,1)S(1)}, f32[16,128]{1,0:T(8,128)S(1)}, f32[8,16,128]{2,1,0:T(8,128)S(1)}, ...) custom-call(f32[16,64,128]{2,1,0:T(8,128)} %refs_0_.1, f32[1,64,128]{2,1,0:T(8,128)} %refs_1_.1, f32[16,128]{1,0:T(8,128)} %refs_2_.1, ...), custom_call_target="tpu_custom_call" | custom-call | tf_op jit(solution)/shard_map/pallas_call | solution.py:240
  2.1 17.4 %all_to_all.10.refs_0_ = f32[8,72,128]{2,1,0:T(8,128)S(1)} all-to-all(f32[8,72,128]{2,1,0:T(8,128)S(1)} %get-tuple-element.14), channel_id=1, replica_groups=mesh['grp'=2,'src'=8,'tgt'=2] {'src'}, dimensions={0} | all-to-all | bytes 589824 | tf_op jit(solution)/shard_map/all_to_all | solution.py:253
  19.5 4.4 %shard_map.87 = (f32[8,1024,256]{2,1,0:T(8,128)S(1)}, bf16[1024,512]{1,0:T(8,128)(2,1)S(1)}, f32[8,16,128]{2,1,0:T(8,128)S(1)}, f32[16,128]{1,0:T(8,128)S(1)}) custom-call(f32[8,72,128]{2,1,0:T(8,128)S(1)} %all_to_all.10.refs_0_, bf16[8,512,256]{2,1,0:T(8,128)(2,1)S(1)} %get-tuple-element.15.refs_1_.refs_2_, f32[8,16,128]{2,1,0:T(8,128)S(1)} %get-tuple-element.16.refs_2_.refs_4_), custom_call_target="tpu_custom_call" | custom-call | tf_op jit(solution)/shard_map/pallas_call | solution.py:254
  23.9 0.1 collective-permute-start
  24.0 1.2 %collective-permute-done.refs_6_ = f32[16,128]{1,0:T(8,128)S(1)} collective-permute-done((f32[16,128]{1,0:T(8,128)S(1)}, f32[16,128]{1,0:T(8,128)S(1)}, u32[]{:S(2)}, u32[]{:S(2)}) %collective-permute-start) | collective-permute-done | bytes 8224 | tf_op jit(solution)/shard_map/ppermute | solution.py:265
  25.1 29.7 %shard_map.88 = (f32[16,128]{1,0:T(8,128)}, f32[8,1,128]{2,1,0:T(1,128)S(1)}) custom-call(f32[8,1024,256]{2,1,0:T(8,128)S(1)} %get-tuple-element.17.refs_0_, bf16[1024,512]{1,0:T(8,128)(2,1)S(1)} %get-tuple-element.18.refs_1_, bf16[8,512,256]{2,1,0:T(8,128)(2,1)S(1)} %get-tuple-element.15.refs_1_.refs_2_, f32[8,16,128]{2,1,0:T(8,128)S(1)} %get-tuple-element.19.refs_3_, ...), custom_call_target="tpu_custom_call" | custom-call | tf_op jit(solution)/shard_map/pallas_call | solution.py:266
  54.9 9.1 %all_to_all.11.values_ref = f32[8,1,128]{2,1,0:T(1,128)S(1)} all-to-all(f32[8,1,128]{2,1,0:T(1,128)S(1)} %get-tuple-element.24), channel_id=1, replica_groups=mesh['grp'=2,'src'=8,'tgt'=2] {'src'}, dimensions={0} | all-to-all | bytes 8192 | tf_op jit(solution)/shard_map/all_to_all | solution.py:276
  64.0 0.5 shard_map.89
Async XLA Ops:
  23.9 1.2 %collective-permute-start = (f32[16,128]{1,0:T(8,128)S(1)}, f32[16,128]{1,0:T(8,128)S(1)}, u32[]{:S(2)}, u32[]{:S(2)}) collective-permute-start(f32[16,128]{1,0:T(8,128)S(1)} %get-tuple-element.20.refs_5_), channel_id=1, source_target_pairs={{0,1},{1,0},{2,3},{3,2},{4,5},{5,4},{6,7},{7,6},{8,9},{9,8},{10,11... | collective-permute-start | bytes 24584 | tf_op jit(solution)/shard_map/ppermute | solution.py:265

commit v3 on v2

--- a/solution.py
+++ b/solution.py
@@ -50,9 +50,8 @@
     bias = weight - (log2e / entropic) * norm
     scaled = target * (2.0 * log2e / entropic)
     below = jnp.broadcast_to(bias, (send_ref.shape[1] - depth, cells))
-    for step in range(shards):
-        send_ref[step, :depth, :] = scaled
-        send_ref[step, depth:, :] = below
+    send_ref[0, :depth, :] = scaled
+    send_ref[0, depth:, :] = below
     own_ref[...] = weight
     mass_out_ref[...] = mass_ref[...]
     support = support_ref[...]
@@ -60,7 +59,7 @@
     used = lax.broadcasted_iota(jnp.int32, support.shape, 0) < counts_ref[...]
     hits = [
         jnp.max(jnp.where(used & (support == block), 0.0, very_low), axis=0, keepdims=True)
-        for block in range(shards)
+        for block in block_order(shards)
     ]
     hits = jnp.concatenate(hits + [jnp.zeros((cells - shards, rows), jnp.float32)], axis=0)
     hits = jnp.concatenate([hits, jnp.zeros((cells, cells - rows), jnp.float32)], axis=1).T
@@ -206,11 +205,30 @@
             sums_ref[step] = jnp.where(used, acc_ref[step * cells : step * cells + 1, :], very_low)
 
 
-def merge_kernel(values_ref, weight_ref, out_ref):
-    values = values_ref[...]
+def merge_kernel(shards, values_ref, weight_ref, out_ref):
+    me = lax.axis_index("src")
+    order = block_order(shards)
+    values = values_ref[:, 0]
+    for place in range(1, shards):
+        values = jnp.where(me == order[place], values_ref[:, place], values)
     top = jnp.max(values, axis=0)
     whole = top + jnp.log2(jnp.sum(jnp.exp2(values - top), axis=0))
     out_ref[...] = -(entropic * ln2) * (whole - weight_ref[...])
+
+
+def block_order(shards):
+    bits = shards.bit_length() - 1
+    return [sum(((place >> bit) & 1) << (bits - 1 - bit) for bit in range(bits)) for place in range(shards)]
+
+
+def pair_gather(array):
+    shards = lax.axis_size("src")
+    apart = shards // 2
+    while apart:
+        pairs = [[i, i + apart] for i in range(shards) if not i & apart]
+        array = lax.all_gather(array, "src", axis=0, tiled=True, axis_index_groups=pairs)
+        apart //= 2
+    return array
 
 
 def f32(*shape):
@@ -241,7 +259,7 @@
         functools.partial(entry_kernel, shards),
         [pl.BlockSpec(memory_space=pltpu.HBM)] * len(args),
         [
-            in_vmem((shards, depth + 8, cells), jnp.float32),
+            in_vmem((1, depth + 8, cells), jnp.float32),
             in_vmem((pairs, 8 * depth, wide), jnp.bfloat16),
             in_vmem((rows, cells), jnp.float32),
             in_vmem((shards, rows, cells), jnp.float32),
@@ -250,7 +268,7 @@
         ],
         [pltpu.VMEM(arg.shape, arg.dtype) for arg in args] + [pltpu.SemaphoreType.DMA((len(args),))],
     )(*args)
-    packs = lax.all_to_all(send, "src", 0, 0)
+    packs = pair_gather(send)
     exps, tall, peaks, own = call(
         functools.partial(row_kernel, shards),
         [VM] * 3,
@@ -273,8 +291,8 @@
             pltpu.VMEM((rows, cells), jnp.float32),
         ],
     )(exps, tall, wide_feat, peaks, mask, own, other, mass, norm)
-    arrived = lax.all_to_all(columns, "src", 0, 0)
-    potential_new = call(merge_kernel, [VM] * 2, f32(1, cells))(arrived, weight)
+    arrived = pair_gather(columns[None])
+    potential_new = call(functools.partial(merge_kernel, shards), [VM] * 2, f32(1, cells))(arrived, weight)
     return potential_src, potential_new
 
 

time: 64.7 us -> 70.1 us (1.083)
  blocking collectives: 26.5 us -> 31.8 us
    all_gather x0 -> x6, blocking collectives: none -> 31.8 us  [pair_gather(): lax.all_gather(array, 'src', axis=0, tiled=True, axis_index_groups=pairs)]
    all_to_all x2 -> x0, blocking collectives: 26.5 us -> none  [the longest x1 17.4 us: dense_device(): packs = lax.all_to_all(send, 'src', 0, 0)]
where the time goes in v3:
time: 70.1 us; the launch traced here: 69.9 us
  Pallas kernels  36.2 us (52%)
  blocking collectives  31.8 us (45%)
  waiting for transfers between devices  1.16 us (2%)
    all_gather x6, blocking collectives, pair_gather(): lax.all_gather(array, 'src', axis=0, tiled=True, axis_index_groups=pairs)  31.8 us
    pallas_call x1, Pallas kernels, dense_device(): call(functools.partial(column_kernel, shards), [VM] * 9, [f32(rows, cells...  29.8 us
    pallas_call x1, Pallas kernels, dense_device(): call(functools.partial(row_kernel, shards), [VM] * 3, [in_vmem((pairs, sh...  4.41 us
    pallas_call x1, Pallas kernels, dense_device(): call(functools.partial(entry_kernel, shards), [pl.BlockSpec(memory_space=...  1.44 us
  transfers between devices with their start and end apart: 1, of which 1 were waited for; matrix products, arithmetic and copies ran while one was open for 0% of the time, Pallas kernels for 0%

profile of v3, /device:TPU:0, one launch (start us, length us, event | category | flops | bytes accessed | tf_op | source)
XLA Modules:
  0.0 69.9 jit_solution(16553376209737187351)
XLA Ops:
  0.6 1.4 %shard_map.86 = (f32[1,72,128]{2,1,0:T(8,128)S(1)}, bf16[8,512,256]{2,1,0:T(8,128)(2,1)S(1)}, f32[16,128]{1,0:T(8,128)S(1)}, f32[8,16,128]{2,1,0:T(8,128)S(1)}, ...) custom-call(f32[16,64,128]{2,1,0:T(8,128)} %refs_0_.1, f32[1,64,128]{2,1,0:T(8,128)} %refs_1_.1, f32[16,128]{1,0:T(8,128)} %refs_2_.1, ...), custom_call_target="tpu_custom_call" | custom-call | tf_op jit(solution)/shard_map/pallas_call | solution.py:258
  2.1 7.0 %all_gather.18 = f32[2,72,128]{2,1,0:T(8,128)S(1)} all-gather(f32[1,72,128]{2,1,0:T(8,128)S(1)} %get-tuple-element.14), channel_id=1, replica_groups={{0,8},{2,10},{4,12},{6,14},{1,9},{3,11},{5,13},{7,15},{16,24},{18,26},{..., dimensions={0}, use_global_device_ids=true | all-gather | bytes 110592 | tf_op jit(solution)/shard_map/all_gather | solution.py:229
  9.1 5.0 %all_gather.19 = f32[4,72,128]{2,1,0:T(8,128)S(1)} all-gather(f32[2,72,128]{2,1,0:T(8,128)S(1)} %all_gather.18), channel_id=1, replica_groups={{0,4},{2,6},{8,12},{10,14},{1,5},{3,7},{9,13},{11,15},{16,20},{18,22},{..., dimensions={0}, use_global_device_ids=true | all-gather | bytes 221184 | tf_op jit(solution)/shard_map/all_gather | solution.py:229
  14.1 5.8 %all_gather.20.refs_0_ = f32[8,72,128]{2,1,0:T(8,128)S(1)} all-gather(f32[4,72,128]{2,1,0:T(8,128)S(1)} %all_gather.19), channel_id=1, replica_groups={{0,2},{4,6},{8,10},{12,14},{1,3},{5,7},{9,11},{13,15},{16,18},{20,22},{..., dimensions={0}, use_global_device_ids=true | all-gather | bytes 442368 | tf_op jit(solution)/shard_map/all_gather | solution.py:229
  19.9 4.4 %shard_map.87 = (f32[8,1024,256]{2,1,0:T(8,128)S(1)}, bf16[1024,512]{1,0:T(8,128)(2,1)S(1)}, f32[8,16,128]{2,1,0:T(8,128)S(1)}, f32[16,128]{1,0:T(8,128)S(1)}) custom-call(f32[8,72,128]{2,1,0:T(8,128)S(1)} %all_gather.20.refs_0_, bf16[8,512,256]{2,1,0:T(8,128)(2,1)S(1)} %get-tuple-element.15.refs_1_.refs_2_, f32[8,16,128]{2,1,0:T(8,128)S(1)} %get-tuple-element.16.refs_2_.refs_4_), custom_call_target="tpu_custom_call" | custom-call | tf_op jit(solution)/shard_map/pallas_call | solution.py:272
  24.3 0.1 collective-permute-start
  24.4 1.2 %collective-permute-done.refs_6_ = f32[16,128]{1,0:T(8,128)S(1)} collective-permute-done((f32[16,128]{1,0:T(8,128)S(1)}, f32[16,128]{1,0:T(8,128)S(1)}, u32[]{:S(2)}, u32[]{:S(2)}) %collective-permute-start) | collective-permute-done | bytes 8224 | tf_op jit(solution)/shard_map/ppermute | solution.py:283
  25.6 29.8 %shard_map.88 = (f32[16,128]{1,0:T(8,128)}, f32[8,1,128]{2,1,0:T(1,128)S(1)}) custom-call(f32[8,1024,256]{2,1,0:T(8,128)S(1)} %get-tuple-element.17.refs_0_, bf16[1024,512]{1,0:T(8,128)(2,1)S(1)} %get-tuple-element.18.refs_1_, bf16[8,512,256]{2,1,0:T(8,128)(2,1)S(1)} %get-tuple-element.15.refs_1_.refs_2_, f32[8,16,128]{2,1,0:T(8,128)S(1)} %get-tuple-element.19.refs_3_, ...), custom_call_target="tpu_custom_call" | custom-call | tf_op jit(solution)/shard_map/pallas_call | solution.py:284
  55.3 5.2 %all-gather = f32[16,1,128]{2,1,0:T(1,128)S(1)} all-gather(f32[8,1,128]{2,1,0:T(1,128)S(1)} %get-tuple-element.24), channel_id=2, replica_groups={{0,8},{2,10},{4,12},{6,14},{1,9},{3,11},{5,13},{7,15},{16,24},{18,26},{..., dimensions={0}, use_global_device_ids=true | all-gather | bytes 12288 | tf_op jit(solution)/shard_map/all_gather | solution.py:229
  60.6 4.4 %all_gather.22 = f32[4,8,1,128]{3,1,2,0:T(8,128)S(1)} all-gather(f32[2,8,1,128]{3,1,2,0:T(8,128)S(1)} %bitcast.9), channel_id=1, replica_groups={{0,4},{2,6},{8,12},{10,14},{1,5},{3,7},{9,13},{11,15},{16,20},{18,22},{..., dimensions={0}, use_global_device_ids=true | all-gather | bytes 24576 | tf_op jit(solution)/shard_map/all_gather | solution.py:229
  64.9 4.4 %all_gather.23 = f32[8,8,1,128]{3,1,2,0:T(8,128)S(1)} all-gather(f32[4,8,1,128]{3,1,2,0:T(8,128)S(1)} %all_gather.22), channel_id=1, replica_groups={{0,2},{4,6},{8,10},{12,14},{1,3},{5,7},{9,11},{13,15},{16,18},{20,22},{..., dimensions={0}, use_global_device_ids=true | all-gather | bytes 49152 | tf_op jit(solution)/shard_map/all_gather | solution.py:229
  69.3 0.6 shard_map.89
Async XLA Ops:
  24.3 1.2 %collective-permute-start = (f32[16,128]{1,0:T(8,128)S(1)}, f32[16,128]{1,0:T(8,128)S(1)}, u32[]{:S(2)}, u32[]{:S(2)}) collective-permute-start(f32[16,128]{1,0:T(8,128)S(1)} %get-tuple-element.20.refs_5_), channel_id=1, source_target_pairs={{0,1},{1,0},{2,3},{3,2},{4,5},{5,4},{6,7},{7,6},{8,9},{9,8},{10,11... | collective-permute-start | bytes 24584 | tf_op jit(solution)/shard_map/ppermute | solution.py:283

commit v4 on v2

--- a/solution.py
+++ b/solution.py
@@ -34,39 +34,59 @@
     return (mass + poten / entropic) * log2e
 
 
-def entry_kernel(shards, *refs):
-    hbm, outs, held, sems = refs[:7], refs[7:13], refs[13:20], refs[20]
-    send_ref, wide_ref, norm_ref, mask_ref, own_ref, mass_out_ref = outs
-    feat_ref, target_ref, mass_ref, tmass_ref, tpoten_ref, support_ref, counts_ref = held
+def partners(shards):
+    found, apart = [0], shards // 2
+    while apart:
+        found += [other ^ apart for other in found]
+        apart //= 2
+    return found
+
+
+def read_all(hbm, held, sems):
     copies = [pltpu.make_async_copy(src, dst, sems.at[i]) for i, (src, dst) in enumerate(zip(hbm, held))]
-    for copy in copies[1:] + copies[:1]:
+    for copy in copies:
         copy.start()
-    for copy in copies[1:]:
+    return copies
+
+
+def pack_kernel(*refs):
+    hbm, (send_ref, weight_ref), held, sems = refs[:3], refs[3:5], refs[5:8], refs[8]
+    for copy in read_all(hbm, held, sems):
         copy.wait()
-    target = target_ref[0]
-    depth, cells = target.shape
-    weight = target_weight(tmass_ref[...], tpoten_ref[...])
-    norm = jnp.sum(target * target, axis=0, keepdims=True)
+    feat_ref, mass_ref, poten_ref = held
+    feat = feat_ref[0]
+    depth, cells = feat.shape
+    weight = target_weight(mass_ref[...], poten_ref[...])
+    norm = jnp.sum(feat * feat, axis=0, keepdims=True)
     bias = weight - (log2e / entropic) * norm
-    scaled = target * (2.0 * log2e / entropic)
-    below = jnp.broadcast_to(bias, (send_ref.shape[1] - depth, cells))
-    for step in range(shards):
-        send_ref[step, :depth, :] = scaled
-        send_ref[step, depth:, :] = below
-    own_ref[...] = weight
+    send_ref[0, :depth, :] = feat * (2.0 * log2e / entropic)
+    send_ref[0, depth:, :] = jnp.broadcast_to(bias, (send_ref.shape[1] - depth, cells))
+    weight_ref[...] = weight
+
+
+def source_kernel(shards, *refs):
+    hbm, outs, held, sems = refs[:4], refs[4:8], refs[8:12], refs[12]
+    wide_ref, norm_ref, mask_ref, mass_out_ref = outs
+    mass_ref, support_ref, counts_ref, feat_ref = held
+    copies = read_all(hbm, held, sems)
+    for copy in copies[:3]:
+        copy.wait()
     mass_out_ref[...] = mass_ref[...]
     support = support_ref[...]
     slots, rows = support.shape
+    cells = mass_ref.shape[1]
+    me = lax.axis_index("src")
     used = lax.broadcasted_iota(jnp.int32, support.shape, 0) < counts_ref[...]
     hits = [
-        jnp.max(jnp.where(used & (support == block), 0.0, very_low), axis=0, keepdims=True)
-        for block in range(shards)
+        jnp.max(jnp.where(used & (support == (me ^ other)), 0.0, very_low), axis=0, keepdims=True)
+        for other in partners(shards)
     ]
     hits = jnp.concatenate(hits + [jnp.zeros((cells - shards, rows), jnp.float32)], axis=0)
     hits = jnp.concatenate([hits, jnp.zeros((cells, cells - rows), jnp.float32)], axis=1).T
-    for block in range(shards):
-        mask_ref[block] = jnp.broadcast_to(hits[:rows, block : block + 1], (rows, cells))
-    copies[0].wait()
+    for place in range(shards):
+        mask_ref[place] = jnp.broadcast_to(hits[:rows, place : place + 1], (rows, cells))
+    copies[3].wait()
+    depth = feat_ref.shape[1]
     one = jnp.ones((2 * depth, 2 * cells), jnp.bfloat16)
     for pair in range(rows // 2):
         for half in range(2):
@@ -81,23 +101,30 @@
         wide_ref[pair, 6 * depth : 8 * depth, :] = one
 
 
-def row_kernel(shards, *refs):
-    packs_ref, wide_ref, mask_ref, exps_ref, tall_ref, peak_ref, rowsum_ref, total_ref = refs
-    packs = [packs_ref.at[step] for step in range(shards)]
+def join_kernel(*refs):
+    ins, out_ref = refs[:-2], refs[-1]
+    start = 0
+    for ref in ins:
+        out_ref[start : start + ref.shape[0]] = ref[...]
+        start += ref.shape[0]
+
+
+def tile_kernel(packs_ref, wide_ref, exps_ref, tall_ref, peak_ref, total_ref):
+    blocks = packs_ref.shape[0]
     pairs, _, both = wide_ref.shape
     cells = both // 2
     depth = cells // 2
     lane = lax.broadcasted_iota(jnp.int32, (cells, cells), 1)
-    biases = jnp.concatenate([pack[depth : depth + 1, :] for pack in packs], axis=0)
+    biases = jnp.concatenate([packs_ref[place, depth : depth + 1, :] for place in range(blocks)], axis=0)
     bias_pieces = jnp.concatenate(list(pieces(biases)), axis=0)
-    padded = jnp.concatenate([bias_pieces, jnp.zeros((cells - 3 * shards, cells), jnp.float32)], axis=0)
+    padded = jnp.concatenate([bias_pieces, jnp.zeros((cells - 3 * blocks, cells), jnp.float32)], axis=0)
     bias_lanes = padded.T
-    for step, pack in enumerate(packs):
-        feat = pack[:depth, :]
+    for place in range(blocks):
+        feat = packs_ref[place, :depth, :]
         turned = jnp.concatenate([feat, feat], axis=0).T
         high, mid, low = pieces(turned)
-        own = jnp.where(lax.rem(lane, shards) == step, bias_lanes, 0.0)
-        rows = slice(step * cells, (step + 1) * cells)
+        own = jnp.where(lax.rem(lane, blocks) == place, bias_lanes, 0.0)
+        rows = slice(place * cells, (place + 1) * cells)
         tall_ref[rows, 0:cells] = high.astype(jnp.bfloat16)
         tall_ref[rows, cells : 2 * cells] = mid.astype(jnp.bfloat16)
         tall_ref[rows, 2 * cells : 3 * cells] = jnp.where(lane < depth, high, low).astype(jnp.bfloat16)
@@ -105,8 +132,8 @@
 
     def body(pair, carry):
         weights = wide_ref[pair]
-        for step in range(shards):
-            rows = slice(step * cells, (step + 1) * cells)
+        for place in range(blocks):
+            rows = slice(place * cells, (place + 1) * cells)
             score = jnp.dot(tall_ref[rows, :], weights, preferred_element_type=jnp.float32)
             peak = jnp.max(score, axis=0, keepdims=True)
             exps = jnp.exp2(score - peak)
@@ -114,16 +141,24 @@
             total = jnp.sum(exps, axis=0, keepdims=True)
             for half in range(2):
                 lanes = slice(half * cells, (half + 1) * cells)
-                peak_ref[step, pl.ds(2 * pair + half, 1), :] = peak[:, lanes]
-                total_ref[step, pl.ds(2 * pair + half, 1), :] = total[:, lanes]
+                peak_ref[place, pl.ds(2 * pair + half, 1), :] = peak[:, lanes]
+                total_ref[place, pl.ds(2 * pair + half, 1), :] = total[:, lanes]
         return carry
 
     lax.fori_loop(0, pairs, body, 0)
-    masked = [peak_ref[step] + mask_ref[step] for step in range(shards)]
-    top = functools.reduce(jnp.maximum, masked)
-    summed = sum(total_ref[step] * jnp.exp2(masked[step] - top) for step in range(shards))
-    for step in range(shards):
-        peak_ref[step] = masked[step]
+
+
+def row_kernel(groups, *refs):
+    mask_ref, peak_refs, total_refs = refs[0], refs[1 : 1 + groups], refs[1 + groups : 1 + 2 * groups]
+    peaks_ref, rowsum_ref = refs[1 + 2 * groups :]
+    place = 0
+    for ref in peak_refs:
+        for index in range(ref.shape[0]):
+            peaks_ref[place] = ref[index] + mask_ref[place]
+            place += 1
+    totals = [ref[index] for ref in total_refs for index in range(ref.shape[0])]
+    top = functools.reduce(jnp.maximum, [peaks_ref[index] for index in range(place)])
+    summed = sum(total * jnp.exp2(peaks_ref[index] - top) for index, total in enumerate(totals))
     rowsum_ref[...] = top + jnp.log2(summed)
 
 
@@ -136,74 +171,65 @@
     return sum(parts)[0:1, :]
 
 
-def column_kernel(shards, *refs):
-    ins, rest = refs[:9], refs[9:]
-    exps_ref, tall_ref, wide_ref, peak_ref, mask_ref, own_ref, other_ref, mass_ref, norm_ref = ins
-    poten_ref, sums_ref, weight_ref, acc_ref, shift_ref = rest
+def column_kernel(groups, *refs):
+    exps_refs, tall_refs, rest = refs[:groups], refs[groups : 2 * groups], refs[2 * groups :]
+    wide_ref, peak_ref, mask_ref, own_ref, other_ref, mass_ref, norm_ref = rest[:7]
+    poten_ref, sums_ref, weight_ref, acc_ref, shift_ref = rest[7:]
     pairs, _, both = wide_ref.shape
     cells = both // 2
+    shards = mask_ref.shape[0]
     own, other = own_ref[...], other_ref[...]
     top = jnp.maximum(own, other)
     whole = top + jnp.log2(jnp.exp2(own - top) + jnp.exp2(other - top))
     poten_ref[...] = norm_ref[...] - (entropic * ln2) * whole
     shift = mass_ref[...] * log2e - whole
     shift_ref[...] = shift
-    for step in range(shards):
-        weight_ref[step] = jnp.exp2(peak_ref[step] + shift)
-    for step in range(shards):
-        rows = slice(step * cells, (step + 1) * cells)
+    for place in range(shards):
+        weight_ref[place] = jnp.exp2(peak_ref[place] + shift)
+    spots = [
+        (group, slice(index * cells, (index + 1) * cells))
+        for group, ref in enumerate(tall_refs)
+        for index in range(ref.shape[0] // cells)
+    ]
+    for place, (group, rows) in enumerate(spots):
         acc = jnp.zeros((cells, cells), jnp.float32)
         for pair in range(pairs):
-            acc = acc + exps_ref[pair, rows, :cells] * weight_ref[step, 2 * pair : 2 * pair + 1, :]
-            acc = acc + exps_ref[pair, rows, cells:] * weight_ref[step, 2 * pair + 1 : 2 * pair + 2, :]
-        acc_ref[rows, :] = acc
+            acc = acc + exps_refs[group][pair, rows, :cells] * weight_ref[place, 2 * pair : 2 * pair + 1, :]
+            acc = acc + exps_refs[group][pair, rows, cells:] * weight_ref[place, 2 * pair + 1 : 2 * pair + 2, :]
+        acc_ref[place * cells : (place + 1) * cells, :] = acc
     sums = lane_sums(acc_ref[...])
+    me = lax.axis_index("src")
+    owners = [me ^ other for other in partners(shards)]
+    used = [jnp.max(mask_ref[place], axis=0, keepdims=True) > 0.5 * very_low for place in range(shards)]
     worst = jnp.full((1, cells), 1.0, jnp.float32)
-    for step in range(shards):
-        used = jnp.max(mask_ref[step], axis=0, keepdims=True) > 0.5 * very_low
-        here = sums[:, step * cells : (step + 1) * cells]
-        sums_ref[step] = jnp.where(used, jnp.log2(here), very_low)
-        worst = jnp.minimum(worst, jnp.where(used, here, 1.0))
+    for place in range(shards):
+        here = sums[:, place * cells : (place + 1) * cells]
+        sums_ref[owners[place]] = jnp.where(used[place], jnp.log2(here), very_low)
+        worst = jnp.minimum(worst, jnp.where(used[place], here, 1.0))
 
     @pl.when(jnp.min(worst) < least_sum)
     def _():
-        acc_ref[...] = jnp.full(acc_ref.shape, very_low, jnp.float32)
-
-        def exponents(pair, step):
-            score = jnp.dot(
-                tall_ref[pl.ds(pl.multiple_of(step * cells, cells), cells), :],
-                wide_ref[pair],
-                preferred_element_type=jnp.float32,
-            )
-            add = shift_ref[pl.ds(2 * pair, 2), :] + mask_ref[step, pl.ds(2 * pair, 2), :]
-            return score[:, :cells] + add[0:1, :], score[:, cells:] + add[1:2, :]
-
-        def highest(index, carry):
-            pair, step = index // shards, lax.rem(index, shards)
-            rows = pl.ds(pl.multiple_of(step * cells, cells), cells)
-            first, second = exponents(pair, step)
-            acc_ref[rows, :] = jnp.maximum(acc_ref[rows, :], jnp.maximum(first, second))
-            return carry
-
-        lax.fori_loop(0, pairs * shards, highest, 0)
-
-        def total(step, carry):
-            rows = pl.ds(pl.multiple_of(step * cells, cells), cells)
-            peak = jnp.max(acc_ref[rows, :], axis=1, keepdims=True)
-
-            def add(pair, sums):
-                first, second = exponents(pair, step)
+        for place, (group, rows) in enumerate(spots):
+
+            def exponents(pair):
+                score = jnp.dot(tall_refs[group][rows, :], wide_ref[pair], preferred_element_type=jnp.float32)
+                add = shift_ref[pl.ds(2 * pair, 2), :] + mask_ref[place, pl.ds(2 * pair, 2), :]
+                return score[:, :cells] + add[0:1, :], score[:, cells:] + add[1:2, :]
+
+            def highest(pair, peak):
+                first, second = exponents(pair)
+                return jnp.maximum(peak, jnp.maximum(first, second))
+
+            peak = lax.fori_loop(0, pairs, highest, jnp.full((cells, cells), very_low, jnp.float32))
+            peak = jnp.broadcast_to(jnp.max(peak, axis=1, keepdims=True), (cells, cells))
+
+            def add_up(pair, sums):
+                first, second = exponents(pair)
                 return sums + jnp.exp2(first - peak) + jnp.exp2(second - peak)
 
-            sums = lax.fori_loop(0, pairs, add, jnp.zeros((cells, cells), jnp.float32))
-            along = jnp.broadcast_to(peak, (cells, cells)).T
-            acc_ref[rows, :] = along[0:1, :] + jnp.log2(lane_sums(sums)) + jnp.zeros((cells, 1), jnp.float32)
-            return carry
-
-        lax.fori_loop(0, shards, total, 0)
-        for step in range(shards):
-            used = jnp.max(mask_ref[step], axis=0, keepdims=True) > 0.5 * very_low
-            sums_ref[step] = jnp.where(used, acc_ref[step * cells : step * cells + 1, :], very_low)
+            sums = lax.fori_loop(0, pairs, add_up, jnp.zeros((cells, cells), jnp.float32))
+            logs = peak.T[0:1, :] + jnp.log2(lane_sums(sums))
+            sums_ref[owners[place]] = jnp.where(used[place], logs, very_low)
 
 
 def merge_kernel(values_ref, weight_ref, out_ref):
@@ -224,7 +250,7 @@
     rows, depth, cells = source_feat.shape
     pairs, wide = rows // 2, 2 * cells
 
-    def call(kernel, ins, out_shape, scratch=()):
+    def call(kernel, ins, out_shape, scratch=(), cost=None):
         many = isinstance(out_shape, list)
         return pl.pallas_call(
             kernel,
@@ -233,46 +259,84 @@
             out_shape=out_shape,
             scratch_shapes=list(scratch),
             compiler_params=PARAMS,
+            cost_estimate=cost,
         )
 
-    args = [source_feat, target_feat, log_mass_src, log_mass_tgt, potential_tgt, support[:, 0, :].T, counts.T]
-    args = [pltpu.with_memory_space_constraint(arg, pltpu.HBM) for arg in args]
-    send, wide_feat, norm, mask, weight, mass = call(
-        functools.partial(entry_kernel, shards),
-        [pl.BlockSpec(memory_space=pltpu.HBM)] * len(args),
+    def reading(kernel, args, out_shape, cost):
+        return call(
+            kernel,
+            [pl.BlockSpec(memory_space=pltpu.HBM)] * len(args),
+            out_shape,
+            [pltpu.VMEM(arg.shape, arg.dtype) for arg in args] + [pltpu.SemaphoreType.DMA((len(args),))],
+            cost,
+        )(*[pltpu.with_memory_space_constraint(arg, pltpu.HBM) for arg in args])
+
+    def cost_of(flops):
+        return pl.CostEstimate(flops=flops, bytes_accessed=rows * depth * cells * 4, transcendentals=0)
+
+    pack, weight = reading(
+        pack_kernel,
+        [target_feat, log_mass_tgt, potential_tgt],
+        [in_vmem((1, depth + 8, cells), jnp.float32), in_vmem((1, cells), jnp.float32)],
+        None,
+    )
+    wide_feat, norm, mask, mass = reading(
+        functools.partial(source_kernel, shards),
+        [log_mass_src, support[:, 0, :].T, counts.T, source_feat],
         [
-            in_vmem((shards, depth + 8, cells), jnp.float32),
             in_vmem((pairs, 8 * depth, wide), jnp.bfloat16),
             in_vmem((rows, cells), jnp.float32),
             in_vmem((shards, rows, cells), jnp.float32),
-            in_vmem((1, cells), jnp.float32),
             in_vmem((rows, cells), jnp.float32),
         ],
-        [pltpu.VMEM(arg.shape, arg.dtype) for arg in args] + [pltpu.SemaphoreType.DMA((len(args),))],
-    )(*args)
-    packs = lax.all_to_all(send, "src", 0, 0)
-    exps, tall, peaks, own = call(
-        functools.partial(row_kernel, shards),
-        [VM] * 3,
-        [
-            in_vmem((pairs, shards * cells, wide), jnp.float32),
-            in_vmem((shards * cells, 8 * depth), jnp.bfloat16),
-            in_vmem((shards, rows, cells), jnp.float32),
-            in_vmem((rows, cells), jnp.float32),
-        ],
-        [pltpu.VMEM((shards, rows, cells), jnp.float32)],
-    )(packs, wide_feat, mask)
+        cost_of(10**9),
+    )
+
+    def tiles(packs):
+        blocks = packs.shape[0]
+        return call(
+            tile_kernel,
+            [VM] * 2,
+            [
+                in_vmem((pairs, blocks * cells, wide), jnp.float32),
+                in_vmem((blocks * cells, 8 * depth), jnp.bfloat16),
+                in_vmem((blocks, rows, cells), jnp.float32),
+                in_vmem((blocks, rows, cells), jnp.float32),
+            ],
+            cost=cost_of(2 * blocks * cells * pairs * wide * 8 * depth),
+        )(packs, wide_feat)
+
+    held, found, apart = pack, [tiles(pack)], shards // 2
+    while apart:
+        there = lax.ppermute(held, "src", [(i, i ^ apart) for i in range(shards)])
+        before = found[-1][-1]
+        found.append(tiles(there))
+        apart //= 2
+        if apart:
+            count = 2 * held.shape[0]
+            held = call(
+                join_kernel,
+                [VM] * 2 + [pl.BlockSpec(memory_space=pl.ANY)],
+                in_vmem((count,) + held.shape[1:], jnp.float32),
+            )(held, there, before)
+    exps, tall, peaks, totals = zip(*found)
+    groups = len(found)
+    peaks, own = call(
+        functools.partial(row_kernel, groups),
+        [VM] * (1 + 2 * groups),
+        [in_vmem((shards, rows, cells), jnp.float32), in_vmem((rows, cells), jnp.float32)],
+    )(mask, *peaks, *totals)
     other = lax.ppermute(own, "tgt", [(0, 1), (1, 0)])
     potential_src, columns = call(
-        functools.partial(column_kernel, shards),
-        [VM] * 9,
+        functools.partial(column_kernel, groups),
+        [VM] * (2 * groups + 7),
         [f32(rows, cells), in_vmem((shards, 1, cells), jnp.float32)],
         [
             pltpu.VMEM((shards, rows, cells), jnp.float32),
             pltpu.VMEM((shards * cells, cells), jnp.float32),
             pltpu.VMEM((rows, cells), jnp.float32),
         ],
-    )(exps, tall, wide_feat, peaks, mask, own, other, mass, norm)
+    )(*exps, *tall, wide_feat, peaks, mask, own, other, mass, norm)
     arrived = lax.all_to_all(columns, "src", 0, 0)
     potential_new = call(merge_kernel, [VM] * 2, f32(1, cells))(arrived, weight)
     return potential_src, potential_new

time: 64.7 us -> 64.3 us (level)
  blocking collectives: 26.5 us -> 11.1 us
  starting transfers between devices: 0.07 us -> 7.37 us
  Pallas kernels: 36.2 us -> 41.9 us
  waiting for transfers between devices: 1.16 us -> 3.01 us
    all_to_all x1 -> x0, blocking collectives: 17.4 us -> none  [dense_device(): packs = lax.all_to_all(send, 'src', 0, 0)]
    ppermute x0 -> x3, starting transfers between devices: none -> 7.3 us  [dense_device(): there = lax.ppermute(held, 'src', [(i, i ^ apart) for i in range(shards)])]
    pallas_call x3 -> x10, Pallas kernels: 35.6 us -> 41.3 us  [the longest x1 29.3 us: dense_device(): call(functools.partial(column_kernel, groups), [VM] * (2 * groups + 7), [...]
    all_to_all x1, blocking collectives: 9.1 us -> 11.1 us  [dense_device(): arrived = lax.all_to_all(columns, 'src', 0, 0)]
    ppermute x0 -> x3, waiting for transfers between devices: none -> 1.86 us  [dense_device(): there = lax.ppermute(held, 'src', [(i, i ^ apart) for i in range(shards)])]
  transfers between devices with their start and end apart: 1 -> 4, of which waited for: 1 -> 3; matrix products, arithmetic and copies ran while one was open for 0% -> 0% of each run, Pallas kernels for 0% -> 12%
where the time goes in v4:
time: 64.3 us; the launch traced here: 64 us
  Pallas kernels  41.9 us (65%)
  blocking collectives  11.1 us (17%)
  starting transfers between devices  7.37 us (11%)
  waiting for transfers between devices  3.01 us (5%)
  between operations  0.7 us (1%)
    pallas_call x1, Pallas kernels, dense_device(): call(functools.partial(column_kernel, groups), [VM] * (2 * groups + 7), [...  29.3 us
    all_to_all x1, blocking collectives, dense_device(): arrived = lax.all_to_all(columns, 'src', 0, 0)  11.1 us
    pallas_call x4, Pallas kernels, tiles(): call(tile_kernel, [VM] * 2, [in_vmem((pairs, blocks * cells, wide), jnp.f...  9.81 us
    ppermute x3, starting transfers between devices, dense_device(): there = lax.ppermute(held, 'src', [(i, i ^ apart) for i in range(shards)])  7.3 us
    pallas_call x2, Pallas kernels, reading(): call(kernel, [pl.BlockSpec(memory_space=pltpu.HBM)] * len(args), out_shap...  2.17 us
    ppermute x3, waiting for transfers between devices, dense_device(): there = lax.ppermute(held, 'src', [(i, i ^ apart) for i in range(shards)])  1.86 us
  transfers between devices with their start and end apart: 4, of which 3 were waited for; matrix products, arithmetic and copies ran while one was open for 0% of the time, Pallas kernels for 12%

profile of v4, /device:TPU:0, one launch (start us, length us, event | category | flops | bytes accessed | tf_op | source)
XLA Modules:
  0.0 64.0 jit_solution(8268016192467883153)
XLA Ops:
  0.6 0.8 %shard_map.86 = (f32[1,72,128]{2,1,0:T(8,128)S(1)}, f32[1,128]{1,0:T(1,128)S(1)}) custom-call(f32[1,64,128]{2,1,0:T(8,128)} %refs_0_.2, f32[1,128]{1,0:T(1,128)} %refs_1_.1, f32[1,128]{1,0:T(1,128)} %refs_2_.1), custom_call_target="tpu_custom_call" | custom-call | tf_op jit(solution)/shard_map/pallas_call | solution.py:266
  1.4 4.1 %collective-permute-start = (f32[1,72,128]{2,1,0:T(8,128)S(1)}, f32[1,72,128]{2,1,0:T(8,128)S(1)}, u32[]{:S(2)}, u32[]{:S(2)}) collective-permute-start(f32[1,72,128]{2,1,0:T(8,128)S(1)} %get-tuple-element.28.packs_ref.refs_0_), channel_id=1, source_target_pairs={{0,8},{2,10},{4,12},{6,14},{8,0},{10,2},{12,4},{14,6},{1,9},{3,11}... | collective-permute-start | bytes 110600 | tf_op jit(solution)/shard_map/ppermute | solution.py:311
  5.5 1.4 %shard_map.87 = (bf16[8,512,256]{2,1,0:T(8,128)(2,1)S(1)}, f32[16,128]{1,0:T(8,128)S(1)}, f32[8,16,128]{2,1,0:T(8,128)S(1)}, f32[16,128]{1,0:T(8,128)S(1)}) custom-call(f32[16,128]{1,0:T(8,128)} %refs_0_.3, s32[8,16]{1,0:T(8,128)} %bitcast.4, s32[1,16]{1,0:T(1,128)} %bitcast.5, f32[16,64,128]{2,1,0:T(8,128)} %refs_3_.1), custom_call_target="tpu_custom_call" | custom-call | flops 1000000000 | bytes 524288 | tf_op jit(solution)/shard_map/pallas_call | solution.py:266
  6.9 2.0 %shard_map.88 = (f32[8,128,256]{2,1,0:T(8,128)S(1)}, bf16[128,512]{1,0:T(8,128)(2,1)S(1)}, f32[1,16,128]{2,1,0:T(8,128)S(1)}, f32[1,16,128]{2,1,0:T(8,128)S(1)}) custom-call(f32[1,72,128]{2,1,0:T(8,128)S(1)} %get-tuple-element.28.packs_ref.refs_0_, bf16[8,512,256]{2,1,0:T(8,128)(2,1)S(1)} %get-tuple-element.29.wide_ref.refs_8_), custom_call_target="tpu_custom_call" | custom-call | flops 268435456 | bytes 524288 | tf_op jit(solution)/shard_map/pallas_call | solution.py:297
  9.0 0.0 collective-permute-done.packs_ref.refs_1_
  9.0 1.6 %collective-permute-start.1 = (f32[2,72,128]{2,1,0:T(8,128)S(1)}, f32[2,72,128]{2,1,0:T(8,128)S(1)}, u32[]{:S(2)}, u32[]{:S(2)}) collective-permute-start(f32[2,72,128]{2,1,0:T(8,128)S(1)} %shard_map.90.refs_0_), channel_id=1, source_target_pairs={{0,4},{2,6},{4,0},{6,2},{8,12},{10,14},{12,8},{14,10},{1,5},{3,7},... | collective-permute-start | bytes 221192 | tf_op jit(solution)/shard_map/ppermute | solution.py:311
  10.6 2.0 %shard_map.89 = (f32[8,128,256]{2,1,0:T(8,128)S(1)}, bf16[128,512]{1,0:T(8,128)(2,1)S(1)}, f32[1,16,128]{2,1,0:T(8,128)S(1)}, f32[1,16,128]{2,1,0:T(8,128)S(1)}) custom-call(f32[1,72,128]{2,1,0:T(8,128)S(1)} %collective-permute-done.packs_ref.refs_1_, bf16[8,512,256]{2,1,0:T(8,128)(2,1)S(1)} %get-tuple-element.29.wide_ref.refs_8_), custom_call_target="tpu_custom_call" | custom-call | flops 268435456 | bytes 524288 | tf_op jit(solution)/shard_map/pallas_call | solution.py:297
  12.7 0.7 %collective-permute-done.1.packs_ref.refs_1_ = f32[2,72,128]{2,1,0:T(8,128)S(1)} collective-permute-done((f32[2,72,128]{2,1,0:T(8,128)S(1)}, f32[2,72,128]{2,1,0:T(8,128)S(1)}, u32[]{:S(2)}, u32[]{:S(2)}) %collective-permute-start.1) | collective-permute-done | bytes 73760 | tf_op jit(solution)/shard_map/ppermute | solution.py:311
  13.4 1.6 %collective-permute-start.2 = (f32[4,72,128]{2,1,0:T(8,128)S(1)}, f32[4,72,128]{2,1,0:T(8,128)S(1)}, u32[]{:S(2)}, u32[]{:S(2)}) collective-permute-start(f32[4,72,128]{2,1,0:T(8,128)S(1)} %shard_map.92), channel_id=1, source_target_pairs={{0,2},{2,0},{4,6},{6,4},{8,10},{10,8},{12,14},{14,12},{1,3},{3,1},... | collective-permute-start | bytes 442376 | tf_op jit(solution)/shard_map/ppermute | solution.py:311
  15.0 2.5 %shard_map.91 = (f32[8,256,256]{2,1,0:T(8,128)S(1)}, bf16[256,512]{1,0:T(8,128)(2,1)S(1)}, f32[2,16,128]{2,1,0:T(8,128)S(1)}, f32[2,16,128]{2,1,0:T(8,128)S(1)}) custom-call(f32[2,72,128]{2,1,0:T(8,128)S(1)} %collective-permute-done.1.packs_ref.refs_1_, bf16[8,512,256]{2,1,0:T(8,128)(2,1)S(1)} %get-tuple-element.29.wide_ref.refs_8_), custom_call_target="tpu_custom_call" | custom-call | flops 536870912 | bytes 524288 | tf_op jit(solution)/shard_map/pallas_call | solution.py:297
  17.5 1.1 %collective-permute-done.2.packs_ref = f32[4,72,128]{2,1,0:T(8,128)S(1)} collective-permute-done((f32[4,72,128]{2,1,0:T(8,128)S(1)}, f32[4,72,128]{2,1,0:T(8,128)S(1)}, u32[]{:S(2)}, u32[]{:S(2)}) %collective-permute-start.2) | collective-permute-done | bytes 147488 | tf_op jit(solution)/shard_map/ppermute | solution.py:311
  18.6 3.2 %shard_map.93 = (f32[8,512,256]{2,1,0:T(8,128)S(1)}, bf16[512,512]{1,0:T(8,128)(2,1)S(1)}, f32[4,16,128]{2,1,0:T(8,128)S(1)}, f32[4,16,128]{2,1,0:T(8,128)S(1)}) custom-call(f32[4,72,128]{2,1,0:T(8,128)S(1)} %collective-permute-done.2.packs_ref, bf16[8,512,256]{2,1,0:T(8,128)(2,1)S(1)} %get-tuple-element.29.wide_ref.refs_8_), custom_call_target="tpu_custom_call" | custom-call | flops 1073741824 | bytes 524288 | tf_op jit(solution)/shard_map/pallas_call | solution.py:297
  21.9 0.1 collective-permute-start.3
  22.0 1.2 %collective-permute-done.3.refs_12_ = f32[16,128]{1,0:T(8,128)S(1)} collective-permute-done((f32[16,128]{1,0:T(8,128)S(1)}, f32[16,128]{1,0:T(8,128)S(1)}, u32[]{:S(2)}, u32[]{:S(2)}) %collective-permute-start.3) | collective-permute-done | bytes 8224 | tf_op jit(solution)/shard_map/ppermute | solution.py:329
  23.1 29.3 %shard_map.95 = (f32[16,128]{1,0:T(8,128)}, f32[8,1,128]{2,1,0:T(1,128)S(1)}) custom-call(f32[8,128,256]{2,1,0:T(8,128)S(1)} %get-tuple-element.30.refs_0_, f32[8,128,256]{2,1,0:T(8,128)S(1)} %get-tuple-element.31.refs_1_, f32[8,256,256]{2,1,0:T(8,128)S(1)} %get-tuple-element.33.refs_2_, f32[8,512,256]{2,1,0:T(8,128)S(1)} %get-tuple-element.35.refs_3_, ...), custom_call_target="tpu_custom_call" | custom-call | tf_op jit(solution)/shard_map/pallas_call | solution.py:330
  52.4 11.1 %all_to_all.5.values_ref = f32[8,1,128]{2,1,0:T(1,128)S(1)} all-to-all(f32[8,1,128]{2,1,0:T(1,128)S(1)} %get-tuple-element.52), channel_id=1, replica_groups=mesh['grp'=2,'src'=8,'tgt'=2] {'src'}, dimensions={0} | all-to-all | bytes 8192 | tf_op jit(solution)/shard_map/all_to_all | solution.py:340
  63.5 0.5 shard_map.96
  (3 shorter events, 0.1 us)
Async XLA Ops:
  1.4 7.5 %collective-permute-start = (f32[1,72,128]{2,1,0:T(8,128)S(1)}, f32[1,72,128]{2,1,0:T(8,128)S(1)}, u32[]{:S(2)}, u32[]{:S(2)}) collective-permute-start(f32[1,72,128]{2,1,0:T(8,128)S(1)} %get-tuple-element.28.packs_ref.refs_0_), channel_id=1, source_target_pairs={{0,8},{2,10},{4,12},{6,14},{8,0},{10,2},{12,4},{14,6},{1,9},{3,11}... | collective-permute-start | bytes 110600 | tf_op jit(solution)/shard_map/ppermute | solution.py:311
  9.0 4.4 %collective-permute-start.1 = (f32[2,72,128]{2,1,0:T(8,128)S(1)}, f32[2,72,128]{2,1,0:T(8,128)S(1)}, u32[]{:S(2)}, u32[]{:S(2)}) collective-permute-start(f32[2,72,128]{2,1,0:T(8,128)S(1)} %shard_map.90.refs_0_), channel_id=1, source_target_pairs={{0,4},{2,6},{4,0},{6,2},{8,12},{10,14},{12,8},{14,10},{1,5},{3,7},... | collective-permute-start | bytes 221192 | tf_op jit(solution)/shard_map/ppermute | solution.py:311
  13.4 5.2 %collective-permute-start.2 = (f32[4,72,128]{2,1,0:T(8,128)S(1)}, f32[4,72,128]{2,1,0:T(8,128)S(1)}, u32[]{:S(2)}, u32[]{:S(2)}) collective-permute-start(f32[4,72,128]{2,1,0:T(8,128)S(1)} %shard_map.92), channel_id=1, source_target_pairs={{0,2},{2,0},{4,6},{6,4},{8,10},{10,8},{12,14},{14,12},{1,3},{3,1},... | collective-permute-start | bytes 442376 | tf_op jit(solution)/shard_map/ppermute | solution.py:311
  21.9 1.2 %collective-permute-start.3 = (f32[16,128]{1,0:T(8,128)S(1)}, f32[16,128]{1,0:T(8,128)S(1)}, u32[]{:S(2)}, u32[]{:S(2)}) collective-permute-start(f32[16,128]{1,0:T(8,128)S(1)} %get-tuple-element.48.refs_11_), channel_id=1, source_target_pairs={{0,1},{1,0},{2,3},{3,2},{4,5},{5,4},{6,7},{7,6},{8,9},{9,8},{10,11... | collective-permute-start | bytes 24584 | tf_op jit(solution)/shard_map/ppermute | solution.py:329

commit v5 on v4

--- a/solution.py
+++ b/solution.py
@@ -34,12 +34,10 @@
     return (mass + poten / entropic) * log2e
 
 
-def partners(shards):
-    found, apart = [0], shards // 2
-    while apart:
-        found += [other ^ apart for other in found]
-        apart //= 2
-    return found
+def blocks_at(shards):
+    odd = lax.rem(lax.axis_index("src"), 2)
+    half = shards // 2
+    return [2 * place + odd for place in range(half)] + [2 * place + 1 - odd for place in range(half)]
 
 
 def read_all(hbm, held, sems):
@@ -59,8 +57,11 @@
     weight = target_weight(mass_ref[...], poten_ref[...])
     norm = jnp.sum(feat * feat, axis=0, keepdims=True)
     bias = weight - (log2e / entropic) * norm
-    send_ref[0, :depth, :] = feat * (2.0 * log2e / entropic)
-    send_ref[0, depth:, :] = jnp.broadcast_to(bias, (send_ref.shape[1] - depth, cells))
+    scaled = feat * (2.0 * log2e / entropic)
+    below = jnp.broadcast_to(bias, (send_ref.shape[1] - depth, cells))
+    for copy in range(send_ref.shape[0]):
+        send_ref[copy, :depth, :] = scaled
+        send_ref[copy, depth:, :] = below
     weight_ref[...] = weight
 
 
@@ -75,11 +76,10 @@
     support = support_ref[...]
     slots, rows = support.shape
     cells = mass_ref.shape[1]
-    me = lax.axis_index("src")
     used = lax.broadcasted_iota(jnp.int32, support.shape, 0) < counts_ref[...]
     hits = [
-        jnp.max(jnp.where(used & (support == (me ^ other)), 0.0, very_low), axis=0, keepdims=True)
-        for other in partners(shards)
+        jnp.max(jnp.where(used & (support == block), 0.0, very_low), axis=0, keepdims=True)
+        for block in blocks_at(shards)
     ]
     hits = jnp.concatenate(hits + [jnp.zeros((cells - shards, rows), jnp.float32)], axis=0)
     hits = jnp.concatenate([hits, jnp.zeros((cells, cells - rows), jnp.float32)], axis=1).T
@@ -99,14 +99,6 @@
             wide_ref[pair, 2 * depth : 4 * depth, lanes] = top
             wide_ref[pair, 4 * depth : 6 * depth, lanes] = jnp.concatenate([low, high], axis=0).astype(jnp.bfloat16)
         wide_ref[pair, 6 * depth : 8 * depth, :] = one
-
-
-def join_kernel(*refs):
-    ins, out_ref = refs[:-2], refs[-1]
-    start = 0
-    for ref in ins:
-        out_ref[start : start + ref.shape[0]] = ref[...]
-        start += ref.shape[0]
 
 
 def tile_kernel(packs_ref, wide_ref, exps_ref, tall_ref, peak_ref, total_ref):
@@ -131,10 +123,10 @@
         tall_ref[rows, 3 * cells : 4 * cells] = own.astype(jnp.bfloat16)
 
     def body(pair, carry):
-        weights = wide_ref[pair]
+        scores = jnp.dot(tall_ref[...], wide_ref[pair], preferred_element_type=jnp.float32)
         for place in range(blocks):
             rows = slice(place * cells, (place + 1) * cells)
-            score = jnp.dot(tall_ref[rows, :], weights, preferred_element_type=jnp.float32)
+            score = scores[rows]
             peak = jnp.max(score, axis=0, keepdims=True)
             exps = jnp.exp2(score - peak)
             exps_ref[pair, rows, :] = exps
@@ -145,7 +137,7 @@
                 total_ref[place, pl.ds(2 * pair + half, 1), :] = total[:, lanes]
         return carry
 
-    lax.fori_loop(0, pairs, body, 0)
+    lax.fori_loop(0, pairs, body, 0, unroll=2)
 
 
 def row_kernel(groups, *refs):
@@ -162,19 +154,16 @@
     rowsum_ref[...] = top + jnp.log2(summed)
 
 
-def lane_sums(values):
-    ones = jnp.ones((8, values.shape[1]), jnp.bfloat16)
-    parts = [
-        lax.dot_general(ones, part.astype(jnp.bfloat16), (((1,), (1,)), ((), ())), preferred_element_type=jnp.float32)
-        for part in pieces(values)
-    ]
-    return sum(parts)[0:1, :]
+def across(column):
+    shape = (column.shape[0],) * 2
+    same = lax.broadcasted_iota(jnp.int32, shape, 0) == lax.broadcasted_iota(jnp.int32, shape, 1)
+    return jnp.sum(jnp.where(same, jnp.broadcast_to(column, shape), 0.0), axis=0, keepdims=True)
 
 
 def column_kernel(groups, *refs):
     exps_refs, tall_refs, rest = refs[:groups], refs[groups : 2 * groups], refs[2 * groups :]
     wide_ref, peak_ref, mask_ref, own_ref, other_ref, mass_ref, norm_ref = rest[:7]
-    poten_ref, sums_ref, weight_ref, acc_ref, shift_ref = rest[7:]
+    poten_ref, sums_ref, weight_ref, shift_ref = rest[7:]
     pairs, _, both = wide_ref.shape
     cells = both // 2
     shards = mask_ref.shape[0]
@@ -191,19 +180,15 @@
         for group, ref in enumerate(tall_refs)
         for index in range(ref.shape[0] // cells)
     ]
+    used = [jnp.max(mask_ref[place], axis=0, keepdims=True) > 0.5 * very_low for place in range(shards)]
+    worst = jnp.full((1, cells), 1.0, jnp.float32)
+    owners = blocks_at(shards)
     for place, (group, rows) in enumerate(spots):
         acc = jnp.zeros((cells, cells), jnp.float32)
         for pair in range(pairs):
             acc = acc + exps_refs[group][pair, rows, :cells] * weight_ref[place, 2 * pair : 2 * pair + 1, :]
             acc = acc + exps_refs[group][pair, rows, cells:] * weight_ref[place, 2 * pair + 1 : 2 * pair + 2, :]
-        acc_ref[place * cells : (place + 1) * cells, :] = acc
-    sums = lane_sums(acc_ref[...])
-    me = lax.axis_index("src")
-    owners = [me ^ other for other in partners(shards)]
-    used = [jnp.max(mask_ref[place], axis=0, keepdims=True) > 0.5 * very_low for place in range(shards)]
-    worst = jnp.full((1, cells), 1.0, jnp.float32)
-    for place in range(shards):
-        here = sums[:, place * cells : (place + 1) * cells]
+        here = across(jnp.sum(acc, axis=1, keepdims=True))
         sums_ref[owners[place]] = jnp.where(used[place], jnp.log2(here), very_low)
         worst = jnp.minimum(worst, jnp.where(used[place], here, 1.0))
 
@@ -221,18 +206,19 @@
                 return jnp.maximum(peak, jnp.maximum(first, second))
 
             peak = lax.fori_loop(0, pairs, highest, jnp.full((cells, cells), very_low, jnp.float32))
-            peak = jnp.broadcast_to(jnp.max(peak, axis=1, keepdims=True), (cells, cells))
+            peak = jnp.max(peak, axis=1, keepdims=True)
 
             def add_up(pair, sums):
                 first, second = exponents(pair)
                 return sums + jnp.exp2(first - peak) + jnp.exp2(second - peak)
 
             sums = lax.fori_loop(0, pairs, add_up, jnp.zeros((cells, cells), jnp.float32))
-            logs = peak.T[0:1, :] + jnp.log2(lane_sums(sums))
+            logs = across(peak) + jnp.log2(across(jnp.sum(sums, axis=1, keepdims=True)))
             sums_ref[owners[place]] = jnp.where(used[place], logs, very_low)
 
 
-def merge_kernel(values_ref, weight_ref, out_ref):
+def merge_kernel(values_ref, weight_ref, poten_ref, out_ref, poten_out_ref):
+    poten_out_ref[...] = poten_ref[...]
     values = values_ref[...]
     top = jnp.max(values, axis=0)
     whole = top + jnp.log2(jnp.sum(jnp.exp2(values - top), axis=0))
@@ -277,7 +263,7 @@
     pack, weight = reading(
         pack_kernel,
         [target_feat, log_mass_tgt, potential_tgt],
-        [in_vmem((1, depth + 8, cells), jnp.float32), in_vmem((1, cells), jnp.float32)],
+        [in_vmem((shards // 2, depth + 8, cells), jnp.float32), in_vmem((1, cells), jnp.float32)],
         None,
     )
     wide_feat, norm, mask, mass = reading(
@@ -306,19 +292,10 @@
             cost=cost_of(2 * blocks * cells * pairs * wide * 8 * depth),
         )(packs, wide_feat)
 
-    held, found, apart = pack, [tiles(pack)], shards // 2
-    while apart:
-        there = lax.ppermute(held, "src", [(i, i ^ apart) for i in range(shards)])
-        before = found[-1][-1]
-        found.append(tiles(there))
-        apart //= 2
-        if apart:
-            count = 2 * held.shape[0]
-            held = call(
-                join_kernel,
-                [VM] * 2 + [pl.BlockSpec(memory_space=pl.ANY)],
-                in_vmem((count,) + held.shape[1:], jnp.float32),
-            )(held, there, before)
+    same = [list(range(odd, shards, 2)) for odd in range(2)]
+    near = lax.all_to_all(pack, "src", 0, 0, axis_index_groups=same)
+    far = lax.ppermute(near, "src", [(i, i ^ 1) for i in range(shards)])
+    found = [tiles(near), tiles(far)]
     exps, tall, peaks, totals = zip(*found)
     groups = len(found)
     peaks, own = call(
@@ -330,15 +307,15 @@
     potential_src, columns = call(
         functools.partial(column_kernel, groups),
         [VM] * (2 * groups + 7),
-        [f32(rows, cells), in_vmem((shards, 1, cells), jnp.float32)],
+        [in_vmem((rows, cells), jnp.float32), in_vmem((shards, 1, cells), jnp.float32)],
         [
             pltpu.VMEM((shards, rows, cells), jnp.float32),
-            pltpu.VMEM((shards * cells, cells), jnp.float32),
             pltpu.VMEM((rows, cells), jnp.float32),
         ],
     )(*exps, *tall, wide_feat, peaks, mask, own, other, mass, norm)
     arrived = lax.all_to_all(columns, "src", 0, 0)
-    potential_new = call(merge_kernel, [VM] * 2, f32(1, cells))(arrived, weight)
+    outs = [f32(1, cells), f32(rows, cells)]
+    potential_new, potential_src = call(merge_kernel, [VM] * 3, outs)(arrived, weight, potential_src)
     return potential_src, potential_new
 
 

time: 64.3 us -> 61.3 us (0.953)
  blocking collectives: 11.1 us -> 22.4 us
  Pallas kernels: 41.9 us -> 35.3 us
  starting transfers between devices: 7.37 us -> 1.56 us
  waiting for transfers between devices: 3.01 us -> 1.16 us
    all_to_all x0 -> x1, blocking collectives: none -> 12.8 us  [dense_device(): near = lax.all_to_all(pack, 'src', 0, 0, axis_index_groups=same)]
    ppermute x3 -> x1, starting transfers between devices: 7.3 us -> 1.49 us  [dense_device(): far = lax.ppermute(near, 'src', [(i, i ^ 1) for i in range(shards)])]
    pallas_call x4 -> x2, Pallas kernels: 9.81 us -> 4.69 us  [tiles(): call(tile_kernel, [VM] * 2, [in_vmem((pairs, blocks * cells, wide), jnp.f...]
    ppermute x3 -> x1, waiting for transfers between devices: 1.86 us -> 0.01 us  [dense_device(): far = lax.ppermute(near, 'src', [(i, i ^ 1) for i in range(shards)])]
    pallas_call x1, Pallas kernels: 29.3 us -> 27.8 us  [dense_device(): call(functools.partial(column_kernel, groups), [VM] * (2 * groups + 7), [...]
    all_to_all x1, blocking collectives: 11.1 us -> 9.6 us  [dense_device(): arrived = lax.all_to_all(columns, 'src', 0, 0)]
  transfers between devices with their start and end apart: 4 -> 2, of which waited for: 3 -> 1; matrix products, arithmetic and copies ran while one was open for 0% -> 0% of each run, Pallas kernels for 12% -> 6%
where the time goes in v5:
time: 61.3 us; the launch traced here: 61.1 us
  Pallas kernels  35.3 us (58%)
  blocking collectives  22.4 us (37%)
  starting transfers between devices  1.56 us (3%)
  waiting for transfers between devices  1.16 us (2%)
  between operations  0.68 us (1%)
    pallas_call x1, Pallas kernels, dense_device(): call(functools.partial(column_kernel, groups), [VM] * (2 * groups + 7), [...  27.8 us
    all_to_all x1, blocking collectives, dense_device(): near = lax.all_to_all(pack, 'src', 0, 0, axis_index_groups=same)  12.8 us
    all_to_all x1, blocking collectives, dense_device(): arrived = lax.all_to_all(columns, 'src', 0, 0)  9.6 us
    pallas_call x2, Pallas kernels, tiles(): call(tile_kernel, [VM] * 2, [in_vmem((pairs, blocks * cells, wide), jnp.f...  4.69 us
    pallas_call x2, Pallas kernels, reading(): call(kernel, [pl.BlockSpec(memory_space=pltpu.HBM)] * len(args), out_shap...  2.17 us
    ppermute x1, starting transfers between devices, dense_device(): far = lax.ppermute(near, 'src', [(i, i ^ 1) for i in range(shards)])  1.49 us
  transfers between devices with their start and end apart: 2, of which 1 were waited for; matrix products, arithmetic and copies ran while one was open for 0% of the time, Pallas kernels for 6%

profile of v5, /device:TPU:0, one launch (start us, length us, event | category | flops | bytes accessed | tf_op | source)
XLA Modules:
  0.0 61.1 jit_solution(7130656553076947010)
XLA Ops:
  0.6 0.8 %shard_map.86 = (f32[4,72,128]{2,1,0:T(8,128)S(1)}, f32[1,128]{1,0:T(1,128)S(1)}) custom-call(f32[1,64,128]{2,1,0:T(8,128)} %refs_0_.2, f32[1,128]{1,0:T(1,128)} %refs_1_.1, f32[1,128]{1,0:T(1,128)} %refs_2_.1), custom_call_target="tpu_custom_call" | custom-call | tf_op jit(solution)/shard_map/pallas_call | solution.py:252
  1.4 12.8 %all_to_all.10.packs_ref = f32[4,72,128]{2,1,0:T(8,128)S(1)} all-to-all(f32[4,72,128]{2,1,0:T(8,128)S(1)} %get-tuple-element.22), channel_id=1, replica_groups={{0,4,8,12},{2,6,10,14},{1,5,9,13},{3,7,11,15},{16,20,24,28},{18,22,26,3..., dimensions={0} | all-to-all | bytes 294912 | tf_op jit(solution)/shard_map/all_to_all | solution.py:296
  14.2 1.5 %collective-permute-start = (f32[4,72,128]{2,1,0:T(8,128)S(1)}, f32[4,72,128]{2,1,0:T(8,128)S(1)}, u32[]{:S(2)}, u32[]{:S(2)}) collective-permute-start(f32[4,72,128]{2,1,0:T(8,128)S(1)} %all_to_all.10.packs_ref), channel_id=1, source_target_pairs={{0,2},{2,0},{4,6},{6,4},{8,10},{10,8},{12,14},{14,12},{1,3},{3,1},... | collective-permute-start | bytes 442376 | tf_op jit(solution)/shard_map/ppermute | solution.py:297
  15.7 1.4 %shard_map.87 = (bf16[8,512,256]{2,1,0:T(8,128)(2,1)S(1)}, f32[16,128]{1,0:T(8,128)S(1)}, f32[8,16,128]{2,1,0:T(8,128)S(1)}, f32[16,128]{1,0:T(8,128)S(1)}) custom-call(f32[16,128]{1,0:T(8,128)} %refs_0_.3, s32[8,16]{1,0:T(8,128)} %bitcast.4, s32[1,16]{1,0:T(1,128)} %bitcast.5, f32[16,64,128]{2,1,0:T(8,128)} %refs_3_.1), custom_call_target="tpu_custom_call" | custom-call | flops 1000000000 | bytes 524288 | tf_op jit(solution)/shard_map/pallas_call | solution.py:252
  17.1 2.3 %shard_map.88 = (f32[8,512,256]{2,1,0:T(8,128)S(1)}, bf16[512,512]{1,0:T(8,128)(2,1)S(1)}, f32[4,16,128]{2,1,0:T(8,128)S(1)}, f32[4,16,128]{2,1,0:T(8,128)S(1)}) custom-call(f32[4,72,128]{2,1,0:T(8,128)S(1)} %all_to_all.10.packs_ref, bf16[8,512,256]{2,1,0:T(8,128)(2,1)S(1)} %get-tuple-element.23.wide_ref.refs_4_), custom_call_target="tpu_custom_call" | custom-call | flops 1073741824 | bytes 524288 | tf_op jit(solution)/shard_map/pallas_call | solution.py:283
  19.4 0.0 collective-permute-done.packs_ref
  19.4 2.3 %shard_map.89 = (f32[8,512,256]{2,1,0:T(8,128)S(1)}, bf16[512,512]{1,0:T(8,128)(2,1)S(1)}, f32[4,16,128]{2,1,0:T(8,128)S(1)}, f32[4,16,128]{2,1,0:T(8,128)S(1)}) custom-call(f32[4,72,128]{2,1,0:T(8,128)S(1)} %collective-permute-done.packs_ref, bf16[8,512,256]{2,1,0:T(8,128)(2,1)S(1)} %get-tuple-element.23.wide_ref.refs_4_), custom_call_target="tpu_custom_call" | custom-call | flops 1073741824 | bytes 524288 | tf_op jit(solution)/shard_map/pallas_call | solution.py:283
  21.8 0.1 collective-permute-start.1
  21.9 1.2 %collective-permute-done.1.refs_8_ = f32[16,128]{1,0:T(8,128)S(1)} collective-permute-done((f32[16,128]{1,0:T(8,128)S(1)}, f32[16,128]{1,0:T(8,128)S(1)}, u32[]{:S(2)}, u32[]{:S(2)}) %collective-permute-start.1) | collective-permute-done | bytes 8224 | tf_op jit(solution)/shard_map/ppermute | solution.py:306
  23.1 27.8 %shard_map.91 = (f32[16,128]{1,0:T(8,128)S(1)}, f32[8,1,128]{2,1,0:T(1,128)S(1)}) custom-call(f32[8,512,256]{2,1,0:T(8,128)S(1)} %get-tuple-element.24.refs_0_, f32[8,512,256]{2,1,0:T(8,128)S(1)} %get-tuple-element.25.refs_1_, bf16[512,512]{1,0:T(8,128)(2,1)S(1)} %get-tuple-element.26.refs_2_, bf16[512,512]{1,0:T(8,128)(2,1)S(1)} %get-tuple-element.27.refs_3_, ...), custom_call_target="tpu_custom_call" | custom-call | tf_op jit(solution)/shard_map/pallas_call | solution.py:307
  50.8 9.6 %all_to_all.11.values_ref = f32[8,1,128]{2,1,0:T(1,128)S(1)} all-to-all(f32[8,1,128]{2,1,0:T(1,128)S(1)} %get-tuple-element.37), channel_id=1, replica_groups=mesh['grp'=2,'src'=8,'tgt'=2] {'src'}, dimensions={0} | all-to-all | bytes 8192 | tf_op jit(solution)/shard_map/all_to_all | solution.py:316
  60.5 0.6 shard_map.92
  (1 shorter events, 0.0 us)
Async XLA Ops:
  14.2 5.2 %collective-permute-start = (f32[4,72,128]{2,1,0:T(8,128)S(1)}, f32[4,72,128]{2,1,0:T(8,128)S(1)}, u32[]{:S(2)}, u32[]{:S(2)}) collective-permute-start(f32[4,72,128]{2,1,0:T(8,128)S(1)} %all_to_all.10.packs_ref), channel_id=1, source_target_pairs={{0,2},{2,0},{4,6},{6,4},{8,10},{10,8},{12,14},{14,12},{1,3},{3,1},... | collective-permute-start | bytes 442376 | tf_op jit(solution)/shard_map/ppermute | solution.py:297
  21.8 1.2 %collective-permute-start.1 = (f32[16,128]{1,0:T(8,128)S(1)}, f32[16,128]{1,0:T(8,128)S(1)}, u32[]{:S(2)}, u32[]{:S(2)}) collective-permute-start(f32[16,128]{1,0:T(8,128)S(1)} %get-tuple-element.34.refs_7_), channel_id=1, source_target_pairs={{0,1},{1,0},{2,3},{3,2},{4,5},{5,4},{6,7},{7,6},{8,9},{9,8},{10,11... | collective-permute-start | bytes 24584 | tf_op jit(solution)/shard_map/ppermute | solution.py:306

commit v6 on v5

--- a/solution.py
+++ b/solution.py
@@ -59,9 +59,8 @@
     bias = weight - (log2e / entropic) * norm
     scaled = feat * (2.0 * log2e / entropic)
     below = jnp.broadcast_to(bias, (send_ref.shape[1] - depth, cells))
-    for copy in range(send_ref.shape[0]):
-        send_ref[copy, :depth, :] = scaled
-        send_ref[copy, depth:, :] = below
+    send_ref[0, :depth, :] = scaled
+    send_ref[0, depth:, :] = below
     weight_ref[...] = weight
 
 
@@ -101,18 +100,40 @@
         wide_ref[pair, 6 * depth : 8 * depth, :] = one
 
 
-def tile_kernel(packs_ref, wide_ref, exps_ref, tall_ref, peak_ref, total_ref):
-    blocks = packs_ref.shape[0]
+def bundle_kernel(first_ref, second_ref, out_ref):
+    count = first_ref.shape[0]
+    out_ref[:count] = first_ref[...]
+    out_ref[count:] = second_ref[...]
+
+
+def order_kernel(line, *refs):
+    own_ref, up_refs, down_refs = refs[0], refs[1:line], refs[line : 2 * line - 1]
+    out_refs = refs[2 * line - 1 :]
+    here = lax.axis_index("src") // 2
+    for block in range(line):
+        value = own_ref[0]
+        for at in range(line):
+            if at < block:
+                value = jnp.where(here == at, down_refs[line - 2 - at][block - at - 1], value)
+            if at > block:
+                value = jnp.where(here == at, up_refs[at - 1][block], value)
+        out_refs[block // (line // 2)][block % (line // 2)] = value
+
+
+def tile_kernel(parts, *refs):
+    packs = [ref.at[index] for ref in refs[:parts] for index in range(ref.shape[0])]
+    wide_ref, exps_ref, tall_ref, peak_ref, total_ref = refs[parts:]
+    blocks = len(packs)
     pairs, _, both = wide_ref.shape
     cells = both // 2
     depth = cells // 2
     lane = lax.broadcasted_iota(jnp.int32, (cells, cells), 1)
-    biases = jnp.concatenate([packs_ref[place, depth : depth + 1, :] for place in range(blocks)], axis=0)
+    biases = jnp.concatenate([pack[depth : depth + 1, :] for pack in packs], axis=0)
     bias_pieces = jnp.concatenate(list(pieces(biases)), axis=0)
     padded = jnp.concatenate([bias_pieces, jnp.zeros((cells - 3 * blocks, cells), jnp.float32)], axis=0)
     bias_lanes = padded.T
-    for place in range(blocks):
-        feat = packs_ref[place, :depth, :]
+    for place, pack in enumerate(packs):
+        feat = pack[:depth, :]
         turned = jnp.concatenate([feat, feat], axis=0).T
         high, mid, low = pieces(turned)
         own = jnp.where(lax.rem(lane, blocks) == place, bias_lanes, 0.0)
@@ -137,7 +158,7 @@
                 total_ref[place, pl.ds(2 * pair + half, 1), :] = total[:, lanes]
         return carry
 
-    lax.fori_loop(0, pairs, body, 0, unroll=2)
+    lax.fori_loop(0, pairs, body, 0, unroll=max(1, 2 * pairs // blocks))
 
 
 def row_kernel(groups, *refs):
@@ -263,7 +284,7 @@
     pack, weight = reading(
         pack_kernel,
         [target_feat, log_mass_tgt, potential_tgt],
-        [in_vmem((shards // 2, depth + 8, cells), jnp.float32), in_vmem((1, cells), jnp.float32)],
+        [in_vmem((1, depth + 8, cells), jnp.float32), in_vmem((1, cells), jnp.float32)],
         None,
     )
     wide_feat, norm, mask, mass = reading(
@@ -278,11 +299,11 @@
         cost_of(10**9),
     )
 
-    def tiles(packs):
-        blocks = packs.shape[0]
+    def tiles(*packs):
+        blocks = sum(pack.shape[0] for pack in packs)
         return call(
-            tile_kernel,
-            [VM] * 2,
+            functools.partial(tile_kernel, len(packs)),
+            [VM] * (len(packs) + 1),
             [
                 in_vmem((pairs, blocks * cells, wide), jnp.float32),
                 in_vmem((blocks * cells, 8 * depth), jnp.bfloat16),
@@ -290,12 +311,28 @@
                 in_vmem((blocks, rows, cells), jnp.float32),
             ],
             cost=cost_of(2 * blocks * cells * pairs * wide * 8 * depth),
-        )(packs, wide_feat)
-
-    same = [list(range(odd, shards, 2)) for odd in range(2)]
-    near = lax.all_to_all(pack, "src", 0, 0, axis_index_groups=same)
-    far = lax.ppermute(near, "src", [(i, i ^ 1) for i in range(shards)])
-    found = [tiles(near), tiles(far)]
+        )(*packs, wide_feat)
+
+    line = shards // 2
+
+    def moved(array, start, end):
+        return lax.ppermute(array, "src", [(2 * start + odd, 2 * end + odd) for odd in range(2)])
+
+    def bundle(first, second):
+        shape = (first.shape[0] + second.shape[0],) + pack.shape[1:]
+        return call(bundle_kernel, [VM] * 2, in_vmem(shape, jnp.float32))(first, second)
+
+    up, down = [], []
+    for at in range(line - 1):
+        down.append(moved(bundle(pack, down[-1]) if at else pack, line - 1 - at, line - 2 - at))
+        up.append(moved(bundle(up[-1], pack) if at else pack, at, at + 1))
+    near = call(
+        functools.partial(order_kernel, line),
+        [VM] * (2 * line - 1),
+        [in_vmem((line // 2,) + pack.shape[1:], jnp.float32)] * 2,
+    )(pack, *up, *down)
+    far = [lax.ppermute(half, "src", [(i, i ^ 1) for i in range(shards)]) for half in near]
+    found = [tiles(*near)] + [tiles(half) for half in far]
     exps, tall, peaks, totals = zip(*found)
     groups = len(found)
     peaks, own = call(
@@ -446,7 +483,7 @@
     shards = lax.axis_size("src")
     rows, depth, cells = source_feat.shape
     few = shards == 8 and target_feat.shape[0] == 1 and lax.axis_size("tgt") == 2
-    if few and rows % 2 == 0 and cells == 128 and depth == 64:
+    if few and rows % 8 == 0 and cells == 128 and depth == 64:
         return dense_device(source_feat, target_feat, *others)
     return general_device(source_feat, target_feat, *others)
 

time: 61.3 us -> 67.5 us (1.10)
  blocking collectives: 22.4 us -> 8.83 us
  waiting for transfers between devices: 1.16 us -> 12.3 us
  starting transfers between devices: 1.56 us -> 11 us
  Pallas kernels: 35.3 us -> 34.2 us
    all_to_all x1 -> x0, blocking collectives: 12.8 us -> none  [dense_device(): near = lax.all_to_all(pack, 'src', 0, 0, axis_index_groups=same)]
    ppermute x1 -> x8, waiting for transfers between devices: 0.01 us -> 11.1 us  [the longest x6 10.1 us: moved(): lax.ppermute(array, 'src', [(2 * start + odd, 2 * end + odd) for odd in r...]
    ppermute x1 -> x8, starting transfers between devices: 1.49 us -> 11 us  [the longest x6 8.87 us: moved(): lax.ppermute(array, 'src', [(2 * start + odd, 2 * end + odd) for odd in r...]
    pallas_call x2 -> x8, Pallas kernels: 4.69 us -> 3.69 us  [the longest x3 3.62 us: tiles(): call(functools.partial(tile_kernel, len(packs)), [VM] * (len(packs) + 1),...]
    all_to_all x1, blocking collectives: 9.6 us -> 8.83 us  [dense_device(): arrived = lax.all_to_all(columns, 'src', 0, 0)]
  transfers between devices with their start and end apart: 2 -> 9, of which waited for: 1 -> 5; matrix products, arithmetic and copies ran while one was open for 0% -> 0% of each run, Pallas kernels for 6% -> 6%
where the time goes in v6:
time: 67.5 us; the launch traced here: 67.1 us
  Pallas kernels  34.2 us (51%)
  waiting for transfers between devices  12.3 us (18%)
  starting transfers between devices  11 us (16%)
  blocking collectives  8.83 us (13%)
  between operations  0.78 us (1%)
    pallas_call x1, Pallas kernels, dense_device(): call(functools.partial(column_kernel, groups), [VM] * (2 * groups + 7), [...  27.7 us
    ppermute x6, waiting for transfers between devices, moved(): lax.ppermute(array, 'src', [(2 * start + odd, 2 * end + odd) for odd in r...  10.1 us
    ppermute x6, starting transfers between devices, moved(): lax.ppermute(array, 'src', [(2 * start + odd, 2 * end + odd) for odd in r...  8.87 us
    all_to_all x1, blocking collectives, dense_device(): arrived = lax.all_to_all(columns, 'src', 0, 0)  8.83 us
    pallas_call x3, Pallas kernels, tiles(): call(functools.partial(tile_kernel, len(packs)), [VM] * (len(packs) + 1),...  3.62 us
    pallas_call x2, Pallas kernels, reading(): call(kernel, [pl.BlockSpec(memory_space=pltpu.HBM)] * len(args), out_shap...  2.18 us
    ppermute x2, starting transfers between devices, dense_device(): lax.ppermute(half, 'src', [(i, i ^ 1) for i in range(shards)])  2.09 us
  transfers between devices with their start and end apart: 9, of which 5 were waited for; matrix products, arithmetic and copies ran while one was open for 0% of the time, Pallas kernels for 6%

profile of v6, /device:TPU:0, one launch (start us, length us, event | category | flops | bytes accessed | tf_op | source)
XLA Modules:
  0.0 67.1 jit_solution(14329919351477085844)
XLA Ops:
  0.6 0.8 %shard_map.86 = (f32[1,72,128]{2,1,0:T(8,128)S(1)}, f32[1,128]{1,0:T(1,128)S(1)}) custom-call(f32[1,64,128]{2,1,0:T(8,128)} %refs_0_.2, f32[1,128]{1,0:T(1,128)} %refs_1_.1, f32[1,128]{1,0:T(1,128)} %refs_2_.1), custom_call_target="tpu_custom_call" | custom-call | tf_op jit(solution)/shard_map/pallas_call | solution.py:273
  1.4 4.9 %collective-permute-start = (f32[1,72,128]{2,1,0:T(8,128)S(1)}, f32[1,72,128]{2,1,0:T(8,128)S(1)}, u32[]{:S(2)}, u32[]{:S(2)}) collective-permute-start(f32[1,72,128]{2,1,0:T(8,128)S(1)} %get-tuple-element.28.second_ref.first_ref.refs_0_), channel_id=1, source_target_pairs={{0,4},{2,6},{1,5},{3,7},{16,20},{18,22},{17,21},{19,23}} | collective-permute-start | bytes 110600 | tf_op jit(solution)/shard_map/ppermute | solution.py:319
  6.4 0.7 collective-permute-start.3
  7.1 0.9 %collective-permute-done.first_ref.refs_1_ = f32[1,72,128]{2,1,0:T(8,128)S(1)} collective-permute-done((f32[1,72,128]{2,1,0:T(8,128)S(1)}, f32[1,72,128]{2,1,0:T(8,128)S(1)}, u32[]{:S(2)}, u32[]{:S(2)}) %collective-permute-start) | collective-permute-done | bytes 36896 | tf_op jit(solution)/shard_map/ppermute | solution.py:319
  8.0 0.7 collective-permute-start.1
  8.7 0.0 collective-permute-done.3.second_ref.refs_4_
  8.7 0.7 collective-permute-start.4
  9.4 0.0 collective-permute-done.1.first_ref.refs_2_
  9.4 0.7 collective-permute-start.2
  10.1 0.0 collective-permute-done.4.second_ref.refs_5_
  10.1 1.3 %collective-permute-start.5 = (f32[3,72,128]{2,1,0:T(8,128)S(1)}, f32[3,72,128]{2,1,0:T(8,128)S(1)}, u32[]{:S(2)}, u32[]{:S(2)}) collective-permute-start(f32[3,72,128]{2,1,0:T(8,128)S(1)} %shard_map.90), channel_id=1, source_target_pairs={{4,0},{6,2},{5,1},{7,3},{20,16},{22,18},{21,17},{23,19}} | collective-permute-start | bytes 331784 | tf_op jit(solution)/shard_map/ppermute | solution.py:319
  11.4 1.4 %shard_map.92 = (bf16[8,512,256]{2,1,0:T(8,128)(2,1)S(1)}, f32[16,128]{1,0:T(8,128)S(1)}, f32[8,16,128]{2,1,0:T(8,128)S(1)}, f32[16,128]{1,0:T(8,128)S(1)}) custom-call(f32[16,128]{1,0:T(8,128)} %refs_0_.3, s32[8,16]{1,0:T(8,128)} %bitcast.4, s32[1,16]{1,0:T(1,128)} %bitcast.5, f32[16,64,128]{2,1,0:T(8,128)} %refs_3_.1), custom_call_target="tpu_custom_call" | custom-call | flops 1000000000 | bytes 524288 | tf_op jit(solution)/shard_map/pallas_call | solution.py:273
  12.8 0.0 collective-permute-done.2.refs_3_
  12.8 9.1 %collective-permute-done.5.refs_6_ = f32[3,72,128]{2,1,0:T(8,128)S(1)} collective-permute-done((f32[3,72,128]{2,1,0:T(8,128)S(1)}, f32[3,72,128]{2,1,0:T(8,128)S(1)}, u32[]{:S(2)}, u32[]{:S(2)}) %collective-permute-start.5) | collective-permute-done | bytes 110624 | tf_op jit(solution)/shard_map/ppermute | solution.py:319
  21.9 1.6 %collective-permute-start.6 = (f32[2,72,128]{2,1,0:T(8,128)S(1)}, f32[2,72,128]{2,1,0:T(8,128)S(1)}, u32[]{:S(2)}, u32[]{:S(2)}) collective-permute-start(f32[2,72,128]{2,1,0:T(8,128)S(1)} %get-tuple-element.29.refs_0_), channel_id=1, source_target_pairs={{0,2},{2,0},{4,6},{6,4},{8,10},{10,8},{12,14},{14,12},{1,3},{3,1},... | collective-permute-start | bytes 221192 | tf_op jit(solution)/shard_map/ppermute | solution.py:334
  23.5 0.5 collective-permute-start.7
  24.0 1.9 %shard_map.93 = (f32[8,512,256]{2,1,0:T(8,128)S(1)}, bf16[512,512]{1,0:T(8,128)(2,1)S(1)}, f32[4,16,128]{2,1,0:T(8,128)S(1)}, f32[4,16,128]{2,1,0:T(8,128)S(1)}) custom-call(f32[2,72,128]{2,1,0:T(8,128)S(1)} %get-tuple-element.29.refs_0_, f32[2,72,128]{2,1,0:T(8,128)S(1)} %get-tuple-element.30.refs_1_, ...), custom_call_target="tpu_custom_call" | custom-call | flops 1073741824 | bytes 524288 | tf_op jit(solution)/shard_map/pallas_call | solution.py:304
  25.9 0.4 collective-permute-done.6.refs_0_
  26.4 0.9 %shard_map.94 = (f32[8,256,256]{2,1,0:T(8,128)S(1)}, bf16[256,512]{1,0:T(8,128)(2,1)S(1)}, f32[2,16,128]{2,1,0:T(8,128)S(1)}, f32[2,16,128]{2,1,0:T(8,128)S(1)}) custom-call(f32[2,72,128]{2,1,0:T(8,128)S(1)} %collective-permute-done.6.refs_0_, bf16[8,512,256]{2,1,0:T(8,128)(2,1)S(1)} %get-tuple-element.31.refs_2_.refs_1_.refs_6_), custom_call_target="tpu_custom_call" | custom-call | flops 536870912 | bytes 524288 | tf_op jit(solution)/shard_map/pallas_call | solution.py:304
  27.2 0.6 collective-permute-done.7.refs_0_
  27.9 0.9 %shard_map.95 = (f32[8,256,256]{2,1,0:T(8,128)S(1)}, bf16[256,512]{1,0:T(8,128)(2,1)S(1)}, f32[2,16,128]{2,1,0:T(8,128)S(1)}, f32[2,16,128]{2,1,0:T(8,128)S(1)}) custom-call(f32[2,72,128]{2,1,0:T(8,128)S(1)} %collective-permute-done.7.refs_0_, bf16[8,512,256]{2,1,0:T(8,128)(2,1)S(1)} %get-tuple-element.31.refs_2_.refs_1_.refs_6_), custom_call_target="tpu_custom_call" | custom-call | flops 536870912 | bytes 524288 | tf_op jit(solution)/shard_map/pallas_call | solution.py:304
  28.8 0.1 collective-permute-start.8
  28.8 1.2 %collective-permute-done.8.refs_10_ = f32[16,128]{1,0:T(8,128)S(1)} collective-permute-done((f32[16,128]{1,0:T(8,128)S(1)}, f32[16,128]{1,0:T(8,128)S(1)}, u32[]{:S(2)}, u32[]{:S(2)}) %collective-permute-start.8) | collective-permute-done | bytes 8224 | tf_op jit(solution)/shard_map/ppermute | solution.py:343
  30.0 27.7 %shard_map.97 = (f32[16,128]{1,0:T(8,128)S(1)}, f32[8,1,128]{2,1,0:T(1,128)S(1)}) custom-call(f32[8,512,256]{2,1,0:T(8,128)S(1)} %get-tuple-element.32.refs_0_, f32[8,256,256]{2,1,0:T(8,128)S(1)} %get-tuple-element.33.refs_1_, f32[8,256,256]{2,1,0:T(8,128)S(1)} %get-tuple-element.34.refs_2_, bf16[512,512]{1,0:T(8,128)(2,1)S(1)} %get-tuple-element.35.refs_3_, ...), custom_call_target="tpu_custom_call" | custom-call | tf_op jit(solution)/shard_map/pallas_call | solution.py:344
  57.7 8.8 %all_to_all.5.values_ref = f32[8,1,128]{2,1,0:T(1,128)S(1)} all-to-all(f32[8,1,128]{2,1,0:T(1,128)S(1)} %get-tuple-element.49), channel_id=1, replica_groups=mesh['grp'=2,'src'=8,'tgt'=2] {'src'}, dimensions={0} | all-to-all | bytes 8192 | tf_op jit(solution)/shard_map/all_to_all | solution.py:353
  66.5 0.6 shard_map.98
  (6 shorter events, 0.1 us)
Async XLA Ops:
  1.4 6.6 %collective-permute-start = (f32[1,72,128]{2,1,0:T(8,128)S(1)}, f32[1,72,128]{2,1,0:T(8,128)S(1)}, u32[]{:S(2)}, u32[]{:S(2)}) collective-permute-start(f32[1,72,128]{2,1,0:T(8,128)S(1)} %get-tuple-element.28.second_ref.first_ref.refs_0_), channel_id=1, source_target_pairs={{0,4},{2,6},{1,5},{3,7},{16,20},{18,22},{17,21},{19,23}} | collective-permute-start | bytes 110600 | tf_op jit(solution)/shard_map/ppermute | solution.py:319
  6.4 2.3 %collective-permute-start.3 = (f32[1,72,128]{2,1,0:T(8,128)S(1)}, f32[1,72,128]{2,1,0:T(8,128)S(1)}, u32[]{:S(2)}, u32[]{:S(2)}) collective-permute-start(f32[1,72,128]{2,1,0:T(8,128)S(1)} %get-tuple-element.28.second_ref.first_ref.refs_0_), channel_id=1, source_target_pairs={{12,8},{14,10},{13,9},{15,11},{28,24},{30,26},{29,25},{31,27}} | collective-permute-start | bytes 110600 | tf_op jit(solution)/shard_map/ppermute | solution.py:319
  8.0 1.4 %collective-permute-start.1 = (f32[2,72,128]{2,1,0:T(8,128)S(1)}, f32[2,72,128]{2,1,0:T(8,128)S(1)}, u32[]{:S(2)}, u32[]{:S(2)}) collective-permute-start(f32[2,72,128]{2,1,0:T(8,128)S(1)} %shard_map.87), channel_id=1, source_target_pairs={{4,8},{6,10},{5,9},{7,11},{20,24},{22,26},{21,25},{23,27}} | collective-permute-start | bytes 221192 | tf_op jit(solution)/shard_map/ppermute | solution.py:319
  8.7 1.4 %collective-permute-start.4 = (f32[2,72,128]{2,1,0:T(8,128)S(1)}, f32[2,72,128]{2,1,0:T(8,128)S(1)}, u32[]{:S(2)}, u32[]{:S(2)}) collective-permute-start(f32[2,72,128]{2,1,0:T(8,128)S(1)} %shard_map.89), channel_id=1, source_target_pairs={{8,4},{10,6},{9,5},{11,7},{24,20},{26,22},{25,21},{27,23}} | collective-permute-start | bytes 221192 | tf_op jit(solution)/shard_map/ppermute | solution.py:319
  9.4 3.4 %collective-permute-start.2 = (f32[3,72,128]{2,1,0:T(8,128)S(1)}, f32[3,72,128]{2,1,0:T(8,128)S(1)}, u32[]{:S(2)}, u32[]{:S(2)}) collective-permute-start(f32[3,72,128]{2,1,0:T(8,128)S(1)} %shard_map.88), channel_id=1, source_target_pairs={{8,12},{10,14},{9,13},{11,15},{24,28},{26,30},{25,29},{27,31}} | collective-permute-start | bytes 331784 | tf_op jit(solution)/shard_map/ppermute | solution.py:319
  10.1 11.8 %collective-permute-start.5 = (f32[3,72,128]{2,1,0:T(8,128)S(1)}, f32[3,72,128]{2,1,0:T(8,128)S(1)}, u32[]{:S(2)}, u32[]{:S(2)}) collective-permute-start(f32[3,72,128]{2,1,0:T(8,128)S(1)} %shard_map.90), channel_id=1, source_target_pairs={{4,0},{6,2},{5,1},{7,3},{20,16},{22,18},{21,17},{23,19}} | collective-permute-start | bytes 331784 | tf_op jit(solution)/shard_map/ppermute | solution.py:319
  21.9 4.4 %collective-permute-start.6 = (f32[2,72,128]{2,1,0:T(8,128)S(1)}, f32[2,72,128]{2,1,0:T(8,128)S(1)}, u32[]{:S(2)}, u32[]{:S(2)}) collective-permute-start(f32[2,72,128]{2,1,0:T(8,128)S(1)} %get-tuple-element.29.refs_0_), channel_id=1, source_target_pairs={{0,2},{2,0},{4,6},{6,4},{8,10},{10,8},{12,14},{14,12},{1,3},{3,1},... | collective-permute-start | bytes 221192 | tf_op jit(solution)/shard_map/ppermute | solution.py:334
  23.5 4.4 %collective-permute-start.7 = (f32[2,72,128]{2,1,0:T(8,128)S(1)}, f32[2,72,128]{2,1,0:T(8,128)S(1)}, u32[]{:S(2)}, u32[]{:S(2)}) collective-permute-start(f32[2,72,128]{2,1,0:T(8,128)S(1)} %get-tuple-element.30.refs_1_), channel_id=1, source_target_pairs={{0,2},{2,0},{4,6},{6,4},{8,10},{10,8},{12,14},{14,12},{1,3},{3,1},... | collective-permute-start | bytes 221192 | tf_op jit(solution)/shard_map/ppermute | solution.py:334
  28.8 1.2 %collective-permute-start.8 = (f32[16,128]{1,0:T(8,128)S(1)}, f32[16,128]{1,0:T(8,128)S(1)}, u32[]{:S(2)}, u32[]{:S(2)}) collective-permute-start(f32[16,128]{1,0:T(8,128)S(1)} %get-tuple-element.46.refs_9_), channel_id=1, source_target_pairs={{0,1},{1,0},{2,3},{3,2},{4,5},{5,4},{6,7},{7,6},{8,9},{9,8},{10,11... | collective-permute-start | bytes 24584 | tf_op jit(solution)/shard_map/ppermute | solution.py:343

commit v7 on v6

--- a/solution.py
+++ b/solution.py
@@ -34,10 +34,14 @@
     return (mass + poten / entropic) * log2e
 
 
+def line_steps(shards):
+    return [2 * (i ^ (i >> 1)) for i in range(shards // 2 - 1, 0, -1)]
+
+
 def blocks_at(shards):
-    odd = lax.rem(lax.axis_index("src"), 2)
-    half = shards // 2
-    return [2 * place + odd for place in range(half)] + [2 * place + 1 - odd for place in range(half)]
+    near = [0] + line_steps(shards)
+    me = lax.axis_index("src")
+    return [me ^ other for other in near + [step ^ 1 for step in near]]
 
 
 def read_all(hbm, held, sems):
@@ -100,24 +104,9 @@
         wide_ref[pair, 6 * depth : 8 * depth, :] = one
 
 
-def bundle_kernel(first_ref, second_ref, out_ref):
-    count = first_ref.shape[0]
-    out_ref[:count] = first_ref[...]
-    out_ref[count:] = second_ref[...]
-
-
-def order_kernel(line, *refs):
-    own_ref, up_refs, down_refs = refs[0], refs[1:line], refs[line : 2 * line - 1]
-    out_refs = refs[2 * line - 1 :]
-    here = lax.axis_index("src") // 2
-    for block in range(line):
-        value = own_ref[0]
-        for at in range(line):
-            if at < block:
-                value = jnp.where(here == at, down_refs[line - 2 - at][block - at - 1], value)
-            if at > block:
-                value = jnp.where(here == at, up_refs[at - 1][block], value)
-        out_refs[block // (line // 2)][block % (line // 2)] = value
+def join_kernel(*refs):
+    refs[-1][0] = refs[0][0]
+    refs[-1][1] = refs[1][0]
 
 
 def tile_kernel(parts, *refs):
@@ -158,7 +147,7 @@
                 total_ref[place, pl.ds(2 * pair + half, 1), :] = total[:, lanes]
         return carry
 
-    lax.fori_loop(0, pairs, body, 0, unroll=max(1, 2 * pairs // blocks))
+    lax.fori_loop(0, pairs, body, 0, unroll=min(pairs, 16 // blocks & -4 or 2))
 
 
 def row_kernel(groups, *refs):
@@ -313,26 +302,22 @@
             cost=cost_of(2 * blocks * cells * pairs * wide * 8 * depth),
         )(*packs, wide_feat)
 
-    line = shards // 2
-
-    def moved(array, start, end):
-        return lax.ppermute(array, "src", [(2 * start + odd, 2 * end + odd) for odd in range(2)])
-
-    def bundle(first, second):
-        shape = (first.shape[0] + second.shape[0],) + pack.shape[1:]
-        return call(bundle_kernel, [VM] * 2, in_vmem(shape, jnp.float32))(first, second)
-
-    up, down = [], []
-    for at in range(line - 1):
-        down.append(moved(bundle(pack, down[-1]) if at else pack, line - 1 - at, line - 2 - at))
-        up.append(moved(bundle(up[-1], pack) if at else pack, at, at + 1))
-    near = call(
-        functools.partial(order_kernel, line),
-        [VM] * (2 * line - 1),
-        [in_vmem((line // 2,) + pack.shape[1:], jnp.float32)] * 2,
-    )(pack, *up, *down)
-    far = [lax.ppermute(half, "src", [(i, i ^ 1) for i in range(shards)]) for half in near]
-    found = [tiles(*near)] + [tiles(half) for half in far]
+    def swapped(array, step):
+        return lax.ppermute(array, "src", [(i, i ^ step) for i in range(shards)])
+
+    there = {step: swapped(pack, step) for step in reversed(line_steps(shards))}
+    near = [pack] + [there[step] for step in line_steps(shards)]
+    found = [tiles(pack)]
+    halves = [
+        call(
+            join_kernel,
+            [VM] * 2 + [pl.BlockSpec(memory_space=pl.ANY)],
+            in_vmem((2,) + pack.shape[1:], jnp.float32),
+        )(near[at], near[at + 1], found[0][-1])
+        for at in range(0, len(near), 2)
+    ]
+    far = [swapped(half, 1) for half in halves]
+    found += [tiles(*near[1:])] + [tiles(half) for half in far]
     exps, tall, peaks, totals = zip(*found)
     groups = len(found)
     peaks, own = call(

time: 67.5 us -> 56.9 us (0.84)
  waiting for transfers between devices: 12.3 us -> 2.27 us
  starting transfers between devices: 11 us -> 8.86 us
  blocking collectives: 8.83 us -> 10.4 us
    ppermute x8 -> x5, waiting for transfers between devices: 11.1 us -> 1.11 us  [swapped(): return lax.ppermute(array, 'src', [(i, i ^ step) for i in range(shards)])]
    ppermute x8 -> x5, starting transfers between devices: 11 us -> 8.79 us  [swapped(): return lax.ppermute(array, 'src', [(i, i ^ step) for i in range(shards)])]
    all_to_all x1, blocking collectives: 8.83 us -> 10.4 us  [dense_device(): arrived = lax.all_to_all(columns, 'src', 0, 0)]
    pallas_call x3 -> x4, Pallas kernels: 3.62 us -> 3.83 us  [tiles(): call(functools.partial(tile_kernel, len(packs)), [VM] * (len(packs) + 1),...]
  transfers between devices with their start and end apart: 9 -> 6, of which waited for: 5 -> 3; matrix products, arithmetic and copies ran while one was open for 0% -> 0% of each run, Pallas kernels for 6% -> 8%
where the time goes in v7:
time: 56.9 us; the launch traced here: 56.6 us
  Pallas kernels  34.4 us (60%)
  blocking collectives  10.4 us (18%)
  starting transfers between devices  8.86 us (16%)
  waiting for transfers between devices  2.27 us (4%)
  between operations  0.7 us (1%)
    pallas_call x1, Pallas kernels, dense_device(): call(functools.partial(column_kernel, groups), [VM] * (2 * groups + 7), [...  27.7 us
    all_to_all x1, blocking collectives, dense_device(): arrived = lax.all_to_all(columns, 'src', 0, 0)  10.4 us
    ppermute x5, starting transfers between devices, swapped(): return lax.ppermute(array, 'src', [(i, i ^ step) for i in range(shards)])  8.79 us
    pallas_call x4, Pallas kernels, tiles(): call(functools.partial(tile_kernel, len(packs)), [VM] * (len(packs) + 1),...  3.83 us
    pallas_call x2, Pallas kernels, reading(): call(kernel, [pl.BlockSpec(memory_space=pltpu.HBM)] * len(args), out_shap...  2.17 us
    ppermute x1, waiting for transfers between devices, dense_device(): other = lax.ppermute(own, 'tgt', [(0, 1), (1, 0)])  1.16 us
  transfers between devices with their start and end apart: 6, of which 3 were waited for; matrix products, arithmetic and copies ran while one was open for 0% of the time, Pallas kernels for 8%

profile of v7, /device:TPU:0, one launch (start us, length us, event | category | flops | bytes accessed | tf_op | source)
XLA Modules:
  0.0 56.6 jit_solution(12388495849132311728)
XLA Ops:
  0.6 0.8 %shard_map.86 = (f32[1,72,128]{2,1,0:T(8,128)S(1)}, f32[1,128]{1,0:T(1,128)S(1)}) custom-call(f32[1,64,128]{2,1,0:T(8,128)} %refs_0_.2, f32[1,128]{1,0:T(1,128)} %refs_1_.1, f32[1,128]{1,0:T(1,128)} %refs_2_.1), custom_call_target="tpu_custom_call" | custom-call | tf_op jit(solution)/shard_map/pallas_call | solution.py:262
  1.4 4.1 %collective-permute-start = (f32[1,72,128]{2,1,0:T(8,128)S(1)}, f32[1,72,128]{2,1,0:T(8,128)S(1)}, u32[]{:S(2)}, u32[]{:S(2)}) collective-permute-start(f32[1,72,128]{2,1,0:T(8,128)S(1)} %get-tuple-element.30.refs_0_), channel_id=1, source_target_pairs={{0,8},{2,10},{4,12},{6,14},{8,0},{10,2},{12,4},{14,6},{1,9},{3,11}... | collective-permute-start | bytes 110600 | tf_op jit(solution)/shard_map/ppermute | solution.py:306
  5.5 1.3 %collective-permute-start.1 = (f32[1,72,128]{2,1,0:T(8,128)S(1)}, f32[1,72,128]{2,1,0:T(8,128)S(1)}, u32[]{:S(2)}, u32[]{:S(2)}) collective-permute-start(f32[1,72,128]{2,1,0:T(8,128)S(1)} %get-tuple-element.30.refs_0_), channel_id=1, source_target_pairs={{0,12},{2,14},{4,8},{6,10},{8,4},{10,6},{12,0},{14,2},{1,13},{3,15... | collective-permute-start | bytes 110600 | tf_op jit(solution)/shard_map/ppermute | solution.py:306
  6.9 0.2 collective-permute-start.2
  7.1 1.4 %shard_map.87 = (bf16[8,512,256]{2,1,0:T(8,128)(2,1)S(1)}, f32[16,128]{1,0:T(8,128)S(1)}, f32[8,16,128]{2,1,0:T(8,128)S(1)}, f32[16,128]{1,0:T(8,128)S(1)}) custom-call(f32[16,128]{1,0:T(8,128)} %refs_0_.3, s32[8,16]{1,0:T(8,128)} %bitcast.4, s32[1,16]{1,0:T(1,128)} %bitcast.5, f32[16,64,128]{2,1,0:T(8,128)} %refs_3_.1), custom_call_target="tpu_custom_call" | custom-call | flops 1000000000 | bytes 524288 | tf_op jit(solution)/shard_map/pallas_call | solution.py:262
  8.5 0.6 %shard_map.88 = (f32[8,128,256]{2,1,0:T(8,128)S(1)}, bf16[128,512]{1,0:T(8,128)(2,1)S(1)}, f32[1,16,128]{2,1,0:T(8,128)S(1)}, f32[1,16,128]{2,1,0:T(8,128)S(1)}) custom-call(f32[1,72,128]{2,1,0:T(8,128)S(1)} %get-tuple-element.30.refs_0_, bf16[8,512,256]{2,1,0:T(8,128)(2,1)S(1)} %get-tuple-element.31.refs_1_.refs_3_.refs_8_), custom_call_target="tpu_custom_call" | custom-call | flops 268435456 | bytes 524288 | tf_op jit(solution)/shard_map/pallas_call | solution.py:293
  9.1 0.0 collective-permute-done.refs_0_.refs_1_
  9.1 1.6 %collective-permute-start.3 = (f32[2,72,128]{2,1,0:T(8,128)S(1)}, f32[2,72,128]{2,1,0:T(8,128)S(1)}, u32[]{:S(2)}, u32[]{:S(2)}) collective-permute-start(f32[2,72,128]{2,1,0:T(8,128)S(1)} %shard_map.90), channel_id=1, source_target_pairs={{0,2},{2,0},{4,6},{6,4},{8,10},{10,8},{12,14},{14,12},{1,3},{3,1},... | collective-permute-start | bytes 221192 | tf_op jit(solution)/shard_map/ppermute | solution.py:306
  10.7 0.6 %collective-permute-done.1.refs_1_.refs_0_ = f32[1,72,128]{2,1,0:T(8,128)S(1)} collective-permute-done((f32[1,72,128]{2,1,0:T(8,128)S(1)}, f32[1,72,128]{2,1,0:T(8,128)S(1)}, u32[]{:S(2)}, u32[]{:S(2)}) %collective-permute-start.1) | collective-permute-done | bytes 36896 | tf_op jit(solution)/shard_map/ppermute | solution.py:306
  11.3 0.0 collective-permute-done.2.refs_2_.refs_1_
  11.3 1.6 %collective-permute-start.4 = (f32[2,72,128]{2,1,0:T(8,128)S(1)}, f32[2,72,128]{2,1,0:T(8,128)S(1)}, u32[]{:S(2)}, u32[]{:S(2)}) collective-permute-start(f32[2,72,128]{2,1,0:T(8,128)S(1)} %shard_map.92), channel_id=1, source_target_pairs={{0,2},{2,0},{4,6},{6,4},{8,10},{10,8},{12,14},{14,12},{1,3},{3,1},... | collective-permute-start | bytes 221192 | tf_op jit(solution)/shard_map/ppermute | solution.py:306
  12.9 1.5 %shard_map.89 = (f32[8,384,256]{2,1,0:T(8,128)S(1)}, bf16[384,512]{1,0:T(8,128)(2,1)S(1)}, f32[3,16,128]{2,1,0:T(8,128)S(1)}, f32[3,16,128]{2,1,0:T(8,128)S(1)}) custom-call(f32[1,72,128]{2,1,0:T(8,128)S(1)} %collective-permute-done.refs_0_.refs_1_, f32[1,72,128]{2,1,0:T(8,128)S(1)} %collective-permute-done.1.refs_1_.refs_0_, ...), custom_call_target="tpu_custom_call" | custom-call | flops 805306368 | bytes 524288 | tf_op jit(solution)/shard_map/pallas_call | solution.py:293
  14.4 0.0 collective-permute-done.3.refs_0_
  14.4 0.9 %shard_map.91 = (f32[8,256,256]{2,1,0:T(8,128)S(1)}, bf16[256,512]{1,0:T(8,128)(2,1)S(1)}, f32[2,16,128]{2,1,0:T(8,128)S(1)}, f32[2,16,128]{2,1,0:T(8,128)S(1)}) custom-call(f32[2,72,128]{2,1,0:T(8,128)S(1)} %collective-permute-done.3.refs_0_, bf16[8,512,256]{2,1,0:T(8,128)(2,1)S(1)} %get-tuple-element.31.refs_1_.refs_3_.refs_8_), custom_call_target="tpu_custom_call" | custom-call | flops 536870912 | bytes 524288 | tf_op jit(solution)/shard_map/pallas_call | solution.py:293
  15.3 0.5 collective-permute-done.4.refs_0_
  15.7 0.9 %shard_map.93 = (f32[8,256,256]{2,1,0:T(8,128)S(1)}, bf16[256,512]{1,0:T(8,128)(2,1)S(1)}, f32[2,16,128]{2,1,0:T(8,128)S(1)}, f32[2,16,128]{2,1,0:T(8,128)S(1)}) custom-call(f32[2,72,128]{2,1,0:T(8,128)S(1)} %collective-permute-done.4.refs_0_, bf16[8,512,256]{2,1,0:T(8,128)(2,1)S(1)} %get-tuple-element.31.refs_1_.refs_3_.refs_8_), custom_call_target="tpu_custom_call" | custom-call | flops 536870912 | bytes 524288 | tf_op jit(solution)/shard_map/pallas_call | solution.py:293
  16.6 0.1 collective-permute-start.5
  16.7 1.2 %collective-permute-done.5.refs_12_ = f32[16,128]{1,0:T(8,128)S(1)} collective-permute-done((f32[16,128]{1,0:T(8,128)S(1)}, f32[16,128]{1,0:T(8,128)S(1)}, u32[]{:S(2)}, u32[]{:S(2)}) %collective-permute-start.5) | collective-permute-done | bytes 8224 | tf_op jit(solution)/shard_map/ppermute | solution.py:328
  17.9 27.7 %shard_map.95 = (f32[16,128]{1,0:T(8,128)S(1)}, f32[8,1,128]{2,1,0:T(1,128)S(1)}) custom-call(f32[8,128,256]{2,1,0:T(8,128)S(1)} %get-tuple-element.32.refs_0_, f32[8,384,256]{2,1,0:T(8,128)S(1)} %get-tuple-element.33.refs_1_, f32[8,256,256]{2,1,0:T(8,128)S(1)} %get-tuple-element.35.refs_2_, f32[8,256,256]{2,1,0:T(8,128)S(1)} %get-tuple-element.36.refs_3_, ...), custom_call_target="tpu_custom_call" | custom-call | tf_op jit(solution)/shard_map/pallas_call | solution.py:329
  45.6 10.4 %all_to_all.5.values_ref = f32[8,1,128]{2,1,0:T(1,128)S(1)} all-to-all(f32[8,1,128]{2,1,0:T(1,128)S(1)} %get-tuple-element.53), channel_id=1, replica_groups=mesh['grp'=2,'src'=8,'tgt'=2] {'src'}, dimensions={0} | all-to-all | bytes 8192 | tf_op jit(solution)/shard_map/all_to_all | solution.py:338
  56.0 0.6 %shard_map.96 = (f32[1,128]{1,0:T(1,128)}, f32[16,128]{1,0:T(8,128)}) custom-call(f32[8,1,128]{2,1,0:T(1,128)S(1)} %all_to_all.5.values_ref, f32[1,128]{1,0:T(1,128)S(1)} %get-tuple-element.54.weight_ref, f32[16,128]{1,0:T(8,128)S(1)} %get-tuple-element.55.poten_ref), custom_call_target="tpu_custom_call" | custom-call | tf_op jit(solution)/shard_map/pallas_call | solution.py:340
  (3 shorter events, 0.1 us)
Async XLA Ops:
  1.4 7.6 %collective-permute-start = (f32[1,72,128]{2,1,0:T(8,128)S(1)}, f32[1,72,128]{2,1,0:T(8,128)S(1)}, u32[]{:S(2)}, u32[]{:S(2)}) collective-permute-start(f32[1,72,128]{2,1,0:T(8,128)S(1)} %get-tuple-element.30.refs_0_), channel_id=1, source_target_pairs={{0,8},{2,10},{4,12},{6,14},{8,0},{10,2},{12,4},{14,6},{1,9},{3,11}... | collective-permute-start | bytes 110600 | tf_op jit(solution)/shard_map/ppermute | solution.py:306
  5.5 5.8 %collective-permute-start.1 = (f32[1,72,128]{2,1,0:T(8,128)S(1)}, f32[1,72,128]{2,1,0:T(8,128)S(1)}, u32[]{:S(2)}, u32[]{:S(2)}) collective-permute-start(f32[1,72,128]{2,1,0:T(8,128)S(1)} %get-tuple-element.30.refs_0_), channel_id=1, source_target_pairs={{0,12},{2,14},{4,8},{6,10},{8,4},{10,6},{12,0},{14,2},{1,13},{3,15... | collective-permute-start | bytes 110600 | tf_op jit(solution)/shard_map/ppermute | solution.py:306
  6.9 4.4 %collective-permute-start.2 = (f32[1,72,128]{2,1,0:T(8,128)S(1)}, f32[1,72,128]{2,1,0:T(8,128)S(1)}, u32[]{:S(2)}, u32[]{:S(2)}) collective-permute-start(f32[1,72,128]{2,1,0:T(8,128)S(1)} %get-tuple-element.30.refs_0_), channel_id=1, source_target_pairs={{0,4},{2,6},{4,0},{6,2},{8,12},{10,14},{12,8},{14,10},{1,5},{3,7},... | collective-permute-start | bytes 110600 | tf_op jit(solution)/shard_map/ppermute | solution.py:306
  9.1 5.3 %collective-permute-start.3 = (f32[2,72,128]{2,1,0:T(8,128)S(1)}, f32[2,72,128]{2,1,0:T(8,128)S(1)}, u32[]{:S(2)}, u32[]{:S(2)}) collective-permute-start(f32[2,72,128]{2,1,0:T(8,128)S(1)} %shard_map.90), channel_id=1, source_target_pairs={{0,2},{2,0},{4,6},{6,4},{8,10},{10,8},{12,14},{14,12},{1,3},{3,1},... | collective-permute-start | bytes 221192 | tf_op jit(solution)/shard_map/ppermute | solution.py:306
  11.3 4.4 %collective-permute-start.4 = (f32[2,72,128]{2,1,0:T(8,128)S(1)}, f32[2,72,128]{2,1,0:T(8,128)S(1)}, u32[]{:S(2)}, u32[]{:S(2)}) collective-permute-start(f32[2,72,128]{2,1,0:T(8,128)S(1)} %shard_map.92), channel_id=1, source_target_pairs={{0,2},{2,0},{4,6},{6,4},{8,10},{10,8},{12,14},{14,12},{1,3},{3,1},... | collective-permute-start | bytes 221192 | tf_op jit(solution)/shard_map/ppermute | solution.py:306
  16.6 1.2 %collective-permute-start.5 = (f32[16,128]{1,0:T(8,128)S(1)}, f32[16,128]{1,0:T(8,128)S(1)}, u32[]{:S(2)}, u32[]{:S(2)}) collective-permute-start(f32[16,128]{1,0:T(8,128)S(1)} %get-tuple-element.50.refs_11_), channel_id=1, source_target_pairs={{0,1},{1,0},{2,3},{3,2},{4,5},{5,4},{6,7},{7,6},{8,9},{9,8},{10,11... | collective-permute-start | bytes 24584 | tf_op jit(solution)/shard_map/ppermute | solution.py:328

commit v8 on v7

--- a/solution.py
+++ b/solution.py
@@ -12,7 +12,8 @@
 very_low = -1e30
 log2e = 1.0 / math.log(2.0)
 ln2 = math.log(2.0)
-least_sum = 1e-28
+row_bounds = (2.0**-30, 2.0**100)
+column_bounds = (1e-19, 1e30)
 
 VM = pl.BlockSpec(memory_space=pltpu.VMEM)
 PARAMS = pltpu.CompilerParams(vmem_limit_bytes=40 * 2**20)
@@ -105,16 +106,13 @@
 
 
 def join_kernel(*refs):
-    refs[-1][0] = refs[0][0]
-    refs[-1][1] = refs[1][0]
-
-
-def tile_kernel(parts, *refs):
-    packs = [ref.at[index] for ref in refs[:parts] for index in range(ref.shape[0])]
-    wide_ref, exps_ref, tall_ref, peak_ref, total_ref = refs[parts:]
+    for place, ref in enumerate(refs[:-2]):
+        refs[-1][place] = ref[0]
+
+
+def fill_tall(packs, tall_ref):
     blocks = len(packs)
-    pairs, _, both = wide_ref.shape
-    cells = both // 2
+    cells = packs[0].shape[1]
     depth = cells // 2
     lane = lax.broadcasted_iota(jnp.int32, (cells, cells), 1)
     biases = jnp.concatenate([pack[depth : depth + 1, :] for pack in packs], axis=0)
@@ -132,36 +130,94 @@
         tall_ref[rows, 2 * cells : 3 * cells] = jnp.where(lane < depth, high, low).astype(jnp.bfloat16)
         tall_ref[rows, 3 * cells : 4 * cells] = own.astype(jnp.bfloat16)
 
+
+def put_rows(ref, pair, values):
+    cells = values.shape[1] // 2
+    ref[pl.ds(2 * pair, 1), :] = values[:, :cells]
+    ref[pl.ds(2 * pair + 1, 1), :] = values[:, cells:]
+
+
+def two_rows(ref, pair):
+    return jnp.concatenate([ref[pl.ds(2 * pair, 1), :], ref[pl.ds(2 * pair + 1, 1), :]], axis=1)
+
+
+def own_kernel(pack_ref, wide_ref, exps_ref, tall_ref, total_ref, shift_ref):
+    fill_tall([pack_ref.at[0]], tall_ref)
+    pairs = wide_ref.shape[0]
+
+    def body(pair, carry):
+        score = jnp.dot(tall_ref[...], wide_ref[pair], preferred_element_type=jnp.float32)
+        peak = jnp.max(score, axis=0, keepdims=True)
+        exps = jnp.exp2(score - peak)
+        exps_ref[pair] = exps
+        put_rows(shift_ref, pair, peak)
+        put_rows(total_ref.at[0], pair, jnp.sum(exps, axis=0, keepdims=True))
+        return carry
+
+    lax.fori_loop(0, pairs, body, 0, unroll=pairs)
+
+
+def tile_kernel(parts, *refs):
+    packs = [ref.at[index] for ref in refs[:parts] for index in range(ref.shape[0])]
+    wide_ref, shift_ref, _, exps_ref, tall_ref, total_ref = refs[parts:]
+    fill_tall(packs, tall_ref)
+    blocks = len(packs)
+    pairs, _, both = wide_ref.shape
+    cells = both // 2
+
     def body(pair, carry):
         scores = jnp.dot(tall_ref[...], wide_ref[pair], preferred_element_type=jnp.float32)
+        shift = two_rows(shift_ref, pair)
         for place in range(blocks):
             rows = slice(place * cells, (place + 1) * cells)
-            score = scores[rows]
-            peak = jnp.max(score, axis=0, keepdims=True)
-            exps = jnp.exp2(score - peak)
+            exps = jnp.exp2(scores[rows] - shift)
             exps_ref[pair, rows, :] = exps
-            total = jnp.sum(exps, axis=0, keepdims=True)
-            for half in range(2):
-                lanes = slice(half * cells, (half + 1) * cells)
-                peak_ref[place, pl.ds(2 * pair + half, 1), :] = peak[:, lanes]
-                total_ref[place, pl.ds(2 * pair + half, 1), :] = total[:, lanes]
+            put_rows(total_ref.at[place], pair, jnp.sum(exps, axis=0, keepdims=True))
         return carry
 
     lax.fori_loop(0, pairs, body, 0, unroll=min(pairs, 16 // blocks & -4 or 2))
 
 
+def inside(values, bounds):
+    return (values >= bounds[0]) & (values <= bounds[1])
+
+
+def spots_of(tall_refs, cells):
+    return [
+        (group, slice(index * cells, (index + 1) * cells))
+        for group, ref in enumerate(tall_refs)
+        for index in range(ref.shape[0] // cells)
+    ]
+
+
 def row_kernel(groups, *refs):
-    mask_ref, peak_refs, total_refs = refs[0], refs[1 : 1 + groups], refs[1 + groups : 1 + 2 * groups]
-    peaks_ref, rowsum_ref = refs[1 + 2 * groups :]
-    place = 0
-    for ref in peak_refs:
-        for index in range(ref.shape[0]):
-            peaks_ref[place] = ref[index] + mask_ref[place]
-            place += 1
+    mask_ref, shift_ref, wide_ref = refs[:3]
+    total_refs, tall_refs = refs[3 : 3 + groups], refs[3 + groups : 3 + 2 * groups]
+    rowsum_ref, exact_ref = refs[3 + 2 * groups :]
+    pairs, _, both = wide_ref.shape
+    cells = both // 2
     totals = [ref[index] for ref in total_refs for index in range(ref.shape[0])]
-    top = functools.reduce(jnp.maximum, [peaks_ref[index] for index in range(place)])
-    summed = sum(total * jnp.exp2(peaks_ref[index] - top) for index, total in enumerate(totals))
-    rowsum_ref[...] = top + jnp.log2(summed)
+    summed = sum(jnp.where(mask_ref[place] > 0.5 * very_low, total, 0.0) for place, total in enumerate(totals))
+    rowsum_ref[...] = shift_ref[...] + jnp.log2(summed)
+    served = jnp.min(jnp.where(inside(summed, row_bounds), 1.0, 0.0))
+    exact_ref[...] = jnp.zeros(exact_ref.shape, jnp.float32) + (1.0 - served)
+
+    @pl.when(served < 0.5)
+    def _():
+        spots = spots_of(tall_refs, cells)
+
+        def body(pair, carry):
+            def scores():
+                for place, (group, rows) in enumerate(spots):
+                    score = jnp.dot(tall_refs[group][rows, :], wide_ref[pair], preferred_element_type=jnp.float32)
+                    yield score + two_rows(mask_ref.at[place], pair)
+
+            peak = functools.reduce(jnp.maximum, [jnp.max(score, axis=0, keepdims=True) for score in scores()])
+            sums = [jnp.sum(jnp.exp2(score - peak), axis=0, keepdims=True) for score in scores()]
+            put_rows(rowsum_ref, pair, peak + jnp.log2(sum(sums)))
+            return carry
+
+        lax.fori_loop(0, pairs, body, 0)
 
 
 def across(column):
@@ -172,8 +228,8 @@
 
 def column_kernel(groups, *refs):
     exps_refs, tall_refs, rest = refs[:groups], refs[groups : 2 * groups], refs[2 * groups :]
-    wide_ref, peak_ref, mask_ref, own_ref, other_ref, mass_ref, norm_ref = rest[:7]
-    poten_ref, sums_ref, weight_ref, shift_ref = rest[7:]
+    wide_ref, peak_ref, exact_ref, mask_ref, own_ref, other_ref, mass_ref, norm_ref = rest[:8]
+    poten_ref, sums_ref, weight_ref, shift_ref = rest[8:]
     pairs, _, both = wide_ref.shape
     cells = both // 2
     shards = mask_ref.shape[0]
@@ -183,15 +239,12 @@
     poten_ref[...] = norm_ref[...] - (entropic * ln2) * whole
     shift = mass_ref[...] * log2e - whole
     shift_ref[...] = shift
+    weight = jnp.exp2(peak_ref[...] + shift)
     for place in range(shards):
-        weight_ref[place] = jnp.exp2(peak_ref[place] + shift)
-    spots = [
-        (group, slice(index * cells, (index + 1) * cells))
-        for group, ref in enumerate(tall_refs)
-        for index in range(ref.shape[0] // cells)
-    ]
+        weight_ref[place] = jnp.where(mask_ref[place] > 0.5 * very_low, weight, 0.0)
+    spots = spots_of(tall_refs, cells)
     used = [jnp.max(mask_ref[place], axis=0, keepdims=True) > 0.5 * very_low for place in range(shards)]
-    worst = jnp.full((1, cells), 1.0, jnp.float32)
+    served = 1.0 - exact_ref[0:1, :]
     owners = blocks_at(shards)
     for place, (group, rows) in enumerate(spots):
         acc = jnp.zeros((cells, cells), jnp.float32)
@@ -200,9 +253,9 @@
             acc = acc + exps_refs[group][pair, rows, cells:] * weight_ref[place, 2 * pair + 1 : 2 * pair + 2, :]
         here = across(jnp.sum(acc, axis=1, keepdims=True))
         sums_ref[owners[place]] = jnp.where(used[place], jnp.log2(here), very_low)
-        worst = jnp.minimum(worst, jnp.where(used[place], here, 1.0))
-
-    @pl.when(jnp.min(worst) < least_sum)
+        served = jnp.where(inside(here, column_bounds) | ~used[place], served, 0.0)
+
+    @pl.when(jnp.min(served) < 0.5)
     def _():
         for place, (group, rows) in enumerate(spots):
 
@@ -288,53 +341,56 @@
         cost_of(10**9),
     )
 
-    def tiles(*packs):
+    def tiles(*packs, after=None):
         blocks = sum(pack.shape[0] for pack in packs)
+        own = after is None
         return call(
-            functools.partial(tile_kernel, len(packs)),
-            [VM] * (len(packs) + 1),
+            own_kernel if own else functools.partial(tile_kernel, len(packs)),
+            [VM] * (len(packs) + 1) + [VM, pl.BlockSpec(memory_space=pl.ANY)] * (not own),
             [
                 in_vmem((pairs, blocks * cells, wide), jnp.float32),
                 in_vmem((blocks * cells, 8 * depth), jnp.bfloat16),
                 in_vmem((blocks, rows, cells), jnp.float32),
-                in_vmem((blocks, rows, cells), jnp.float32),
-            ],
+            ]
+            + [in_vmem((rows, cells), jnp.float32)] * own,
             cost=cost_of(2 * blocks * cells * pairs * wide * 8 * depth),
-        )(*packs, wide_feat)
+        )(*packs, wide_feat, *([] if own else [shift, after]))
 
     def swapped(array, step):
         return lax.ppermute(array, "src", [(i, i ^ step) for i in range(shards)])
 
     there = {step: swapped(pack, step) for step in reversed(line_steps(shards))}
     near = [pack] + [there[step] for step in line_steps(shards)]
-    found = [tiles(pack)]
-    halves = [
-        call(
+    *first, shift = tiles(pack)
+
+    def joined(parts):
+        return call(
             join_kernel,
-            [VM] * 2 + [pl.BlockSpec(memory_space=pl.ANY)],
-            in_vmem((2,) + pack.shape[1:], jnp.float32),
-        )(near[at], near[at + 1], found[0][-1])
-        for at in range(0, len(near), 2)
-    ]
-    far = [swapped(half, 1) for half in halves]
-    found += [tiles(*near[1:])] + [tiles(half) for half in far]
-    exps, tall, peaks, totals = zip(*found)
+            [VM] * len(parts) + [pl.BlockSpec(memory_space=pl.ANY)],
+            in_vmem((len(parts),) + pack.shape[1:], jnp.float32),
+        )(*parts, shift)
+
+    far = [swapped(joined(parts), 1) for parts in (near[:-1], near[-1:])]
+    found = [first]
+    for packs in [near[1:]] + [[some] for some in far]:
+        found.append(tiles(*packs, after=found[-1][-1]))
+    exps, tall, totals = zip(*found)
     groups = len(found)
-    peaks, own = call(
+    own, exact = call(
         functools.partial(row_kernel, groups),
-        [VM] * (1 + 2 * groups),
-        [in_vmem((shards, rows, cells), jnp.float32), in_vmem((rows, cells), jnp.float32)],
-    )(mask, *peaks, *totals)
+        [VM] * (3 + 2 * groups),
+        [in_vmem((rows, cells), jnp.float32), in_vmem((8, cells), jnp.float32)],
+    )(mask, shift, wide_feat, *totals, *tall)
     other = lax.ppermute(own, "tgt", [(0, 1), (1, 0)])
     potential_src, columns = call(
         functools.partial(column_kernel, groups),
-        [VM] * (2 * groups + 7),
+        [VM] * (2 * groups + 8),
         [in_vmem((rows, cells), jnp.float32), in_vmem((shards, 1, cells), jnp.float32)],
         [
             pltpu.VMEM((shards, rows, cells), jnp.float32),
             pltpu.VMEM((rows, cells), jnp.float32),
         ],
-    )(*exps, *tall, wide_feat, peaks, mask, own, other, mass, norm)
+    )(*exps, *tall, wide_feat, shift, exact, mask, own, other, mass, norm)
     arrived = lax.all_to_all(columns, "src", 0, 0)
     outs = [f32(1, cells), f32(rows, cells)]
     potential_new, potential_src = call(merge_kernel, [VM] * 3, outs)(arrived, weight, potential_src)

time: 56.9 us -> 63.9 us (1.12)
  Pallas kernels: 34.4 us -> 39.5 us
  waiting for transfers between devices: 2.27 us -> 5.71 us
  starting transfers between devices: 8.86 us -> 7.84 us
    pallas_call x8, Pallas kernels: 31.6 us -> 36.7 us  [the longest x1 27.8 us: dense_device(): call(functools.partial(column_kernel, groups), [VM] * (2 * groups + 8), [...]
    ppermute x5, waiting for transfers between devices: 1.11 us -> 4.55 us  [swapped(): return lax.ppermute(array, 'src', [(i, i ^ step) for i in range(shards)])]
    ppermute x5, starting transfers between devices: 8.79 us -> 7.77 us  [swapped(): return lax.ppermute(array, 'src', [(i, i ^ step) for i in range(shards)])]
  transfers between devices with their start and end apart: 6 -> 6, of which waited for: 3 -> 4; matrix products, arithmetic and copies ran while one was open for 0% -> 0% of each run, Pallas kernels for 8% -> 7%
where the time goes in v8:
time: 63.9 us; the launch traced here: 63.7 us
  Pallas kernels  39.5 us (62%)
  blocking collectives  9.9 us (15%)
  starting transfers between devices  7.84 us (12%)
  waiting for transfers between devices  5.71 us (9%)
  between operations  0.71 us (1%)
    pallas_call x1, Pallas kernels, dense_device(): call(functools.partial(column_kernel, groups), [VM] * (2 * groups + 8), [...  27.8 us
    all_to_all x1, blocking collectives, dense_device(): arrived = lax.all_to_all(columns, 'src', 0, 0)  9.9 us
    ppermute x5, starting transfers between devices, swapped(): return lax.ppermute(array, 'src', [(i, i ^ step) for i in range(shards)])  7.77 us
    pallas_call x1, Pallas kernels, dense_device(): call(functools.partial(row_kernel, groups), [VM] * (3 + 2 * groups), [in_...  5.11 us
    ppermute x5, waiting for transfers between devices, swapped(): return lax.ppermute(array, 'src', [(i, i ^ step) for i in range(shards)])  4.55 us
    pallas_call x4, Pallas kernels, tiles(): call(own_kernel if own else functools.partial(tile_kernel, len(packs)), [...  3.79 us
    pallas_call x2, Pallas kernels, reading(): call(kernel, [pl.BlockSpec(memory_space=pltpu.HBM)] * len(args), out_shap...  2.17 us
  transfers between devices with their start and end apart: 6, of which 4 were waited for; matrix products, arithmetic and copies ran while one was open for 0% of the time, Pallas kernels for 7%

profile of v8, /device:TPU:0, one launch (start us, length us, event | category | flops | bytes accessed | tf_op | source)
XLA Modules:
  0.0 63.7 jit_solution(17229361594219665187)
XLA Ops:
  0.6 0.8 %shard_map.86 = (f32[1,72,128]{2,1,0:T(8,128)S(1)}, f32[1,128]{1,0:T(1,128)S(1)}) custom-call(f32[1,64,128]{2,1,0:T(8,128)} %refs_0_.2, f32[1,128]{1,0:T(1,128)} %refs_1_.1, f32[1,128]{1,0:T(1,128)} %refs_2_.1), custom_call_target="tpu_custom_call" | custom-call | tf_op jit(solution)/shard_map/pallas_call | solution.py:315
  1.4 3.1 %collective-permute-start.2 = (f32[1,72,128]{2,1,0:T(8,128)S(1)}, f32[1,72,128]{2,1,0:T(8,128)S(1)}, u32[]{:S(2)}, u32[]{:S(2)}) collective-permute-start(f32[1,72,128]{2,1,0:T(8,128)S(1)} %get-tuple-element.27.pack_ref.refs_0_), channel_id=1, source_target_pairs={{0,4},{2,6},{4,0},{6,2},{8,12},{10,14},{12,8},{14,10},{1,5},{3,7},... | collective-permute-start | bytes 110600 | tf_op jit(solution)/shard_map/ppermute | solution.py:360
  4.5 2.5 %collective-permute-start.1 = (f32[1,72,128]{2,1,0:T(8,128)S(1)}, f32[1,72,128]{2,1,0:T(8,128)S(1)}, u32[]{:S(2)}, u32[]{:S(2)}) collective-permute-start(f32[1,72,128]{2,1,0:T(8,128)S(1)} %get-tuple-element.27.pack_ref.refs_0_), channel_id=1, source_target_pairs={{0,12},{2,14},{4,8},{6,10},{8,4},{10,6},{12,0},{14,2},{1,13},{3,15... | collective-permute-start | bytes 110600 | tf_op jit(solution)/shard_map/ppermute | solution.py:360
  7.0 0.1 collective-permute-start
  7.1 1.4 %shard_map.87 = (bf16[8,512,256]{2,1,0:T(8,128)(2,1)S(1)}, f32[16,128]{1,0:T(8,128)S(1)}, f32[8,16,128]{2,1,0:T(8,128)S(1)}, f32[16,128]{1,0:T(8,128)S(1)}) custom-call(f32[16,128]{1,0:T(8,128)} %refs_0_.3, s32[8,16]{1,0:T(8,128)} %bitcast.4, s32[1,16]{1,0:T(1,128)} %bitcast.5, f32[16,64,128]{2,1,0:T(8,128)} %refs_3_.1), custom_call_target="tpu_custom_call" | custom-call | flops 1000000000 | bytes 524288 | tf_op jit(solution)/shard_map/pallas_call | solution.py:315
  8.5 0.6 shard_map.88
  9.1 1.7 %collective-permute-done.1.refs_1_.refs_2_ = f32[1,72,128]{2,1,0:T(8,128)S(1)} collective-permute-done((f32[1,72,128]{2,1,0:T(8,128)S(1)}, f32[1,72,128]{2,1,0:T(8,128)S(1)}, u32[]{:S(2)}, u32[]{:S(2)}) %collective-permute-start.1) | collective-permute-done | bytes 36896 | tf_op jit(solution)/shard_map/ppermute | solution.py:360
  10.8 1.5 %collective-permute-done.refs_0_.refs_1_ = f32[1,72,128]{2,1,0:T(8,128)S(1)} collective-permute-done((f32[1,72,128]{2,1,0:T(8,128)S(1)}, f32[1,72,128]{2,1,0:T(8,128)S(1)}, u32[]{:S(2)}, u32[]{:S(2)}) %collective-permute-start) | collective-permute-done | bytes 36896 | tf_op jit(solution)/shard_map/ppermute | solution.py:360
  12.3 1.6 %collective-permute-start.3 = (f32[3,72,128]{2,1,0:T(8,128)S(1)}, f32[3,72,128]{2,1,0:T(8,128)S(1)}, u32[]{:S(2)}, u32[]{:S(2)}) collective-permute-start(f32[3,72,128]{2,1,0:T(8,128)S(1)} %shard_map.90), channel_id=1, source_target_pairs={{0,2},{2,0},{4,6},{6,4},{8,10},{10,8},{12,14},{14,12},{1,3},{3,1},... | collective-permute-start | bytes 331784 | tf_op jit(solution)/shard_map/ppermute | solution.py:360
  13.8 0.0 collective-permute-done.2.refs_2_.refs_0_
  13.8 0.5 collective-permute-start.4
  14.4 1.3 %shard_map.89 = (f32[8,384,256]{2,1,0:T(8,128)S(1)}, bf16[384,512]{1,0:T(8,128)(2,1)S(1)}, f32[3,16,128]{2,1,0:T(8,128)S(1)}) custom-call(f32[1,72,128]{2,1,0:T(8,128)S(1)} %collective-permute-done.refs_0_.refs_1_, f32[1,72,128]{2,1,0:T(8,128)S(1)} %collective-permute-done.1.refs_1_.refs_2_, f32[1,72,128]{2,1,0:T(8,128)S(1)} %collective-permute-done.2.refs_2_.refs_0_, ...), custom_call_target="tpu_custom_call" | custom-call | flops 805306368 | bytes 524288 | tf_op jit(solution)/shard_map/pallas_call | solution.py:347
  15.7 1.4 %collective-permute-done.3.refs_0_ = f32[3,72,128]{2,1,0:T(8,128)S(1)} collective-permute-done((f32[3,72,128]{2,1,0:T(8,128)S(1)}, f32[3,72,128]{2,1,0:T(8,128)S(1)}, u32[]{:S(2)}, u32[]{:S(2)}) %collective-permute-start.3) | collective-permute-done | bytes 110624 | tf_op jit(solution)/shard_map/ppermute | solution.py:360
  17.1 1.3 %shard_map.91 = (f32[8,384,256]{2,1,0:T(8,128)S(1)}, bf16[384,512]{1,0:T(8,128)(2,1)S(1)}, f32[3,16,128]{2,1,0:T(8,128)S(1)}) custom-call(f32[3,72,128]{2,1,0:T(8,128)S(1)} %collective-permute-done.3.refs_0_, bf16[8,512,256]{2,1,0:T(8,128)(2,1)S(1)} %get-tuple-element.28.wide_ref.refs_3_.refs_1_.refs_2_.refs_8_, ...), custom_call_target="tpu_custom_call" | custom-call | flops 805306368 | bytes 524288 | tf_op jit(solution)/shard_map/pallas_call | solution.py:347
  18.4 0.0 collective-permute-done.4.refs_0_
  18.5 0.5 shard_map.93
  19.0 5.1 %shard_map.94 = (f32[16,128]{1,0:T(8,128)S(1)}, f32[8,128]{1,0:T(8,128)S(1)}) custom-call(f32[8,16,128]{2,1,0:T(8,128)S(1)} %get-tuple-element.41.refs_0_.refs_11_, f32[16,128]{1,0:T(8,128)S(1)} %get-tuple-element.30.refs_4_.refs_3_.refs_2_.refs_1_.refs_9_, bf16[8,512,256]{2,1,0:T(8,128)(2,1)S(1)} %get-tuple-element.28.wide_ref.refs_3_.refs_1_.refs_2_.refs_8_, ...), custom_call_target="tpu_custom_call" | custom-call | tf_op jit(solution)/shard_map/pallas_call | solution.py:379
  24.1 0.1 collective-permute-start.5
  24.2 1.2 %collective-permute-done.5.refs_13_ = f32[16,128]{1,0:T(8,128)S(1)} collective-permute-done((f32[16,128]{1,0:T(8,128)S(1)}, f32[16,128]{1,0:T(8,128)S(1)}, u32[]{:S(2)}, u32[]{:S(2)}) %collective-permute-start.5) | collective-permute-done | bytes 8224 | tf_op jit(solution)/shard_map/ppermute | solution.py:384
  25.3 27.8 %shard_map.95 = (f32[16,128]{1,0:T(8,128)S(1)}, f32[8,1,128]{2,1,0:T(1,128)S(1)}) custom-call(f32[8,128,256]{2,1,0:T(8,128)S(1)} %get-tuple-element.29.refs_0_, f32[8,384,256]{2,1,0:T(8,128)S(1)} %get-tuple-element.32.refs_1_, f32[8,384,256]{2,1,0:T(8,128)S(1)} %get-tuple-element.34.refs_2_, f32[8,128,256]{2,1,0:T(8,128)S(1)} %get-tuple-element.36.refs_3_, ...), custom_call_target="tpu_custom_call" | custom-call | tf_op jit(solution)/shard_map/pallas_call | solution.py:385
  53.2 9.9 %all_to_all.5.values_ref = f32[8,1,128]{2,1,0:T(1,128)S(1)} all-to-all(f32[8,1,128]{2,1,0:T(1,128)S(1)} %get-tuple-element.47), channel_id=1, replica_groups=mesh['grp'=2,'src'=8,'tgt'=2] {'src'}, dimensions={0} | all-to-all | bytes 8192 | tf_op jit(solution)/shard_map/all_to_all | solution.py:394
  63.1 0.6 shard_map.96
  (2 shorter events, 0.0 us)
Async XLA Ops:
  1.4 12.4 %collective-permute-start.2 = (f32[1,72,128]{2,1,0:T(8,128)S(1)}, f32[1,72,128]{2,1,0:T(8,128)S(1)}, u32[]{:S(2)}, u32[]{:S(2)}) collective-permute-start(f32[1,72,128]{2,1,0:T(8,128)S(1)} %get-tuple-element.27.pack_ref.refs_0_), channel_id=1, source_target_pairs={{0,4},{2,6},{4,0},{6,2},{8,12},{10,14},{12,8},{14,10},{1,5},{3,7},... | collective-permute-start | bytes 110600 | tf_op jit(solution)/shard_map/ppermute | solution.py:360
  4.5 6.2 %collective-permute-start.1 = (f32[1,72,128]{2,1,0:T(8,128)S(1)}, f32[1,72,128]{2,1,0:T(8,128)S(1)}, u32[]{:S(2)}, u32[]{:S(2)}) collective-permute-start(f32[1,72,128]{2,1,0:T(8,128)S(1)} %get-tuple-element.27.pack_ref.refs_0_), channel_id=1, source_target_pairs={{0,12},{2,14},{4,8},{6,10},{8,4},{10,6},{12,0},{14,2},{1,13},{3,15... | collective-permute-start | bytes 110600 | tf_op jit(solution)/shard_map/ppermute | solution.py:360
  7.0 5.3 %collective-permute-start = (f32[1,72,128]{2,1,0:T(8,128)S(1)}, f32[1,72,128]{2,1,0:T(8,128)S(1)}, u32[]{:S(2)}, u32[]{:S(2)}) collective-permute-start(f32[1,72,128]{2,1,0:T(8,128)S(1)} %get-tuple-element.27.pack_ref.refs_0_), channel_id=1, source_target_pairs={{0,8},{2,10},{4,12},{6,14},{8,0},{10,2},{12,4},{14,6},{1,9},{3,11}... | collective-permute-start | bytes 110600 | tf_op jit(solution)/shard_map/ppermute | solution.py:360
  12.3 4.8 %collective-permute-start.3 = (f32[3,72,128]{2,1,0:T(8,128)S(1)}, f32[3,72,128]{2,1,0:T(8,128)S(1)}, u32[]{:S(2)}, u32[]{:S(2)}) collective-permute-start(f32[3,72,128]{2,1,0:T(8,128)S(1)} %shard_map.90), channel_id=1, source_target_pairs={{0,2},{2,0},{4,6},{6,4},{8,10},{10,8},{12,14},{14,12},{1,3},{3,1},... | collective-permute-start | bytes 331784 | tf_op jit(solution)/shard_map/ppermute | solution.py:360
  13.8 4.6 %collective-permute-start.4 = (f32[1,72,128]{2,1,0:T(8,128)S(1)}, f32[1,72,128]{2,1,0:T(8,128)S(1)}, u32[]{:S(2)}, u32[]{:S(2)}) collective-permute-start(f32[1,72,128]{2,1,0:T(8,128)S(1)} %shard_map.92), channel_id=1, source_target_pairs={{0,2},{2,0},{4,6},{6,4},{8,10},{10,8},{12,14},{14,12},{1,3},{3,1},... | collective-permute-start | bytes 110600 | tf_op jit(solution)/shard_map/ppermute | solution.py:360
  24.1 1.2 %collective-permute-start.5 = (f32[16,128]{1,0:T(8,128)S(1)}, f32[16,128]{1,0:T(8,128)S(1)}, u32[]{:S(2)}, u32[]{:S(2)}) collective-permute-start(f32[16,128]{1,0:T(8,128)S(1)} %get-tuple-element.44.refs_12_), channel_id=1, source_target_pairs={{0,1},{1,0},{2,3},{3,2},{4,5},{5,4},{6,7},{7,6},{8,9},{9,8},{10,11... | collective-permute-start | bytes 24584 | tf_op jit(solution)/shard_map/ppermute | solution.py:384

commit v9 on v7

--- a/solution.py
+++ b/solution.py
@@ -109,7 +109,27 @@
     refs[-1][1] = refs[1][0]
 
 
-def tile_kernel(parts, *refs):
+def on_core(core, work, idle):
+    if core is None:
+        work()
+    else:
+        here = lax.axis_index("tgt") == core
+        pl.when(here)(work)
+        pl.when(jnp.logical_not(here))(idle)
+
+
+def tile_kernel(parts, core, *refs):
+    peak_ref, total_ref = refs[-2:]
+
+    def idle():
+        peak_ref[...] = jnp.zeros(peak_ref.shape, jnp.float32)
+        total_ref[...] = jnp.zeros(total_ref.shape, jnp.float32)
+
+    ins = refs[: parts + 1] + refs[-4:]
+    on_core(core, functools.partial(make_tiles, parts, *ins), idle)
+
+
+def make_tiles(parts, *refs):
     packs = [ref.at[index] for ref in refs[:parts] for index in range(ref.shape[0])]
     wide_ref, exps_ref, tall_ref, peak_ref, total_ref = refs[parts:]
     blocks = len(packs)
@@ -170,7 +190,17 @@
     return jnp.sum(jnp.where(same, jnp.broadcast_to(column, shape), 0.0), axis=0, keepdims=True)
 
 
-def column_kernel(groups, *refs):
+def column_kernel(groups, core, *refs):
+    ins, outs, scratch = refs[: 2 * groups + 7], refs[-4:-2], refs[-2:]
+
+    def idle():
+        for given, out in zip(refs[2 * groups + 7 : -4], outs):
+            out[...] = given[...]
+
+    on_core(core, functools.partial(sum_columns, groups, *ins, *outs, *scratch), idle)
+
+
+def sum_columns(groups, *refs):
     exps_refs, tall_refs, rest = refs[:groups], refs[groups : 2 * groups], refs[2 * groups :]
     wide_ref, peak_ref, mask_ref, own_ref, other_ref, mass_ref, norm_ref = rest[:7]
     poten_ref, sums_ref, weight_ref, shift_ref = rest[7:]
@@ -288,11 +318,12 @@
         cost_of(10**9),
     )
 
-    def tiles(*packs):
+    def tiles(*packs, core=None, after=None):
         blocks = sum(pack.shape[0] for pack in packs)
+        more = [] if after is None else [after]
         return call(
-            functools.partial(tile_kernel, len(packs)),
-            [VM] * (len(packs) + 1),
+            functools.partial(tile_kernel, len(packs), core),
+            [VM] * (len(packs) + 1) + [pl.BlockSpec(memory_space=pl.ANY)] * len(more),
             [
                 in_vmem((pairs, blocks * cells, wide), jnp.float32),
                 in_vmem((blocks * cells, 8 * depth), jnp.bfloat16),
@@ -300,7 +331,7 @@
                 in_vmem((blocks, rows, cells), jnp.float32),
             ],
             cost=cost_of(2 * blocks * cells * pairs * wide * 8 * depth),
-        )(*packs, wide_feat)
+        )(*packs, wide_feat, *more)
 
     def swapped(array, step):
         return lax.ppermute(array, "src", [(i, i ^ step) for i in range(shards)])
@@ -317,24 +348,36 @@
         for at in range(0, len(near), 2)
     ]
     far = [swapped(half, 1) for half in halves]
-    found += [tiles(*near[1:])] + [tiles(half) for half in far]
-    exps, tall, peaks, totals = zip(*found)
-    groups = len(found)
-    peaks, own = call(
-        functools.partial(row_kernel, groups),
-        [VM] * (1 + 2 * groups),
-        [in_vmem((shards, rows, cells), jnp.float32), in_vmem((rows, cells), jnp.float32)],
-    )(mask, *peaks, *totals)
-    other = lax.ppermute(own, "tgt", [(0, 1), (1, 0)])
-    potential_src, columns = call(
-        functools.partial(column_kernel, groups),
-        [VM] * (2 * groups + 7),
-        [in_vmem((rows, cells), jnp.float32), in_vmem((shards, 1, cells), jnp.float32)],
-        [
-            pltpu.VMEM((shards, rows, cells), jnp.float32),
-            pltpu.VMEM((rows, cells), jnp.float32),
-        ],
-    )(*exps, *tall, wide_feat, peaks, mask, own, other, mass, norm)
+    found += [tiles(*near[1:]), tiles(far[0])]
+    groups = len(found) + 1
+
+    def log_sums(last):
+        _, _, peaks, totals = zip(*found, last)
+        return call(
+            functools.partial(row_kernel, groups),
+            [VM] * (1 + 2 * groups),
+            [in_vmem((shards, rows, cells), jnp.float32), in_vmem((rows, cells), jnp.float32)],
+        )(mask, *peaks, *totals)
+
+    def columns_of(core, last, peaks, own, other, given):
+        exps, tall, _, _ = zip(*found, last)
+        return call(
+            functools.partial(column_kernel, groups, core),
+            [VM] * (2 * groups + 7 + len(given)),
+            [in_vmem((rows, cells), jnp.float32), in_vmem((shards, 1, cells), jnp.float32)],
+            [pltpu.VMEM((shards, rows, cells), jnp.float32), pltpu.VMEM((rows, cells), jnp.float32)],
+            cost_of(10**9),
+        )(*exps, *tall, wide_feat, peaks, mask, own, other, mass, norm, *given)
+
+    between = [(0, 1), (1, 0)]
+    last_one = tiles(far[1], core=1)
+    peaks_one, own_one = log_sums(last_one)
+    other_zero = lax.ppermute(own_one, "tgt", between)
+    last_zero = tiles(far[1], core=0, after=own_one)
+    peaks_zero, own_zero = log_sums(last_zero)
+    other_one = lax.ppermute(own_zero, "tgt", between)
+    given = columns_of(0, last_zero, peaks_zero, own_zero, other_zero, [])
+    potential_src, columns = columns_of(1, last_one, peaks_one, own_one, other_one, given)
     arrived = lax.all_to_all(columns, "src", 0, 0)
     outs = [f32(1, cells), f32(rows, cells)]
     potential_new, potential_src = call(merge_kernel, [VM] * 3, outs)(arrived, weight, potential_src)

time: 56.9 us -> 56.1 us (0.986)
  waiting for transfers between devices: 2.27 us -> 1.24 us
    ppermute x1 -> x2, waiting for transfers between devices: 1.16 us -> 0.14 us  [the longest x1 0.14 us: dense_device(): other_zero = lax.ppermute(own_one, 'tgt', between)]
    pallas_call x6 -> x9, Pallas kernels: 31.6 us -> 31.8 us  [the longest x2 27.8 us: columns_of(): call(functools.partial(column_kernel, groups, core), [VM] * (2 * groups +...]
  transfers between devices with their start and end apart: 6 -> 7, of which waited for: 3 -> 3; matrix products, arithmetic and copies ran while one was open for 0% -> 0% of each run, Pallas kernels for 8% -> 59%
where the time goes in v9:
time: 56.1 us; the launch traced here: 55.9 us
  Pallas kernels  34.6 us (62%)
  blocking collectives  10.4 us (19%)
  starting transfers between devices  8.93 us (16%)
  waiting for transfers between devices  1.24 us (2%)
  between operations  0.74 us (1%)
    pallas_call x2, Pallas kernels, columns_of(): call(functools.partial(column_kernel, groups, core), [VM] * (2 * groups +...  27.8 us
    all_to_all x1, blocking collectives, dense_device(): arrived = lax.all_to_all(columns, 'src', 0, 0)  10.4 us
    ppermute x5, starting transfers between devices, swapped(): return lax.ppermute(array, 'src', [(i, i ^ step) for i in range(shards)])  8.78 us
    pallas_call x5, Pallas kernels, tiles(): call(functools.partial(tile_kernel, len(packs), core), [VM] * (len(packs)...  3.88 us
    pallas_call x2, Pallas kernels, reading(): call(kernel, [pl.BlockSpec(memory_space=pltpu.HBM)] * len(args), out_shap...  2.17 us
  transfers between devices with their start and end apart: 7, of which 3 were waited for; matrix products, arithmetic and copies ran while one was open for 0% of the time, Pallas kernels for 59%

profile of v9, /device:TPU:0, one launch (start us, length us, event | category | flops | bytes accessed | tf_op | source)
XLA Modules:
  0.0 55.9 jit_solution(7826940900506633963)
XLA Ops:
  0.6 0.8 %shard_map.86 = (f32[1,72,128]{2,1,0:T(8,128)S(1)}, f32[1,128]{1,0:T(1,128)S(1)}) custom-call(f32[1,64,128]{2,1,0:T(8,128)} %refs_0_.2, f32[1,128]{1,0:T(1,128)} %refs_1_.1, f32[1,128]{1,0:T(1,128)} %refs_2_.1), custom_call_target="tpu_custom_call" | custom-call | tf_op jit(solution)/shard_map/pallas_call | solution.py:292
  1.4 4.1 %collective-permute-start = (f32[1,72,128]{2,1,0:T(8,128)S(1)}, f32[1,72,128]{2,1,0:T(8,128)S(1)}, u32[]{:S(2)}, u32[]{:S(2)}) collective-permute-start(f32[1,72,128]{2,1,0:T(8,128)S(1)} %get-tuple-element.38.refs_0_), channel_id=1, source_target_pairs={{0,8},{2,10},{4,12},{6,14},{8,0},{10,2},{12,4},{14,6},{1,9},{3,11}... | collective-permute-start | bytes 110600 | tf_op jit(solution)/shard_map/ppermute | solution.py:337
  5.5 1.3 %collective-permute-start.1 = (f32[1,72,128]{2,1,0:T(8,128)S(1)}, f32[1,72,128]{2,1,0:T(8,128)S(1)}, u32[]{:S(2)}, u32[]{:S(2)}) collective-permute-start(f32[1,72,128]{2,1,0:T(8,128)S(1)} %get-tuple-element.38.refs_0_), channel_id=1, source_target_pairs={{0,12},{2,14},{4,8},{6,10},{8,4},{10,6},{12,0},{14,2},{1,13},{3,15... | collective-permute-start | bytes 110600 | tf_op jit(solution)/shard_map/ppermute | solution.py:337
  6.9 0.2 collective-permute-start.2
  7.1 1.4 %shard_map.87 = (bf16[8,512,256]{2,1,0:T(8,128)(2,1)S(1)}, f32[16,128]{1,0:T(8,128)S(1)}, f32[8,16,128]{2,1,0:T(8,128)S(1)}, f32[16,128]{1,0:T(8,128)S(1)}) custom-call(f32[16,128]{1,0:T(8,128)} %refs_0_.3, s32[8,16]{1,0:T(8,128)} %bitcast.4, s32[1,16]{1,0:T(1,128)} %bitcast.5, f32[16,64,128]{2,1,0:T(8,128)} %refs_3_.1), custom_call_target="tpu_custom_call" | custom-call | flops 1000000000 | bytes 524288 | tf_op jit(solution)/shard_map/pallas_call | solution.py:292
  8.5 0.6 %shard_map.88 = (f32[8,128,256]{2,1,0:T(8,128)S(1)}, bf16[128,512]{1,0:T(8,128)(2,1)S(1)}, f32[1,16,128]{2,1,0:T(8,128)S(1)}, f32[1,16,128]{2,1,0:T(8,128)S(1)}) custom-call(f32[1,72,128]{2,1,0:T(8,128)S(1)} %get-tuple-element.38.refs_0_, bf16[8,512,256]{2,1,0:T(8,128)(2,1)S(1)} %get-tuple-element.39.refs_1_.refs_3_.refs_8_), custom_call_target="tpu_custom_call" | custom-call | flops 268435456 | bytes 524288 | tf_op jit(solution)/shard_map/pallas_call | solution.py:324
  9.1 0.0 collective-permute-done.refs_0_.refs_1_
  9.1 1.5 %collective-permute-start.3 = (f32[2,72,128]{2,1,0:T(8,128)S(1)}, f32[2,72,128]{2,1,0:T(8,128)S(1)}, u32[]{:S(2)}, u32[]{:S(2)}) collective-permute-start(f32[2,72,128]{2,1,0:T(8,128)S(1)} %shard_map.90), channel_id=1, source_target_pairs={{0,2},{2,0},{4,6},{6,4},{8,10},{10,8},{12,14},{14,12},{1,3},{3,1},... | collective-permute-start | bytes 221192 | tf_op jit(solution)/shard_map/ppermute | solution.py:337
  10.6 0.7 %collective-permute-done.1.refs_1_.refs_0_ = f32[1,72,128]{2,1,0:T(8,128)S(1)} collective-permute-done((f32[1,72,128]{2,1,0:T(8,128)S(1)}, f32[1,72,128]{2,1,0:T(8,128)S(1)}, u32[]{:S(2)}, u32[]{:S(2)}) %collective-permute-start.1) | collective-permute-done | bytes 36896 | tf_op jit(solution)/shard_map/ppermute | solution.py:337
  11.3 0.0 collective-permute-done.2.refs_2_.refs_1_
  11.3 1.6 %collective-permute-start.4 = (f32[2,72,128]{2,1,0:T(8,128)S(1)}, f32[2,72,128]{2,1,0:T(8,128)S(1)}, u32[]{:S(2)}, u32[]{:S(2)}) collective-permute-start(f32[2,72,128]{2,1,0:T(8,128)S(1)} %shard_map.92), channel_id=1, source_target_pairs={{0,2},{2,0},{4,6},{6,4},{8,10},{10,8},{12,14},{14,12},{1,3},{3,1},... | collective-permute-start | bytes 221192 | tf_op jit(solution)/shard_map/ppermute | solution.py:337
  12.9 1.5 %shard_map.89 = (f32[8,384,256]{2,1,0:T(8,128)S(1)}, bf16[384,512]{1,0:T(8,128)(2,1)S(1)}, f32[3,16,128]{2,1,0:T(8,128)S(1)}, f32[3,16,128]{2,1,0:T(8,128)S(1)}) custom-call(f32[1,72,128]{2,1,0:T(8,128)S(1)} %collective-permute-done.refs_0_.refs_1_, f32[1,72,128]{2,1,0:T(8,128)S(1)} %collective-permute-done.1.refs_1_.refs_0_, ...), custom_call_target="tpu_custom_call" | custom-call | flops 805306368 | bytes 524288 | tf_op jit(solution)/shard_map/pallas_call | solution.py:324
  14.4 0.0 collective-permute-done.3.refs_0_
  14.4 0.9 %shard_map.91 = (f32[8,256,256]{2,1,0:T(8,128)S(1)}, bf16[256,512]{1,0:T(8,128)(2,1)S(1)}, f32[2,16,128]{2,1,0:T(8,128)S(1)}, f32[2,16,128]{2,1,0:T(8,128)S(1)}) custom-call(f32[2,72,128]{2,1,0:T(8,128)S(1)} %collective-permute-done.3.refs_0_, bf16[8,512,256]{2,1,0:T(8,128)(2,1)S(1)} %get-tuple-element.39.refs_1_.refs_3_.refs_8_), custom_call_target="tpu_custom_call" | custom-call | flops 536870912 | bytes 524288 | tf_op jit(solution)/shard_map/pallas_call | solution.py:324
  15.3 0.4 collective-permute-done.4.refs_0_
  15.8 0.1 collective-permute-start.6
  15.9 0.9 %shard_map.95 = (f32[8,256,256]{2,1,0:T(8,128)S(1)}, bf16[256,512]{1,0:T(8,128)(2,1)S(1)}, f32[2,16,128]{2,1,0:T(8,128)S(1)}, f32[2,16,128]{2,1,0:T(8,128)S(1)}) custom-call(f32[2,72,128]{2,1,0:T(8,128)S(1)} %collective-permute-done.4.refs_0_, bf16[8,512,256]{2,1,0:T(8,128)(2,1)S(1)} %get-tuple-element.39.refs_1_.refs_3_.refs_8_, ...), custom_call_target="tpu_custom_call" | custom-call | flops 536870912 | bytes 524288 | tf_op jit(solution)/shard_map/pallas_call | solution.py:324
  16.8 0.1 collective-permute-start.5
  16.9 0.1 collective-permute-done.6.refs_12_
  17.0 27.8 %shard_map.97 = (f32[16,128]{1,0:T(8,128)S(1)}, f32[8,1,128]{2,1,0:T(1,128)S(1)}) custom-call(f32[8,128,256]{2,1,0:T(8,128)S(1)} %get-tuple-element.40.refs_0_, f32[8,384,256]{2,1,0:T(8,128)S(1)} %get-tuple-element.41.refs_1_, f32[8,256,256]{2,1,0:T(8,128)S(1)} %get-tuple-element.43.refs_2_, f32[8,256,256]{2,1,0:T(8,128)S(1)} %get-tuple-element.64.refs_3_, ...), custom_call_target="tpu_custom_call" | custom-call | flops 1000000000 | bytes 524288 | tf_op jit(solution)/shard_map/pallas_call | solution.py:364
  44.8 0.0 collective-permute-done.5.refs_12_
  44.8 10.4 %all_to_all.5.values_ref = f32[8,1,128]{2,1,0:T(1,128)S(1)} all-to-all(f32[8,1,128]{2,1,0:T(1,128)S(1)} %get-tuple-element.69), channel_id=1, replica_groups=mesh['grp'=2,'src'=8,'tgt'=2] {'src'}, dimensions={0} | all-to-all | bytes 8192 | tf_op jit(solution)/shard_map/all_to_all | solution.py:381
  55.3 0.6 %shard_map.99 = (f32[1,128]{1,0:T(1,128)}, f32[16,128]{1,0:T(8,128)}) custom-call(f32[8,1,128]{2,1,0:T(1,128)S(1)} %all_to_all.5.values_ref, f32[1,128]{1,0:T(1,128)S(1)} %get-tuple-element.70.weight_ref, f32[16,128]{1,0:T(8,128)S(1)} %get-tuple-element.71.poten_ref), custom_call_target="tpu_custom_call" | custom-call | tf_op jit(solution)/shard_map/pallas_call | solution.py:383
  (6 shorter events, 0.1 us)
Async XLA Ops:
  1.4 7.6 %collective-permute-start = (f32[1,72,128]{2,1,0:T(8,128)S(1)}, f32[1,72,128]{2,1,0:T(8,128)S(1)}, u32[]{:S(2)}, u32[]{:S(2)}) collective-permute-start(f32[1,72,128]{2,1,0:T(8,128)S(1)} %get-tuple-element.38.refs_0_), channel_id=1, source_target_pairs={{0,8},{2,10},{4,12},{6,14},{8,0},{10,2},{12,4},{14,6},{1,9},{3,11}... | collective-permute-start | bytes 110600 | tf_op jit(solution)/shard_map/ppermute | solution.py:337
  5.5 5.8 %collective-permute-start.1 = (f32[1,72,128]{2,1,0:T(8,128)S(1)}, f32[1,72,128]{2,1,0:T(8,128)S(1)}, u32[]{:S(2)}, u32[]{:S(2)}) collective-permute-start(f32[1,72,128]{2,1,0:T(8,128)S(1)} %get-tuple-element.38.refs_0_), channel_id=1, source_target_pairs={{0,12},{2,14},{4,8},{6,10},{8,4},{10,6},{12,0},{14,2},{1,13},{3,15... | collective-permute-start | bytes 110600 | tf_op jit(solution)/shard_map/ppermute | solution.py:337
  6.9 4.4 %collective-permute-start.2 = (f32[1,72,128]{2,1,0:T(8,128)S(1)}, f32[1,72,128]{2,1,0:T(8,128)S(1)}, u32[]{:S(2)}, u32[]{:S(2)}) collective-permute-start(f32[1,72,128]{2,1,0:T(8,128)S(1)} %get-tuple-element.38.refs_0_), channel_id=1, source_target_pairs={{0,4},{2,6},{4,0},{6,2},{8,12},{10,14},{12,8},{14,10},{1,5},{3,7},... | collective-permute-start | bytes 110600 | tf_op jit(solution)/shard_map/ppermute | solution.py:337
  9.1 5.3 %collective-permute-start.3 = (f32[2,72,128]{2,1,0:T(8,128)S(1)}, f32[2,72,128]{2,1,0:T(8,128)S(1)}, u32[]{:S(2)}, u32[]{:S(2)}) collective-permute-start(f32[2,72,128]{2,1,0:T(8,128)S(1)} %shard_map.90), channel_id=1, source_target_pairs={{0,2},{2,0},{4,6},{6,4},{8,10},{10,8},{12,14},{14,12},{1,3},{3,1},... | collective-permute-start | bytes 221192 | tf_op jit(solution)/shard_map/ppermute | solution.py:337
  11.3 4.4 %collective-permute-start.4 = (f32[2,72,128]{2,1,0:T(8,128)S(1)}, f32[2,72,128]{2,1,0:T(8,128)S(1)}, u32[]{:S(2)}, u32[]{:S(2)}) collective-permute-start(f32[2,72,128]{2,1,0:T(8,128)S(1)} %shard_map.92), channel_id=1, source_target_pairs={{0,2},{2,0},{4,6},{6,4},{8,10},{10,8},{12,14},{14,12},{1,3},{3,1},... | collective-permute-start | bytes 221192 | tf_op jit(solution)/shard_map/ppermute | solution.py:337
  15.8 1.2 %collective-permute-start.6 = (f32[16,128]{1,0:T(8,128)S(1)}, f32[16,128]{1,0:T(8,128)S(1)}, u32[]{:S(2)}, u32[]{:S(2)}) collective-permute-start(f32[16,128]{1,0:T(8,128)S(1)} %get-tuple-element.58.refs_2_.refs_11_), channel_id=1, source_target_pairs={{0,1},{1,0},{2,3},{3,2},{4,5},{5,4},{6,7},{7,6},{8,9},{9,8},{10,11... | collective-permute-start | bytes 24584 | tf_op jit(solution)/shard_map/ppermute | solution.py:375
  16.8 28.0 %collective-permute-start.5 = (f32[16,128]{1,0:T(8,128)S(1)}, f32[16,128]{1,0:T(8,128)S(1)}, u32[]{:S(2)}, u32[]{:S(2)}) collective-permute-start(f32[16,128]{1,0:T(8,128)S(1)} %get-tuple-element.61.refs_11_), channel_id=1, source_target_pairs={{0,1},{1,0},{2,3},{3,2},{4,5},{5,4},{6,7},{7,6},{8,9},{9,8},{10,11... | collective-permute-start | bytes 24584 | tf_op jit(solution)/shard_map/ppermute | solution.py:378

commit v10 on v9

--- a/solution.py
+++ b/solution.py
@@ -62,9 +62,8 @@
     norm = jnp.sum(feat * feat, axis=0, keepdims=True)
     bias = weight - (log2e / entropic) * norm
     scaled = feat * (2.0 * log2e / entropic)
-    below = jnp.broadcast_to(bias, (send_ref.shape[1] - depth, cells))
-    send_ref[0, :depth, :] = scaled
-    send_ref[0, depth:, :] = below
+    send_ref[0, :depth, 0, :] = scaled
+    send_ref[0, depth, 0:1, :] = bias
     weight_ref[...] = weight
 
 
@@ -137,12 +136,12 @@
     cells = both // 2
     depth = cells // 2
     lane = lax.broadcasted_iota(jnp.int32, (cells, cells), 1)
-    biases = jnp.concatenate([pack[depth : depth + 1, :] for pack in packs], axis=0)
+    biases = jnp.concatenate([pack[depth, 0:1, :] for pack in packs], axis=0)
     bias_pieces = jnp.concatenate(list(pieces(biases)), axis=0)
     padded = jnp.concatenate([bias_pieces, jnp.zeros((cells - 3 * blocks, cells), jnp.float32)], axis=0)
     bias_lanes = padded.T
     for place, pack in enumerate(packs):
-        feat = pack[:depth, :]
+        feat = pack[:depth, 0, :]
         turned = jnp.concatenate([feat, feat], axis=0).T
         high, mid, low = pieces(turned)
         own = jnp.where(lax.rem(lane, blocks) == place, bias_lanes, 0.0)
@@ -303,7 +302,7 @@
     pack, weight = reading(
         pack_kernel,
         [target_feat, log_mass_tgt, potential_tgt],
-        [in_vmem((1, depth + 8, cells), jnp.float32), in_vmem((1, cells), jnp.float32)],
+        [in_vmem((1, depth + 1, 1, cells), jnp.float32), in_vmem((1, cells), jnp.float32)],
         None,
     )
     wide_feat, norm, mask, mass = reading(

time: 56.1 us -> 56 us (level)
  no operation moved by 1% of the time
where the time goes in v10:
time: 56 us; the launch traced here: 55.8 us
  Pallas kernels  34.6 us (62%)
  blocking collectives  10.4 us (19%)
  starting transfers between devices  8.92 us (16%)
  waiting for transfers between devices  1.1 us (2%)
  between operations  0.74 us (1%)
    pallas_call x2, Pallas kernels, columns_of(): call(functools.partial(column_kernel, groups, core), [VM] * (2 * groups +...  27.8 us
    all_to_all x1, blocking collectives, dense_device(): arrived = lax.all_to_all(columns, 'src', 0, 0)  10.4 us
    ppermute x5, starting transfers between devices, swapped(): return lax.ppermute(array, 'src', [(i, i ^ step) for i in range(shards)])  8.78 us
    pallas_call x5, Pallas kernels, tiles(): call(functools.partial(tile_kernel, len(packs), core), [VM] * (len(packs)...  3.91 us
    pallas_call x2, Pallas kernels, reading(): call(kernel, [pl.BlockSpec(memory_space=pltpu.HBM)] * len(args), out_shap...  2.18 us
  transfers between devices with their start and end apart: 7, of which 3 were waited for; matrix products, arithmetic and copies ran while one was open for 0% of the time, Pallas kernels for 59%

profile of v10, /device:TPU:0, one launch (start us, length us, event | category | flops | bytes accessed | tf_op | source)
XLA Modules:
  0.0 55.8 jit_solution(8664448298475852630)
XLA Ops:
  0.6 0.8 %shard_map.86 = (f32[1,65,1,128]{3,2,1,0:T(1,128)S(1)}, f32[1,128]{1,0:T(1,128)S(1)}) custom-call(f32[1,64,128]{2,1,0:T(8,128)} %refs_0_.2, f32[1,128]{1,0:T(1,128)} %refs_1_.1, f32[1,128]{1,0:T(1,128)} %refs_2_.1), custom_call_target="tpu_custom_call" | custom-call | tf_op jit(solution)/shard_map/pallas_call | solution.py:291
  1.5 4.1 %collective-permute-start = (f32[1,65,1,128]{3,2,1,0:T(1,128)S(1)}, f32[1,65,1,128]{3,2,1,0:T(1,128)S(1)}, u32[]{:S(2)}, u32[]{:S(2)}) collective-permute-start(f32[1,65,1,128]{3,2,1,0:T(1,128)S(1)} %get-tuple-element.38.refs_0_), channel_id=1, source_target_pairs={{0,8},{2,10},{4,12},{6,14},{8,0},{10,2},{12,4},{14,6},{1,9},{3,11}... | collective-permute-start | bytes 99848 | tf_op jit(solution)/shard_map/ppermute | solution.py:336
  5.6 1.3 %collective-permute-start.1 = (f32[1,65,1,128]{3,2,1,0:T(1,128)S(1)}, f32[1,65,1,128]{3,2,1,0:T(1,128)S(1)}, u32[]{:S(2)}, u32[]{:S(2)}) collective-permute-start(f32[1,65,1,128]{3,2,1,0:T(1,128)S(1)} %get-tuple-element.38.refs_0_), channel_id=1, source_target_pairs={{0,12},{2,14},{4,8},{6,10},{8,4},{10,6},{12,0},{14,2},{1,13},{3,15... | collective-permute-start | bytes 99848 | tf_op jit(solution)/shard_map/ppermute | solution.py:336
  6.9 0.2 collective-permute-start.2
  7.1 1.4 %shard_map.87 = (bf16[8,512,256]{2,1,0:T(8,128)(2,1)S(1)}, f32[16,128]{1,0:T(8,128)S(1)}, f32[8,16,128]{2,1,0:T(8,128)S(1)}, f32[16,128]{1,0:T(8,128)S(1)}) custom-call(f32[16,128]{1,0:T(8,128)} %refs_0_.3, s32[8,16]{1,0:T(8,128)} %bitcast.4, s32[1,16]{1,0:T(1,128)} %bitcast.5, f32[16,64,128]{2,1,0:T(8,128)} %refs_3_.1), custom_call_target="tpu_custom_call" | custom-call | flops 1000000000 | bytes 524288 | tf_op jit(solution)/shard_map/pallas_call | solution.py:291
  8.5 0.6 %shard_map.88 = (f32[8,128,256]{2,1,0:T(8,128)S(1)}, bf16[128,512]{1,0:T(8,128)(2,1)S(1)}, f32[1,16,128]{2,1,0:T(8,128)S(1)}, f32[1,16,128]{2,1,0:T(8,128)S(1)}) custom-call(f32[1,65,1,128]{3,2,1,0:T(1,128)S(1)} %get-tuple-element.38.refs_0_, bf16[8,512,256]{2,1,0:T(8,128)(2,1)S(1)} %get-tuple-element.39.refs_1_.refs_3_.refs_8_), custom_call_target="tpu_custom_call" | custom-call | flops 268435456 | bytes 524288 | tf_op jit(solution)/shard_map/pallas_call | solution.py:323
  9.1 0.0 collective-permute-done.refs_0_.refs_1_
  9.1 1.5 %collective-permute-start.3 = (f32[2,65,1,128]{3,2,1,0:T(1,128)S(1)}, f32[2,65,1,128]{3,2,1,0:T(1,128)S(1)}, u32[]{:S(2)}, u32[]{:S(2)}) collective-permute-start(f32[2,65,1,128]{3,2,1,0:T(1,128)S(1)} %shard_map.90), channel_id=1, source_target_pairs={{0,2},{2,0},{4,6},{6,4},{8,10},{10,8},{12,14},{14,12},{1,3},{3,1},... | collective-permute-start | bytes 199688 | tf_op jit(solution)/shard_map/ppermute | solution.py:336
  10.7 0.6 %collective-permute-done.1.refs_1_.refs_0_ = f32[1,65,1,128]{3,2,1,0:T(1,128)S(1)} collective-permute-done((f32[1,65,1,128]{3,2,1,0:T(1,128)S(1)}, f32[1,65,1,128]{3,2,1,0:T(1,128)S(1)}, u32[]{:S(2)}, u32[]{:S(2)}) %collective-permute-start.1) | collective-permute-done | bytes 33312 | tf_op jit(solution)/shard_map/ppermute | solution.py:336
  11.3 0.0 collective-permute-done.2.refs_2_.refs_1_
  11.3 1.6 %collective-permute-start.4 = (f32[2,65,1,128]{3,2,1,0:T(1,128)S(1)}, f32[2,65,1,128]{3,2,1,0:T(1,128)S(1)}, u32[]{:S(2)}, u32[]{:S(2)}) collective-permute-start(f32[2,65,1,128]{3,2,1,0:T(1,128)S(1)} %shard_map.92), channel_id=1, source_target_pairs={{0,2},{2,0},{4,6},{6,4},{8,10},{10,8},{12,14},{14,12},{1,3},{3,1},... | collective-permute-start | bytes 199688 | tf_op jit(solution)/shard_map/ppermute | solution.py:336
  12.8 1.5 %shard_map.89 = (f32[8,384,256]{2,1,0:T(8,128)S(1)}, bf16[384,512]{1,0:T(8,128)(2,1)S(1)}, f32[3,16,128]{2,1,0:T(8,128)S(1)}, f32[3,16,128]{2,1,0:T(8,128)S(1)}) custom-call(f32[1,65,1,128]{3,2,1,0:T(1,128)S(1)} %collective-permute-done.refs_0_.refs_1_, f32[1,65,1,128]{3,2,1,0:T(1,128)S(1)} %collective-permute-done.1.refs_1_.refs_0_, ...), custom_call_target="tpu_custom_call" | custom-call | flops 805306368 | bytes 524288 | tf_op jit(solution)/shard_map/pallas_call | solution.py:323
  14.4 0.0 collective-permute-done.3.refs_0_
  14.4 0.9 %shard_map.91 = (f32[8,256,256]{2,1,0:T(8,128)S(1)}, bf16[256,512]{1,0:T(8,128)(2,1)S(1)}, f32[2,16,128]{2,1,0:T(8,128)S(1)}, f32[2,16,128]{2,1,0:T(8,128)S(1)}) custom-call(f32[2,65,1,128]{3,2,1,0:T(1,128)S(1)} %collective-permute-done.3.refs_0_, bf16[8,512,256]{2,1,0:T(8,128)(2,1)S(1)} %get-tuple-element.39.refs_1_.refs_3_.refs_8_), custom_call_target="tpu_custom_call" | custom-call | flops 536870912 | bytes 524288 | tf_op jit(solution)/shard_map/pallas_call | solution.py:323
  15.3 0.3 collective-permute-done.4.refs_0_
  15.7 0.1 collective-permute-start.6
  15.7 0.9 %shard_map.95 = (f32[8,256,256]{2,1,0:T(8,128)S(1)}, bf16[256,512]{1,0:T(8,128)(2,1)S(1)}, f32[2,16,128]{2,1,0:T(8,128)S(1)}, f32[2,16,128]{2,1,0:T(8,128)S(1)}) custom-call(f32[2,65,1,128]{3,2,1,0:T(1,128)S(1)} %collective-permute-done.4.refs_0_, bf16[8,512,256]{2,1,0:T(8,128)(2,1)S(1)} %get-tuple-element.39.refs_1_.refs_3_.refs_8_, ...), custom_call_target="tpu_custom_call" | custom-call | flops 536870912 | bytes 524288 | tf_op jit(solution)/shard_map/pallas_call | solution.py:323
  16.7 0.1 collective-permute-start.5
  16.8 0.1 collective-permute-done.6.refs_12_
  16.9 27.8 %shard_map.97 = (f32[16,128]{1,0:T(8,128)S(1)}, f32[8,1,128]{2,1,0:T(1,128)S(1)}) custom-call(f32[8,128,256]{2,1,0:T(8,128)S(1)} %get-tuple-element.40.refs_0_, f32[8,384,256]{2,1,0:T(8,128)S(1)} %get-tuple-element.41.refs_1_, f32[8,256,256]{2,1,0:T(8,128)S(1)} %get-tuple-element.43.refs_2_, f32[8,256,256]{2,1,0:T(8,128)S(1)} %get-tuple-element.64.refs_3_, ...), custom_call_target="tpu_custom_call" | custom-call | flops 1000000000 | bytes 524288 | tf_op jit(solution)/shard_map/pallas_call | solution.py:363
  44.7 0.0 collective-permute-done.5.refs_12_
  44.7 10.4 %all_to_all.5.values_ref = f32[8,1,128]{2,1,0:T(1,128)S(1)} all-to-all(f32[8,1,128]{2,1,0:T(1,128)S(1)} %get-tuple-element.69), channel_id=1, replica_groups=mesh['grp'=2,'src'=8,'tgt'=2] {'src'}, dimensions={0} | all-to-all | bytes 8192 | tf_op jit(solution)/shard_map/all_to_all | solution.py:380
  55.2 0.6 %shard_map.99 = (f32[1,128]{1,0:T(1,128)}, f32[16,128]{1,0:T(8,128)}) custom-call(f32[8,1,128]{2,1,0:T(1,128)S(1)} %all_to_all.5.values_ref, f32[1,128]{1,0:T(1,128)S(1)} %get-tuple-element.70.weight_ref, f32[16,128]{1,0:T(8,128)S(1)} %get-tuple-element.71.poten_ref), custom_call_target="tpu_custom_call" | custom-call | tf_op jit(solution)/shard_map/pallas_call | solution.py:382
  (6 shorter events, 0.1 us)
Async XLA Ops:
  1.5 7.6 %collective-permute-start = (f32[1,65,1,128]{3,2,1,0:T(1,128)S(1)}, f32[1,65,1,128]{3,2,1,0:T(1,128)S(1)}, u32[]{:S(2)}, u32[]{:S(2)}) collective-permute-start(f32[1,65,1,128]{3,2,1,0:T(1,128)S(1)} %get-tuple-element.38.refs_0_), channel_id=1, source_target_pairs={{0,8},{2,10},{4,12},{6,14},{8,0},{10,2},{12,4},{14,6},{1,9},{3,11}... | collective-permute-start | bytes 99848 | tf_op jit(solution)/shard_map/ppermute | solution.py:336
  5.6 5.7 %collective-permute-start.1 = (f32[1,65,1,128]{3,2,1,0:T(1,128)S(1)}, f32[1,65,1,128]{3,2,1,0:T(1,128)S(1)}, u32[]{:S(2)}, u32[]{:S(2)}) collective-permute-start(f32[1,65,1,128]{3,2,1,0:T(1,128)S(1)} %get-tuple-element.38.refs_0_), channel_id=1, source_target_pairs={{0,12},{2,14},{4,8},{6,10},{8,4},{10,6},{12,0},{14,2},{1,13},{3,15... | collective-permute-start | bytes 99848 | tf_op jit(solution)/shard_map/ppermute | solution.py:336
  6.9 4.4 %collective-permute-start.2 = (f32[1,65,1,128]{3,2,1,0:T(1,128)S(1)}, f32[1,65,1,128]{3,2,1,0:T(1,128)S(1)}, u32[]{:S(2)}, u32[]{:S(2)}) collective-permute-start(f32[1,65,1,128]{3,2,1,0:T(1,128)S(1)} %get-tuple-element.38.refs_0_), channel_id=1, source_target_pairs={{0,4},{2,6},{4,0},{6,2},{8,12},{10,14},{12,8},{14,10},{1,5},{3,7},... | collective-permute-start | bytes 99848 | tf_op jit(solution)/shard_map/ppermute | solution.py:336
  9.1 5.3 %collective-permute-start.3 = (f32[2,65,1,128]{3,2,1,0:T(1,128)S(1)}, f32[2,65,1,128]{3,2,1,0:T(1,128)S(1)}, u32[]{:S(2)}, u32[]{:S(2)}) collective-permute-start(f32[2,65,1,128]{3,2,1,0:T(1,128)S(1)} %shard_map.90), channel_id=1, source_target_pairs={{0,2},{2,0},{4,6},{6,4},{8,10},{10,8},{12,14},{14,12},{1,3},{3,1},... | collective-permute-start | bytes 199688 | tf_op jit(solution)/shard_map/ppermute | solution.py:336
  11.3 4.3 %collective-permute-start.4 = (f32[2,65,1,128]{3,2,1,0:T(1,128)S(1)}, f32[2,65,1,128]{3,2,1,0:T(1,128)S(1)}, u32[]{:S(2)}, u32[]{:S(2)}) collective-permute-start(f32[2,65,1,128]{3,2,1,0:T(1,128)S(1)} %shard_map.92), channel_id=1, source_target_pairs={{0,2},{2,0},{4,6},{6,4},{8,10},{10,8},{12,14},{14,12},{1,3},{3,1},... | collective-permute-start | bytes 199688 | tf_op jit(solution)/shard_map/ppermute | solution.py:336
  15.7 1.2 %collective-permute-start.6 = (f32[16,128]{1,0:T(8,128)S(1)}, f32[16,128]{1,0:T(8,128)S(1)}, u32[]{:S(2)}, u32[]{:S(2)}) collective-permute-start(f32[16,128]{1,0:T(8,128)S(1)} %get-tuple-element.58.refs_2_.refs_11_), channel_id=1, source_target_pairs={{0,1},{1,0},{2,3},{3,2},{4,5},{5,4},{6,7},{7,6},{8,9},{9,8},{10,11... | collective-permute-start | bytes 24584 | tf_op jit(solution)/shard_map/ppermute | solution.py:374
  16.7 28.0 %collective-permute-start.5 = (f32[16,128]{1,0:T(8,128)S(1)}, f32[16,128]{1,0:T(8,128)S(1)}, u32[]{:S(2)}, u32[]{:S(2)}) collective-permute-start(f32[16,128]{1,0:T(8,128)S(1)} %get-tuple-element.61.refs_11_), channel_id=1, source_target_pairs={{0,1},{1,0},{2,3},{3,2},{4,5},{5,4},{6,7},{7,6},{8,9},{9,8},{10,11... | collective-permute-start | bytes 24584 | tf_op jit(solution)/shard_map/ppermute | solution.py:377

commit v11 on v10

--- a/solution.py
+++ b/solution.py
@@ -220,18 +220,21 @@
         for index in range(ref.shape[0] // cells)
     ]
     used = [jnp.max(mask_ref[place], axis=0, keepdims=True) > 0.5 * very_low for place in range(shards)]
-    worst = jnp.full((1, cells), 1.0, jnp.float32)
     owners = blocks_at(shards)
+    sums = []
     for place, (group, rows) in enumerate(spots):
         acc = jnp.zeros((cells, cells), jnp.float32)
         for pair in range(pairs):
             acc = acc + exps_refs[group][pair, rows, :cells] * weight_ref[place, 2 * pair : 2 * pair + 1, :]
             acc = acc + exps_refs[group][pair, rows, cells:] * weight_ref[place, 2 * pair + 1 : 2 * pair + 2, :]
-        here = across(jnp.sum(acc, axis=1, keepdims=True))
-        sums_ref[owners[place]] = jnp.where(used[place], jnp.log2(here), very_low)
-        worst = jnp.minimum(worst, jnp.where(used[place], here, 1.0))
-
-    @pl.when(jnp.min(worst) < least_sum)
+        sums.append(jnp.sum(acc.T, axis=0, keepdims=True))
+    whole_sums = jnp.concatenate([jnp.where(here, one, 1.0) for here, one in zip(used, sums)], axis=0)
+    worst = jnp.min(whole_sums)
+    logs = jnp.log2(whole_sums)
+    for place in range(shards):
+        sums_ref[owners[place]] = jnp.where(used[place], logs[place : place + 1, :], very_low)
+
+    @pl.when(worst < least_sum)
     def _():
         for place, (group, rows) in enumerate(spots):
 

time: 56 us -> 55.8 us (level)
  no operation moved by 1% of the time
where the time goes in v11:
time: 55.8 us; the launch traced here: 55.5 us
  Pallas kernels  34.3 us (61%)
  blocking collectives  10.4 us (19%)
  starting transfers between devices  8.92 us (16%)
  waiting for transfers between devices  1.1 us (2%)
  between operations  0.74 us (1%)
    pallas_call x2, Pallas kernels, columns_of(): call(functools.partial(column_kernel, groups, core), [VM] * (2 * groups +...  27.6 us
    all_to_all x1, blocking collectives, dense_device(): arrived = lax.all_to_all(columns, 'src', 0, 0)  10.4 us
    ppermute x5, starting transfers between devices, swapped(): return lax.ppermute(array, 'src', [(i, i ^ step) for i in range(shards)])  8.78 us
    pallas_call x5, Pallas kernels, tiles(): call(functools.partial(tile_kernel, len(packs), core), [VM] * (len(packs)...  3.91 us
    pallas_call x2, Pallas kernels, reading(): call(kernel, [pl.BlockSpec(memory_space=pltpu.HBM)] * len(args), out_shap...  2.18 us
  transfers between devices with their start and end apart: 7, of which 3 were waited for; matrix products, arithmetic and copies ran while one was open for 0% of the time, Pallas kernels for 59%

profile of v11, /device:TPU:0, one launch (start us, length us, event | category | flops | bytes accessed | tf_op | source)
XLA Modules:
  0.0 55.5 jit_solution(3501878650444904555)
XLA Ops:
  0.6 0.8 %shard_map.86 = (f32[1,65,1,128]{3,2,1,0:T(1,128)S(1)}, f32[1,128]{1,0:T(1,128)S(1)}) custom-call(f32[1,64,128]{2,1,0:T(8,128)} %refs_0_.2, f32[1,128]{1,0:T(1,128)} %refs_1_.1, f32[1,128]{1,0:T(1,128)} %refs_2_.1), custom_call_target="tpu_custom_call" | custom-call | tf_op jit(solution)/shard_map/pallas_call | solution.py:294
  1.5 4.1 %collective-permute-start = (f32[1,65,1,128]{3,2,1,0:T(1,128)S(1)}, f32[1,65,1,128]{3,2,1,0:T(1,128)S(1)}, u32[]{:S(2)}, u32[]{:S(2)}) collective-permute-start(f32[1,65,1,128]{3,2,1,0:T(1,128)S(1)} %get-tuple-element.38.refs_0_), channel_id=1, source_target_pairs={{0,8},{2,10},{4,12},{6,14},{8,0},{10,2},{12,4},{14,6},{1,9},{3,11}... | collective-permute-start | bytes 99848 | tf_op jit(solution)/shard_map/ppermute | solution.py:339
  5.6 1.3 %collective-permute-start.1 = (f32[1,65,1,128]{3,2,1,0:T(1,128)S(1)}, f32[1,65,1,128]{3,2,1,0:T(1,128)S(1)}, u32[]{:S(2)}, u32[]{:S(2)}) collective-permute-start(f32[1,65,1,128]{3,2,1,0:T(1,128)S(1)} %get-tuple-element.38.refs_0_), channel_id=1, source_target_pairs={{0,12},{2,14},{4,8},{6,10},{8,4},{10,6},{12,0},{14,2},{1,13},{3,15... | collective-permute-start | bytes 99848 | tf_op jit(solution)/shard_map/ppermute | solution.py:339
  6.9 0.2 collective-permute-start.2
  7.1 1.4 %shard_map.87 = (bf16[8,512,256]{2,1,0:T(8,128)(2,1)S(1)}, f32[16,128]{1,0:T(8,128)S(1)}, f32[8,16,128]{2,1,0:T(8,128)S(1)}, f32[16,128]{1,0:T(8,128)S(1)}) custom-call(f32[16,128]{1,0:T(8,128)} %refs_0_.3, s32[8,16]{1,0:T(8,128)} %bitcast.4, s32[1,16]{1,0:T(1,128)} %bitcast.5, f32[16,64,128]{2,1,0:T(8,128)} %refs_3_.1), custom_call_target="tpu_custom_call" | custom-call | flops 1000000000 | bytes 524288 | tf_op jit(solution)/shard_map/pallas_call | solution.py:294
  8.5 0.6 %shard_map.88 = (f32[8,128,256]{2,1,0:T(8,128)S(1)}, bf16[128,512]{1,0:T(8,128)(2,1)S(1)}, f32[1,16,128]{2,1,0:T(8,128)S(1)}, f32[1,16,128]{2,1,0:T(8,128)S(1)}) custom-call(f32[1,65,1,128]{3,2,1,0:T(1,128)S(1)} %get-tuple-element.38.refs_0_, bf16[8,512,256]{2,1,0:T(8,128)(2,1)S(1)} %get-tuple-element.39.refs_1_.refs_3_.refs_8_), custom_call_target="tpu_custom_call" | custom-call | flops 268435456 | bytes 524288 | tf_op jit(solution)/shard_map/pallas_call | solution.py:326
  9.1 0.0 collective-permute-done.refs_0_.refs_1_
  9.1 1.5 %collective-permute-start.3 = (f32[2,65,1,128]{3,2,1,0:T(1,128)S(1)}, f32[2,65,1,128]{3,2,1,0:T(1,128)S(1)}, u32[]{:S(2)}, u32[]{:S(2)}) collective-permute-start(f32[2,65,1,128]{3,2,1,0:T(1,128)S(1)} %shard_map.90), channel_id=1, source_target_pairs={{0,2},{2,0},{4,6},{6,4},{8,10},{10,8},{12,14},{14,12},{1,3},{3,1},... | collective-permute-start | bytes 199688 | tf_op jit(solution)/shard_map/ppermute | solution.py:339
  10.7 0.6 %collective-permute-done.1.refs_1_.refs_0_ = f32[1,65,1,128]{3,2,1,0:T(1,128)S(1)} collective-permute-done((f32[1,65,1,128]{3,2,1,0:T(1,128)S(1)}, f32[1,65,1,128]{3,2,1,0:T(1,128)S(1)}, u32[]{:S(2)}, u32[]{:S(2)}) %collective-permute-start.1) | collective-permute-done | bytes 33312 | tf_op jit(solution)/shard_map/ppermute | solution.py:339
  11.3 0.0 collective-permute-done.2.refs_2_.refs_1_
  11.3 1.6 %collective-permute-start.4 = (f32[2,65,1,128]{3,2,1,0:T(1,128)S(1)}, f32[2,65,1,128]{3,2,1,0:T(1,128)S(1)}, u32[]{:S(2)}, u32[]{:S(2)}) collective-permute-start(f32[2,65,1,128]{3,2,1,0:T(1,128)S(1)} %shard_map.92), channel_id=1, source_target_pairs={{0,2},{2,0},{4,6},{6,4},{8,10},{10,8},{12,14},{14,12},{1,3},{3,1},... | collective-permute-start | bytes 199688 | tf_op jit(solution)/shard_map/ppermute | solution.py:339
  12.8 1.5 %shard_map.89 = (f32[8,384,256]{2,1,0:T(8,128)S(1)}, bf16[384,512]{1,0:T(8,128)(2,1)S(1)}, f32[3,16,128]{2,1,0:T(8,128)S(1)}, f32[3,16,128]{2,1,0:T(8,128)S(1)}) custom-call(f32[1,65,1,128]{3,2,1,0:T(1,128)S(1)} %collective-permute-done.refs_0_.refs_1_, f32[1,65,1,128]{3,2,1,0:T(1,128)S(1)} %collective-permute-done.1.refs_1_.refs_0_, ...), custom_call_target="tpu_custom_call" | custom-call | flops 805306368 | bytes 524288 | tf_op jit(solution)/shard_map/pallas_call | solution.py:326
  14.4 0.0 collective-permute-done.3.refs_0_
  14.4 0.9 %shard_map.91 = (f32[8,256,256]{2,1,0:T(8,128)S(1)}, bf16[256,512]{1,0:T(8,128)(2,1)S(1)}, f32[2,16,128]{2,1,0:T(8,128)S(1)}, f32[2,16,128]{2,1,0:T(8,128)S(1)}) custom-call(f32[2,65,1,128]{3,2,1,0:T(1,128)S(1)} %collective-permute-done.3.refs_0_, bf16[8,512,256]{2,1,0:T(8,128)(2,1)S(1)} %get-tuple-element.39.refs_1_.refs_3_.refs_8_), custom_call_target="tpu_custom_call" | custom-call | flops 536870912 | bytes 524288 | tf_op jit(solution)/shard_map/pallas_call | solution.py:326
  15.3 0.3 collective-permute-done.4.refs_0_
  15.7 0.1 collective-permute-start.6
  15.7 0.9 %shard_map.95 = (f32[8,256,256]{2,1,0:T(8,128)S(1)}, bf16[256,512]{1,0:T(8,128)(2,1)S(1)}, f32[2,16,128]{2,1,0:T(8,128)S(1)}, f32[2,16,128]{2,1,0:T(8,128)S(1)}) custom-call(f32[2,65,1,128]{3,2,1,0:T(1,128)S(1)} %collective-permute-done.4.refs_0_, bf16[8,512,256]{2,1,0:T(8,128)(2,1)S(1)} %get-tuple-element.39.refs_1_.refs_3_.refs_8_, ...), custom_call_target="tpu_custom_call" | custom-call | flops 536870912 | bytes 524288 | tf_op jit(solution)/shard_map/pallas_call | solution.py:326
  16.7 0.1 collective-permute-start.5
  16.8 0.1 collective-permute-done.6.refs_12_
  16.9 27.5 %shard_map.97 = (f32[16,128]{1,0:T(8,128)S(1)}, f32[8,1,128]{2,1,0:T(1,128)S(1)}) custom-call(f32[8,128,256]{2,1,0:T(8,128)S(1)} %get-tuple-element.40.refs_0_, f32[8,384,256]{2,1,0:T(8,128)S(1)} %get-tuple-element.41.refs_1_, f32[8,256,256]{2,1,0:T(8,128)S(1)} %get-tuple-element.43.refs_2_, f32[8,256,256]{2,1,0:T(8,128)S(1)} %get-tuple-element.64.refs_3_, ...), custom_call_target="tpu_custom_call" | custom-call | flops 1000000000 | bytes 524288 | tf_op jit(solution)/shard_map/pallas_call | solution.py:366
  44.4 0.0 collective-permute-done.5.refs_12_
  44.5 10.4 %all_to_all.5.values_ref = f32[8,1,128]{2,1,0:T(1,128)S(1)} all-to-all(f32[8,1,128]{2,1,0:T(1,128)S(1)} %get-tuple-element.69), channel_id=1, replica_groups=mesh['grp'=2,'src'=8,'tgt'=2] {'src'}, dimensions={0} | all-to-all | bytes 8192 | tf_op jit(solution)/shard_map/all_to_all | solution.py:383
  54.9 0.6 %shard_map.99 = (f32[1,128]{1,0:T(1,128)}, f32[16,128]{1,0:T(8,128)}) custom-call(f32[8,1,128]{2,1,0:T(1,128)S(1)} %all_to_all.5.values_ref, f32[1,128]{1,0:T(1,128)S(1)} %get-tuple-element.70.weight_ref, f32[16,128]{1,0:T(8,128)S(1)} %get-tuple-element.71.poten_ref), custom_call_target="tpu_custom_call" | custom-call | tf_op jit(solution)/shard_map/pallas_call | solution.py:385
  (6 shorter events, 0.1 us)
Async XLA Ops:
  1.5 7.6 %collective-permute-start = (f32[1,65,1,128]{3,2,1,0:T(1,128)S(1)}, f32[1,65,1,128]{3,2,1,0:T(1,128)S(1)}, u32[]{:S(2)}, u32[]{:S(2)}) collective-permute-start(f32[1,65,1,128]{3,2,1,0:T(1,128)S(1)} %get-tuple-element.38.refs_0_), channel_id=1, source_target_pairs={{0,8},{2,10},{4,12},{6,14},{8,0},{10,2},{12,4},{14,6},{1,9},{3,11}... | collective-permute-start | bytes 99848 | tf_op jit(solution)/shard_map/ppermute | solution.py:339
  5.6 5.7 %collective-permute-start.1 = (f32[1,65,1,128]{3,2,1,0:T(1,128)S(1)}, f32[1,65,1,128]{3,2,1,0:T(1,128)S(1)}, u32[]{:S(2)}, u32[]{:S(2)}) collective-permute-start(f32[1,65,1,128]{3,2,1,0:T(1,128)S(1)} %get-tuple-element.38.refs_0_), channel_id=1, source_target_pairs={{0,12},{2,14},{4,8},{6,10},{8,4},{10,6},{12,0},{14,2},{1,13},{3,15... | collective-permute-start | bytes 99848 | tf_op jit(solution)/shard_map/ppermute | solution.py:339
  6.9 4.4 %collective-permute-start.2 = (f32[1,65,1,128]{3,2,1,0:T(1,128)S(1)}, f32[1,65,1,128]{3,2,1,0:T(1,128)S(1)}, u32[]{:S(2)}, u32[]{:S(2)}) collective-permute-start(f32[1,65,1,128]{3,2,1,0:T(1,128)S(1)} %get-tuple-element.38.refs_0_), channel_id=1, source_target_pairs={{0,4},{2,6},{4,0},{6,2},{8,12},{10,14},{12,8},{14,10},{1,5},{3,7},... | collective-permute-start | bytes 99848 | tf_op jit(solution)/shard_map/ppermute | solution.py:339
  9.1 5.3 %collective-permute-start.3 = (f32[2,65,1,128]{3,2,1,0:T(1,128)S(1)}, f32[2,65,1,128]{3,2,1,0:T(1,128)S(1)}, u32[]{:S(2)}, u32[]{:S(2)}) collective-permute-start(f32[2,65,1,128]{3,2,1,0:T(1,128)S(1)} %shard_map.90), channel_id=1, source_target_pairs={{0,2},{2,0},{4,6},{6,4},{8,10},{10,8},{12,14},{14,12},{1,3},{3,1},... | collective-permute-start | bytes 199688 | tf_op jit(solution)/shard_map/ppermute | solution.py:339
  11.3 4.3 %collective-permute-start.4 = (f32[2,65,1,128]{3,2,1,0:T(1,128)S(1)}, f32[2,65,1,128]{3,2,1,0:T(1,128)S(1)}, u32[]{:S(2)}, u32[]{:S(2)}) collective-permute-start(f32[2,65,1,128]{3,2,1,0:T(1,128)S(1)} %shard_map.92), channel_id=1, source_target_pairs={{0,2},{2,0},{4,6},{6,4},{8,10},{10,8},{12,14},{14,12},{1,3},{3,1},... | collective-permute-start | bytes 199688 | tf_op jit(solution)/shard_map/ppermute | solution.py:339
  15.7 1.2 %collective-permute-start.6 = (f32[16,128]{1,0:T(8,128)S(1)}, f32[16,128]{1,0:T(8,128)S(1)}, u32[]{:S(2)}, u32[]{:S(2)}) collective-permute-start(f32[16,128]{1,0:T(8,128)S(1)} %get-tuple-element.58.refs_2_.refs_11_), channel_id=1, source_target_pairs={{0,1},{1,0},{2,3},{3,2},{4,5},{5,4},{6,7},{7,6},{8,9},{9,8},{10,11... | collective-permute-start | bytes 24584 | tf_op jit(solution)/shard_map/ppermute | solution.py:377
  16.7 27.8 %collective-permute-start.5 = (f32[16,128]{1,0:T(8,128)S(1)}, f32[16,128]{1,0:T(8,128)S(1)}, u32[]{:S(2)}, u32[]{:S(2)}) collective-permute-start(f32[16,128]{1,0:T(8,128)S(1)} %get-tuple-element.61.refs_11_), channel_id=1, source_target_pairs={{0,1},{1,0},{2,3},{3,2},{4,5},{5,4},{6,7},{7,6},{8,9},{9,8},{10,11... | collective-permute-start | bytes 24584 | tf_op jit(solution)/shard_map/ppermute | solution.py:380

commit v12 on v11

--- a/solution.py
+++ b/solution.py
@@ -104,8 +104,8 @@
 
 
 def join_kernel(*refs):
-    refs[-1][0] = refs[0][0]
-    refs[-1][1] = refs[1][0]
+    for place, ref in enumerate(refs[:-2]):
+        refs[-1][place] = ref[0]
 
 
 def on_core(core, work, idle):
@@ -338,19 +338,22 @@
     def swapped(array, step):
         return lax.ppermute(array, "src", [(i, i ^ step) for i in range(shards)])
 
-    there = {step: swapped(pack, step) for step in reversed(line_steps(shards))}
-    near = [pack] + [there[step] for step in line_steps(shards)]
-    found = [tiles(pack)]
-    halves = [
-        call(
+    def joined(blocks, after):
+        return call(
             join_kernel,
-            [VM] * 2 + [pl.BlockSpec(memory_space=pl.ANY)],
-            in_vmem((2,) + pack.shape[1:], jnp.float32),
-        )(near[at], near[at + 1], found[0][-1])
-        for at in range(0, len(near), 2)
-    ]
-    far = [swapped(half, 1) for half in halves]
-    found += [tiles(*near[1:]), tiles(far[0])]
+            [VM] * len(blocks) + [pl.BlockSpec(memory_space=pl.ANY)],
+            in_vmem((len(blocks),) + pack.shape[1:], jnp.float32),
+        )(*blocks, after)
+
+    steps = line_steps(shards)
+    there = [swapped(pack, step) for step in reversed(steps)][::-1]
+    first = joined([pack, there[0]], norm)
+    found = [tiles(pack, after=first)]
+    far = [swapped(joined([block], found[0][-1]), 1) for block in reversed(there[1:])][::-1]
+    far = [swapped(first, 1)] + far
+    found.append(tiles(*there))
+    for some in far[:-1]:
+        found.append(tiles(some, after=found[-1][-1]))
     groups = len(found) + 1
 
     def log_sums(last):
@@ -372,10 +375,10 @@
         )(*exps, *tall, wide_feat, peaks, mask, own, other, mass, norm, *given)
 
     between = [(0, 1), (1, 0)]
-    last_one = tiles(far[1], core=1)
+    last_one = tiles(far[-1], core=1, after=found[-1][-1])
     peaks_one, own_one = log_sums(last_one)
     other_zero = lax.ppermute(own_one, "tgt", between)
-    last_zero = tiles(far[1], core=0, after=own_one)
+    last_zero = tiles(far[-1], core=0, after=own_one)
     peaks_zero, own_zero = log_sums(last_zero)
     other_one = lax.ppermute(own_zero, "tgt", between)
     given = columns_of(0, last_zero, peaks_zero, own_zero, other_zero, [])

time: 55.8 us -> 56.8 us (1.018)
    ppermute x5 -> x6, starting transfers between devices: 8.78 us -> 9.26 us  [swapped(): return lax.ppermute(array, 'src', [(i, i ^ step) for i in range(shards)])]
    pallas_call x5 -> x6, Pallas kernels: 3.91 us -> 4.19 us  [tiles(): call(functools.partial(tile_kernel, len(packs), core), [VM] * (len(packs)...]
  transfers between devices with their start and end apart: 7 -> 8, of which waited for: 3 -> 3; matrix products, arithmetic and copies ran while one was open for 0% -> 0% of each run, Pallas kernels for 59% -> 59%
where the time goes in v12:
time: 56.8 us; the launch traced here: 56.6 us
  Pallas kernels  34.6 us (61%)
  blocking collectives  10.4 us (18%)
  starting transfers between devices  9.41 us (17%)
  waiting for transfers between devices  1.39 us (2%)
  between operations  0.75 us (1%)
    pallas_call x2, Pallas kernels, columns_of(): call(functools.partial(column_kernel, groups, core), [VM] * (2 * groups +...  27.6 us
    all_to_all x1, blocking collectives, dense_device(): arrived = lax.all_to_all(columns, 'src', 0, 0)  10.4 us
    ppermute x6, starting transfers between devices, swapped(): return lax.ppermute(array, 'src', [(i, i ^ step) for i in range(shards)])  9.26 us
    pallas_call x6, Pallas kernels, tiles(): call(functools.partial(tile_kernel, len(packs), core), [VM] * (len(packs)...  4.19 us
    pallas_call x2, Pallas kernels, reading(): call(kernel, [pl.BlockSpec(memory_space=pltpu.HBM)] * len(args), out_shap...  2.18 us
  transfers between devices with their start and end apart: 8, of which 3 were waited for; matrix products, arithmetic and copies ran while one was open for 0% of the time, Pallas kernels for 59%

profile of v12, /device:TPU:0, one launch (start us, length us, event | category | flops | bytes accessed | tf_op | source)
XLA Modules:
  0.0 56.6 jit_solution(15727852431133999756)
XLA Ops:
  0.6 0.8 %shard_map.86 = (f32[1,65,1,128]{3,2,1,0:T(1,128)S(1)}, f32[1,128]{1,0:T(1,128)S(1)}) custom-call(f32[1,64,128]{2,1,0:T(8,128)} %refs_0_.2, f32[1,128]{1,0:T(1,128)} %refs_1_.1, f32[1,128]{1,0:T(1,128)} %refs_2_.1), custom_call_target="tpu_custom_call" | custom-call | tf_op jit(solution)/shard_map/pallas_call | solution.py:294
  1.5 4.1 %collective-permute-start = (f32[1,65,1,128]{3,2,1,0:T(1,128)S(1)}, f32[1,65,1,128]{3,2,1,0:T(1,128)S(1)}, u32[]{:S(2)}, u32[]{:S(2)}) collective-permute-start(f32[1,65,1,128]{3,2,1,0:T(1,128)S(1)} %get-tuple-element.42.refs_0_), channel_id=1, source_target_pairs={{0,8},{2,10},{4,12},{6,14},{8,0},{10,2},{12,4},{14,6},{1,9},{3,11}... | collective-permute-start | bytes 99848 | tf_op jit(solution)/shard_map/ppermute | solution.py:339
  5.6 1.3 %collective-permute-start.1 = (f32[1,65,1,128]{3,2,1,0:T(1,128)S(1)}, f32[1,65,1,128]{3,2,1,0:T(1,128)S(1)}, u32[]{:S(2)}, u32[]{:S(2)}) collective-permute-start(f32[1,65,1,128]{3,2,1,0:T(1,128)S(1)} %get-tuple-element.42.refs_0_), channel_id=1, source_target_pairs={{0,12},{2,14},{4,8},{6,10},{8,4},{10,6},{12,0},{14,2},{1,13},{3,15... | collective-permute-start | bytes 99848 | tf_op jit(solution)/shard_map/ppermute | solution.py:339
  6.9 0.2 collective-permute-start.2
  7.1 1.4 %shard_map.87 = (bf16[8,512,256]{2,1,0:T(8,128)(2,1)S(1)}, f32[16,128]{1,0:T(8,128)S(1)}, f32[8,16,128]{2,1,0:T(8,128)S(1)}, f32[16,128]{1,0:T(8,128)S(1)}) custom-call(f32[16,128]{1,0:T(8,128)} %refs_0_.3, s32[8,16]{1,0:T(8,128)} %bitcast.4, s32[1,16]{1,0:T(1,128)} %bitcast.5, f32[16,64,128]{2,1,0:T(8,128)} %refs_3_.1), custom_call_target="tpu_custom_call" | custom-call | flops 1000000000 | bytes 524288 | tf_op jit(solution)/shard_map/pallas_call | solution.py:294
  8.5 0.0 collective-permute-done.refs_1_.refs_0_
  8.5 1.6 %collective-permute-start.3 = (f32[2,65,1,128]{3,2,1,0:T(1,128)S(1)}, f32[2,65,1,128]{3,2,1,0:T(1,128)S(1)}, u32[]{:S(2)}, u32[]{:S(2)}) collective-permute-start(f32[2,65,1,128]{3,2,1,0:T(1,128)S(1)} %shard_map.88.refs_2_), channel_id=1, source_target_pairs={{0,2},{2,0},{4,6},{6,4},{8,10},{10,8},{12,14},{14,12},{1,3},{3,1},... | collective-permute-start | bytes 199688 | tf_op jit(solution)/shard_map/ppermute | solution.py:339
  10.1 0.6 %shard_map.89 = (f32[8,128,256]{2,1,0:T(8,128)S(1)}, bf16[128,512]{1,0:T(8,128)(2,1)S(1)}, f32[1,16,128]{2,1,0:T(8,128)S(1)}, f32[1,16,128]{2,1,0:T(8,128)S(1)}) custom-call(f32[1,65,1,128]{3,2,1,0:T(1,128)S(1)} %get-tuple-element.42.refs_0_, bf16[8,512,256]{2,1,0:T(8,128)(2,1)S(1)} %get-tuple-element.43.refs_1_.refs_3_.refs_10_, ...), custom_call_target="tpu_custom_call" | custom-call | flops 268435456 | bytes 524288 | tf_op jit(solution)/shard_map/pallas_call | solution.py:326
  10.7 0.6 %collective-permute-done.1.refs_1_.refs_0_ = f32[1,65,1,128]{3,2,1,0:T(1,128)S(1)} collective-permute-done((f32[1,65,1,128]{3,2,1,0:T(1,128)S(1)}, f32[1,65,1,128]{3,2,1,0:T(1,128)S(1)}, u32[]{:S(2)}, u32[]{:S(2)}) %collective-permute-start.1) | collective-permute-done | bytes 33312 | tf_op jit(solution)/shard_map/ppermute | solution.py:339
  11.3 1.5 %collective-permute-start.4 = (f32[1,65,1,128]{3,2,1,0:T(1,128)S(1)}, f32[1,65,1,128]{3,2,1,0:T(1,128)S(1)}, u32[]{:S(2)}, u32[]{:S(2)}) collective-permute-start(f32[1,65,1,128]{3,2,1,0:T(1,128)S(1)} %shard_map.92), channel_id=1, source_target_pairs={{0,2},{2,0},{4,6},{6,4},{8,10},{10,8},{12,14},{14,12},{1,3},{3,1},... | collective-permute-start | bytes 99848 | tf_op jit(solution)/shard_map/ppermute | solution.py:339
  12.8 0.0 collective-permute-done.2.refs_2_.refs_0_
  12.8 0.5 collective-permute-start.5
  13.3 1.5 %shard_map.90 = (f32[8,384,256]{2,1,0:T(8,128)S(1)}, bf16[384,512]{1,0:T(8,128)(2,1)S(1)}, f32[3,16,128]{2,1,0:T(8,128)S(1)}, f32[3,16,128]{2,1,0:T(8,128)S(1)}) custom-call(f32[1,65,1,128]{3,2,1,0:T(1,128)S(1)} %collective-permute-done.refs_1_.refs_0_, f32[1,65,1,128]{3,2,1,0:T(1,128)S(1)} %collective-permute-done.1.refs_1_.refs_0_, ...), custom_call_target="tpu_custom_call" | custom-call | flops 805306368 | bytes 524288 | tf_op jit(solution)/shard_map/pallas_call | solution.py:326
  14.9 0.0 collective-permute-done.3.refs_0_
  14.9 0.9 %shard_map.91 = (f32[8,256,256]{2,1,0:T(8,128)S(1)}, bf16[256,512]{1,0:T(8,128)(2,1)S(1)}, f32[2,16,128]{2,1,0:T(8,128)S(1)}, f32[2,16,128]{2,1,0:T(8,128)S(1)}) custom-call(f32[2,65,1,128]{3,2,1,0:T(1,128)S(1)} %collective-permute-done.3.refs_0_, bf16[8,512,256]{2,1,0:T(8,128)(2,1)S(1)} %get-tuple-element.43.refs_1_.refs_3_.refs_10_, ...), custom_call_target="tpu_custom_call" | custom-call | flops 536870912 | bytes 524288 | tf_op jit(solution)/shard_map/pallas_call | solution.py:326
  15.8 0.0 collective-permute-done.4.refs_0_
  15.8 0.6 %shard_map.93 = (f32[8,128,256]{2,1,0:T(8,128)S(1)}, bf16[128,512]{1,0:T(8,128)(2,1)S(1)}, f32[1,16,128]{2,1,0:T(8,128)S(1)}, f32[1,16,128]{2,1,0:T(8,128)S(1)}) custom-call(f32[1,65,1,128]{3,2,1,0:T(1,128)S(1)} %collective-permute-done.4.refs_0_, bf16[8,512,256]{2,1,0:T(8,128)(2,1)S(1)} %get-tuple-element.43.refs_1_.refs_3_.refs_10_, ...), custom_call_target="tpu_custom_call" | custom-call | flops 268435456 | bytes 524288 | tf_op jit(solution)/shard_map/pallas_call | solution.py:326
  16.4 0.3 collective-permute-done.5.refs_0_
  16.7 0.1 collective-permute-start.7
  16.8 0.6 %shard_map.97 = (f32[8,128,256]{2,1,0:T(8,128)S(1)}, bf16[128,512]{1,0:T(8,128)(2,1)S(1)}, f32[1,16,128]{2,1,0:T(8,128)S(1)}, f32[1,16,128]{2,1,0:T(8,128)S(1)}) custom-call(f32[1,65,1,128]{3,2,1,0:T(1,128)S(1)} %collective-permute-done.5.refs_0_, bf16[8,512,256]{2,1,0:T(8,128)(2,1)S(1)} %get-tuple-element.43.refs_1_.refs_3_.refs_10_, ...), custom_call_target="tpu_custom_call" | custom-call | flops 268435456 | bytes 524288 | tf_op jit(solution)/shard_map/pallas_call | solution.py:326
  17.5 0.1 collective-permute-start.6
  17.5 0.4 collective-permute-done.7.refs_14_
  18.0 27.5 %shard_map.99 = (f32[16,128]{1,0:T(8,128)S(1)}, f32[8,1,128]{2,1,0:T(1,128)S(1)}) custom-call(f32[8,128,256]{2,1,0:T(8,128)S(1)} %get-tuple-element.45.refs_0_, f32[8,384,256]{2,1,0:T(8,128)S(1)} %get-tuple-element.46.refs_1_, f32[8,256,256]{2,1,0:T(8,128)S(1)} %get-tuple-element.48.refs_2_, f32[8,128,256]{2,1,0:T(8,128)S(1)} %get-tuple-element.51.refs_3_, ...), custom_call_target="tpu_custom_call" | custom-call | flops 1000000000 | bytes 524288 | tf_op jit(solution)/shard_map/pallas_call | solution.py:369
  45.5 0.0 collective-permute-done.6.refs_14_
  45.6 10.4 %all_to_all.5.values_ref = f32[8,1,128]{2,1,0:T(1,128)S(1)} all-to-all(f32[8,1,128]{2,1,0:T(1,128)S(1)} %get-tuple-element.77), channel_id=1, replica_groups=mesh['grp'=2,'src'=8,'tgt'=2] {'src'}, dimensions={0} | all-to-all | bytes 8192 | tf_op jit(solution)/shard_map/all_to_all | solution.py:386
  56.0 0.6 %shard_map.101 = (f32[1,128]{1,0:T(1,128)}, f32[16,128]{1,0:T(8,128)}) custom-call(f32[8,1,128]{2,1,0:T(1,128)S(1)} %all_to_all.5.values_ref, f32[1,128]{1,0:T(1,128)S(1)} %get-tuple-element.78.weight_ref, f32[16,128]{1,0:T(8,128)S(1)} %get-tuple-element.79.poten_ref), custom_call_target="tpu_custom_call" | custom-call | tf_op jit(solution)/shard_map/pallas_call | solution.py:388
  (7 shorter events, 0.1 us)
Async XLA Ops:
  1.5 7.1 %collective-permute-start = (f32[1,65,1,128]{3,2,1,0:T(1,128)S(1)}, f32[1,65,1,128]{3,2,1,0:T(1,128)S(1)}, u32[]{:S(2)}, u32[]{:S(2)}) collective-permute-start(f32[1,65,1,128]{3,2,1,0:T(1,128)S(1)} %get-tuple-element.42.refs_0_), channel_id=1, source_target_pairs={{0,8},{2,10},{4,12},{6,14},{8,0},{10,2},{12,4},{14,6},{1,9},{3,11}... | collective-permute-start | bytes 99848 | tf_op jit(solution)/shard_map/ppermute | solution.py:339
  5.6 5.7 %collective-permute-start.1 = (f32[1,65,1,128]{3,2,1,0:T(1,128)S(1)}, f32[1,65,1,128]{3,2,1,0:T(1,128)S(1)}, u32[]{:S(2)}, u32[]{:S(2)}) collective-permute-start(f32[1,65,1,128]{3,2,1,0:T(1,128)S(1)} %get-tuple-element.42.refs_0_), channel_id=1, source_target_pairs={{0,12},{2,14},{4,8},{6,10},{8,4},{10,6},{12,0},{14,2},{1,13},{3,15... | collective-permute-start | bytes 99848 | tf_op jit(solution)/shard_map/ppermute | solution.py:339
  6.9 5.9 %collective-permute-start.2 = (f32[1,65,1,128]{3,2,1,0:T(1,128)S(1)}, f32[1,65,1,128]{3,2,1,0:T(1,128)S(1)}, u32[]{:S(2)}, u32[]{:S(2)}) collective-permute-start(f32[1,65,1,128]{3,2,1,0:T(1,128)S(1)} %get-tuple-element.42.refs_0_), channel_id=1, source_target_pairs={{0,4},{2,6},{4,0},{6,2},{8,12},{10,14},{12,8},{14,10},{1,5},{3,7},... | collective-permute-start | bytes 99848 | tf_op jit(solution)/shard_map/ppermute | solution.py:339
  8.5 6.3 %collective-permute-start.3 = (f32[2,65,1,128]{3,2,1,0:T(1,128)S(1)}, f32[2,65,1,128]{3,2,1,0:T(1,128)S(1)}, u32[]{:S(2)}, u32[]{:S(2)}) collective-permute-start(f32[2,65,1,128]{3,2,1,0:T(1,128)S(1)} %shard_map.88.refs_2_), channel_id=1, source_target_pairs={{0,2},{2,0},{4,6},{6,4},{8,10},{10,8},{12,14},{14,12},{1,3},{3,1},... | collective-permute-start | bytes 199688 | tf_op jit(solution)/shard_map/ppermute | solution.py:339
  11.3 4.5 %collective-permute-start.4 = (f32[1,65,1,128]{3,2,1,0:T(1,128)S(1)}, f32[1,65,1,128]{3,2,1,0:T(1,128)S(1)}, u32[]{:S(2)}, u32[]{:S(2)}) collective-permute-start(f32[1,65,1,128]{3,2,1,0:T(1,128)S(1)} %shard_map.92), channel_id=1, source_target_pairs={{0,2},{2,0},{4,6},{6,4},{8,10},{10,8},{12,14},{14,12},{1,3},{3,1},... | collective-permute-start | bytes 99848 | tf_op jit(solution)/shard_map/ppermute | solution.py:339
  12.8 3.9 %collective-permute-start.5 = (f32[1,65,1,128]{3,2,1,0:T(1,128)S(1)}, f32[1,65,1,128]{3,2,1,0:T(1,128)S(1)}, u32[]{:S(2)}, u32[]{:S(2)}) collective-permute-start(f32[1,65,1,128]{3,2,1,0:T(1,128)S(1)} %shard_map.94), channel_id=1, source_target_pairs={{0,2},{2,0},{4,6},{6,4},{8,10},{10,8},{12,14},{14,12},{1,3},{3,1},... | collective-permute-start | bytes 99848 | tf_op jit(solution)/shard_map/ppermute | solution.py:339
  16.7 1.2 %collective-permute-start.7 = (f32[16,128]{1,0:T(8,128)S(1)}, f32[16,128]{1,0:T(8,128)S(1)}, u32[]{:S(2)}, u32[]{:S(2)}) collective-permute-start(f32[16,128]{1,0:T(8,128)S(1)} %get-tuple-element.67.refs_2_.refs_13_), channel_id=1, source_target_pairs={{0,1},{1,0},{2,3},{3,2},{4,5},{5,4},{6,7},{7,6},{8,9},{9,8},{10,11... | collective-permute-start | bytes 24584 | tf_op jit(solution)/shard_map/ppermute | solution.py:380
  17.5 28.1 %collective-permute-start.6 = (f32[16,128]{1,0:T(8,128)S(1)}, f32[16,128]{1,0:T(8,128)S(1)}, u32[]{:S(2)}, u32[]{:S(2)}) collective-permute-start(f32[16,128]{1,0:T(8,128)S(1)} %get-tuple-element.70.refs_13_), channel_id=1, source_target_pairs={{0,1},{1,0},{2,3},{3,2},{4,5},{5,4},{6,7},{7,6},{8,9},{9,8},{10,11... | collective-permute-start | bytes 24584 | tf_op jit(solution)/shard_map/ppermute | solution.py:383

commit v13 on v11

--- a/solution.py
+++ b/solution.py
@@ -220,7 +220,7 @@
         for index in range(ref.shape[0] // cells)
     ]
     used = [jnp.max(mask_ref[place], axis=0, keepdims=True) > 0.5 * very_low for place in range(shards)]
-    owners = blocks_at(shards)
+    ranks = [shards - 1 - block for block in blocks_at(shards)]
     sums = []
     for place, (group, rows) in enumerate(spots):
         acc = jnp.zeros((cells, cells), jnp.float32)
@@ -232,7 +232,7 @@
     worst = jnp.min(whole_sums)
     logs = jnp.log2(whole_sums)
     for place in range(shards):
-        sums_ref[owners[place]] = jnp.where(used[place], logs[place : place + 1, :], very_low)
+        sums_ref[ranks[place]] = jnp.where(used[place], logs[place : place + 1, :], very_low)
 
     @pl.when(worst < least_sum)
     def _():
@@ -256,7 +256,7 @@
 
             sums = lax.fori_loop(0, pairs, add_up, jnp.zeros((cells, cells), jnp.float32))
             logs = across(peak) + jnp.log2(across(jnp.sum(sums, axis=1, keepdims=True)))
-            sums_ref[owners[place]] = jnp.where(used[place], logs, very_low)
+            sums_ref[ranks[place]] = jnp.where(used[place], logs, very_low)
 
 
 def merge_kernel(values_ref, weight_ref, poten_ref, out_ref, poten_out_ref):
@@ -380,7 +380,7 @@
     other_one = lax.ppermute(own_zero, "tgt", between)
     given = columns_of(0, last_zero, peaks_zero, own_zero, other_zero, [])
     potential_src, columns = columns_of(1, last_one, peaks_one, own_one, other_one, given)
-    arrived = lax.all_to_all(columns, "src", 0, 0)
+    arrived = lax.all_to_all(columns, "src", 0, 0, axis_index_groups=[list(range(shards))[::-1]])
     outs = [f32(1, cells), f32(rows, cells)]
     potential_new, potential_src = call(merge_kernel, [VM] * 3, outs)(arrived, weight, potential_src)
     return potential_src, potential_new

time: 55.8 us -> 53.5 us (0.959)
  blocking collectives: 10.4 us -> 8.15 us
    all_to_all x1, blocking collectives: 10.4 us -> 8.15 us  [dense_device(): lax.all_to_all(columns, 'src', 0, 0, axis_index_groups=[list(range(shards...]
  transfers between devices with their start and end apart: 7 -> 7, of which waited for: 3 -> 3; matrix products, arithmetic and copies ran while one was open for 0% -> 0% of each run, Pallas kernels for 59% -> 62%
where the time goes in v13:
time: 53.5 us; the launch traced here: 53.2 us
  Pallas kernels  34.3 us (64%)
  starting transfers between devices  8.92 us (17%)
  blocking collectives  8.15 us (15%)
  waiting for transfers between devices  1.1 us (2%)
  between operations  0.74 us (1%)
    pallas_call x2, Pallas kernels, columns_of(): call(functools.partial(column_kernel, groups, core), [VM] * (2 * groups +...  27.6 us
    ppermute x5, starting transfers between devices, swapped(): return lax.ppermute(array, 'src', [(i, i ^ step) for i in range(shards)])  8.78 us
    all_to_all x1, blocking collectives, dense_device(): lax.all_to_all(columns, 'src', 0, 0, axis_index_groups=[list(range(shards...  8.15 us
    pallas_call x5, Pallas kernels, tiles(): call(functools.partial(tile_kernel, len(packs), core), [VM] * (len(packs)...  3.91 us
    pallas_call x2, Pallas kernels, reading(): call(kernel, [pl.BlockSpec(memory_space=pltpu.HBM)] * len(args), out_shap...  2.18 us
  transfers between devices with their start and end apart: 7, of which 3 were waited for; matrix products, arithmetic and copies ran while one was open for 0% of the time, Pallas kernels for 62%

profile of v13, /device:TPU:0, one launch (start us, length us, event | category | flops | bytes accessed | tf_op | source)
XLA Modules:
  0.0 53.2 jit_solution(11082230761715134366)
XLA Ops:
  0.6 0.8 %shard_map.86 = (f32[1,65,1,128]{3,2,1,0:T(1,128)S(1)}, f32[1,128]{1,0:T(1,128)S(1)}) custom-call(f32[1,64,128]{2,1,0:T(8,128)} %refs_0_.2, f32[1,128]{1,0:T(1,128)} %refs_1_.1, f32[1,128]{1,0:T(1,128)} %refs_2_.1), custom_call_target="tpu_custom_call" | custom-call | tf_op jit(solution)/shard_map/pallas_call | solution.py:294
  1.5 4.1 %collective-permute-start = (f32[1,65,1,128]{3,2,1,0:T(1,128)S(1)}, f32[1,65,1,128]{3,2,1,0:T(1,128)S(1)}, u32[]{:S(2)}, u32[]{:S(2)}) collective-permute-start(f32[1,65,1,128]{3,2,1,0:T(1,128)S(1)} %get-tuple-element.38.refs_0_), channel_id=1, source_target_pairs={{0,8},{2,10},{4,12},{6,14},{8,0},{10,2},{12,4},{14,6},{1,9},{3,11}... | collective-permute-start | bytes 99848 | tf_op jit(solution)/shard_map/ppermute | solution.py:339
  5.6 1.3 %collective-permute-start.1 = (f32[1,65,1,128]{3,2,1,0:T(1,128)S(1)}, f32[1,65,1,128]{3,2,1,0:T(1,128)S(1)}, u32[]{:S(2)}, u32[]{:S(2)}) collective-permute-start(f32[1,65,1,128]{3,2,1,0:T(1,128)S(1)} %get-tuple-element.38.refs_0_), channel_id=1, source_target_pairs={{0,12},{2,14},{4,8},{6,10},{8,4},{10,6},{12,0},{14,2},{1,13},{3,15... | collective-permute-start | bytes 99848 | tf_op jit(solution)/shard_map/ppermute | solution.py:339
  6.9 0.2 collective-permute-start.2
  7.1 1.4 %shard_map.87 = (bf16[8,512,256]{2,1,0:T(8,128)(2,1)S(1)}, f32[16,128]{1,0:T(8,128)S(1)}, f32[8,16,128]{2,1,0:T(8,128)S(1)}, f32[16,128]{1,0:T(8,128)S(1)}) custom-call(f32[16,128]{1,0:T(8,128)} %refs_0_.3, s32[8,16]{1,0:T(8,128)} %bitcast.4, s32[1,16]{1,0:T(1,128)} %bitcast.5, f32[16,64,128]{2,1,0:T(8,128)} %refs_3_.1), custom_call_target="tpu_custom_call" | custom-call | flops 1000000000 | bytes 524288 | tf_op jit(solution)/shard_map/pallas_call | solution.py:294
  8.5 0.6 %shard_map.88 = (f32[8,128,256]{2,1,0:T(8,128)S(1)}, bf16[128,512]{1,0:T(8,128)(2,1)S(1)}, f32[1,16,128]{2,1,0:T(8,128)S(1)}, f32[1,16,128]{2,1,0:T(8,128)S(1)}) custom-call(f32[1,65,1,128]{3,2,1,0:T(1,128)S(1)} %get-tuple-element.38.refs_0_, bf16[8,512,256]{2,1,0:T(8,128)(2,1)S(1)} %get-tuple-element.39.refs_1_.refs_3_.refs_8_), custom_call_target="tpu_custom_call" | custom-call | flops 268435456 | bytes 524288 | tf_op jit(solution)/shard_map/pallas_call | solution.py:326
  9.1 0.0 collective-permute-done.refs_0_.refs_1_
  9.1 1.5 %collective-permute-start.3 = (f32[2,65,1,128]{3,2,1,0:T(1,128)S(1)}, f32[2,65,1,128]{3,2,1,0:T(1,128)S(1)}, u32[]{:S(2)}, u32[]{:S(2)}) collective-permute-start(f32[2,65,1,128]{3,2,1,0:T(1,128)S(1)} %shard_map.90), channel_id=1, source_target_pairs={{0,2},{2,0},{4,6},{6,4},{8,10},{10,8},{12,14},{14,12},{1,3},{3,1},... | collective-permute-start | bytes 199688 | tf_op jit(solution)/shard_map/ppermute | solution.py:339
  10.7 0.6 %collective-permute-done.1.refs_1_.refs_0_ = f32[1,65,1,128]{3,2,1,0:T(1,128)S(1)} collective-permute-done((f32[1,65,1,128]{3,2,1,0:T(1,128)S(1)}, f32[1,65,1,128]{3,2,1,0:T(1,128)S(1)}, u32[]{:S(2)}, u32[]{:S(2)}) %collective-permute-start.1) | collective-permute-done | bytes 33312 | tf_op jit(solution)/shard_map/ppermute | solution.py:339
  11.3 0.0 collective-permute-done.2.refs_2_.refs_1_
  11.3 1.6 %collective-permute-start.4 = (f32[2,65,1,128]{3,2,1,0:T(1,128)S(1)}, f32[2,65,1,128]{3,2,1,0:T(1,128)S(1)}, u32[]{:S(2)}, u32[]{:S(2)}) collective-permute-start(f32[2,65,1,128]{3,2,1,0:T(1,128)S(1)} %shard_map.92), channel_id=1, source_target_pairs={{0,2},{2,0},{4,6},{6,4},{8,10},{10,8},{12,14},{14,12},{1,3},{3,1},... | collective-permute-start | bytes 199688 | tf_op jit(solution)/shard_map/ppermute | solution.py:339
  12.8 1.5 %shard_map.89 = (f32[8,384,256]{2,1,0:T(8,128)S(1)}, bf16[384,512]{1,0:T(8,128)(2,1)S(1)}, f32[3,16,128]{2,1,0:T(8,128)S(1)}, f32[3,16,128]{2,1,0:T(8,128)S(1)}) custom-call(f32[1,65,1,128]{3,2,1,0:T(1,128)S(1)} %collective-permute-done.refs_0_.refs_1_, f32[1,65,1,128]{3,2,1,0:T(1,128)S(1)} %collective-permute-done.1.refs_1_.refs_0_, ...), custom_call_target="tpu_custom_call" | custom-call | flops 805306368 | bytes 524288 | tf_op jit(solution)/shard_map/pallas_call | solution.py:326
  14.4 0.0 collective-permute-done.3.refs_0_
  14.4 0.9 %shard_map.91 = (f32[8,256,256]{2,1,0:T(8,128)S(1)}, bf16[256,512]{1,0:T(8,128)(2,1)S(1)}, f32[2,16,128]{2,1,0:T(8,128)S(1)}, f32[2,16,128]{2,1,0:T(8,128)S(1)}) custom-call(f32[2,65,1,128]{3,2,1,0:T(1,128)S(1)} %collective-permute-done.3.refs_0_, bf16[8,512,256]{2,1,0:T(8,128)(2,1)S(1)} %get-tuple-element.39.refs_1_.refs_3_.refs_8_), custom_call_target="tpu_custom_call" | custom-call | flops 536870912 | bytes 524288 | tf_op jit(solution)/shard_map/pallas_call | solution.py:326
  15.3 0.3 collective-permute-done.4.refs_0_
  15.7 0.1 collective-permute-start.6
  15.7 0.9 %shard_map.95 = (f32[8,256,256]{2,1,0:T(8,128)S(1)}, bf16[256,512]{1,0:T(8,128)(2,1)S(1)}, f32[2,16,128]{2,1,0:T(8,128)S(1)}, f32[2,16,128]{2,1,0:T(8,128)S(1)}) custom-call(f32[2,65,1,128]{3,2,1,0:T(1,128)S(1)} %collective-permute-done.4.refs_0_, bf16[8,512,256]{2,1,0:T(8,128)(2,1)S(1)} %get-tuple-element.39.refs_1_.refs_3_.refs_8_, ...), custom_call_target="tpu_custom_call" | custom-call | flops 536870912 | bytes 524288 | tf_op jit(solution)/shard_map/pallas_call | solution.py:326
  16.7 0.1 collective-permute-start.5
  16.8 0.1 collective-permute-done.6.refs_12_
  16.9 27.5 %shard_map.97 = (f32[16,128]{1,0:T(8,128)S(1)}, f32[8,1,128]{2,1,0:T(1,128)S(1)}) custom-call(f32[8,128,256]{2,1,0:T(8,128)S(1)} %get-tuple-element.40.refs_0_, f32[8,384,256]{2,1,0:T(8,128)S(1)} %get-tuple-element.41.refs_1_, f32[8,256,256]{2,1,0:T(8,128)S(1)} %get-tuple-element.43.refs_2_, f32[8,256,256]{2,1,0:T(8,128)S(1)} %get-tuple-element.64.refs_3_, ...), custom_call_target="tpu_custom_call" | custom-call | flops 1000000000 | bytes 524288 | tf_op jit(solution)/shard_map/pallas_call | solution.py:366
  44.4 0.0 collective-permute-done.5.refs_12_
  44.5 8.2 %all_to_all.5.values_ref = f32[8,1,128]{2,1,0:T(1,128)S(1)} all-to-all(f32[8,1,128]{2,1,0:T(1,128)S(1)} %get-tuple-element.69), channel_id=1, replica_groups={{14,12,10,8,6,4,2,0},{15,13,11,9,7,5,3,1},{30,28,26,24,22,20,18,16},{31..., dimensions={0} | all-to-all | bytes 8192 | tf_op jit(solution)/shard_map/all_to_all | solution.py:383
  52.6 0.6 %shard_map.99 = (f32[1,128]{1,0:T(1,128)}, f32[16,128]{1,0:T(8,128)}) custom-call(f32[8,1,128]{2,1,0:T(1,128)S(1)} %all_to_all.5.values_ref, f32[1,128]{1,0:T(1,128)S(1)} %get-tuple-element.70.weight_ref, f32[16,128]{1,0:T(8,128)S(1)} %get-tuple-element.71.poten_ref), custom_call_target="tpu_custom_call" | custom-call | tf_op jit(solution)/shard_map/pallas_call | solution.py:385
  (6 shorter events, 0.1 us)
Async XLA Ops:
  1.5 7.6 %collective-permute-start = (f32[1,65,1,128]{3,2,1,0:T(1,128)S(1)}, f32[1,65,1,128]{3,2,1,0:T(1,128)S(1)}, u32[]{:S(2)}, u32[]{:S(2)}) collective-permute-start(f32[1,65,1,128]{3,2,1,0:T(1,128)S(1)} %get-tuple-element.38.refs_0_), channel_id=1, source_target_pairs={{0,8},{2,10},{4,12},{6,14},{8,0},{10,2},{12,4},{14,6},{1,9},{3,11}... | collective-permute-start | bytes 99848 | tf_op jit(solution)/shard_map/ppermute | solution.py:339
  5.6 5.7 %collective-permute-start.1 = (f32[1,65,1,128]{3,2,1,0:T(1,128)S(1)}, f32[1,65,1,128]{3,2,1,0:T(1,128)S(1)}, u32[]{:S(2)}, u32[]{:S(2)}) collective-permute-start(f32[1,65,1,128]{3,2,1,0:T(1,128)S(1)} %get-tuple-element.38.refs_0_), channel_id=1, source_target_pairs={{0,12},{2,14},{4,8},{6,10},{8,4},{10,6},{12,0},{14,2},{1,13},{3,15... | collective-permute-start | bytes 99848 | tf_op jit(solution)/shard_map/ppermute | solution.py:339
  6.9 4.4 %collective-permute-start.2 = (f32[1,65,1,128]{3,2,1,0:T(1,128)S(1)}, f32[1,65,1,128]{3,2,1,0:T(1,128)S(1)}, u32[]{:S(2)}, u32[]{:S(2)}) collective-permute-start(f32[1,65,1,128]{3,2,1,0:T(1,128)S(1)} %get-tuple-element.38.refs_0_), channel_id=1, source_target_pairs={{0,4},{2,6},{4,0},{6,2},{8,12},{10,14},{12,8},{14,10},{1,5},{3,7},... | collective-permute-start | bytes 99848 | tf_op jit(solution)/shard_map/ppermute | solution.py:339
  9.1 5.3 %collective-permute-start.3 = (f32[2,65,1,128]{3,2,1,0:T(1,128)S(1)}, f32[2,65,1,128]{3,2,1,0:T(1,128)S(1)}, u32[]{:S(2)}, u32[]{:S(2)}) collective-permute-start(f32[2,65,1,128]{3,2,1,0:T(1,128)S(1)} %shard_map.90), channel_id=1, source_target_pairs={{0,2},{2,0},{4,6},{6,4},{8,10},{10,8},{12,14},{14,12},{1,3},{3,1},... | collective-permute-start | bytes 199688 | tf_op jit(solution)/shard_map/ppermute | solution.py:339
  11.3 4.3 %collective-permute-start.4 = (f32[2,65,1,128]{3,2,1,0:T(1,128)S(1)}, f32[2,65,1,128]{3,2,1,0:T(1,128)S(1)}, u32[]{:S(2)}, u32[]{:S(2)}) collective-permute-start(f32[2,65,1,128]{3,2,1,0:T(1,128)S(1)} %shard_map.92), channel_id=1, source_target_pairs={{0,2},{2,0},{4,6},{6,4},{8,10},{10,8},{12,14},{14,12},{1,3},{3,1},... | collective-permute-start | bytes 199688 | tf_op jit(solution)/shard_map/ppermute | solution.py:339
  15.7 1.2 %collective-permute-start.6 = (f32[16,128]{1,0:T(8,128)S(1)}, f32[16,128]{1,0:T(8,128)S(1)}, u32[]{:S(2)}, u32[]{:S(2)}) collective-permute-start(f32[16,128]{1,0:T(8,128)S(1)} %get-tuple-element.58.refs_2_.refs_11_), channel_id=1, source_target_pairs={{0,1},{1,0},{2,3},{3,2},{4,5},{5,4},{6,7},{7,6},{8,9},{9,8},{10,11... | collective-permute-start | bytes 24584 | tf_op jit(solution)/shard_map/ppermute | solution.py:377
  16.7 27.8 %collective-permute-start.5 = (f32[16,128]{1,0:T(8,128)S(1)}, f32[16,128]{1,0:T(8,128)S(1)}, u32[]{:S(2)}, u32[]{:S(2)}) collective-permute-start(f32[16,128]{1,0:T(8,128)S(1)} %get-tuple-element.61.refs_11_), channel_id=1, source_target_pairs={{0,1},{1,0},{2,3},{3,2},{4,5},{5,4},{6,7},{7,6},{8,9},{9,8},{10,11... | collective-permute-start | bytes 24584 | tf_op jit(solution)/shard_map/ppermute | solution.py:380

commit v14 on v13

--- a/solution.py
+++ b/solution.py
@@ -13,6 +13,8 @@
 log2e = 1.0 / math.log(2.0)
 ln2 = math.log(2.0)
 least_sum = 1e-28
+
+room = 2**24
 
 VM = pl.BlockSpec(memory_space=pltpu.VMEM)
 PARAMS = pltpu.CompilerParams(vmem_limit_bytes=40 * 2**20)
@@ -338,19 +340,23 @@
     def swapped(array, step):
         return lax.ppermute(array, "src", [(i, i ^ step) for i in range(shards)])
 
-    there = {step: swapped(pack, step) for step in reversed(line_steps(shards))}
-    near = [pack] + [there[step] for step in line_steps(shards)]
-    found = [tiles(pack)]
-    halves = [
-        call(
+    def joined(first, second, after):
+        return call(
             join_kernel,
             [VM] * 2 + [pl.BlockSpec(memory_space=pl.ANY)],
             in_vmem((2,) + pack.shape[1:], jnp.float32),
-        )(near[at], near[at + 1], found[0][-1])
-        for at in range(0, len(near), 2)
-    ]
+        )(first, second, after)
+
+    steps = line_steps(shards)
+    there = [swapped(pack, step) for step in reversed(steps)][::-1]
+    near = [pack] + there
+    halves = [joined(near[0], near[1], norm)]
+    found = [tiles(pack, after=halves[0])]
+    halves += [joined(near[at], near[at + 1], found[0][-1]) for at in range(2, shards // 2, 2)]
     far = [swapped(half, 1) for half in halves]
-    found += [tiles(*near[1:]), tiles(far[0])]
+    found.append(tiles(*there))
+    for half in far[:-1]:
+        found.append(tiles(half, after=found[-1][-1]))
     groups = len(found) + 1
 
     def log_sums(last):
@@ -372,10 +378,10 @@
         )(*exps, *tall, wide_feat, peaks, mask, own, other, mass, norm, *given)
 
     between = [(0, 1), (1, 0)]
-    last_one = tiles(far[1], core=1)
+    last_one = tiles(far[-1], core=1, after=found[-1][-1])
     peaks_one, own_one = log_sums(last_one)
     other_zero = lax.ppermute(own_one, "tgt", between)
-    last_zero = tiles(far[1], core=0, after=own_one)
+    last_zero = tiles(far[-1], core=0, after=own_one)
     peaks_zero, own_zero = log_sums(last_zero)
     other_one = lax.ppermute(own_zero, "tgt", between)
     given = columns_of(0, last_zero, peaks_zero, own_zero, other_zero, [])
@@ -512,8 +518,9 @@
 def per_device(source_feat, target_feat, *others):
     shards = lax.axis_size("src")
     rows, depth, cells = source_feat.shape
-    few = shards == 8 and target_feat.shape[0] == 1 and lax.axis_size("tgt") == 2
-    if few and rows % 8 == 0 and cells == 128 and depth == 64:
+    paired = shards >= 4 and shards & (shards - 1) == 0 and lax.axis_size("tgt") == 2
+    shaped = target_feat.shape[0] == 1 and rows % 2 == 0 and cells == 2 * depth and cells % 128 == 0
+    if paired and shaped and 4 * rows * cells * shards * cells <= room:
         return dense_device(source_feat, target_feat, *others)
     return general_device(source_feat, target_feat, *others)
 

time: 53.5 us -> 53.5 us (level)
  no operation moved by 1% of the time
where the time goes in v14:
time: 53.5 us; the launch traced here: 53.2 us
  Pallas kernels  34.3 us (64%)
  starting transfers between devices  8.94 us (17%)
  blocking collectives  8.14 us (15%)
  waiting for transfers between devices  1.1 us (2%)
  between operations  0.74 us (1%)
    pallas_call x2, Pallas kernels, columns_of(): call(functools.partial(column_kernel, groups, core), [VM] * (2 * groups +...  27.6 us
    ppermute x5, starting transfers between devices, swapped(): return lax.ppermute(array, 'src', [(i, i ^ step) for i in range(shards)])  8.79 us
    all_to_all x1, blocking collectives, dense_device(): lax.all_to_all(columns, 'src', 0, 0, axis_index_groups=[list(range(shards...  8.14 us
    pallas_call x5, Pallas kernels, tiles(): call(functools.partial(tile_kernel, len(packs), core), [VM] * (len(packs)...  3.9 us
    pallas_call x2, Pallas kernels, reading(): call(kernel, [pl.BlockSpec(memory_space=pltpu.HBM)] * len(args), out_shap...  2.18 us
  transfers between devices with their start and end apart: 7, of which 3 were waited for; matrix products, arithmetic and copies ran while one was open for 0% of the time, Pallas kernels for 62%

profile of v14, /device:TPU:0, one launch (start us, length us, event | category | flops | bytes accessed | tf_op | source)
XLA Modules:
  0.0 53.2 jit_solution(3171300471236263200)
XLA Ops:
  0.6 0.8 %shard_map.86 = (f32[1,65,1,128]{3,2,1,0:T(1,128)S(1)}, f32[1,128]{1,0:T(1,128)S(1)}) custom-call(f32[1,64,128]{2,1,0:T(8,128)} %refs_0_.2, f32[1,128]{1,0:T(1,128)} %refs_1_.1, f32[1,128]{1,0:T(1,128)} %refs_2_.1), custom_call_target="tpu_custom_call" | custom-call | tf_op jit(solution)/shard_map/pallas_call | solution.py:296
  1.5 4.1 %collective-permute-start = (f32[1,65,1,128]{3,2,1,0:T(1,128)S(1)}, f32[1,65,1,128]{3,2,1,0:T(1,128)S(1)}, u32[]{:S(2)}, u32[]{:S(2)}) collective-permute-start(f32[1,65,1,128]{3,2,1,0:T(1,128)S(1)} %get-tuple-element.38.refs_0_), channel_id=1, source_target_pairs={{0,8},{2,10},{4,12},{6,14},{8,0},{10,2},{12,4},{14,6},{1,9},{3,11}... | collective-permute-start | bytes 99848 | tf_op jit(solution)/shard_map/ppermute | solution.py:341
  5.6 1.3 %collective-permute-start.1 = (f32[1,65,1,128]{3,2,1,0:T(1,128)S(1)}, f32[1,65,1,128]{3,2,1,0:T(1,128)S(1)}, u32[]{:S(2)}, u32[]{:S(2)}) collective-permute-start(f32[1,65,1,128]{3,2,1,0:T(1,128)S(1)} %get-tuple-element.38.refs_0_), channel_id=1, source_target_pairs={{0,12},{2,14},{4,8},{6,10},{8,4},{10,6},{12,0},{14,2},{1,13},{3,15... | collective-permute-start | bytes 99848 | tf_op jit(solution)/shard_map/ppermute | solution.py:341
  6.9 0.2 collective-permute-start.2
  7.1 1.4 %shard_map.87 = (bf16[8,512,256]{2,1,0:T(8,128)(2,1)S(1)}, f32[16,128]{1,0:T(8,128)S(1)}, f32[8,16,128]{2,1,0:T(8,128)S(1)}, f32[16,128]{1,0:T(8,128)S(1)}) custom-call(f32[16,128]{1,0:T(8,128)} %refs_0_.3, s32[8,16]{1,0:T(8,128)} %bitcast.4, s32[1,16]{1,0:T(1,128)} %bitcast.5, f32[16,64,128]{2,1,0:T(8,128)} %refs_3_.1), custom_call_target="tpu_custom_call" | custom-call | flops 1000000000 | bytes 524288 | tf_op jit(solution)/shard_map/pallas_call | solution.py:296
  8.5 0.0 collective-permute-done.refs_1_.refs_0_
  8.5 1.6 %collective-permute-start.3 = (f32[2,65,1,128]{3,2,1,0:T(1,128)S(1)}, f32[2,65,1,128]{3,2,1,0:T(1,128)S(1)}, u32[]{:S(2)}, u32[]{:S(2)}) collective-permute-start(f32[2,65,1,128]{3,2,1,0:T(1,128)S(1)} %shard_map.88.refs_2_), channel_id=1, source_target_pairs={{0,2},{2,0},{4,6},{6,4},{8,10},{10,8},{12,14},{14,12},{1,3},{3,1},... | collective-permute-start | bytes 199688 | tf_op jit(solution)/shard_map/ppermute | solution.py:341
  10.1 0.6 %shard_map.89 = (f32[8,128,256]{2,1,0:T(8,128)S(1)}, bf16[128,512]{1,0:T(8,128)(2,1)S(1)}, f32[1,16,128]{2,1,0:T(8,128)S(1)}, f32[1,16,128]{2,1,0:T(8,128)S(1)}) custom-call(f32[1,65,1,128]{3,2,1,0:T(1,128)S(1)} %get-tuple-element.38.refs_0_, bf16[8,512,256]{2,1,0:T(8,128)(2,1)S(1)} %get-tuple-element.39.refs_1_.refs_3_.refs_8_, ...), custom_call_target="tpu_custom_call" | custom-call | flops 268435456 | bytes 524288 | tf_op jit(solution)/shard_map/pallas_call | solution.py:328
  10.7 0.6 %collective-permute-done.1.refs_1_.refs_0_ = f32[1,65,1,128]{3,2,1,0:T(1,128)S(1)} collective-permute-done((f32[1,65,1,128]{3,2,1,0:T(1,128)S(1)}, f32[1,65,1,128]{3,2,1,0:T(1,128)S(1)}, u32[]{:S(2)}, u32[]{:S(2)}) %collective-permute-start.1) | collective-permute-done | bytes 33312 | tf_op jit(solution)/shard_map/ppermute | solution.py:341
  11.3 0.0 collective-permute-done.2.refs_2_.refs_1_
  11.3 1.6 %collective-permute-start.4 = (f32[2,65,1,128]{3,2,1,0:T(1,128)S(1)}, f32[2,65,1,128]{3,2,1,0:T(1,128)S(1)}, u32[]{:S(2)}, u32[]{:S(2)}) collective-permute-start(f32[2,65,1,128]{3,2,1,0:T(1,128)S(1)} %shard_map.92), channel_id=1, source_target_pairs={{0,2},{2,0},{4,6},{6,4},{8,10},{10,8},{12,14},{14,12},{1,3},{3,1},... | collective-permute-start | bytes 199688 | tf_op jit(solution)/shard_map/ppermute | solution.py:341
  12.8 1.5 %shard_map.90 = (f32[8,384,256]{2,1,0:T(8,128)S(1)}, bf16[384,512]{1,0:T(8,128)(2,1)S(1)}, f32[3,16,128]{2,1,0:T(8,128)S(1)}, f32[3,16,128]{2,1,0:T(8,128)S(1)}) custom-call(f32[1,65,1,128]{3,2,1,0:T(1,128)S(1)} %collective-permute-done.refs_1_.refs_0_, f32[1,65,1,128]{3,2,1,0:T(1,128)S(1)} %collective-permute-done.1.refs_1_.refs_0_, ...), custom_call_target="tpu_custom_call" | custom-call | flops 805306368 | bytes 524288 | tf_op jit(solution)/shard_map/pallas_call | solution.py:328
  14.4 0.0 collective-permute-done.3.refs_0_
  14.4 0.9 %shard_map.91 = (f32[8,256,256]{2,1,0:T(8,128)S(1)}, bf16[256,512]{1,0:T(8,128)(2,1)S(1)}, f32[2,16,128]{2,1,0:T(8,128)S(1)}, f32[2,16,128]{2,1,0:T(8,128)S(1)}) custom-call(f32[2,65,1,128]{3,2,1,0:T(1,128)S(1)} %collective-permute-done.3.refs_0_, bf16[8,512,256]{2,1,0:T(8,128)(2,1)S(1)} %get-tuple-element.39.refs_1_.refs_3_.refs_8_, ...), custom_call_target="tpu_custom_call" | custom-call | flops 536870912 | bytes 524288 | tf_op jit(solution)/shard_map/pallas_call | solution.py:328
  15.3 0.3 collective-permute-done.4.refs_0_
  15.7 0.1 collective-permute-start.6
  15.7 0.9 %shard_map.95 = (f32[8,256,256]{2,1,0:T(8,128)S(1)}, bf16[256,512]{1,0:T(8,128)(2,1)S(1)}, f32[2,16,128]{2,1,0:T(8,128)S(1)}, f32[2,16,128]{2,1,0:T(8,128)S(1)}) custom-call(f32[2,65,1,128]{3,2,1,0:T(1,128)S(1)} %collective-permute-done.4.refs_0_, bf16[8,512,256]{2,1,0:T(8,128)(2,1)S(1)} %get-tuple-element.39.refs_1_.refs_3_.refs_8_, ...), custom_call_target="tpu_custom_call" | custom-call | flops 536870912 | bytes 524288 | tf_op jit(solution)/shard_map/pallas_call | solution.py:328
  16.7 0.1 collective-permute-start.5
  16.8 0.1 collective-permute-done.6.refs_12_
  16.9 27.5 %shard_map.97 = (f32[16,128]{1,0:T(8,128)S(1)}, f32[8,1,128]{2,1,0:T(1,128)S(1)}) custom-call(f32[8,128,256]{2,1,0:T(8,128)S(1)} %get-tuple-element.41.refs_0_, f32[8,384,256]{2,1,0:T(8,128)S(1)} %get-tuple-element.42.refs_1_, f32[8,256,256]{2,1,0:T(8,128)S(1)} %get-tuple-element.44.refs_2_, f32[8,256,256]{2,1,0:T(8,128)S(1)} %get-tuple-element.64.refs_3_, ...), custom_call_target="tpu_custom_call" | custom-call | flops 1000000000 | bytes 524288 | tf_op jit(solution)/shard_map/pallas_call | solution.py:372
  44.5 0.0 collective-permute-done.5.refs_12_
  44.5 8.1 %all_to_all.5.values_ref = f32[8,1,128]{2,1,0:T(1,128)S(1)} all-to-all(f32[8,1,128]{2,1,0:T(1,128)S(1)} %get-tuple-element.69), channel_id=1, replica_groups={{14,12,10,8,6,4,2,0},{15,13,11,9,7,5,3,1},{30,28,26,24,22,20,18,16},{31..., dimensions={0} | all-to-all | bytes 8192 | tf_op jit(solution)/shard_map/all_to_all | solution.py:389
  52.6 0.6 %shard_map.99 = (f32[1,128]{1,0:T(1,128)}, f32[16,128]{1,0:T(8,128)}) custom-call(f32[8,1,128]{2,1,0:T(1,128)S(1)} %all_to_all.5.values_ref, f32[1,128]{1,0:T(1,128)S(1)} %get-tuple-element.70.weight_ref, f32[16,128]{1,0:T(8,128)S(1)} %get-tuple-element.71.poten_ref), custom_call_target="tpu_custom_call" | custom-call | tf_op jit(solution)/shard_map/pallas_call | solution.py:391
  (6 shorter events, 0.1 us)
Async XLA Ops:
  1.5 7.1 %collective-permute-start = (f32[1,65,1,128]{3,2,1,0:T(1,128)S(1)}, f32[1,65,1,128]{3,2,1,0:T(1,128)S(1)}, u32[]{:S(2)}, u32[]{:S(2)}) collective-permute-start(f32[1,65,1,128]{3,2,1,0:T(1,128)S(1)} %get-tuple-element.38.refs_0_), channel_id=1, source_target_pairs={{0,8},{2,10},{4,12},{6,14},{8,0},{10,2},{12,4},{14,6},{1,9},{3,11}... | collective-permute-start | bytes 99848 | tf_op jit(solution)/shard_map/ppermute | solution.py:341
  5.6 5.7 %collective-permute-start.1 = (f32[1,65,1,128]{3,2,1,0:T(1,128)S(1)}, f32[1,65,1,128]{3,2,1,0:T(1,128)S(1)}, u32[]{:S(2)}, u32[]{:S(2)}) collective-permute-start(f32[1,65,1,128]{3,2,1,0:T(1,128)S(1)} %get-tuple-element.38.refs_0_), channel_id=1, source_target_pairs={{0,12},{2,14},{4,8},{6,10},{8,4},{10,6},{12,0},{14,2},{1,13},{3,15... | collective-permute-start | bytes 99848 | tf_op jit(solution)/shard_map/ppermute | solution.py:341
  6.9 4.4 %collective-permute-start.2 = (f32[1,65,1,128]{3,2,1,0:T(1,128)S(1)}, f32[1,65,1,128]{3,2,1,0:T(1,128)S(1)}, u32[]{:S(2)}, u32[]{:S(2)}) collective-permute-start(f32[1,65,1,128]{3,2,1,0:T(1,128)S(1)} %get-tuple-element.38.refs_0_), channel_id=1, source_target_pairs={{0,4},{2,6},{4,0},{6,2},{8,12},{10,14},{12,8},{14,10},{1,5},{3,7},... | collective-permute-start | bytes 99848 | tf_op jit(solution)/shard_map/ppermute | solution.py:341
  8.5 5.9 %collective-permute-start.3 = (f32[2,65,1,128]{3,2,1,0:T(1,128)S(1)}, f32[2,65,1,128]{3,2,1,0:T(1,128)S(1)}, u32[]{:S(2)}, u32[]{:S(2)}) collective-permute-start(f32[2,65,1,128]{3,2,1,0:T(1,128)S(1)} %shard_map.88.refs_2_), channel_id=1, source_target_pairs={{0,2},{2,0},{4,6},{6,4},{8,10},{10,8},{12,14},{14,12},{1,3},{3,1},... | collective-permute-start | bytes 199688 | tf_op jit(solution)/shard_map/ppermute | solution.py:341
  11.3 4.3 %collective-permute-start.4 = (f32[2,65,1,128]{3,2,1,0:T(1,128)S(1)}, f32[2,65,1,128]{3,2,1,0:T(1,128)S(1)}, u32[]{:S(2)}, u32[]{:S(2)}) collective-permute-start(f32[2,65,1,128]{3,2,1,0:T(1,128)S(1)} %shard_map.92), channel_id=1, source_target_pairs={{0,2},{2,0},{4,6},{6,4},{8,10},{10,8},{12,14},{14,12},{1,3},{3,1},... | collective-permute-start | bytes 199688 | tf_op jit(solution)/shard_map/ppermute | solution.py:341
  15.7 1.2 %collective-permute-start.6 = (f32[16,128]{1,0:T(8,128)S(1)}, f32[16,128]{1,0:T(8,128)S(1)}, u32[]{:S(2)}, u32[]{:S(2)}) collective-permute-start(f32[16,128]{1,0:T(8,128)S(1)} %get-tuple-element.59.refs_2_.refs_11_), channel_id=1, source_target_pairs={{0,1},{1,0},{2,3},{3,2},{4,5},{5,4},{6,7},{7,6},{8,9},{9,8},{10,11... | collective-permute-start | bytes 24584 | tf_op jit(solution)/shard_map/ppermute | solution.py:383
  16.7 27.8 %collective-permute-start.5 = (f32[16,128]{1,0:T(8,128)S(1)}, f32[16,128]{1,0:T(8,128)S(1)}, u32[]{:S(2)}, u32[]{:S(2)}) collective-permute-start(f32[16,128]{1,0:T(8,128)S(1)} %get-tuple-element.62.refs_11_), channel_id=1, source_target_pairs={{0,1},{1,0},{2,3},{3,2},{4,5},{5,4},{6,7},{7,6},{8,9},{9,8},{10,11... | collective-permute-start | bytes 24584 | tf_op jit(solution)/shard_map/ppermute | solution.py:386

commit v15 on v14

--- a/solution.py
+++ b/solution.py
@@ -222,7 +222,7 @@
         for index in range(ref.shape[0] // cells)
     ]
     used = [jnp.max(mask_ref[place], axis=0, keepdims=True) > 0.5 * very_low for place in range(shards)]
-    ranks = [shards - 1 - block for block in blocks_at(shards)]
+    ranks = [lax.rem(block + shards - 1, shards) for block in blocks_at(shards)]
     sums = []
     for place, (group, rows) in enumerate(spots):
         acc = jnp.zeros((cells, cells), jnp.float32)
@@ -386,7 +386,7 @@
     other_one = lax.ppermute(own_zero, "tgt", between)
     given = columns_of(0, last_zero, peaks_zero, own_zero, other_zero, [])
     potential_src, columns = columns_of(1, last_one, peaks_one, own_one, other_one, given)
-    arrived = lax.all_to_all(columns, "src", 0, 0, axis_index_groups=[list(range(shards))[::-1]])
+    arrived = lax.all_to_all(columns, "src", 0, 0, axis_index_groups=[list(range(1, shards)) + [0]])
     outs = [f32(1, cells), f32(rows, cells)]
     potential_new, potential_src = call(merge_kernel, [VM] * 3, outs)(arrived, weight, potential_src)
     return potential_src, potential_new

time: 53.5 us -> 55.7 us (1.041)
  blocking collectives: 8.14 us -> 10.3 us
    all_to_all x1, blocking collectives: 8.14 us -> 10.3 us  [dense_device(): lax.all_to_all(columns, 'src', 0, 0, axis_index_groups=[list(range(1, sha...]
  transfers between devices with their start and end apart: 7 -> 7, of which waited for: 3 -> 3; matrix products, arithmetic and copies ran while one was open for 0% -> 0% of each run, Pallas kernels for 62% -> 59%
where the time goes in v15:
time: 55.7 us; the launch traced here: 55.4 us
  Pallas kernels  34.3 us (62%)
  blocking collectives  10.3 us (18%)
  starting transfers between devices  8.94 us (16%)
  waiting for transfers between devices  1.1 us (2%)
  between operations  0.74 us (1%)
    pallas_call x2, Pallas kernels, columns_of(): call(functools.partial(column_kernel, groups, core), [VM] * (2 * groups +...  27.6 us
    all_to_all x1, blocking collectives, dense_device(): lax.all_to_all(columns, 'src', 0, 0, axis_index_groups=[list(range(1, sha...  10.3 us
    ppermute x5, starting transfers between devices, swapped(): return lax.ppermute(array, 'src', [(i, i ^ step) for i in range(shards)])  8.79 us
    pallas_call x5, Pallas kernels, tiles(): call(functools.partial(tile_kernel, len(packs), core), [VM] * (len(packs)...  3.9 us
    pallas_call x2, Pallas kernels, reading(): call(kernel, [pl.BlockSpec(memory_space=pltpu.HBM)] * len(args), out_shap...  2.18 us
  transfers between devices with their start and end apart: 7, of which 3 were waited for; matrix products, arithmetic and copies ran while one was open for 0% of the time, Pallas kernels for 59%

profile of v15, /device:TPU:0, one launch (start us, length us, event | category | flops | bytes accessed | tf_op | source)
XLA Modules:
  0.0 55.4 jit_solution(16040242561186386772)
XLA Ops:
  0.6 0.8 %shard_map.86 = (f32[1,65,1,128]{3,2,1,0:T(1,128)S(1)}, f32[1,128]{1,0:T(1,128)S(1)}) custom-call(f32[1,64,128]{2,1,0:T(8,128)} %refs_0_.2, f32[1,128]{1,0:T(1,128)} %refs_1_.1, f32[1,128]{1,0:T(1,128)} %refs_2_.1), custom_call_target="tpu_custom_call" | custom-call | tf_op jit(solution)/shard_map/pallas_call | solution.py:296
  1.5 4.1 %collective-permute-start = (f32[1,65,1,128]{3,2,1,0:T(1,128)S(1)}, f32[1,65,1,128]{3,2,1,0:T(1,128)S(1)}, u32[]{:S(2)}, u32[]{:S(2)}) collective-permute-start(f32[1,65,1,128]{3,2,1,0:T(1,128)S(1)} %get-tuple-element.38.refs_0_), channel_id=1, source_target_pairs={{0,8},{2,10},{4,12},{6,14},{8,0},{10,2},{12,4},{14,6},{1,9},{3,11}... | collective-permute-start | bytes 99848 | tf_op jit(solution)/shard_map/ppermute | solution.py:341
  5.6 1.3 %collective-permute-start.1 = (f32[1,65,1,128]{3,2,1,0:T(1,128)S(1)}, f32[1,65,1,128]{3,2,1,0:T(1,128)S(1)}, u32[]{:S(2)}, u32[]{:S(2)}) collective-permute-start(f32[1,65,1,128]{3,2,1,0:T(1,128)S(1)} %get-tuple-element.38.refs_0_), channel_id=1, source_target_pairs={{0,12},{2,14},{4,8},{6,10},{8,4},{10,6},{12,0},{14,2},{1,13},{3,15... | collective-permute-start | bytes 99848 | tf_op jit(solution)/shard_map/ppermute | solution.py:341
  6.9 0.2 collective-permute-start.2
  7.1 1.4 %shard_map.87 = (bf16[8,512,256]{2,1,0:T(8,128)(2,1)S(1)}, f32[16,128]{1,0:T(8,128)S(1)}, f32[8,16,128]{2,1,0:T(8,128)S(1)}, f32[16,128]{1,0:T(8,128)S(1)}) custom-call(f32[16,128]{1,0:T(8,128)} %refs_0_.3, s32[8,16]{1,0:T(8,128)} %bitcast.4, s32[1,16]{1,0:T(1,128)} %bitcast.5, f32[16,64,128]{2,1,0:T(8,128)} %refs_3_.1), custom_call_target="tpu_custom_call" | custom-call | flops 1000000000 | bytes 524288 | tf_op jit(solution)/shard_map/pallas_call | solution.py:296
  8.5 0.0 collective-permute-done.refs_1_.refs_0_
  8.5 1.6 %collective-permute-start.3 = (f32[2,65,1,128]{3,2,1,0:T(1,128)S(1)}, f32[2,65,1,128]{3,2,1,0:T(1,128)S(1)}, u32[]{:S(2)}, u32[]{:S(2)}) collective-permute-start(f32[2,65,1,128]{3,2,1,0:T(1,128)S(1)} %shard_map.88.refs_2_), channel_id=1, source_target_pairs={{0,2},{2,0},{4,6},{6,4},{8,10},{10,8},{12,14},{14,12},{1,3},{3,1},... | collective-permute-start | bytes 199688 | tf_op jit(solution)/shard_map/ppermute | solution.py:341
  10.1 0.6 %shard_map.89 = (f32[8,128,256]{2,1,0:T(8,128)S(1)}, bf16[128,512]{1,0:T(8,128)(2,1)S(1)}, f32[1,16,128]{2,1,0:T(8,128)S(1)}, f32[1,16,128]{2,1,0:T(8,128)S(1)}) custom-call(f32[1,65,1,128]{3,2,1,0:T(1,128)S(1)} %get-tuple-element.38.refs_0_, bf16[8,512,256]{2,1,0:T(8,128)(2,1)S(1)} %get-tuple-element.39.refs_1_.refs_3_.refs_8_, ...), custom_call_target="tpu_custom_call" | custom-call | flops 268435456 | bytes 524288 | tf_op jit(solution)/shard_map/pallas_call | solution.py:328
  10.7 0.6 %collective-permute-done.1.refs_1_.refs_0_ = f32[1,65,1,128]{3,2,1,0:T(1,128)S(1)} collective-permute-done((f32[1,65,1,128]{3,2,1,0:T(1,128)S(1)}, f32[1,65,1,128]{3,2,1,0:T(1,128)S(1)}, u32[]{:S(2)}, u32[]{:S(2)}) %collective-permute-start.1) | collective-permute-done | bytes 33312 | tf_op jit(solution)/shard_map/ppermute | solution.py:341
  11.3 0.0 collective-permute-done.2.refs_2_.refs_1_
  11.3 1.6 %collective-permute-start.4 = (f32[2,65,1,128]{3,2,1,0:T(1,128)S(1)}, f32[2,65,1,128]{3,2,1,0:T(1,128)S(1)}, u32[]{:S(2)}, u32[]{:S(2)}) collective-permute-start(f32[2,65,1,128]{3,2,1,0:T(1,128)S(1)} %shard_map.92), channel_id=1, source_target_pairs={{0,2},{2,0},{4,6},{6,4},{8,10},{10,8},{12,14},{14,12},{1,3},{3,1},... | collective-permute-start | bytes 199688 | tf_op jit(solution)/shard_map/ppermute | solution.py:341
  12.8 1.5 %shard_map.90 = (f32[8,384,256]{2,1,0:T(8,128)S(1)}, bf16[384,512]{1,0:T(8,128)(2,1)S(1)}, f32[3,16,128]{2,1,0:T(8,128)S(1)}, f32[3,16,128]{2,1,0:T(8,128)S(1)}) custom-call(f32[1,65,1,128]{3,2,1,0:T(1,128)S(1)} %collective-permute-done.refs_1_.refs_0_, f32[1,65,1,128]{3,2,1,0:T(1,128)S(1)} %collective-permute-done.1.refs_1_.refs_0_, ...), custom_call_target="tpu_custom_call" | custom-call | flops 805306368 | bytes 524288 | tf_op jit(solution)/shard_map/pallas_call | solution.py:328
  14.4 0.0 collective-permute-done.3.refs_0_
  14.4 0.9 %shard_map.91 = (f32[8,256,256]{2,1,0:T(8,128)S(1)}, bf16[256,512]{1,0:T(8,128)(2,1)S(1)}, f32[2,16,128]{2,1,0:T(8,128)S(1)}, f32[2,16,128]{2,1,0:T(8,128)S(1)}) custom-call(f32[2,65,1,128]{3,2,1,0:T(1,128)S(1)} %collective-permute-done.3.refs_0_, bf16[8,512,256]{2,1,0:T(8,128)(2,1)S(1)} %get-tuple-element.39.refs_1_.refs_3_.refs_8_, ...), custom_call_target="tpu_custom_call" | custom-call | flops 536870912 | bytes 524288 | tf_op jit(solution)/shard_map/pallas_call | solution.py:328
  15.3 0.3 collective-permute-done.4.refs_0_
  15.7 0.1 collective-permute-start.6
  15.7 0.9 %shard_map.95 = (f32[8,256,256]{2,1,0:T(8,128)S(1)}, bf16[256,512]{1,0:T(8,128)(2,1)S(1)}, f32[2,16,128]{2,1,0:T(8,128)S(1)}, f32[2,16,128]{2,1,0:T(8,128)S(1)}) custom-call(f32[2,65,1,128]{3,2,1,0:T(1,128)S(1)} %collective-permute-done.4.refs_0_, bf16[8,512,256]{2,1,0:T(8,128)(2,1)S(1)} %get-tuple-element.39.refs_1_.refs_3_.refs_8_, ...), custom_call_target="tpu_custom_call" | custom-call | flops 536870912 | bytes 524288 | tf_op jit(solution)/shard_map/pallas_call | solution.py:328
  16.7 0.1 collective-permute-start.5
  16.8 0.1 collective-permute-done.6.refs_12_
  16.9 27.5 %shard_map.97 = (f32[16,128]{1,0:T(8,128)S(1)}, f32[8,1,128]{2,1,0:T(1,128)S(1)}) custom-call(f32[8,128,256]{2,1,0:T(8,128)S(1)} %get-tuple-element.41.refs_0_, f32[8,384,256]{2,1,0:T(8,128)S(1)} %get-tuple-element.42.refs_1_, f32[8,256,256]{2,1,0:T(8,128)S(1)} %get-tuple-element.44.refs_2_, f32[8,256,256]{2,1,0:T(8,128)S(1)} %get-tuple-element.64.refs_3_, ...), custom_call_target="tpu_custom_call" | custom-call | flops 1000000000 | bytes 524288 | tf_op jit(solution)/shard_map/pallas_call | solution.py:372
  44.5 0.0 collective-permute-done.5.refs_12_
  44.5 10.3 %all_to_all.5.values_ref = f32[8,1,128]{2,1,0:T(1,128)S(1)} all-to-all(f32[8,1,128]{2,1,0:T(1,128)S(1)} %get-tuple-element.69), channel_id=1, replica_groups={{2,4,6,8,10,12,14,0},{3,5,7,9,11,13,15,1},{18,20,22,24,26,28,30,16},{19..., dimensions={0} | all-to-all | bytes 8192 | tf_op jit(solution)/shard_map/all_to_all | solution.py:389
  54.8 0.6 %shard_map.99 = (f32[1,128]{1,0:T(1,128)}, f32[16,128]{1,0:T(8,128)}) custom-call(f32[8,1,128]{2,1,0:T(1,128)S(1)} %all_to_all.5.values_ref, f32[1,128]{1,0:T(1,128)S(1)} %get-tuple-element.70.weight_ref, f32[16,128]{1,0:T(8,128)S(1)} %get-tuple-element.71.poten_ref), custom_call_target="tpu_custom_call" | custom-call | tf_op jit(solution)/shard_map/pallas_call | solution.py:391
  (6 shorter events, 0.1 us)
Async XLA Ops:
  1.5 7.1 %collective-permute-start = (f32[1,65,1,128]{3,2,1,0:T(1,128)S(1)}, f32[1,65,1,128]{3,2,1,0:T(1,128)S(1)}, u32[]{:S(2)}, u32[]{:S(2)}) collective-permute-start(f32[1,65,1,128]{3,2,1,0:T(1,128)S(1)} %get-tuple-element.38.refs_0_), channel_id=1, source_target_pairs={{0,8},{2,10},{4,12},{6,14},{8,0},{10,2},{12,4},{14,6},{1,9},{3,11}... | collective-permute-start | bytes 99848 | tf_op jit(solution)/shard_map/ppermute | solution.py:341
  5.6 5.7 %collective-permute-start.1 = (f32[1,65,1,128]{3,2,1,0:T(1,128)S(1)}, f32[1,65,1,128]{3,2,1,0:T(1,128)S(1)}, u32[]{:S(2)}, u32[]{:S(2)}) collective-permute-start(f32[1,65,1,128]{3,2,1,0:T(1,128)S(1)} %get-tuple-element.38.refs_0_), channel_id=1, source_target_pairs={{0,12},{2,14},{4,8},{6,10},{8,4},{10,6},{12,0},{14,2},{1,13},{3,15... | collective-permute-start | bytes 99848 | tf_op jit(solution)/shard_map/ppermute | solution.py:341
  6.9 4.4 %collective-permute-start.2 = (f32[1,65,1,128]{3,2,1,0:T(1,128)S(1)}, f32[1,65,1,128]{3,2,1,0:T(1,128)S(1)}, u32[]{:S(2)}, u32[]{:S(2)}) collective-permute-start(f32[1,65,1,128]{3,2,1,0:T(1,128)S(1)} %get-tuple-element.38.refs_0_), channel_id=1, source_target_pairs={{0,4},{2,6},{4,0},{6,2},{8,12},{10,14},{12,8},{14,10},{1,5},{3,7},... | collective-permute-start | bytes 99848 | tf_op jit(solution)/shard_map/ppermute | solution.py:341
  8.5 5.9 %collective-permute-start.3 = (f32[2,65,1,128]{3,2,1,0:T(1,128)S(1)}, f32[2,65,1,128]{3,2,1,0:T(1,128)S(1)}, u32[]{:S(2)}, u32[]{:S(2)}) collective-permute-start(f32[2,65,1,128]{3,2,1,0:T(1,128)S(1)} %shard_map.88.refs_2_), channel_id=1, source_target_pairs={{0,2},{2,0},{4,6},{6,4},{8,10},{10,8},{12,14},{14,12},{1,3},{3,1},... | collective-permute-start | bytes 199688 | tf_op jit(solution)/shard_map/ppermute | solution.py:341
  11.3 4.3 %collective-permute-start.4 = (f32[2,65,1,128]{3,2,1,0:T(1,128)S(1)}, f32[2,65,1,128]{3,2,1,0:T(1,128)S(1)}, u32[]{:S(2)}, u32[]{:S(2)}) collective-permute-start(f32[2,65,1,128]{3,2,1,0:T(1,128)S(1)} %shard_map.92), channel_id=1, source_target_pairs={{0,2},{2,0},{4,6},{6,4},{8,10},{10,8},{12,14},{14,12},{1,3},{3,1},... | collective-permute-start | bytes 199688 | tf_op jit(solution)/shard_map/ppermute | solution.py:341
  15.7 1.2 %collective-permute-start.6 = (f32[16,128]{1,0:T(8,128)S(1)}, f32[16,128]{1,0:T(8,128)S(1)}, u32[]{:S(2)}, u32[]{:S(2)}) collective-permute-start(f32[16,128]{1,0:T(8,128)S(1)} %get-tuple-element.59.refs_2_.refs_11_), channel_id=1, source_target_pairs={{0,1},{1,0},{2,3},{3,2},{4,5},{5,4},{6,7},{7,6},{8,9},{9,8},{10,11... | collective-permute-start | bytes 24584 | tf_op jit(solution)/shard_map/ppermute | solution.py:383
  16.7 27.8 %collective-permute-start.5 = (f32[16,128]{1,0:T(8,128)S(1)}, f32[16,128]{1,0:T(8,128)S(1)}, u32[]{:S(2)}, u32[]{:S(2)}) collective-permute-start(f32[16,128]{1,0:T(8,128)S(1)} %get-tuple-element.62.refs_11_), channel_id=1, source_target_pairs={{0,1},{1,0},{2,3},{3,2},{4,5},{5,4},{6,7},{7,6},{8,9},{9,8},{10,11... | collective-permute-start | bytes 24584 | tf_op jit(solution)/shard_map/ppermute | solution.py:386

commit v16 on v14

--- a/solution.py
+++ b/solution.py
@@ -319,7 +319,7 @@
             in_vmem((shards, rows, cells), jnp.float32),
             in_vmem((rows, cells), jnp.float32),
         ],
-        cost_of(10**9),
+        cost_of(10**8),
     )
 
     def tiles(*packs, core=None, after=None):
@@ -351,10 +351,11 @@
     there = [swapped(pack, step) for step in reversed(steps)][::-1]
     near = [pack] + there
     halves = [joined(near[0], near[1], norm)]
-    found = [tiles(pack, after=halves[0])]
-    halves += [joined(near[at], near[at + 1], found[0][-1]) for at in range(2, shards // 2, 2)]
+    for at in range(2, shards // 2, 2):
+        halves.append(joined(near[at], near[at + 1], halves[-1]))
     far = [swapped(half, 1) for half in halves]
-    found.append(tiles(*there))
+    found = [tiles(pack, after=halves[-1])]
+    found.append(tiles(*there, after=found[0][-1]))
     for half in far[:-1]:
         found.append(tiles(half, after=found[-1][-1]))
     groups = len(found) + 1

time: 53.5 us -> 53.7 us (level)
  transfers between devices with their start and end apart: 7 -> 7, of which waited for: 3 -> 2; matrix products, arithmetic and copies ran while one was open for 0% -> 0% of each run, Pallas kernels for 62% -> 61%
where the time goes in v16:
time: 53.7 us; the launch traced here: 53.5 us
  Pallas kernels  34.4 us (64%)
  starting transfers between devices  8.94 us (17%)
  blocking collectives  8.12 us (15%)
  waiting for transfers between devices  1.33 us (2%)
  between operations  0.75 us (1%)
    pallas_call x2, Pallas kernels, columns_of(): call(functools.partial(column_kernel, groups, core), [VM] * (2 * groups +...  27.6 us
    ppermute x5, starting transfers between devices, swapped(): return lax.ppermute(array, 'src', [(i, i ^ step) for i in range(shards)])  8.79 us
    all_to_all x1, blocking collectives, dense_device(): lax.all_to_all(columns, 'src', 0, 0, axis_index_groups=[list(range(shards...  8.12 us
    pallas_call x5, Pallas kernels, tiles(): call(functools.partial(tile_kernel, len(packs), core), [VM] * (len(packs)...  3.93 us
    pallas_call x2, Pallas kernels, reading(): call(kernel, [pl.BlockSpec(memory_space=pltpu.HBM)] * len(args), out_shap...  2.18 us
    ppermute x5, waiting for transfers between devices, swapped(): return lax.ppermute(array, 'src', [(i, i ^ step) for i in range(shards)])  1.19 us
  transfers between devices with their start and end apart: 7, of which 2 were waited for; matrix products, arithmetic and copies ran while one was open for 0% of the time, Pallas kernels for 61%

profile of v16, /device:TPU:0, one launch (start us, length us, event | category | flops | bytes accessed | tf_op | source)
XLA Modules:
  0.0 53.5 jit_solution(14708415169252496247)
XLA Ops:
  0.6 0.8 %shard_map.86 = (f32[1,65,1,128]{3,2,1,0:T(1,128)S(1)}, f32[1,128]{1,0:T(1,128)S(1)}) custom-call(f32[1,64,128]{2,1,0:T(8,128)} %refs_0_.2, f32[1,128]{1,0:T(1,128)} %refs_1_.1, f32[1,128]{1,0:T(1,128)} %refs_2_.1), custom_call_target="tpu_custom_call" | custom-call | tf_op jit(solution)/shard_map/pallas_call | solution.py:296
  1.5 4.1 %collective-permute-start.2 = (f32[1,65,1,128]{3,2,1,0:T(1,128)S(1)}, f32[1,65,1,128]{3,2,1,0:T(1,128)S(1)}, u32[]{:S(2)}, u32[]{:S(2)}) collective-permute-start(f32[1,65,1,128]{3,2,1,0:T(1,128)S(1)} %get-tuple-element.38.refs_0_), channel_id=1, source_target_pairs={{0,8},{2,10},{4,12},{6,14},{8,0},{10,2},{12,4},{14,6},{1,9},{3,11}... | collective-permute-start | bytes 99848 | tf_op jit(solution)/shard_map/ppermute | solution.py:341
  5.6 1.3 %collective-permute-start = (f32[1,65,1,128]{3,2,1,0:T(1,128)S(1)}, f32[1,65,1,128]{3,2,1,0:T(1,128)S(1)}, u32[]{:S(2)}, u32[]{:S(2)}) collective-permute-start(f32[1,65,1,128]{3,2,1,0:T(1,128)S(1)} %get-tuple-element.38.refs_0_), channel_id=1, source_target_pairs={{0,12},{2,14},{4,8},{6,10},{8,4},{10,6},{12,0},{14,2},{1,13},{3,15... | collective-permute-start | bytes 99848 | tf_op jit(solution)/shard_map/ppermute | solution.py:341
  6.9 0.2 collective-permute-start.1
  7.1 1.4 %shard_map.87 = (bf16[8,512,256]{2,1,0:T(8,128)(2,1)S(1)}, f32[16,128]{1,0:T(8,128)S(1)}, f32[8,16,128]{2,1,0:T(8,128)S(1)}, f32[16,128]{1,0:T(8,128)S(1)}) custom-call(f32[16,128]{1,0:T(8,128)} %refs_0_.3, s32[8,16]{1,0:T(8,128)} %bitcast.4, s32[1,16]{1,0:T(1,128)} %bitcast.5, f32[16,64,128]{2,1,0:T(8,128)} %refs_3_.1), custom_call_target="tpu_custom_call" | custom-call | flops 100000000 | bytes 524288 | tf_op jit(solution)/shard_map/pallas_call | solution.py:296
  8.5 0.0 collective-permute-done.2.refs_1_.refs_0_
  8.5 1.6 %collective-permute-start.3 = (f32[2,65,1,128]{3,2,1,0:T(1,128)S(1)}, f32[2,65,1,128]{3,2,1,0:T(1,128)S(1)}, u32[]{:S(2)}, u32[]{:S(2)}) collective-permute-start(f32[2,65,1,128]{3,2,1,0:T(1,128)S(1)} %shard_map.88.refs_2_), channel_id=1, source_target_pairs={{0,2},{2,0},{4,6},{6,4},{8,10},{10,8},{12,14},{14,12},{1,3},{3,1},... | collective-permute-start | bytes 199688 | tf_op jit(solution)/shard_map/ppermute | solution.py:341
  10.1 1.2 %collective-permute-done.refs_0_.refs_1_ = f32[1,65,1,128]{3,2,1,0:T(1,128)S(1)} collective-permute-done((f32[1,65,1,128]{3,2,1,0:T(1,128)S(1)}, f32[1,65,1,128]{3,2,1,0:T(1,128)S(1)}, u32[]{:S(2)}, u32[]{:S(2)}) %collective-permute-start) | collective-permute-done | bytes 33312 | tf_op jit(solution)/shard_map/ppermute | solution.py:341
  11.3 0.0 collective-permute-done.1.refs_1_.refs_2_
  11.3 1.6 %collective-permute-start.4 = (f32[2,65,1,128]{3,2,1,0:T(1,128)S(1)}, f32[2,65,1,128]{3,2,1,0:T(1,128)S(1)}, u32[]{:S(2)}, u32[]{:S(2)}) collective-permute-start(f32[2,65,1,128]{3,2,1,0:T(1,128)S(1)} %shard_map.89.refs_2_), channel_id=1, source_target_pairs={{0,2},{2,0},{4,6},{6,4},{8,10},{10,8},{12,14},{14,12},{1,3},{3,1},... | collective-permute-start | bytes 199688 | tf_op jit(solution)/shard_map/ppermute | solution.py:341
  12.8 0.6 %shard_map.90 = (f32[8,128,256]{2,1,0:T(8,128)S(1)}, bf16[128,512]{1,0:T(8,128)(2,1)S(1)}, f32[1,16,128]{2,1,0:T(8,128)S(1)}, f32[1,16,128]{2,1,0:T(8,128)S(1)}) custom-call(f32[1,65,1,128]{3,2,1,0:T(1,128)S(1)} %get-tuple-element.38.refs_0_, bf16[8,512,256]{2,1,0:T(8,128)(2,1)S(1)} %get-tuple-element.39.refs_1_.refs_3_.refs_8_, ...), custom_call_target="tpu_custom_call" | custom-call | flops 268435456 | bytes 524288 | tf_op jit(solution)/shard_map/pallas_call | solution.py:328
  13.4 1.5 %shard_map.91 = (f32[8,384,256]{2,1,0:T(8,128)S(1)}, bf16[384,512]{1,0:T(8,128)(2,1)S(1)}, f32[3,16,128]{2,1,0:T(8,128)S(1)}, f32[3,16,128]{2,1,0:T(8,128)S(1)}) custom-call(f32[1,65,1,128]{3,2,1,0:T(1,128)S(1)} %collective-permute-done.2.refs_1_.refs_0_, f32[1,65,1,128]{3,2,1,0:T(1,128)S(1)} %collective-permute-done.refs_0_.refs_1_, ...), custom_call_target="tpu_custom_call" | custom-call | flops 805306368 | bytes 524288 | tf_op jit(solution)/shard_map/pallas_call | solution.py:328
  15.0 0.0 collective-permute-done.3.refs_0_
  15.0 0.9 %shard_map.92 = (f32[8,256,256]{2,1,0:T(8,128)S(1)}, bf16[256,512]{1,0:T(8,128)(2,1)S(1)}, f32[2,16,128]{2,1,0:T(8,128)S(1)}, f32[2,16,128]{2,1,0:T(8,128)S(1)}) custom-call(f32[2,65,1,128]{3,2,1,0:T(1,128)S(1)} %collective-permute-done.3.refs_0_, bf16[8,512,256]{2,1,0:T(8,128)(2,1)S(1)} %get-tuple-element.39.refs_1_.refs_3_.refs_8_, ...), custom_call_target="tpu_custom_call" | custom-call | flops 536870912 | bytes 524288 | tf_op jit(solution)/shard_map/pallas_call | solution.py:328
  15.9 0.0 collective-permute-done.4.refs_0_
  16.0 0.1 collective-permute-start.6
  16.0 0.9 %shard_map.95 = (f32[8,256,256]{2,1,0:T(8,128)S(1)}, bf16[256,512]{1,0:T(8,128)(2,1)S(1)}, f32[2,16,128]{2,1,0:T(8,128)S(1)}, f32[2,16,128]{2,1,0:T(8,128)S(1)}) custom-call(f32[2,65,1,128]{3,2,1,0:T(1,128)S(1)} %collective-permute-done.4.refs_0_, bf16[8,512,256]{2,1,0:T(8,128)(2,1)S(1)} %get-tuple-element.39.refs_1_.refs_3_.refs_8_, ...), custom_call_target="tpu_custom_call" | custom-call | flops 536870912 | bytes 524288 | tf_op jit(solution)/shard_map/pallas_call | solution.py:328
  17.0 0.1 collective-permute-start.5
  17.1 0.1 collective-permute-done.6.refs_12_
  17.2 27.5 %shard_map.97 = (f32[16,128]{1,0:T(8,128)S(1)}, f32[8,1,128]{2,1,0:T(1,128)S(1)}) custom-call(f32[8,128,256]{2,1,0:T(8,128)S(1)} %get-tuple-element.41.refs_0_, f32[8,384,256]{2,1,0:T(8,128)S(1)} %get-tuple-element.43.refs_1_, f32[8,256,256]{2,1,0:T(8,128)S(1)} %get-tuple-element.45.refs_2_, f32[8,256,256]{2,1,0:T(8,128)S(1)} %get-tuple-element.64.refs_3_, ...), custom_call_target="tpu_custom_call" | custom-call | flops 1000000000 | bytes 524288 | tf_op jit(solution)/shard_map/pallas_call | solution.py:373
  44.7 0.0 collective-permute-done.5.refs_12_
  44.8 8.1 %all_to_all.5.values_ref = f32[8,1,128]{2,1,0:T(1,128)S(1)} all-to-all(f32[8,1,128]{2,1,0:T(1,128)S(1)} %get-tuple-element.69), channel_id=1, replica_groups={{14,12,10,8,6,4,2,0},{15,13,11,9,7,5,3,1},{30,28,26,24,22,20,18,16},{31..., dimensions={0} | all-to-all | bytes 8192 | tf_op jit(solution)/shard_map/all_to_all | solution.py:390
  52.9 0.6 %shard_map.99 = (f32[1,128]{1,0:T(1,128)}, f32[16,128]{1,0:T(8,128)}) custom-call(f32[8,1,128]{2,1,0:T(1,128)S(1)} %all_to_all.5.values_ref, f32[1,128]{1,0:T(1,128)S(1)} %get-tuple-element.70.weight_ref, f32[16,128]{1,0:T(8,128)S(1)} %get-tuple-element.71.poten_ref), custom_call_target="tpu_custom_call" | custom-call | tf_op jit(solution)/shard_map/pallas_call | solution.py:392
  (6 shorter events, 0.1 us)
Async XLA Ops:
  1.5 7.1 %collective-permute-start.2 = (f32[1,65,1,128]{3,2,1,0:T(1,128)S(1)}, f32[1,65,1,128]{3,2,1,0:T(1,128)S(1)}, u32[]{:S(2)}, u32[]{:S(2)}) collective-permute-start(f32[1,65,1,128]{3,2,1,0:T(1,128)S(1)} %get-tuple-element.38.refs_0_), channel_id=1, source_target_pairs={{0,8},{2,10},{4,12},{6,14},{8,0},{10,2},{12,4},{14,6},{1,9},{3,11}... | collective-permute-start | bytes 99848 | tf_op jit(solution)/shard_map/ppermute | solution.py:341
  5.6 5.7 %collective-permute-start = (f32[1,65,1,128]{3,2,1,0:T(1,128)S(1)}, f32[1,65,1,128]{3,2,1,0:T(1,128)S(1)}, u32[]{:S(2)}, u32[]{:S(2)}) collective-permute-start(f32[1,65,1,128]{3,2,1,0:T(1,128)S(1)} %get-tuple-element.38.refs_0_), channel_id=1, source_target_pairs={{0,12},{2,14},{4,8},{6,10},{8,4},{10,6},{12,0},{14,2},{1,13},{3,15... | collective-permute-start | bytes 99848 | tf_op jit(solution)/shard_map/ppermute | solution.py:341
  6.9 4.4 %collective-permute-start.1 = (f32[1,65,1,128]{3,2,1,0:T(1,128)S(1)}, f32[1,65,1,128]{3,2,1,0:T(1,128)S(1)}, u32[]{:S(2)}, u32[]{:S(2)}) collective-permute-start(f32[1,65,1,128]{3,2,1,0:T(1,128)S(1)} %get-tuple-element.38.refs_0_), channel_id=1, source_target_pairs={{0,4},{2,6},{4,0},{6,2},{8,12},{10,14},{12,8},{14,10},{1,5},{3,7},... | collective-permute-start | bytes 99848 | tf_op jit(solution)/shard_map/ppermute | solution.py:341
  8.5 6.4 %collective-permute-start.3 = (f32[2,65,1,128]{3,2,1,0:T(1,128)S(1)}, f32[2,65,1,128]{3,2,1,0:T(1,128)S(1)}, u32[]{:S(2)}, u32[]{:S(2)}) collective-permute-start(f32[2,65,1,128]{3,2,1,0:T(1,128)S(1)} %shard_map.88.refs_2_), channel_id=1, source_target_pairs={{0,2},{2,0},{4,6},{6,4},{8,10},{10,8},{12,14},{14,12},{1,3},{3,1},... | collective-permute-start | bytes 199688 | tf_op jit(solution)/shard_map/ppermute | solution.py:341
  11.3 4.6 %collective-permute-start.4 = (f32[2,65,1,128]{3,2,1,0:T(1,128)S(1)}, f32[2,65,1,128]{3,2,1,0:T(1,128)S(1)}, u32[]{:S(2)}, u32[]{:S(2)}) collective-permute-start(f32[2,65,1,128]{3,2,1,0:T(1,128)S(1)} %shard_map.89.refs_2_), channel_id=1, source_target_pairs={{0,2},{2,0},{4,6},{6,4},{8,10},{10,8},{12,14},{14,12},{1,3},{3,1},... | collective-permute-start | bytes 199688 | tf_op jit(solution)/shard_map/ppermute | solution.py:341
  16.0 1.2 %collective-permute-start.6 = (f32[16,128]{1,0:T(8,128)S(1)}, f32[16,128]{1,0:T(8,128)S(1)}, u32[]{:S(2)}, u32[]{:S(2)}) collective-permute-start(f32[16,128]{1,0:T(8,128)S(1)} %get-tuple-element.59.refs_2_.refs_11_), channel_id=1, source_target_pairs={{0,1},{1,0},{2,3},{3,2},{4,5},{5,4},{6,7},{7,6},{8,9},{9,8},{10,11... | collective-permute-start | bytes 24584 | tf_op jit(solution)/shard_map/ppermute | solution.py:384
  17.0 27.8 %collective-permute-start.5 = (f32[16,128]{1,0:T(8,128)S(1)}, f32[16,128]{1,0:T(8,128)S(1)}, u32[]{:S(2)}, u32[]{:S(2)}) collective-permute-start(f32[16,128]{1,0:T(8,128)S(1)} %get-tuple-element.62.refs_11_), channel_id=1, source_target_pairs={{0,1},{1,0},{2,3},{3,2},{4,5},{5,4},{6,7},{7,6},{8,9},{9,8},{10,11... | collective-permute-start | bytes 24584 | tf_op jit(solution)/shard_map/ppermute | solution.py:387

commit v17 on v16

--- a/solution.py
+++ b/solution.py
@@ -36,14 +36,21 @@
     return (mass + poten / entropic) * log2e
 
 
-def line_steps(shards):
-    return [2 * (i ^ (i >> 1)) for i in range(shards // 2 - 1, 0, -1)]
+def line_moves(line):
+    bits = line.bit_length() - 1
+    cycle = [sum(((place >> bit) & 1) << (bits - 1 - bit) for bit in range(bits)) for place in range(line)]
+    shifts = [shift for step in range(1, line // 2) for shift in (step, line - step)] + [line // 2]
+    return [[cycle[(cycle.index(at) + shift) % line] for at in range(line)] for shift in shifts]
 
 
 def blocks_at(shards):
-    near = [0] + line_steps(shards)
     me = lax.axis_index("src")
-    return [me ^ other for other in near + [step ^ 1 for step in near]]
+    at, odd = me // 2, lax.rem(me, 2)
+    near = [me]
+    for receivers in line_moves(shards // 2):
+        senders = [receivers.index(there) for there in range(shards // 2)]
+        near.append(2 * sum(jnp.where(at == there, sender, 0) for there, sender in enumerate(senders)) + odd)
+    return near + [block ^ 1 for block in near]
 
 
 def read_all(hbm, held, sems):
@@ -337,8 +344,12 @@
             cost=cost_of(2 * blocks * cells * pairs * wide * 8 * depth),
         )(*packs, wide_feat, *more)
 
-    def swapped(array, step):
-        return lax.ppermute(array, "src", [(i, i ^ step) for i in range(shards)])
+    def swapped(array):
+        return lax.ppermute(array, "src", [(i, i ^ 1) for i in range(shards)])
+
+    def moved(array, receivers):
+        moves = [(2 * here + odd, 2 * there + odd) for here, there in enumerate(receivers) for odd in range(2)]
+        return lax.ppermute(array, "src", moves)
 
     def joined(first, second, after):
         return call(
@@ -347,13 +358,12 @@
             in_vmem((2,) + pack.shape[1:], jnp.float32),
         )(first, second, after)
 
-    steps = line_steps(shards)
-    there = [swapped(pack, step) for step in reversed(steps)][::-1]
+    there = [moved(pack, receivers) for receivers in line_moves(shards // 2)[::-1]][::-1]
     near = [pack] + there
     halves = [joined(near[0], near[1], norm)]
     for at in range(2, shards // 2, 2):
         halves.append(joined(near[at], near[at + 1], halves[-1]))
-    far = [swapped(half, 1) for half in halves]
+    far = [swapped(half) for half in halves]
     found = [tiles(pack, after=halves[-1])]
     found.append(tiles(*there, after=found[0][-1]))
     for half in far[:-1]:

time: 53.7 us -> 53.1 us (0.989)
  waiting for transfers between devices: 1.33 us -> 0.7 us
    ppermute x5, waiting for transfers between devices: 1.19 us -> 0.55 us  [the longest x3 0.55 us: moved(): return lax.ppermute(array, 'src', moves)]
  transfers between devices with their start and end apart: 7 -> 7, of which waited for: 2 -> 3; matrix products, arithmetic and copies ran while one was open for 0% -> 0% of each run, Pallas kernels for 61% -> 62%
where the time goes in v17:
time: 53.1 us; the launch traced here: 52.9 us
  Pallas kernels  34.4 us (65%)
  starting transfers between devices  8.96 us (17%)
  blocking collectives  8.12 us (15%)
  between operations  0.75 us (1%)
  waiting for transfers between devices  0.7 us (1%)
    pallas_call x2, Pallas kernels, columns_of(): call(functools.partial(column_kernel, groups, core), [VM] * (2 * groups +...  27.6 us
    all_to_all x1, blocking collectives, dense_device(): lax.all_to_all(columns, 'src', 0, 0, axis_index_groups=[list(range(shards...  8.12 us
    ppermute x3, starting transfers between devices, moved(): return lax.ppermute(array, 'src', moves)  5.67 us
    pallas_call x5, Pallas kernels, tiles(): call(functools.partial(tile_kernel, len(packs), core), [VM] * (len(packs)...  3.92 us
    ppermute x2, starting transfers between devices, swapped(): return lax.ppermute(array, 'src', [(i, i ^ 1) for i in range(shards)])  3.15 us
    pallas_call x2, Pallas kernels, reading(): call(kernel, [pl.BlockSpec(memory_space=pltpu.HBM)] * len(args), out_shap...  2.18 us
  transfers between devices with their start and end apart: 7, of which 3 were waited for; matrix products, arithmetic and copies ran while one was open for 0% of the time, Pallas kernels for 62%

profile of v17, /device:TPU:0, one launch (start us, length us, event | category | flops | bytes accessed | tf_op | source)
XLA Modules:
  0.0 52.9 jit_solution(11911835721577227100)
XLA Ops:
  0.6 0.8 %shard_map.86 = (f32[1,65,1,128]{3,2,1,0:T(1,128)S(1)}, f32[1,128]{1,0:T(1,128)S(1)}) custom-call(f32[1,64,128]{2,1,0:T(8,128)} %refs_0_.2, f32[1,128]{1,0:T(1,128)} %refs_1_.1, f32[1,128]{1,0:T(1,128)} %refs_2_.1), custom_call_target="tpu_custom_call" | custom-call | tf_op jit(solution)/shard_map/pallas_call | solution.py:303
  1.5 4.1 %collective-permute-start.2 = (f32[1,65,1,128]{3,2,1,0:T(1,128)S(1)}, f32[1,65,1,128]{3,2,1,0:T(1,128)S(1)}, u32[]{:S(2)}, u32[]{:S(2)}) collective-permute-start(f32[1,65,1,128]{3,2,1,0:T(1,128)S(1)} %get-tuple-element.38.refs_0_), channel_id=1, source_target_pairs={{0,8},{2,10},{4,12},{6,14},{8,4},{10,6},{12,0},{14,2},{1,9},{3,11}... | collective-permute-start | bytes 99848 | tf_op jit(solution)/shard_map/ppermute | solution.py:352
  5.5 1.1 %collective-permute-start = (f32[1,65,1,128]{3,2,1,0:T(1,128)S(1)}, f32[1,65,1,128]{3,2,1,0:T(1,128)S(1)}, u32[]{:S(2)}, u32[]{:S(2)}) collective-permute-start(f32[1,65,1,128]{3,2,1,0:T(1,128)S(1)} %get-tuple-element.38.refs_0_), channel_id=1, source_target_pairs={{0,12},{2,14},{4,8},{6,10},{8,0},{10,2},{12,4},{14,6},{1,13},{3,15... | collective-permute-start | bytes 99848 | tf_op jit(solution)/shard_map/ppermute | solution.py:352
  6.6 0.5 collective-permute-start.1
  7.1 1.4 %shard_map.87 = (bf16[8,512,256]{2,1,0:T(8,128)(2,1)S(1)}, f32[16,128]{1,0:T(8,128)S(1)}, f32[8,16,128]{2,1,0:T(8,128)S(1)}, f32[16,128]{1,0:T(8,128)S(1)}) custom-call(f32[16,128]{1,0:T(8,128)} %refs_0_.3, s32[8,16]{1,0:T(8,128)} %bitcast.4, s32[1,16]{1,0:T(1,128)} %bitcast.5, f32[16,64,128]{2,1,0:T(8,128)} %refs_3_.1), custom_call_target="tpu_custom_call" | custom-call | flops 100000000 | bytes 524288 | tf_op jit(solution)/shard_map/pallas_call | solution.py:303
  8.5 0.0 collective-permute-done.2.refs_1_.refs_0_
  8.5 1.7 %collective-permute-start.3 = (f32[2,65,1,128]{3,2,1,0:T(1,128)S(1)}, f32[2,65,1,128]{3,2,1,0:T(1,128)S(1)}, u32[]{:S(2)}, u32[]{:S(2)}) collective-permute-start(f32[2,65,1,128]{3,2,1,0:T(1,128)S(1)} %shard_map.88.refs_2_), channel_id=1, source_target_pairs={{0,2},{2,0},{4,6},{6,4},{8,10},{10,8},{12,14},{14,12},{1,3},{3,1},... | collective-permute-start | bytes 199688 | tf_op jit(solution)/shard_map/ppermute | solution.py:348
  10.2 0.2 collective-permute-done.refs_0_.refs_1_
  10.4 0.3 collective-permute-done.1.refs_1_.refs_2_
  10.7 1.5 %collective-permute-start.4 = (f32[2,65,1,128]{3,2,1,0:T(1,128)S(1)}, f32[2,65,1,128]{3,2,1,0:T(1,128)S(1)}, u32[]{:S(2)}, u32[]{:S(2)}) collective-permute-start(f32[2,65,1,128]{3,2,1,0:T(1,128)S(1)} %shard_map.89.refs_2_), channel_id=1, source_target_pairs={{0,2},{2,0},{4,6},{6,4},{8,10},{10,8},{12,14},{14,12},{1,3},{3,1},... | collective-permute-start | bytes 199688 | tf_op jit(solution)/shard_map/ppermute | solution.py:348
  12.2 0.6 %shard_map.90 = (f32[8,128,256]{2,1,0:T(8,128)S(1)}, bf16[128,512]{1,0:T(8,128)(2,1)S(1)}, f32[1,16,128]{2,1,0:T(8,128)S(1)}, f32[1,16,128]{2,1,0:T(8,128)S(1)}) custom-call(f32[1,65,1,128]{3,2,1,0:T(1,128)S(1)} %get-tuple-element.38.refs_0_, bf16[8,512,256]{2,1,0:T(8,128)(2,1)S(1)} %get-tuple-element.39.refs_1_.refs_3_.refs_8_, ...), custom_call_target="tpu_custom_call" | custom-call | flops 268435456 | bytes 524288 | tf_op jit(solution)/shard_map/pallas_call | solution.py:335
  12.8 1.5 %shard_map.91 = (f32[8,384,256]{2,1,0:T(8,128)S(1)}, bf16[384,512]{1,0:T(8,128)(2,1)S(1)}, f32[3,16,128]{2,1,0:T(8,128)S(1)}, f32[3,16,128]{2,1,0:T(8,128)S(1)}) custom-call(f32[1,65,1,128]{3,2,1,0:T(1,128)S(1)} %collective-permute-done.2.refs_1_.refs_0_, f32[1,65,1,128]{3,2,1,0:T(1,128)S(1)} %collective-permute-done.refs_0_.refs_1_, ...), custom_call_target="tpu_custom_call" | custom-call | flops 805306368 | bytes 524288 | tf_op jit(solution)/shard_map/pallas_call | solution.py:335
  14.3 0.0 collective-permute-done.3.refs_0_
  14.4 0.9 %shard_map.92 = (f32[8,256,256]{2,1,0:T(8,128)S(1)}, bf16[256,512]{1,0:T(8,128)(2,1)S(1)}, f32[2,16,128]{2,1,0:T(8,128)S(1)}, f32[2,16,128]{2,1,0:T(8,128)S(1)}) custom-call(f32[2,65,1,128]{3,2,1,0:T(1,128)S(1)} %collective-permute-done.3.refs_0_, bf16[8,512,256]{2,1,0:T(8,128)(2,1)S(1)} %get-tuple-element.39.refs_1_.refs_3_.refs_8_, ...), custom_call_target="tpu_custom_call" | custom-call | flops 536870912 | bytes 524288 | tf_op jit(solution)/shard_map/pallas_call | solution.py:335
  15.2 0.0 collective-permute-done.4.refs_0_
  15.3 0.1 collective-permute-start.6
  15.4 0.9 %shard_map.95 = (f32[8,256,256]{2,1,0:T(8,128)S(1)}, bf16[256,512]{1,0:T(8,128)(2,1)S(1)}, f32[2,16,128]{2,1,0:T(8,128)S(1)}, f32[2,16,128]{2,1,0:T(8,128)S(1)}) custom-call(f32[2,65,1,128]{3,2,1,0:T(1,128)S(1)} %collective-permute-done.4.refs_0_, bf16[8,512,256]{2,1,0:T(8,128)(2,1)S(1)} %get-tuple-element.39.refs_1_.refs_3_.refs_8_, ...), custom_call_target="tpu_custom_call" | custom-call | flops 536870912 | bytes 524288 | tf_op jit(solution)/shard_map/pallas_call | solution.py:335
  16.3 0.1 collective-permute-start.5
  16.4 0.1 collective-permute-done.6.refs_12_
  16.6 27.5 %shard_map.97 = (f32[16,128]{1,0:T(8,128)S(1)}, f32[8,1,128]{2,1,0:T(1,128)S(1)}) custom-call(f32[8,128,256]{2,1,0:T(8,128)S(1)} %get-tuple-element.41.refs_0_, f32[8,384,256]{2,1,0:T(8,128)S(1)} %get-tuple-element.43.refs_1_, f32[8,256,256]{2,1,0:T(8,128)S(1)} %get-tuple-element.45.refs_2_, f32[8,256,256]{2,1,0:T(8,128)S(1)} %get-tuple-element.64.refs_3_, ...), custom_call_target="tpu_custom_call" | custom-call | flops 1000000000 | bytes 524288 | tf_op jit(solution)/shard_map/pallas_call | solution.py:383
  44.1 0.0 collective-permute-done.5.refs_12_
  44.1 8.1 %all_to_all.5.values_ref = f32[8,1,128]{2,1,0:T(1,128)S(1)} all-to-all(f32[8,1,128]{2,1,0:T(1,128)S(1)} %get-tuple-element.69), channel_id=1, replica_groups={{14,12,10,8,6,4,2,0},{15,13,11,9,7,5,3,1},{30,28,26,24,22,20,18,16},{31..., dimensions={0} | all-to-all | bytes 8192 | tf_op jit(solution)/shard_map/all_to_all | solution.py:400
  52.3 0.6 %shard_map.99 = (f32[1,128]{1,0:T(1,128)}, f32[16,128]{1,0:T(8,128)}) custom-call(f32[8,1,128]{2,1,0:T(1,128)S(1)} %all_to_all.5.values_ref, f32[1,128]{1,0:T(1,128)S(1)} %get-tuple-element.70.weight_ref, f32[16,128]{1,0:T(8,128)S(1)} %get-tuple-element.71.poten_ref), custom_call_target="tpu_custom_call" | custom-call | tf_op jit(solution)/shard_map/pallas_call | solution.py:402
  (6 shorter events, 0.1 us)
Async XLA Ops:
  1.5 7.0 %collective-permute-start.2 = (f32[1,65,1,128]{3,2,1,0:T(1,128)S(1)}, f32[1,65,1,128]{3,2,1,0:T(1,128)S(1)}, u32[]{:S(2)}, u32[]{:S(2)}) collective-permute-start(f32[1,65,1,128]{3,2,1,0:T(1,128)S(1)} %get-tuple-element.38.refs_0_), channel_id=1, source_target_pairs={{0,8},{2,10},{4,12},{6,14},{8,4},{10,6},{12,0},{14,2},{1,9},{3,11}... | collective-permute-start | bytes 99848 | tf_op jit(solution)/shard_map/ppermute | solution.py:352
  5.5 4.8 %collective-permute-start = (f32[1,65,1,128]{3,2,1,0:T(1,128)S(1)}, f32[1,65,1,128]{3,2,1,0:T(1,128)S(1)}, u32[]{:S(2)}, u32[]{:S(2)}) collective-permute-start(f32[1,65,1,128]{3,2,1,0:T(1,128)S(1)} %get-tuple-element.38.refs_0_), channel_id=1, source_target_pairs={{0,12},{2,14},{4,8},{6,10},{8,0},{10,2},{12,4},{14,6},{1,13},{3,15... | collective-permute-start | bytes 99848 | tf_op jit(solution)/shard_map/ppermute | solution.py:352
  6.6 4.1 %collective-permute-start.1 = (f32[1,65,1,128]{3,2,1,0:T(1,128)S(1)}, f32[1,65,1,128]{3,2,1,0:T(1,128)S(1)}, u32[]{:S(2)}, u32[]{:S(2)}) collective-permute-start(f32[1,65,1,128]{3,2,1,0:T(1,128)S(1)} %get-tuple-element.38.refs_0_), channel_id=1, source_target_pairs={{0,4},{2,6},{4,0},{6,2},{8,12},{10,14},{12,8},{14,10},{1,5},{3,7},... | collective-permute-start | bytes 99848 | tf_op jit(solution)/shard_map/ppermute | solution.py:352
  8.5 5.8 %collective-permute-start.3 = (f32[2,65,1,128]{3,2,1,0:T(1,128)S(1)}, f32[2,65,1,128]{3,2,1,0:T(1,128)S(1)}, u32[]{:S(2)}, u32[]{:S(2)}) collective-permute-start(f32[2,65,1,128]{3,2,1,0:T(1,128)S(1)} %shard_map.88.refs_2_), channel_id=1, source_target_pairs={{0,2},{2,0},{4,6},{6,4},{8,10},{10,8},{12,14},{14,12},{1,3},{3,1},... | collective-permute-start | bytes 199688 | tf_op jit(solution)/shard_map/ppermute | solution.py:348
  10.7 4.5 %collective-permute-start.4 = (f32[2,65,1,128]{3,2,1,0:T(1,128)S(1)}, f32[2,65,1,128]{3,2,1,0:T(1,128)S(1)}, u32[]{:S(2)}, u32[]{:S(2)}) collective-permute-start(f32[2,65,1,128]{3,2,1,0:T(1,128)S(1)} %shard_map.89.refs_2_), channel_id=1, source_target_pairs={{0,2},{2,0},{4,6},{6,4},{8,10},{10,8},{12,14},{14,12},{1,3},{3,1},... | collective-permute-start | bytes 199688 | tf_op jit(solution)/shard_map/ppermute | solution.py:348
  15.3 1.2 %collective-permute-start.6 = (f32[16,128]{1,0:T(8,128)S(1)}, f32[16,128]{1,0:T(8,128)S(1)}, u32[]{:S(2)}, u32[]{:S(2)}) collective-permute-start(f32[16,128]{1,0:T(8,128)S(1)} %get-tuple-element.59.refs_2_.refs_11_), channel_id=1, source_target_pairs={{0,1},{1,0},{2,3},{3,2},{4,5},{5,4},{6,7},{7,6},{8,9},{9,8},{10,11... | collective-permute-start | bytes 24584 | tf_op jit(solution)/shard_map/ppermute | solution.py:394
  16.3 27.8 %collective-permute-start.5 = (f32[16,128]{1,0:T(8,128)S(1)}, f32[16,128]{1,0:T(8,128)S(1)}, u32[]{:S(2)}, u32[]{:S(2)}) collective-permute-start(f32[16,128]{1,0:T(8,128)S(1)} %get-tuple-element.62.refs_11_), channel_id=1, source_target_pairs={{0,1},{1,0},{2,3},{3,2},{4,5},{5,4},{6,7},{7,6},{8,9},{9,8},{10,11... | collective-permute-start | bytes 24584 | tf_op jit(solution)/shard_map/ppermute | solution.py:397

commit v18 on v17

--- a/solution.py
+++ b/solution.py
@@ -361,11 +361,10 @@
     there = [moved(pack, receivers) for receivers in line_moves(shards // 2)[::-1]][::-1]
     near = [pack] + there
     halves = [joined(near[0], near[1], norm)]
-    for at in range(2, shards // 2, 2):
-        halves.append(joined(near[at], near[at + 1], halves[-1]))
+    found = [tiles(pack, after=halves[0])]
+    halves += [joined(near[at], near[at + 1], found[0][-1]) for at in range(2, shards // 2, 2)]
     far = [swapped(half) for half in halves]
-    found = [tiles(pack, after=halves[-1])]
-    found.append(tiles(*there, after=found[0][-1]))
+    found.append(tiles(*there))
     for half in far[:-1]:
         found.append(tiles(half, after=found[-1][-1]))
     groups = len(found) + 1

time: 53.1 us -> 53.4 us (level)
    ppermute x3, waiting for transfers between devices: 0.55 us -> 0.01 us  [moved(): return lax.ppermute(array, 'src', moves)]
  transfers between devices with their start and end apart: 7 -> 7, of which waited for: 3 -> 2; matrix products, arithmetic and copies ran while one was open for 0% -> 0% of each run, Pallas kernels for 62% -> 62%
where the time goes in v18:
time: 53.4 us; the launch traced here: 53.2 us
  Pallas kernels  34.3 us (64%)
  starting transfers between devices  8.88 us (17%)
  blocking collectives  8.56 us (16%)
  between operations  0.76 us (1%)
  waiting for transfers between devices  0.64 us (1%)
    pallas_call x2, Pallas kernels, columns_of(): call(functools.partial(column_kernel, groups, core), [VM] * (2 * groups +...  27.6 us
    all_to_all x1, blocking collectives, dense_device(): lax.all_to_all(columns, 'src', 0, 0, axis_index_groups=[list(range(shards...  8.56 us
    ppermute x3, starting transfers between devices, moved(): return lax.ppermute(array, 'src', moves)  5.67 us
    pallas_call x5, Pallas kernels, tiles(): call(functools.partial(tile_kernel, len(packs), core), [VM] * (len(packs)...  3.91 us
    ppermute x2, starting transfers between devices, swapped(): return lax.ppermute(array, 'src', [(i, i ^ 1) for i in range(shards)])  3.07 us
    pallas_call x2, Pallas kernels, reading(): call(kernel, [pl.BlockSpec(memory_space=pltpu.HBM)] * len(args), out_shap...  2.18 us
  transfers between devices with their start and end apart: 7, of which 2 were waited for; matrix products, arithmetic and copies ran while one was open for 0% of the time, Pallas kernels for 62%

profile of v18, /device:TPU:0, one launch (start us, length us, event | category | flops | bytes accessed | tf_op | source)
XLA Modules:
  0.0 53.2 jit_solution(3564498241172739625)
XLA Ops:
  0.6 0.8 %shard_map.86 = (f32[1,65,1,128]{3,2,1,0:T(1,128)S(1)}, f32[1,128]{1,0:T(1,128)S(1)}) custom-call(f32[1,64,128]{2,1,0:T(8,128)} %refs_0_.2, f32[1,128]{1,0:T(1,128)} %refs_1_.1, f32[1,128]{1,0:T(1,128)} %refs_2_.1), custom_call_target="tpu_custom_call" | custom-call | tf_op jit(solution)/shard_map/pallas_call | solution.py:303
  1.5 4.1 %collective-permute-start = (f32[1,65,1,128]{3,2,1,0:T(1,128)S(1)}, f32[1,65,1,128]{3,2,1,0:T(1,128)S(1)}, u32[]{:S(2)}, u32[]{:S(2)}) collective-permute-start(f32[1,65,1,128]{3,2,1,0:T(1,128)S(1)} %get-tuple-element.38.refs_0_), channel_id=1, source_target_pairs={{0,8},{2,10},{4,12},{6,14},{8,4},{10,6},{12,0},{14,2},{1,9},{3,11}... | collective-permute-start | bytes 99848 | tf_op jit(solution)/shard_map/ppermute | solution.py:352
  5.5 1.1 %collective-permute-start.1 = (f32[1,65,1,128]{3,2,1,0:T(1,128)S(1)}, f32[1,65,1,128]{3,2,1,0:T(1,128)S(1)}, u32[]{:S(2)}, u32[]{:S(2)}) collective-permute-start(f32[1,65,1,128]{3,2,1,0:T(1,128)S(1)} %get-tuple-element.38.refs_0_), channel_id=1, source_target_pairs={{0,12},{2,14},{4,8},{6,10},{8,0},{10,2},{12,4},{14,6},{1,13},{3,15... | collective-permute-start | bytes 99848 | tf_op jit(solution)/shard_map/ppermute | solution.py:352
  6.6 0.5 collective-permute-start.2
  7.1 1.4 %shard_map.87 = (bf16[8,512,256]{2,1,0:T(8,128)(2,1)S(1)}, f32[16,128]{1,0:T(8,128)S(1)}, f32[8,16,128]{2,1,0:T(8,128)S(1)}, f32[16,128]{1,0:T(8,128)S(1)}) custom-call(f32[16,128]{1,0:T(8,128)} %refs_0_.3, s32[8,16]{1,0:T(8,128)} %bitcast.4, s32[1,16]{1,0:T(1,128)} %bitcast.5, f32[16,64,128]{2,1,0:T(8,128)} %refs_3_.1), custom_call_target="tpu_custom_call" | custom-call | flops 100000000 | bytes 524288 | tf_op jit(solution)/shard_map/pallas_call | solution.py:303
  8.5 0.0 collective-permute-done.refs_1_.refs_0_
  8.5 1.7 %collective-permute-start.3 = (f32[2,65,1,128]{3,2,1,0:T(1,128)S(1)}, f32[2,65,1,128]{3,2,1,0:T(1,128)S(1)}, u32[]{:S(2)}, u32[]{:S(2)}) collective-permute-start(f32[2,65,1,128]{3,2,1,0:T(1,128)S(1)} %shard_map.88.refs_2_), channel_id=1, source_target_pairs={{0,2},{2,0},{4,6},{6,4},{8,10},{10,8},{12,14},{14,12},{1,3},{3,1},... | collective-permute-start | bytes 199688 | tf_op jit(solution)/shard_map/ppermute | solution.py:348
  10.2 0.6 %shard_map.89 = (f32[8,128,256]{2,1,0:T(8,128)S(1)}, bf16[128,512]{1,0:T(8,128)(2,1)S(1)}, f32[1,16,128]{2,1,0:T(8,128)S(1)}, f32[1,16,128]{2,1,0:T(8,128)S(1)}) custom-call(f32[1,65,1,128]{3,2,1,0:T(1,128)S(1)} %get-tuple-element.38.refs_0_, bf16[8,512,256]{2,1,0:T(8,128)(2,1)S(1)} %get-tuple-element.39.refs_1_.refs_3_.refs_8_, ...), custom_call_target="tpu_custom_call" | custom-call | flops 268435456 | bytes 524288 | tf_op jit(solution)/shard_map/pallas_call | solution.py:335
  10.8 0.0 collective-permute-done.1.refs_1_.refs_0_
  10.8 0.0 collective-permute-done.2.refs_2_.refs_1_
  10.8 1.4 %collective-permute-start.4 = (f32[2,65,1,128]{3,2,1,0:T(1,128)S(1)}, f32[2,65,1,128]{3,2,1,0:T(1,128)S(1)}, u32[]{:S(2)}, u32[]{:S(2)}) collective-permute-start(f32[2,65,1,128]{3,2,1,0:T(1,128)S(1)} %shard_map.92), channel_id=1, source_target_pairs={{0,2},{2,0},{4,6},{6,4},{8,10},{10,8},{12,14},{14,12},{1,3},{3,1},... | collective-permute-start | bytes 199688 | tf_op jit(solution)/shard_map/ppermute | solution.py:348
  12.2 1.5 %shard_map.90 = (f32[8,384,256]{2,1,0:T(8,128)S(1)}, bf16[384,512]{1,0:T(8,128)(2,1)S(1)}, f32[3,16,128]{2,1,0:T(8,128)S(1)}, f32[3,16,128]{2,1,0:T(8,128)S(1)}) custom-call(f32[1,65,1,128]{3,2,1,0:T(1,128)S(1)} %collective-permute-done.refs_1_.refs_0_, f32[1,65,1,128]{3,2,1,0:T(1,128)S(1)} %collective-permute-done.1.refs_1_.refs_0_, ...), custom_call_target="tpu_custom_call" | custom-call | flops 805306368 | bytes 524288 | tf_op jit(solution)/shard_map/pallas_call | solution.py:335
  13.8 0.0 collective-permute-done.3.refs_0_
  13.8 0.9 %shard_map.91 = (f32[8,256,256]{2,1,0:T(8,128)S(1)}, bf16[256,512]{1,0:T(8,128)(2,1)S(1)}, f32[2,16,128]{2,1,0:T(8,128)S(1)}, f32[2,16,128]{2,1,0:T(8,128)S(1)}) custom-call(f32[2,65,1,128]{3,2,1,0:T(1,128)S(1)} %collective-permute-done.3.refs_0_, bf16[8,512,256]{2,1,0:T(8,128)(2,1)S(1)} %get-tuple-element.39.refs_1_.refs_3_.refs_8_, ...), custom_call_target="tpu_custom_call" | custom-call | flops 536870912 | bytes 524288 | tf_op jit(solution)/shard_map/pallas_call | solution.py:335
  14.7 0.5 collective-permute-done.4.refs_0_
  15.2 0.1 collective-permute-start.6
  15.3 0.9 %shard_map.95 = (f32[8,256,256]{2,1,0:T(8,128)S(1)}, bf16[256,512]{1,0:T(8,128)(2,1)S(1)}, f32[2,16,128]{2,1,0:T(8,128)S(1)}, f32[2,16,128]{2,1,0:T(8,128)S(1)}) custom-call(f32[2,65,1,128]{3,2,1,0:T(1,128)S(1)} %collective-permute-done.4.refs_0_, bf16[8,512,256]{2,1,0:T(8,128)(2,1)S(1)} %get-tuple-element.39.refs_1_.refs_3_.refs_8_, ...), custom_call_target="tpu_custom_call" | custom-call | flops 536870912 | bytes 524288 | tf_op jit(solution)/shard_map/pallas_call | solution.py:335
  16.2 0.1 collective-permute-start.5
  16.3 0.1 collective-permute-done.6.refs_12_
  16.4 27.5 %shard_map.97 = (f32[16,128]{1,0:T(8,128)S(1)}, f32[8,1,128]{2,1,0:T(1,128)S(1)}) custom-call(f32[8,128,256]{2,1,0:T(8,128)S(1)} %get-tuple-element.41.refs_0_, f32[8,384,256]{2,1,0:T(8,128)S(1)} %get-tuple-element.42.refs_1_, f32[8,256,256]{2,1,0:T(8,128)S(1)} %get-tuple-element.44.refs_2_, f32[8,256,256]{2,1,0:T(8,128)S(1)} %get-tuple-element.64.refs_3_, ...), custom_call_target="tpu_custom_call" | custom-call | flops 1000000000 | bytes 524288 | tf_op jit(solution)/shard_map/pallas_call | solution.py:382
  44.0 0.0 collective-permute-done.5.refs_12_
  44.0 8.6 %all_to_all.5.values_ref = f32[8,1,128]{2,1,0:T(1,128)S(1)} all-to-all(f32[8,1,128]{2,1,0:T(1,128)S(1)} %get-tuple-element.69), channel_id=1, replica_groups={{14,12,10,8,6,4,2,0},{15,13,11,9,7,5,3,1},{30,28,26,24,22,20,18,16},{31..., dimensions={0} | all-to-all | bytes 8192 | tf_op jit(solution)/shard_map/all_to_all | solution.py:399
  52.6 0.6 %shard_map.99 = (f32[1,128]{1,0:T(1,128)}, f32[16,128]{1,0:T(8,128)}) custom-call(f32[8,1,128]{2,1,0:T(1,128)S(1)} %all_to_all.5.values_ref, f32[1,128]{1,0:T(1,128)S(1)} %get-tuple-element.70.weight_ref, f32[16,128]{1,0:T(8,128)S(1)} %get-tuple-element.71.poten_ref), custom_call_target="tpu_custom_call" | custom-call | tf_op jit(solution)/shard_map/pallas_call | solution.py:401
  (6 shorter events, 0.1 us)
Async XLA Ops:
  1.5 7.0 %collective-permute-start = (f32[1,65,1,128]{3,2,1,0:T(1,128)S(1)}, f32[1,65,1,128]{3,2,1,0:T(1,128)S(1)}, u32[]{:S(2)}, u32[]{:S(2)}) collective-permute-start(f32[1,65,1,128]{3,2,1,0:T(1,128)S(1)} %get-tuple-element.38.refs_0_), channel_id=1, source_target_pairs={{0,8},{2,10},{4,12},{6,14},{8,4},{10,6},{12,0},{14,2},{1,9},{3,11}... | collective-permute-start | bytes 99848 | tf_op jit(solution)/shard_map/ppermute | solution.py:352
  5.5 5.2 %collective-permute-start.1 = (f32[1,65,1,128]{3,2,1,0:T(1,128)S(1)}, f32[1,65,1,128]{3,2,1,0:T(1,128)S(1)}, u32[]{:S(2)}, u32[]{:S(2)}) collective-permute-start(f32[1,65,1,128]{3,2,1,0:T(1,128)S(1)} %get-tuple-element.38.refs_0_), channel_id=1, source_target_pairs={{0,12},{2,14},{4,8},{6,10},{8,0},{10,2},{12,4},{14,6},{1,13},{3,15... | collective-permute-start | bytes 99848 | tf_op jit(solution)/shard_map/ppermute | solution.py:352
  6.6 4.2 %collective-permute-start.2 = (f32[1,65,1,128]{3,2,1,0:T(1,128)S(1)}, f32[1,65,1,128]{3,2,1,0:T(1,128)S(1)}, u32[]{:S(2)}, u32[]{:S(2)}) collective-permute-start(f32[1,65,1,128]{3,2,1,0:T(1,128)S(1)} %get-tuple-element.38.refs_0_), channel_id=1, source_target_pairs={{0,4},{2,6},{4,0},{6,2},{8,12},{10,14},{12,8},{14,10},{1,5},{3,7},... | collective-permute-start | bytes 99848 | tf_op jit(solution)/shard_map/ppermute | solution.py:352
  8.5 5.2 %collective-permute-start.3 = (f32[2,65,1,128]{3,2,1,0:T(1,128)S(1)}, f32[2,65,1,128]{3,2,1,0:T(1,128)S(1)}, u32[]{:S(2)}, u32[]{:S(2)}) collective-permute-start(f32[2,65,1,128]{3,2,1,0:T(1,128)S(1)} %shard_map.88.refs_2_), channel_id=1, source_target_pairs={{0,2},{2,0},{4,6},{6,4},{8,10},{10,8},{12,14},{14,12},{1,3},{3,1},... | collective-permute-start | bytes 199688 | tf_op jit(solution)/shard_map/ppermute | solution.py:348
  10.8 4.3 %collective-permute-start.4 = (f32[2,65,1,128]{3,2,1,0:T(1,128)S(1)}, f32[2,65,1,128]{3,2,1,0:T(1,128)S(1)}, u32[]{:S(2)}, u32[]{:S(2)}) collective-permute-start(f32[2,65,1,128]{3,2,1,0:T(1,128)S(1)} %shard_map.92), channel_id=1, source_target_pairs={{0,2},{2,0},{4,6},{6,4},{8,10},{10,8},{12,14},{14,12},{1,3},{3,1},... | collective-permute-start | bytes 199688 | tf_op jit(solution)/shard_map/ppermute | solution.py:348
  15.2 1.2 %collective-permute-start.6 = (f32[16,128]{1,0:T(8,128)S(1)}, f32[16,128]{1,0:T(8,128)S(1)}, u32[]{:S(2)}, u32[]{:S(2)}) collective-permute-start(f32[16,128]{1,0:T(8,128)S(1)} %get-tuple-element.59.refs_2_.refs_11_), channel_id=1, source_target_pairs={{0,1},{1,0},{2,3},{3,2},{4,5},{5,4},{6,7},{7,6},{8,9},{9,8},{10,11... | collective-permute-start | bytes 24584 | tf_op jit(solution)/shard_map/ppermute | solution.py:393
  16.2 27.8 %collective-permute-start.5 = (f32[16,128]{1,0:T(8,128)S(1)}, f32[16,128]{1,0:T(8,128)S(1)}, u32[]{:S(2)}, u32[]{:S(2)}) collective-permute-start(f32[16,128]{1,0:T(8,128)S(1)} %get-tuple-element.62.refs_11_), channel_id=1, source_target_pairs={{0,1},{1,0},{2,3},{3,2},{4,5},{5,4},{6,7},{7,6},{8,9},{9,8},{10,11... | collective-permute-start | bytes 24584 | tf_op jit(solution)/shard_map/ppermute | solution.py:396

commit v19 on v17

--- a/solution.py
+++ b/solution.py
@@ -175,7 +175,7 @@
                 total_ref[place, pl.ds(2 * pair + half, 1), :] = total[:, lanes]
         return carry
 
-    lax.fori_loop(0, pairs, body, 0, unroll=min(pairs, 16 // blocks & -4 or 2))
+    lax.fori_loop(0, pairs, body, 0, unroll=max(1, min(pairs, 32 // blocks)))
 
 
 def row_kernel(groups, *refs):
@@ -364,8 +364,7 @@
     for at in range(2, shards // 2, 2):
         halves.append(joined(near[at], near[at + 1], halves[-1]))
     far = [swapped(half) for half in halves]
-    found = [tiles(pack, after=halves[-1])]
-    found.append(tiles(*there, after=found[0][-1]))
+    found = [tiles(*near, after=halves[-1])]
     for half in far[:-1]:
         found.append(tiles(half, after=found[-1][-1]))
     groups = len(found) + 1

time: 53.1 us -> 53 us (level)
    pallas_call x5 -> x4, Pallas kernels: 3.92 us -> 3.42 us  [tiles(): call(functools.partial(tile_kernel, len(packs), core), [VM] * (len(packs)...]
  transfers between devices with their start and end apart: 7 -> 7, of which waited for: 3 -> 4; matrix products, arithmetic and copies ran while one was open for 0% -> 0% of each run, Pallas kernels for 62% -> 61%
where the time goes in v19:
time: 53 us; the launch traced here: 52.8 us
  Pallas kernels  33.9 us (64%)
  starting transfers between devices  8.96 us (17%)
  blocking collectives  8.28 us (16%)
  waiting for transfers between devices  0.94 us (2%)
  between operations  0.73 us (1%)
    pallas_call x2, Pallas kernels, columns_of(): call(functools.partial(column_kernel, groups, core), [VM] * (2 * groups +...  27.6 us
    all_to_all x1, blocking collectives, dense_device(): lax.all_to_all(columns, 'src', 0, 0, axis_index_groups=[list(range(shards...  8.28 us
    ppermute x3, starting transfers between devices, moved(): return lax.ppermute(array, 'src', moves)  5.67 us
    pallas_call x4, Pallas kernels, tiles(): call(functools.partial(tile_kernel, len(packs), core), [VM] * (len(packs)...  3.42 us
    ppermute x2, starting transfers between devices, swapped(): return lax.ppermute(array, 'src', [(i, i ^ 1) for i in range(shards)])  3.15 us
    pallas_call x2, Pallas kernels, reading(): call(kernel, [pl.BlockSpec(memory_space=pltpu.HBM)] * len(args), out_shap...  2.18 us
  transfers between devices with their start and end apart: 7, of which 4 were waited for; matrix products, arithmetic and copies ran while one was open for 0% of the time, Pallas kernels for 61%

profile of v19, /device:TPU:0, one launch (start us, length us, event | category | flops | bytes accessed | tf_op | source)
XLA Modules:
  0.0 52.8 jit_solution(12412478510574414319)
XLA Ops:
  0.6 0.8 %shard_map.86 = (f32[1,65,1,128]{3,2,1,0:T(1,128)S(1)}, f32[1,128]{1,0:T(1,128)S(1)}) custom-call(f32[1,64,128]{2,1,0:T(8,128)} %refs_0_.2, f32[1,128]{1,0:T(1,128)} %refs_1_.1, f32[1,128]{1,0:T(1,128)} %refs_2_.1), custom_call_target="tpu_custom_call" | custom-call | tf_op jit(solution)/shard_map/pallas_call | solution.py:303
  1.5 4.1 %collective-permute-start = (f32[1,65,1,128]{3,2,1,0:T(1,128)S(1)}, f32[1,65,1,128]{3,2,1,0:T(1,128)S(1)}, u32[]{:S(2)}, u32[]{:S(2)}) collective-permute-start(f32[1,65,1,128]{3,2,1,0:T(1,128)S(1)} %get-tuple-element.34.refs_0_), channel_id=1, source_target_pairs={{0,8},{2,10},{4,12},{6,14},{8,4},{10,6},{12,0},{14,2},{1,9},{3,11}... | collective-permute-start | bytes 99848 | tf_op jit(solution)/shard_map/ppermute | solution.py:352
  5.5 1.1 %collective-permute-start.1 = (f32[1,65,1,128]{3,2,1,0:T(1,128)S(1)}, f32[1,65,1,128]{3,2,1,0:T(1,128)S(1)}, u32[]{:S(2)}, u32[]{:S(2)}) collective-permute-start(f32[1,65,1,128]{3,2,1,0:T(1,128)S(1)} %get-tuple-element.34.refs_0_), channel_id=1, source_target_pairs={{0,12},{2,14},{4,8},{6,10},{8,0},{10,2},{12,4},{14,6},{1,13},{3,15... | collective-permute-start | bytes 99848 | tf_op jit(solution)/shard_map/ppermute | solution.py:352
  6.6 0.5 collective-permute-start.2
  7.1 1.4 %shard_map.87 = (bf16[8,512,256]{2,1,0:T(8,128)(2,1)S(1)}, f32[16,128]{1,0:T(8,128)S(1)}, f32[8,16,128]{2,1,0:T(8,128)S(1)}, f32[16,128]{1,0:T(8,128)S(1)}) custom-call(f32[16,128]{1,0:T(8,128)} %refs_0_.3, s32[8,16]{1,0:T(8,128)} %bitcast.4, s32[1,16]{1,0:T(1,128)} %bitcast.5, f32[16,64,128]{2,1,0:T(8,128)} %refs_3_.1), custom_call_target="tpu_custom_call" | custom-call | flops 100000000 | bytes 524288 | tf_op jit(solution)/shard_map/pallas_call | solution.py:303
  8.5 0.0 collective-permute-done.refs_1_
  8.5 1.7 %collective-permute-start.3 = (f32[2,65,1,128]{3,2,1,0:T(1,128)S(1)}, f32[2,65,1,128]{3,2,1,0:T(1,128)S(1)}, u32[]{:S(2)}, u32[]{:S(2)}) collective-permute-start(f32[2,65,1,128]{3,2,1,0:T(1,128)S(1)} %shard_map.88.refs_2_), channel_id=1, source_target_pairs={{0,2},{2,0},{4,6},{6,4},{8,10},{10,8},{12,14},{14,12},{1,3},{3,1},... | collective-permute-start | bytes 199688 | tf_op jit(solution)/shard_map/ppermute | solution.py:348
  10.2 0.2 collective-permute-done.1.refs_0_.refs_2_
  10.4 0.3 collective-permute-done.2.refs_1_.refs_3_
  10.7 1.5 %collective-permute-start.4 = (f32[2,65,1,128]{3,2,1,0:T(1,128)S(1)}, f32[2,65,1,128]{3,2,1,0:T(1,128)S(1)}, u32[]{:S(2)}, u32[]{:S(2)}) collective-permute-start(f32[2,65,1,128]{3,2,1,0:T(1,128)S(1)} %shard_map.89.refs_5_), channel_id=1, source_target_pairs={{0,2},{2,0},{4,6},{6,4},{8,10},{10,8},{12,14},{14,12},{1,3},{3,1},... | collective-permute-start | bytes 199688 | tf_op jit(solution)/shard_map/ppermute | solution.py:348
  12.2 1.6 %shard_map.90 = (f32[8,512,256]{2,1,0:T(8,128)S(1)}, bf16[512,512]{1,0:T(8,128)(2,1)S(1)}, f32[4,16,128]{2,1,0:T(8,128)S(1)}, f32[4,16,128]{2,1,0:T(8,128)S(1)}) custom-call(f32[1,65,1,128]{3,2,1,0:T(1,128)S(1)} %get-tuple-element.34.refs_0_, f32[1,65,1,128]{3,2,1,0:T(1,128)S(1)} %collective-permute-done.refs_1_, ...), custom_call_target="tpu_custom_call" | custom-call | flops 1073741824 | bytes 524288 | tf_op jit(solution)/shard_map/pallas_call | solution.py:335
  13.8 0.0 collective-permute-done.3.refs_0_
  13.9 0.9 %shard_map.91 = (f32[8,256,256]{2,1,0:T(8,128)S(1)}, bf16[256,512]{1,0:T(8,128)(2,1)S(1)}, f32[2,16,128]{2,1,0:T(8,128)S(1)}, f32[2,16,128]{2,1,0:T(8,128)S(1)}) custom-call(f32[2,65,1,128]{3,2,1,0:T(1,128)S(1)} %collective-permute-done.3.refs_0_, bf16[8,512,256]{2,1,0:T(8,128)(2,1)S(1)} %get-tuple-element.35.refs_4_.refs_1_.refs_6_, ...), custom_call_target="tpu_custom_call" | custom-call | flops 536870912 | bytes 524288 | tf_op jit(solution)/shard_map/pallas_call | solution.py:335
  14.7 0.3 collective-permute-done.4.refs_0_
  15.0 0.1 collective-permute-start.6
  15.1 0.9 %shard_map.94 = (f32[8,256,256]{2,1,0:T(8,128)S(1)}, bf16[256,512]{1,0:T(8,128)(2,1)S(1)}, f32[2,16,128]{2,1,0:T(8,128)S(1)}, f32[2,16,128]{2,1,0:T(8,128)S(1)}) custom-call(f32[2,65,1,128]{3,2,1,0:T(1,128)S(1)} %collective-permute-done.4.refs_0_, bf16[8,512,256]{2,1,0:T(8,128)(2,1)S(1)} %get-tuple-element.35.refs_4_.refs_1_.refs_6_, ...), custom_call_target="tpu_custom_call" | custom-call | flops 536870912 | bytes 524288 | tf_op jit(solution)/shard_map/pallas_call | solution.py:335
  16.1 0.1 collective-permute-start.5
  16.2 0.1 collective-permute-done.6.refs_10_
  16.3 27.5 %shard_map.96 = (f32[16,128]{1,0:T(8,128)S(1)}, f32[8,1,128]{2,1,0:T(1,128)S(1)}) custom-call(f32[8,512,256]{2,1,0:T(8,128)S(1)} %get-tuple-element.37.refs_0_, f32[8,256,256]{2,1,0:T(8,128)S(1)} %get-tuple-element.39.refs_1_, f32[8,256,256]{2,1,0:T(8,128)S(1)} %get-tuple-element.56.refs_2_, bf16[512,512]{1,0:T(8,128)(2,1)S(1)} %get-tuple-element.42.refs_3_, ...), custom_call_target="tpu_custom_call" | custom-call | flops 1000000000 | bytes 524288 | tf_op jit(solution)/shard_map/pallas_call | solution.py:382
  43.8 0.0 collective-permute-done.5.refs_10_
  43.9 8.3 %all_to_all.5.values_ref = f32[8,1,128]{2,1,0:T(1,128)S(1)} all-to-all(f32[8,1,128]{2,1,0:T(1,128)S(1)} %get-tuple-element.61), channel_id=1, replica_groups={{14,12,10,8,6,4,2,0},{15,13,11,9,7,5,3,1},{30,28,26,24,22,20,18,16},{31..., dimensions={0} | all-to-all | bytes 8192 | tf_op jit(solution)/shard_map/all_to_all | solution.py:399
  52.2 0.6 %shard_map.98 = (f32[1,128]{1,0:T(1,128)}, f32[16,128]{1,0:T(8,128)}) custom-call(f32[8,1,128]{2,1,0:T(1,128)S(1)} %all_to_all.5.values_ref, f32[1,128]{1,0:T(1,128)S(1)} %get-tuple-element.62.weight_ref, f32[16,128]{1,0:T(8,128)S(1)} %get-tuple-element.63.poten_ref), custom_call_target="tpu_custom_call" | custom-call | tf_op jit(solution)/shard_map/pallas_call | solution.py:401
  (6 shorter events, 0.1 us)
Async XLA Ops:
  1.5 7.0 %collective-permute-start = (f32[1,65,1,128]{3,2,1,0:T(1,128)S(1)}, f32[1,65,1,128]{3,2,1,0:T(1,128)S(1)}, u32[]{:S(2)}, u32[]{:S(2)}) collective-permute-start(f32[1,65,1,128]{3,2,1,0:T(1,128)S(1)} %get-tuple-element.34.refs_0_), channel_id=1, source_target_pairs={{0,8},{2,10},{4,12},{6,14},{8,4},{10,6},{12,0},{14,2},{1,9},{3,11}... | collective-permute-start | bytes 99848 | tf_op jit(solution)/shard_map/ppermute | solution.py:352
  5.5 4.8 %collective-permute-start.1 = (f32[1,65,1,128]{3,2,1,0:T(1,128)S(1)}, f32[1,65,1,128]{3,2,1,0:T(1,128)S(1)}, u32[]{:S(2)}, u32[]{:S(2)}) collective-permute-start(f32[1,65,1,128]{3,2,1,0:T(1,128)S(1)} %get-tuple-element.34.refs_0_), channel_id=1, source_target_pairs={{0,12},{2,14},{4,8},{6,10},{8,0},{10,2},{12,4},{14,6},{1,13},{3,15... | collective-permute-start | bytes 99848 | tf_op jit(solution)/shard_map/ppermute | solution.py:352
  6.6 4.1 %collective-permute-start.2 = (f32[1,65,1,128]{3,2,1,0:T(1,128)S(1)}, f32[1,65,1,128]{3,2,1,0:T(1,128)S(1)}, u32[]{:S(2)}, u32[]{:S(2)}) collective-permute-start(f32[1,65,1,128]{3,2,1,0:T(1,128)S(1)} %get-tuple-element.34.refs_0_), channel_id=1, source_target_pairs={{0,4},{2,6},{4,0},{6,2},{8,12},{10,14},{12,8},{14,10},{1,5},{3,7},... | collective-permute-start | bytes 99848 | tf_op jit(solution)/shard_map/ppermute | solution.py:352
  8.5 5.3 %collective-permute-start.3 = (f32[2,65,1,128]{3,2,1,0:T(1,128)S(1)}, f32[2,65,1,128]{3,2,1,0:T(1,128)S(1)}, u32[]{:S(2)}, u32[]{:S(2)}) collective-permute-start(f32[2,65,1,128]{3,2,1,0:T(1,128)S(1)} %shard_map.88.refs_2_), channel_id=1, source_target_pairs={{0,2},{2,0},{4,6},{6,4},{8,10},{10,8},{12,14},{14,12},{1,3},{3,1},... | collective-permute-start | bytes 199688 | tf_op jit(solution)/shard_map/ppermute | solution.py:348
  10.7 4.3 %collective-permute-start.4 = (f32[2,65,1,128]{3,2,1,0:T(1,128)S(1)}, f32[2,65,1,128]{3,2,1,0:T(1,128)S(1)}, u32[]{:S(2)}, u32[]{:S(2)}) collective-permute-start(f32[2,65,1,128]{3,2,1,0:T(1,128)S(1)} %shard_map.89.refs_5_), channel_id=1, source_target_pairs={{0,2},{2,0},{4,6},{6,4},{8,10},{10,8},{12,14},{14,12},{1,3},{3,1},... | collective-permute-start | bytes 199688 | tf_op jit(solution)/shard_map/ppermute | solution.py:348
  15.0 1.2 %collective-permute-start.6 = (f32[16,128]{1,0:T(8,128)S(1)}, f32[16,128]{1,0:T(8,128)S(1)}, u32[]{:S(2)}, u32[]{:S(2)}) collective-permute-start(f32[16,128]{1,0:T(8,128)S(1)} %get-tuple-element.51.refs_2_.refs_9_), channel_id=1, source_target_pairs={{0,1},{1,0},{2,3},{3,2},{4,5},{5,4},{6,7},{7,6},{8,9},{9,8},{10,11... | collective-permute-start | bytes 24584 | tf_op jit(solution)/shard_map/ppermute | solution.py:393
  16.1 27.8 %collective-permute-start.5 = (f32[16,128]{1,0:T(8,128)S(1)}, f32[16,128]{1,0:T(8,128)S(1)}, u32[]{:S(2)}, u32[]{:S(2)}) collective-permute-start(f32[16,128]{1,0:T(8,128)S(1)} %get-tuple-element.54.refs_9_), channel_id=1, source_target_pairs={{0,1},{1,0},{2,3},{3,2},{4,5},{5,4},{6,7},{7,6},{8,9},{9,8},{10,11... | collective-permute-start | bytes 24584 | tf_op jit(solution)/shard_map/ppermute | solution.py:396

commit v20 on v19

--- a/solution.py
+++ b/solution.py
@@ -126,15 +126,8 @@
         pl.when(jnp.logical_not(here))(idle)
 
 
-def tile_kernel(parts, core, *refs):
-    peak_ref, total_ref = refs[-2:]
-
-    def idle():
-        peak_ref[...] = jnp.zeros(peak_ref.shape, jnp.float32)
-        total_ref[...] = jnp.zeros(total_ref.shape, jnp.float32)
-
-    ins = refs[: parts + 1] + refs[-4:]
-    on_core(core, functools.partial(make_tiles, parts, *ins), idle)
+def tile_kernel(parts, *refs):
+    make_tiles(parts, *refs[: parts + 1], *refs[-4:])
 
 
 def make_tiles(parts, *refs):
@@ -190,6 +183,20 @@
     top = functools.reduce(jnp.maximum, [peaks_ref[index] for index in range(place)])
     summed = sum(total * jnp.exp2(peaks_ref[index] - top) for index, total in enumerate(totals))
     rowsum_ref[...] = top + jnp.log2(summed)
+
+
+def last_kernel(groups, core, *refs):
+    packs_ref, wide_ref, _, mask_ref = refs[:4]
+    peak_refs, total_refs = refs[4 : 3 + groups], refs[3 + groups : 2 + 2 * groups]
+    exps_ref, tall_ref, peak_ref, total_ref, peaks_ref, rowsum_ref = refs[2 + 2 * groups :]
+
+    def idle():
+        peak_ref[...] = jnp.zeros(peak_ref.shape, jnp.float32)
+        total_ref[...] = jnp.zeros(total_ref.shape, jnp.float32)
+
+    work = functools.partial(make_tiles, 1, packs_ref, wide_ref, exps_ref, tall_ref, peak_ref, total_ref)
+    on_core(core, work, idle)
+    row_kernel(groups, mask_ref, *peak_refs, peak_ref, *total_refs, total_ref, peaks_ref, rowsum_ref)
 
 
 def across(column):
@@ -329,20 +336,22 @@
         cost_of(10**8),
     )
 
-    def tiles(*packs, core=None, after=None):
+    def tile_shapes(blocks):
+        return [
+            in_vmem((pairs, blocks * cells, wide), jnp.float32),
+            in_vmem((blocks * cells, 8 * depth), jnp.bfloat16),
+            in_vmem((blocks, rows, cells), jnp.float32),
+            in_vmem((blocks, rows, cells), jnp.float32),
+        ]
+
+    def tiles(*packs, after):
         blocks = sum(pack.shape[0] for pack in packs)
-        more = [] if after is None else [after]
         return call(
-            functools.partial(tile_kernel, len(packs), core),
-            [VM] * (len(packs) + 1) + [pl.BlockSpec(memory_space=pl.ANY)] * len(more),
-            [
-                in_vmem((pairs, blocks * cells, wide), jnp.float32),
-                in_vmem((blocks * cells, 8 * depth), jnp.bfloat16),
-                in_vmem((blocks, rows, cells), jnp.float32),
-                in_vmem((blocks, rows, cells), jnp.float32),
-            ],
+            functools.partial(tile_kernel, len(packs)),
+            [VM] * (len(packs) + 1) + [pl.BlockSpec(memory_space=pl.ANY)],
+            tile_shapes(blocks),
             cost=cost_of(2 * blocks * cells * pairs * wide * 8 * depth),
-        )(*packs, wide_feat, *more)
+        )(*packs, wide_feat, after)
 
     def swapped(array):
         return lax.ppermute(array, "src", [(i, i ^ 1) for i in range(shards)])
@@ -369,13 +378,16 @@
         found.append(tiles(half, after=found[-1][-1]))
     groups = len(found) + 1
 
-    def log_sums(last):
-        _, _, peaks, totals = zip(*found, last)
-        return call(
-            functools.partial(row_kernel, groups),
-            [VM] * (1 + 2 * groups),
-            [in_vmem((shards, rows, cells), jnp.float32), in_vmem((rows, cells), jnp.float32)],
-        )(mask, *peaks, *totals)
+    def last_tiles(core, after):
+        _, _, peaks, totals = zip(*found)
+        blocks = far[-1].shape[0]
+        *last, peaks, own = call(
+            functools.partial(last_kernel, groups, core),
+            [VM] * 2 + [pl.BlockSpec(memory_space=pl.ANY)] + [VM] * (2 * groups - 1),
+            tile_shapes(blocks) + [in_vmem((shards, rows, cells), jnp.float32), in_vmem((rows, cells), jnp.float32)],
+            cost=cost_of(2 * blocks * cells * pairs * wide * 8 * depth),
+        )(far[-1], wide_feat, after, mask, *peaks, *totals)
+        return last, peaks, own
 
     def columns_of(core, last, peaks, own, other, given):
         exps, tall, _, _ = zip(*found, last)
@@ -388,11 +400,9 @@
         )(*exps, *tall, wide_feat, peaks, mask, own, other, mass, norm, *given)
 
     between = [(0, 1), (1, 0)]
-    last_one = tiles(far[-1], core=1, after=found[-1][-1])
-    peaks_one, own_one = log_sums(last_one)
+    last_one, peaks_one, own_one = last_tiles(1, found[-1][-1])
     other_zero = lax.ppermute(own_one, "tgt", between)
-    last_zero = tiles(far[-1], core=0, after=own_one)
-    peaks_zero, own_zero = log_sums(last_zero)
+    last_zero, peaks_zero, own_zero = last_tiles(0, own_one)
     other_one = lax.ppermute(own_zero, "tgt", between)
     given = columns_of(0, last_zero, peaks_zero, own_zero, other_zero, [])
     potential_src, columns = columns_of(1, last_one, peaks_one, own_one, other_one, given)

time: 53 us -> 53.9 us (1.017)
  Pallas kernels: 33.9 us -> 35 us
    pallas_call x6 -> x4, Pallas kernels: 3.49 us -> 4.62 us  [the longest x2 2.52 us: tiles(): call(functools.partial(tile_kernel, len(packs)), [VM] * (len(packs) + 1)...]
  transfers between devices with their start and end apart: 7 -> 7, of which waited for: 4 -> 3; matrix products, arithmetic and copies ran while one was open for 0% -> 0% of each run, Pallas kernels for 61% -> 61%
where the time goes in v20:
time: 53.9 us; the launch traced here: 53.6 us
  Pallas kernels  35 us (65%)
  starting transfers between devices  8.82 us (16%)
  blocking collectives  8.28 us (15%)
  waiting for transfers between devices  0.81 us (2%)
  between operations  0.7 us (1%)
    pallas_call x2, Pallas kernels, columns_of(): call(functools.partial(column_kernel, groups, core), [VM] * (2 * groups +...  27.6 us
    all_to_all x1, blocking collectives, dense_device(): lax.all_to_all(columns, 'src', 0, 0, axis_index_groups=[list(range(shards...  8.28 us
    ppermute x3, starting transfers between devices, moved(): return lax.ppermute(array, 'src', moves)  5.67 us
    ppermute x2, starting transfers between devices, swapped(): return lax.ppermute(array, 'src', [(i, i ^ 1) for i in range(shards)])  3.15 us
    pallas_call x2, Pallas kernels, tiles(): call(functools.partial(tile_kernel, len(packs)), [VM] * (len(packs) + 1)...  2.52 us
    pallas_call x2, Pallas kernels, reading(): call(kernel, [pl.BlockSpec(memory_space=pltpu.HBM)] * len(args), out_shap...  2.18 us
    pallas_call x2, Pallas kernels, last_tiles(): call(functools.partial(last_kernel, groups, core), [VM] * 2 + [pl.BlockSp...  2.11 us
  transfers between devices with their start and end apart: 7, of which 3 were waited for; matrix products, arithmetic and copies ran while one was open for 0% of the time, Pallas kernels for 61%

profile of v20, /device:TPU:0, one launch (start us, length us, event | category | flops | bytes accessed | tf_op | source)
XLA Modules:
  0.0 53.6 jit_solution(9937127017943656386)
XLA Ops:
  0.6 0.8 %shard_map.86 = (f32[1,65,1,128]{3,2,1,0:T(1,128)S(1)}, f32[1,128]{1,0:T(1,128)S(1)}) custom-call(f32[1,64,128]{2,1,0:T(8,128)} %refs_0_.2, f32[1,128]{1,0:T(1,128)} %refs_1_.1, f32[1,128]{1,0:T(1,128)} %refs_2_.1), custom_call_target="tpu_custom_call" | custom-call | tf_op jit(solution)/shard_map/pallas_call | solution.py:310
  1.5 4.1 %collective-permute-start = (f32[1,65,1,128]{3,2,1,0:T(1,128)S(1)}, f32[1,65,1,128]{3,2,1,0:T(1,128)S(1)}, u32[]{:S(2)}, u32[]{:S(2)}) collective-permute-start(f32[1,65,1,128]{3,2,1,0:T(1,128)S(1)} %get-tuple-element.30.refs_0_), channel_id=1, source_target_pairs={{0,8},{2,10},{4,12},{6,14},{8,4},{10,6},{12,0},{14,2},{1,9},{3,11}... | collective-permute-start | bytes 99848 | tf_op jit(solution)/shard_map/ppermute | solution.py:361
  5.5 1.1 %collective-permute-start.1 = (f32[1,65,1,128]{3,2,1,0:T(1,128)S(1)}, f32[1,65,1,128]{3,2,1,0:T(1,128)S(1)}, u32[]{:S(2)}, u32[]{:S(2)}) collective-permute-start(f32[1,65,1,128]{3,2,1,0:T(1,128)S(1)} %get-tuple-element.30.refs_0_), channel_id=1, source_target_pairs={{0,12},{2,14},{4,8},{6,10},{8,0},{10,2},{12,4},{14,6},{1,13},{3,15... | collective-permute-start | bytes 99848 | tf_op jit(solution)/shard_map/ppermute | solution.py:361
  6.6 0.5 collective-permute-start.2
  7.1 1.4 %shard_map.87 = (bf16[8,512,256]{2,1,0:T(8,128)(2,1)S(1)}, f32[16,128]{1,0:T(8,128)S(1)}, f32[8,16,128]{2,1,0:T(8,128)S(1)}, f32[16,128]{1,0:T(8,128)S(1)}) custom-call(f32[16,128]{1,0:T(8,128)} %refs_0_.3, s32[8,16]{1,0:T(8,128)} %bitcast.4, s32[1,16]{1,0:T(1,128)} %bitcast.5, f32[16,64,128]{2,1,0:T(8,128)} %refs_3_.1), custom_call_target="tpu_custom_call" | custom-call | flops 100000000 | bytes 524288 | tf_op jit(solution)/shard_map/pallas_call | solution.py:310
  8.5 0.0 collective-permute-done.refs_1_
  8.5 1.7 %collective-permute-start.3 = (f32[2,65,1,128]{3,2,1,0:T(1,128)S(1)}, f32[2,65,1,128]{3,2,1,0:T(1,128)S(1)}, u32[]{:S(2)}, u32[]{:S(2)}) collective-permute-start(f32[2,65,1,128]{3,2,1,0:T(1,128)S(1)} %shard_map.88.refs_2_), channel_id=1, source_target_pairs={{0,2},{2,0},{4,6},{6,4},{8,10},{10,8},{12,14},{14,12},{1,3},{3,1},... | collective-permute-start | bytes 199688 | tf_op jit(solution)/shard_map/ppermute | solution.py:357
  10.2 0.2 collective-permute-done.1.refs_0_.refs_2_
  10.4 0.3 collective-permute-done.2.refs_1_.refs_3_
  10.7 1.5 %collective-permute-start.4 = (f32[2,65,1,128]{3,2,1,0:T(1,128)S(1)}, f32[2,65,1,128]{3,2,1,0:T(1,128)S(1)}, u32[]{:S(2)}, u32[]{:S(2)}) collective-permute-start(f32[2,65,1,128]{3,2,1,0:T(1,128)S(1)} %shard_map.89.refs_5_), channel_id=1, source_target_pairs={{0,2},{2,0},{4,6},{6,4},{8,10},{10,8},{12,14},{14,12},{1,3},{3,1},... | collective-permute-start | bytes 199688 | tf_op jit(solution)/shard_map/ppermute | solution.py:357
  12.2 1.6 %shard_map.90 = (f32[8,512,256]{2,1,0:T(8,128)S(1)}, bf16[512,512]{1,0:T(8,128)(2,1)S(1)}, f32[4,16,128]{2,1,0:T(8,128)S(1)}, f32[4,16,128]{2,1,0:T(8,128)S(1)}) custom-call(f32[1,65,1,128]{3,2,1,0:T(1,128)S(1)} %get-tuple-element.30.refs_0_, f32[1,65,1,128]{3,2,1,0:T(1,128)S(1)} %collective-permute-done.refs_1_, ...), custom_call_target="tpu_custom_call" | custom-call | flops 1073741824 | bytes 524288 | tf_op jit(solution)/shard_map/pallas_call | solution.py:349
  13.8 0.0 collective-permute-done.3.refs_0_
  13.9 0.9 %shard_map.91 = (f32[8,256,256]{2,1,0:T(8,128)S(1)}, bf16[256,512]{1,0:T(8,128)(2,1)S(1)}, f32[2,16,128]{2,1,0:T(8,128)S(1)}, f32[2,16,128]{2,1,0:T(8,128)S(1)}) custom-call(f32[2,65,1,128]{3,2,1,0:T(1,128)S(1)} %collective-permute-done.3.refs_0_, bf16[8,512,256]{2,1,0:T(8,128)(2,1)S(1)} %get-tuple-element.31.refs_4_.refs_1_.refs_6_, ...), custom_call_target="tpu_custom_call" | custom-call | flops 536870912 | bytes 524288 | tf_op jit(solution)/shard_map/pallas_call | solution.py:349
  14.7 0.3 collective-permute-done.4.refs_0_
  15.0 0.6 %shard_map.92 = (f32[8,256,256]{2,1,0:T(8,128)S(1)}, bf16[256,512]{1,0:T(8,128)(2,1)S(1)}, f32[2,16,128]{2,1,0:T(8,128)}, f32[2,16,128]{2,1,0:T(8,128)}, f32[8,1...) custom-call(f32[2,65,1,128]{3,2,1,0:T(1,128)S(1)} %collective-permute-done.4.refs_0_, ...), custom_call_target="tpu_custom_call" | custom-call | flops 536870912 | bytes 524288 | tf_op jit(solution)/shard_map/pallas_call | solution.py:384
  15.6 0.0 collective-permute-start.6
  15.6 1.5 %shard_map.93 = (f32[8,256,256]{2,1,0:T(8,128)S(1)}, bf16[256,512]{1,0:T(8,128)(2,1)S(1)}, f32[2,16,128]{2,1,0:T(8,128)}, f32[2,16,128]{2,1,0:T(8,128)}, f32[8,1...) custom-call(f32[2,65,1,128]{3,2,1,0:T(1,128)S(1)} %collective-permute-done.4.refs_0_, ...), custom_call_target="tpu_custom_call" | custom-call | flops 536870912 | bytes 524288 | tf_op jit(solution)/shard_map/pallas_call | solution.py:384
  17.1 0.0 collective-permute-start.5
  17.1 0.0 collective-permute-done.6.refs_10_
  17.1 27.6 %shard_map.94 = (f32[16,128]{1,0:T(8,128)S(1)}, f32[8,1,128]{2,1,0:T(1,128)S(1)}) custom-call(f32[8,512,256]{2,1,0:T(8,128)S(1)} %get-tuple-element.33.refs_0_, f32[8,256,256]{2,1,0:T(8,128)S(1)} %get-tuple-element.35.refs_1_, f32[8,256,256]{2,1,0:T(8,128)S(1)} %get-tuple-element.48.refs_2_, bf16[512,512]{1,0:T(8,128)(2,1)S(1)} %get-tuple-element.41.refs_3_, ...), custom_call_target="tpu_custom_call" | custom-call | flops 1000000000 | bytes 524288 | tf_op jit(solution)/shard_map/pallas_call | solution.py:394
  44.7 0.0 collective-permute-done.5.refs_10_
  44.7 8.3 %all_to_all.5.values_ref = f32[8,1,128]{2,1,0:T(1,128)S(1)} all-to-all(f32[8,1,128]{2,1,0:T(1,128)S(1)} %get-tuple-element.53), channel_id=1, replica_groups={{14,12,10,8,6,4,2,0},{15,13,11,9,7,5,3,1},{30,28,26,24,22,20,18,16},{31..., dimensions={0} | all-to-all | bytes 8192 | tf_op jit(solution)/shard_map/all_to_all | solution.py:409
  53.0 0.6 %shard_map.96 = (f32[1,128]{1,0:T(1,128)}, f32[16,128]{1,0:T(8,128)}) custom-call(f32[8,1,128]{2,1,0:T(1,128)S(1)} %all_to_all.5.values_ref, f32[1,128]{1,0:T(1,128)S(1)} %get-tuple-element.54.weight_ref, f32[16,128]{1,0:T(8,128)S(1)} %get-tuple-element.55.poten_ref), custom_call_target="tpu_custom_call" | custom-call | tf_op jit(solution)/shard_map/pallas_call | solution.py:411
  (3 shorter events, 0.0 us)
Async XLA Ops:
  1.5 7.0 %collective-permute-start = (f32[1,65,1,128]{3,2,1,0:T(1,128)S(1)}, f32[1,65,1,128]{3,2,1,0:T(1,128)S(1)}, u32[]{:S(2)}, u32[]{:S(2)}) collective-permute-start(f32[1,65,1,128]{3,2,1,0:T(1,128)S(1)} %get-tuple-element.30.refs_0_), channel_id=1, source_target_pairs={{0,8},{2,10},{4,12},{6,14},{8,4},{10,6},{12,0},{14,2},{1,9},{3,11}... | collective-permute-start | bytes 99848 | tf_op jit(solution)/shard_map/ppermute | solution.py:361
  5.5 4.8 %collective-permute-start.1 = (f32[1,65,1,128]{3,2,1,0:T(1,128)S(1)}, f32[1,65,1,128]{3,2,1,0:T(1,128)S(1)}, u32[]{:S(2)}, u32[]{:S(2)}) collective-permute-start(f32[1,65,1,128]{3,2,1,0:T(1,128)S(1)} %get-tuple-element.30.refs_0_), channel_id=1, source_target_pairs={{0,12},{2,14},{4,8},{6,10},{8,0},{10,2},{12,4},{14,6},{1,13},{3,15... | collective-permute-start | bytes 99848 | tf_op jit(solution)/shard_map/ppermute | solution.py:361
  6.6 4.1 %collective-permute-start.2 = (f32[1,65,1,128]{3,2,1,0:T(1,128)S(1)}, f32[1,65,1,128]{3,2,1,0:T(1,128)S(1)}, u32[]{:S(2)}, u32[]{:S(2)}) collective-permute-start(f32[1,65,1,128]{3,2,1,0:T(1,128)S(1)} %get-tuple-element.30.refs_0_), channel_id=1, source_target_pairs={{0,4},{2,6},{4,0},{6,2},{8,12},{10,14},{12,8},{14,10},{1,5},{3,7},... | collective-permute-start | bytes 99848 | tf_op jit(solution)/shard_map/ppermute | solution.py:361
  8.5 5.3 %collective-permute-start.3 = (f32[2,65,1,128]{3,2,1,0:T(1,128)S(1)}, f32[2,65,1,128]{3,2,1,0:T(1,128)S(1)}, u32[]{:S(2)}, u32[]{:S(2)}) collective-permute-start(f32[2,65,1,128]{3,2,1,0:T(1,128)S(1)} %shard_map.88.refs_2_), channel_id=1, source_target_pairs={{0,2},{2,0},{4,6},{6,4},{8,10},{10,8},{12,14},{14,12},{1,3},{3,1},... | collective-permute-start | bytes 199688 | tf_op jit(solution)/shard_map/ppermute | solution.py:357
  10.7 4.3 %collective-permute-start.4 = (f32[2,65,1,128]{3,2,1,0:T(1,128)S(1)}, f32[2,65,1,128]{3,2,1,0:T(1,128)S(1)}, u32[]{:S(2)}, u32[]{:S(2)}) collective-permute-start(f32[2,65,1,128]{3,2,1,0:T(1,128)S(1)} %shard_map.89.refs_5_), channel_id=1, source_target_pairs={{0,2},{2,0},{4,6},{6,4},{8,10},{10,8},{12,14},{14,12},{1,3},{3,1},... | collective-permute-start | bytes 199688 | tf_op jit(solution)/shard_map/ppermute | solution.py:357
  15.6 1.5 %collective-permute-start.6 = (f32[16,128]{1,0:T(8,128)S(1)}, f32[16,128]{1,0:T(8,128)S(1)}, u32[]{:S(2)}, u32[]{:S(2)}) collective-permute-start(f32[16,128]{1,0:T(8,128)S(1)} %get-tuple-element.45.refs_2_.refs_9_), channel_id=1, source_target_pairs={{0,1},{1,0},{2,3},{3,2},{4,5},{5,4},{6,7},{7,6},{8,9},{9,8},{10,11... | collective-permute-start | bytes 24584 | tf_op jit(solution)/shard_map/ppermute | solution.py:404
  17.1 27.6 %collective-permute-start.5 = (f32[16,128]{1,0:T(8,128)S(1)}, f32[16,128]{1,0:T(8,128)S(1)}, u32[]{:S(2)}, u32[]{:S(2)}) collective-permute-start(f32[16,128]{1,0:T(8,128)S(1)} %get-tuple-element.46.refs_9_), channel_id=1, source_target_pairs={{0,1},{1,0},{2,3},{3,2},{4,5},{5,4},{6,7},{7,6},{8,9},{9,8},{10,11... | collective-permute-start | bytes 24584 | tf_op jit(solution)/shard_map/ppermute | solution.py:406

commit v21 on v20

--- a/solution.py
+++ b/solution.py
@@ -188,7 +188,7 @@
 def last_kernel(groups, core, *refs):
     packs_ref, wide_ref, _, mask_ref = refs[:4]
     peak_refs, total_refs = refs[4 : 3 + groups], refs[3 + groups : 2 + 2 * groups]
-    exps_ref, tall_ref, peak_ref, total_ref, peaks_ref, rowsum_ref = refs[2 + 2 * groups :]
+    exps_ref, tall_ref, peaks_ref, rowsum_ref, peak_ref, total_ref = refs[2 + 2 * groups :]
 
     def idle():
         peak_ref[...] = jnp.zeros(peak_ref.shape, jnp.float32)
@@ -381,16 +381,18 @@
     def last_tiles(core, after):
         _, _, peaks, totals = zip(*found)
         blocks = far[-1].shape[0]
+        exps, tall, *_ = tile_shapes(blocks)
         *last, peaks, own = call(
             functools.partial(last_kernel, groups, core),
             [VM] * 2 + [pl.BlockSpec(memory_space=pl.ANY)] + [VM] * (2 * groups - 1),
-            tile_shapes(blocks) + [in_vmem((shards, rows, cells), jnp.float32), in_vmem((rows, cells), jnp.float32)],
+            [exps, tall, in_vmem((shards, rows, cells), jnp.float32), in_vmem((rows, cells), jnp.float32)],
+            [pltpu.VMEM((blocks, rows, cells), jnp.float32)] * 2,
             cost=cost_of(2 * blocks * cells * pairs * wide * 8 * depth),
         )(far[-1], wide_feat, after, mask, *peaks, *totals)
         return last, peaks, own
 
     def columns_of(core, last, peaks, own, other, given):
-        exps, tall, _, _ = zip(*found, last)
+        exps, tall = zip(*[group[:2] for group in found], last)
         return call(
             functools.partial(column_kernel, groups, core),
             [VM] * (2 * groups + 7 + len(given)),

time: 53.9 us -> 53 us (0.983)
  Pallas kernels: 35 us -> 33.9 us
    pallas_call x2, Pallas kernels: 2.11 us -> 0.97 us  [last_tiles(): call(functools.partial(last_kernel, groups, core), [VM] * 2 + [pl.BlockSp...]
  transfers between devices with their start and end apart: 7 -> 7, of which waited for: 3 -> 4; matrix products, arithmetic and copies ran while one was open for 0% -> 0% of each run, Pallas kernels for 61% -> 61%
where the time goes in v21:
time: 53 us; the launch traced here: 52.8 us
  Pallas kernels  33.9 us (64%)
  starting transfers between devices  8.96 us (17%)
  blocking collectives  8.28 us (16%)
  waiting for transfers between devices  0.94 us (2%)
  between operations  0.73 us (1%)
    pallas_call x2, Pallas kernels, columns_of(): call(functools.partial(column_kernel, groups, core), [VM] * (2 * groups +...  27.6 us
    all_to_all x1, blocking collectives, dense_device(): lax.all_to_all(columns, 'src', 0, 0, axis_index_groups=[list(range(shards...  8.28 us
    ppermute x3, starting transfers between devices, moved(): return lax.ppermute(array, 'src', moves)  5.67 us
    ppermute x2, starting transfers between devices, swapped(): return lax.ppermute(array, 'src', [(i, i ^ 1) for i in range(shards)])  3.15 us
    pallas_call x2, Pallas kernels, tiles(): call(functools.partial(tile_kernel, len(packs)), [VM] * (len(packs) + 1)...  2.52 us
    pallas_call x2, Pallas kernels, reading(): call(kernel, [pl.BlockSpec(memory_space=pltpu.HBM)] * len(args), out_shap...  2.18 us
  transfers between devices with their start and end apart: 7, of which 4 were waited for; matrix products, arithmetic and copies ran while one was open for 0% of the time, Pallas kernels for 61%

profile of v21, /device:TPU:0, one launch (start us, length us, event | category | flops | bytes accessed | tf_op | source)
XLA Modules:
  0.0 52.8 jit_solution(5431808049725851327)
XLA Ops:
  0.6 0.8 %shard_map.86 = (f32[1,65,1,128]{3,2,1,0:T(1,128)S(1)}, f32[1,128]{1,0:T(1,128)S(1)}) custom-call(f32[1,64,128]{2,1,0:T(8,128)} %refs_0_.2, f32[1,128]{1,0:T(1,128)} %refs_1_.1, f32[1,128]{1,0:T(1,128)} %refs_2_.1), custom_call_target="tpu_custom_call" | custom-call | tf_op jit(solution)/shard_map/pallas_call | solution.py:310
  1.5 4.1 %collective-permute-start = (f32[1,65,1,128]{3,2,1,0:T(1,128)S(1)}, f32[1,65,1,128]{3,2,1,0:T(1,128)S(1)}, u32[]{:S(2)}, u32[]{:S(2)}) collective-permute-start(f32[1,65,1,128]{3,2,1,0:T(1,128)S(1)} %get-tuple-element.30.refs_0_), channel_id=1, source_target_pairs={{0,8},{2,10},{4,12},{6,14},{8,4},{10,6},{12,0},{14,2},{1,9},{3,11}... | collective-permute-start | bytes 99848 | tf_op jit(solution)/shard_map/ppermute | solution.py:361
  5.5 1.1 %collective-permute-start.1 = (f32[1,65,1,128]{3,2,1,0:T(1,128)S(1)}, f32[1,65,1,128]{3,2,1,0:T(1,128)S(1)}, u32[]{:S(2)}, u32[]{:S(2)}) collective-permute-start(f32[1,65,1,128]{3,2,1,0:T(1,128)S(1)} %get-tuple-element.30.refs_0_), channel_id=1, source_target_pairs={{0,12},{2,14},{4,8},{6,10},{8,0},{10,2},{12,4},{14,6},{1,13},{3,15... | collective-permute-start | bytes 99848 | tf_op jit(solution)/shard_map/ppermute | solution.py:361
  6.6 0.5 collective-permute-start.2
  7.1 1.4 %shard_map.87 = (bf16[8,512,256]{2,1,0:T(8,128)(2,1)S(1)}, f32[16,128]{1,0:T(8,128)S(1)}, f32[8,16,128]{2,1,0:T(8,128)S(1)}, f32[16,128]{1,0:T(8,128)S(1)}) custom-call(f32[16,128]{1,0:T(8,128)} %refs_0_.3, s32[8,16]{1,0:T(8,128)} %bitcast.4, s32[1,16]{1,0:T(1,128)} %bitcast.5, f32[16,64,128]{2,1,0:T(8,128)} %refs_3_.1), custom_call_target="tpu_custom_call" | custom-call | flops 100000000 | bytes 524288 | tf_op jit(solution)/shard_map/pallas_call | solution.py:310
  8.5 0.0 collective-permute-done.refs_1_
  8.5 1.7 %collective-permute-start.3 = (f32[2,65,1,128]{3,2,1,0:T(1,128)S(1)}, f32[2,65,1,128]{3,2,1,0:T(1,128)S(1)}, u32[]{:S(2)}, u32[]{:S(2)}) collective-permute-start(f32[2,65,1,128]{3,2,1,0:T(1,128)S(1)} %shard_map.88.refs_2_), channel_id=1, source_target_pairs={{0,2},{2,0},{4,6},{6,4},{8,10},{10,8},{12,14},{14,12},{1,3},{3,1},... | collective-permute-start | bytes 199688 | tf_op jit(solution)/shard_map/ppermute | solution.py:357
  10.2 0.2 collective-permute-done.1.refs_0_.refs_2_
  10.4 0.3 collective-permute-done.2.refs_1_.refs_3_
  10.7 1.5 %collective-permute-start.4 = (f32[2,65,1,128]{3,2,1,0:T(1,128)S(1)}, f32[2,65,1,128]{3,2,1,0:T(1,128)S(1)}, u32[]{:S(2)}, u32[]{:S(2)}) collective-permute-start(f32[2,65,1,128]{3,2,1,0:T(1,128)S(1)} %shard_map.89.refs_5_), channel_id=1, source_target_pairs={{0,2},{2,0},{4,6},{6,4},{8,10},{10,8},{12,14},{14,12},{1,3},{3,1},... | collective-permute-start | bytes 199688 | tf_op jit(solution)/shard_map/ppermute | solution.py:357
  12.2 1.6 %shard_map.90 = (f32[8,512,256]{2,1,0:T(8,128)S(1)}, bf16[512,512]{1,0:T(8,128)(2,1)S(1)}, f32[4,16,128]{2,1,0:T(8,128)S(1)}, f32[4,16,128]{2,1,0:T(8,128)S(1)}) custom-call(f32[1,65,1,128]{3,2,1,0:T(1,128)S(1)} %get-tuple-element.30.refs_0_, f32[1,65,1,128]{3,2,1,0:T(1,128)S(1)} %collective-permute-done.refs_1_, ...), custom_call_target="tpu_custom_call" | custom-call | flops 1073741824 | bytes 524288 | tf_op jit(solution)/shard_map/pallas_call | solution.py:349
  13.8 0.0 collective-permute-done.3.refs_0_
  13.9 0.9 %shard_map.91 = (f32[8,256,256]{2,1,0:T(8,128)S(1)}, bf16[256,512]{1,0:T(8,128)(2,1)S(1)}, f32[2,16,128]{2,1,0:T(8,128)S(1)}, f32[2,16,128]{2,1,0:T(8,128)S(1)}) custom-call(f32[2,65,1,128]{3,2,1,0:T(1,128)S(1)} %collective-permute-done.3.refs_0_, bf16[8,512,256]{2,1,0:T(8,128)(2,1)S(1)} %get-tuple-element.31.refs_4_.refs_1_.refs_6_, ...), custom_call_target="tpu_custom_call" | custom-call | flops 536870912 | bytes 524288 | tf_op jit(solution)/shard_map/pallas_call | solution.py:349
  14.7 0.3 collective-permute-done.4.refs_0_
  15.0 0.1 collective-permute-start.6
  15.1 0.9 %shard_map.93 = (f32[8,256,256]{2,1,0:T(8,128)S(1)}, bf16[256,512]{1,0:T(8,128)(2,1)S(1)}, f32[8,16,128]{2,1,0:T(8,128)S(1)}, f32[16,128]{1,0:T(8,128)S(1)}) custom-call(f32[2,65,1,128]{3,2,1,0:T(1,128)S(1)} %collective-permute-done.4.refs_0_, bf16[8,512,256]{2,1,0:T(8,128)(2,1)S(1)} %get-tuple-element.31.refs_4_.refs_1_.refs_6_, ...), custom_call_target="tpu_custom_call" | custom-call | flops 536870912 | bytes 524288 | tf_op jit(solution)/shard_map/pallas_call | solution.py:385
  16.1 0.1 collective-permute-start.5
  16.1 0.1 collective-permute-done.6.refs_10_
  16.3 27.6 %shard_map.94 = (f32[16,128]{1,0:T(8,128)S(1)}, f32[8,1,128]{2,1,0:T(1,128)S(1)}) custom-call(f32[8,512,256]{2,1,0:T(8,128)S(1)} %get-tuple-element.33.refs_0_, f32[8,256,256]{2,1,0:T(8,128)S(1)} %get-tuple-element.35.refs_1_, f32[8,256,256]{2,1,0:T(8,128)S(1)} %get-tuple-element.48.refs_2_, bf16[512,512]{1,0:T(8,128)(2,1)S(1)} %get-tuple-element.41.refs_3_, ...), custom_call_target="tpu_custom_call" | custom-call | flops 1000000000 | bytes 524288 | tf_op jit(solution)/shard_map/pallas_call | solution.py:396
  43.8 0.0 collective-permute-done.5.refs_10_
  43.9 8.3 %all_to_all.5.values_ref = f32[8,1,128]{2,1,0:T(1,128)S(1)} all-to-all(f32[8,1,128]{2,1,0:T(1,128)S(1)} %get-tuple-element.53), channel_id=1, replica_groups={{14,12,10,8,6,4,2,0},{15,13,11,9,7,5,3,1},{30,28,26,24,22,20,18,16},{31..., dimensions={0} | all-to-all | bytes 8192 | tf_op jit(solution)/shard_map/all_to_all | solution.py:411
  52.2 0.6 %shard_map.96 = (f32[1,128]{1,0:T(1,128)}, f32[16,128]{1,0:T(8,128)}) custom-call(f32[8,1,128]{2,1,0:T(1,128)S(1)} %all_to_all.5.values_ref, f32[1,128]{1,0:T(1,128)S(1)} %get-tuple-element.54.weight_ref, f32[16,128]{1,0:T(8,128)S(1)} %get-tuple-element.55.poten_ref), custom_call_target="tpu_custom_call" | custom-call | tf_op jit(solution)/shard_map/pallas_call | solution.py:413
  (4 shorter events, 0.1 us)
Async XLA Ops:
  1.5 7.0 %collective-permute-start = (f32[1,65,1,128]{3,2,1,0:T(1,128)S(1)}, f32[1,65,1,128]{3,2,1,0:T(1,128)S(1)}, u32[]{:S(2)}, u32[]{:S(2)}) collective-permute-start(f32[1,65,1,128]{3,2,1,0:T(1,128)S(1)} %get-tuple-element.30.refs_0_), channel_id=1, source_target_pairs={{0,8},{2,10},{4,12},{6,14},{8,4},{10,6},{12,0},{14,2},{1,9},{3,11}... | collective-permute-start | bytes 99848 | tf_op jit(solution)/shard_map/ppermute | solution.py:361
  5.5 4.8 %collective-permute-start.1 = (f32[1,65,1,128]{3,2,1,0:T(1,128)S(1)}, f32[1,65,1,128]{3,2,1,0:T(1,128)S(1)}, u32[]{:S(2)}, u32[]{:S(2)}) collective-permute-start(f32[1,65,1,128]{3,2,1,0:T(1,128)S(1)} %get-tuple-element.30.refs_0_), channel_id=1, source_target_pairs={{0,12},{2,14},{4,8},{6,10},{8,0},{10,2},{12,4},{14,6},{1,13},{3,15... | collective-permute-start | bytes 99848 | tf_op jit(solution)/shard_map/ppermute | solution.py:361
  6.6 4.1 %collective-permute-start.2 = (f32[1,65,1,128]{3,2,1,0:T(1,128)S(1)}, f32[1,65,1,128]{3,2,1,0:T(1,128)S(1)}, u32[]{:S(2)}, u32[]{:S(2)}) collective-permute-start(f32[1,65,1,128]{3,2,1,0:T(1,128)S(1)} %get-tuple-element.30.refs_0_), channel_id=1, source_target_pairs={{0,4},{2,6},{4,0},{6,2},{8,12},{10,14},{12,8},{14,10},{1,5},{3,7},... | collective-permute-start | bytes 99848 | tf_op jit(solution)/shard_map/ppermute | solution.py:361
  8.5 5.3 %collective-permute-start.3 = (f32[2,65,1,128]{3,2,1,0:T(1,128)S(1)}, f32[2,65,1,128]{3,2,1,0:T(1,128)S(1)}, u32[]{:S(2)}, u32[]{:S(2)}) collective-permute-start(f32[2,65,1,128]{3,2,1,0:T(1,128)S(1)} %shard_map.88.refs_2_), channel_id=1, source_target_pairs={{0,2},{2,0},{4,6},{6,4},{8,10},{10,8},{12,14},{14,12},{1,3},{3,1},... | collective-permute-start | bytes 199688 | tf_op jit(solution)/shard_map/ppermute | solution.py:357
  10.7 4.3 %collective-permute-start.4 = (f32[2,65,1,128]{3,2,1,0:T(1,128)S(1)}, f32[2,65,1,128]{3,2,1,0:T(1,128)S(1)}, u32[]{:S(2)}, u32[]{:S(2)}) collective-permute-start(f32[2,65,1,128]{3,2,1,0:T(1,128)S(1)} %shard_map.89.refs_5_), channel_id=1, source_target_pairs={{0,2},{2,0},{4,6},{6,4},{8,10},{10,8},{12,14},{14,12},{1,3},{3,1},... | collective-permute-start | bytes 199688 | tf_op jit(solution)/shard_map/ppermute | solution.py:357
  15.0 1.2 %collective-permute-start.6 = (f32[16,128]{1,0:T(8,128)S(1)}, f32[16,128]{1,0:T(8,128)S(1)}, u32[]{:S(2)}, u32[]{:S(2)}) collective-permute-start(f32[16,128]{1,0:T(8,128)S(1)} %get-tuple-element.45.refs_2_.refs_9_), channel_id=1, source_target_pairs={{0,1},{1,0},{2,3},{3,2},{4,5},{5,4},{6,7},{7,6},{8,9},{9,8},{10,11... | collective-permute-start | bytes 24584 | tf_op jit(solution)/shard_map/ppermute | solution.py:406
  16.1 27.8 %collective-permute-start.5 = (f32[16,128]{1,0:T(8,128)S(1)}, f32[16,128]{1,0:T(8,128)S(1)}, u32[]{:S(2)}, u32[]{:S(2)}) collective-permute-start(f32[16,128]{1,0:T(8,128)S(1)} %get-tuple-element.46.refs_9_), channel_id=1, source_target_pairs={{0,1},{1,0},{2,3},{3,2},{4,5},{5,4},{6,7},{7,6},{8,9},{9,8},{10,11... | collective-permute-start | bytes 24584 | tf_op jit(solution)/shard_map/ppermute | solution.py:408

commit v22 on v19

--- a/solution.py
+++ b/solution.py
@@ -14,6 +14,7 @@
 ln2 = math.log(2.0)
 least_sum = 1e-28
 
+pack_cuts = 4
 room = 2**24
 
 VM = pl.BlockSpec(memory_space=pltpu.VMEM)
@@ -53,19 +54,24 @@
     return near + [block ^ 1 for block in near]
 
 
-def read_all(hbm, held, sems):
-    copies = [pltpu.make_async_copy(src, dst, sems.at[i]) for i, (src, dst) in enumerate(zip(hbm, held))]
+def read_all(hbm, held, sems, cuts):
+    *whole, (cut_from, cut_to) = zip(hbm, held)
+    size = cut_from.shape[0] // cuts
+    spans = [pl.ds(at * size, size) for at in range(cuts)]
+    moves = [(cut_from.at[span], cut_to.at[span]) for span in spans] + whole
+    copies = [pltpu.make_async_copy(*move, sems.at[at]) for at, move in enumerate(moves)]
     for copy in copies:
         copy.start()
-    return copies
+    return copies[cuts:], copies[:cuts]
 
 
 def pack_kernel(*refs):
     hbm, (send_ref, weight_ref), held, sems = refs[:3], refs[3:5], refs[5:8], refs[8]
-    for copy in read_all(hbm, held, sems):
+    whole, cut = read_all(hbm, held, sems, pack_cuts)
+    for copy in whole + cut:
         copy.wait()
-    feat_ref, mass_ref, poten_ref = held
-    feat = feat_ref[0]
+    mass_ref, poten_ref, feat_ref = held
+    feat = feat_ref[...]
     depth, cells = feat.shape
     weight = target_weight(mass_ref[...], poten_ref[...])
     norm = jnp.sum(feat * feat, axis=0, keepdims=True)
@@ -80,8 +86,9 @@
     hbm, outs, held, sems = refs[:4], refs[4:8], refs[8:12], refs[12]
     wide_ref, norm_ref, mask_ref, mass_out_ref = outs
     mass_ref, support_ref, counts_ref, feat_ref = held
-    copies = read_all(hbm, held, sems)
-    for copy in copies[:3]:
+    rows = feat_ref.shape[0]
+    whole, cut = read_all(hbm, held, sems, rows // 2)
+    for copy in whole:
         copy.wait()
     mass_out_ref[...] = mass_ref[...]
     support = support_ref[...]
@@ -96,10 +103,10 @@
     hits = jnp.concatenate([hits, jnp.zeros((cells, cells - rows), jnp.float32)], axis=1).T
     for place in range(shards):
         mask_ref[place] = jnp.broadcast_to(hits[:rows, place : place + 1], (rows, cells))
-    copies[3].wait()
     depth = feat_ref.shape[1]
     one = jnp.ones((2 * depth, 2 * cells), jnp.bfloat16)
     for pair in range(rows // 2):
+        cut[pair].wait()
         for half in range(2):
             feat = feat_ref[2 * pair + half]
             norm_ref[2 * pair + half : 2 * pair + half + 1, :] = jnp.sum(feat * feat, axis=0, keepdims=True)
@@ -299,12 +306,12 @@
             cost_estimate=cost,
         )
 
-    def reading(kernel, args, out_shape, cost):
+    def reading(kernel, args, out_shape, cost, cuts):
         return call(
             kernel,
             [pl.BlockSpec(memory_space=pltpu.HBM)] * len(args),
             out_shape,
-            [pltpu.VMEM(arg.shape, arg.dtype) for arg in args] + [pltpu.SemaphoreType.DMA((len(args),))],
+            [pltpu.VMEM(arg.shape, arg.dtype) for arg in args] + [pltpu.SemaphoreType.DMA((len(args) - 1 + cuts,))],
             cost,
         )(*[pltpu.with_memory_space_constraint(arg, pltpu.HBM) for arg in args])
 
@@ -313,9 +320,10 @@
 
     pack, weight = reading(
         pack_kernel,
-        [target_feat, log_mass_tgt, potential_tgt],
+        [log_mass_tgt, potential_tgt, target_feat[0]],
         [in_vmem((1, depth + 1, 1, cells), jnp.float32), in_vmem((1, cells), jnp.float32)],
         None,
+        pack_cuts,
     )
     wide_feat, norm, mask, mass = reading(
         functools.partial(source_kernel, shards),
@@ -327,6 +335,7 @@
             in_vmem((rows, cells), jnp.float32),
         ],
         cost_of(10**8),
+        pairs,
     )
 
     def tiles(*packs, core=None, after=None):

time: 53 us -> 53 us (level)
  transfers between devices with their start and end apart: 7 -> 7, of which waited for: 4 -> 4; matrix products, arithmetic and copies ran while one was open for 0% -> 0% of each run, Pallas kernels for 61% -> 62%
where the time goes in v22:
time: 53 us; the launch traced here: 52.8 us
  Pallas kernels  34 us (64%)
  starting transfers between devices  8.87 us (17%)
  blocking collectives  8.27 us (16%)
  waiting for transfers between devices  0.89 us (2%)
  between operations  0.73 us (1%)
    pallas_call x2, Pallas kernels, columns_of(): call(functools.partial(column_kernel, groups, core), [VM] * (2 * groups +...  27.6 us
    all_to_all x1, blocking collectives, dense_device(): lax.all_to_all(columns, 'src', 0, 0, axis_index_groups=[list(range(shards...  8.27 us
    ppermute x3, starting transfers between devices, moved(): return lax.ppermute(array, 'src', moves)  5.67 us
    pallas_call x4, Pallas kernels, tiles(): call(functools.partial(tile_kernel, len(packs), core), [VM] * (len(packs)...  3.41 us
    ppermute x2, starting transfers between devices, swapped(): return lax.ppermute(array, 'src', [(i, i ^ 1) for i in range(shards)])  3.06 us
    pallas_call x2, Pallas kernels, reading(): call(kernel, [pl.BlockSpec(memory_space=pltpu.HBM)] * len(args), out_shap...  2.33 us
  transfers between devices with their start and end apart: 7, of which 4 were waited for; matrix products, arithmetic and copies ran while one was open for 0% of the time, Pallas kernels for 62%

profile of v22, /device:TPU:0, one launch (start us, length us, event | category | flops | bytes accessed | tf_op | source)
XLA Modules:
  0.0 52.8 jit_solution(8360539397357486862)
XLA Ops:
  0.6 0.8 %shard_map.86 = (f32[1,65,1,128]{3,2,1,0:T(1,128)S(1)}, f32[1,128]{1,0:T(1,128)S(1)}) custom-call(f32[1,128]{1,0:T(1,128)} %refs_0_.2, f32[1,128]{1,0:T(1,128)} %refs_1_.1, f32[64,128]{1,0:T(8,128)} %bitcast.5), custom_call_target="tpu_custom_call" | custom-call | tf_op jit(solution)/shard_map/pallas_call | solution.py:310
  1.5 4.1 %collective-permute-start = (f32[1,65,1,128]{3,2,1,0:T(1,128)S(1)}, f32[1,65,1,128]{3,2,1,0:T(1,128)S(1)}, u32[]{:S(2)}, u32[]{:S(2)}) collective-permute-start(f32[1,65,1,128]{3,2,1,0:T(1,128)S(1)} %get-tuple-element.34.refs_0_), channel_id=1, source_target_pairs={{0,8},{2,10},{4,12},{6,14},{8,4},{10,6},{12,0},{14,2},{1,9},{3,11}... | collective-permute-start | bytes 99848 | tf_op jit(solution)/shard_map/ppermute | solution.py:361
  5.6 1.1 %collective-permute-start.1 = (f32[1,65,1,128]{3,2,1,0:T(1,128)S(1)}, f32[1,65,1,128]{3,2,1,0:T(1,128)S(1)}, u32[]{:S(2)}, u32[]{:S(2)}) collective-permute-start(f32[1,65,1,128]{3,2,1,0:T(1,128)S(1)} %get-tuple-element.34.refs_0_), channel_id=1, source_target_pairs={{0,12},{2,14},{4,8},{6,10},{8,0},{10,2},{12,4},{14,6},{1,13},{3,15... | collective-permute-start | bytes 99848 | tf_op jit(solution)/shard_map/ppermute | solution.py:361
  6.6 0.5 collective-permute-start.2
  7.1 1.5 %shard_map.87 = (bf16[8,512,256]{2,1,0:T(8,128)(2,1)S(1)}, f32[16,128]{1,0:T(8,128)S(1)}, f32[8,16,128]{2,1,0:T(8,128)S(1)}, f32[16,128]{1,0:T(8,128)S(1)}) custom-call(f32[16,128]{1,0:T(8,128)} %refs_0_.3, s32[8,16]{1,0:T(8,128)} %bitcast.6, s32[1,16]{1,0:T(1,128)} %bitcast.7, f32[16,64,128]{2,1,0:T(8,128)} %refs_3_.1), custom_call_target="tpu_custom_call" | custom-call | flops 100000000 | bytes 524288 | tf_op jit(solution)/shard_map/pallas_call | solution.py:310
  8.6 0.0 collective-permute-done.refs_1_
  8.7 1.6 %collective-permute-start.3 = (f32[2,65,1,128]{3,2,1,0:T(1,128)S(1)}, f32[2,65,1,128]{3,2,1,0:T(1,128)S(1)}, u32[]{:S(2)}, u32[]{:S(2)}) collective-permute-start(f32[2,65,1,128]{3,2,1,0:T(1,128)S(1)} %shard_map.88.refs_2_), channel_id=1, source_target_pairs={{0,2},{2,0},{4,6},{6,4},{8,10},{10,8},{12,14},{14,12},{1,3},{3,1},... | collective-permute-start | bytes 199688 | tf_op jit(solution)/shard_map/ppermute | solution.py:357
  10.2 0.2 collective-permute-done.1.refs_0_.refs_2_
  10.4 0.3 collective-permute-done.2.refs_1_.refs_3_
  10.7 1.5 %collective-permute-start.4 = (f32[2,65,1,128]{3,2,1,0:T(1,128)S(1)}, f32[2,65,1,128]{3,2,1,0:T(1,128)S(1)}, u32[]{:S(2)}, u32[]{:S(2)}) collective-permute-start(f32[2,65,1,128]{3,2,1,0:T(1,128)S(1)} %shard_map.89.refs_5_), channel_id=1, source_target_pairs={{0,2},{2,0},{4,6},{6,4},{8,10},{10,8},{12,14},{14,12},{1,3},{3,1},... | collective-permute-start | bytes 199688 | tf_op jit(solution)/shard_map/ppermute | solution.py:357
  12.2 1.6 %shard_map.90 = (f32[8,512,256]{2,1,0:T(8,128)S(1)}, bf16[512,512]{1,0:T(8,128)(2,1)S(1)}, f32[4,16,128]{2,1,0:T(8,128)S(1)}, f32[4,16,128]{2,1,0:T(8,128)S(1)}) custom-call(f32[1,65,1,128]{3,2,1,0:T(1,128)S(1)} %get-tuple-element.34.refs_0_, f32[1,65,1,128]{3,2,1,0:T(1,128)S(1)} %collective-permute-done.refs_1_, ...), custom_call_target="tpu_custom_call" | custom-call | flops 1073741824 | bytes 524288 | tf_op jit(solution)/shard_map/pallas_call | solution.py:344
  13.9 0.0 collective-permute-done.3.refs_0_
  13.9 0.9 %shard_map.91 = (f32[8,256,256]{2,1,0:T(8,128)S(1)}, bf16[256,512]{1,0:T(8,128)(2,1)S(1)}, f32[2,16,128]{2,1,0:T(8,128)S(1)}, f32[2,16,128]{2,1,0:T(8,128)S(1)}) custom-call(f32[2,65,1,128]{3,2,1,0:T(1,128)S(1)} %collective-permute-done.3.refs_0_, bf16[8,512,256]{2,1,0:T(8,128)(2,1)S(1)} %get-tuple-element.35.refs_4_.refs_1_.refs_6_, ...), custom_call_target="tpu_custom_call" | custom-call | flops 536870912 | bytes 524288 | tf_op jit(solution)/shard_map/pallas_call | solution.py:344
  14.8 0.3 collective-permute-done.4.refs_0_
  15.1 0.1 collective-permute-start.6
  15.1 0.9 %shard_map.94 = (f32[8,256,256]{2,1,0:T(8,128)S(1)}, bf16[256,512]{1,0:T(8,128)(2,1)S(1)}, f32[2,16,128]{2,1,0:T(8,128)S(1)}, f32[2,16,128]{2,1,0:T(8,128)S(1)}) custom-call(f32[2,65,1,128]{3,2,1,0:T(1,128)S(1)} %collective-permute-done.4.refs_0_, bf16[8,512,256]{2,1,0:T(8,128)(2,1)S(1)} %get-tuple-element.35.refs_4_.refs_1_.refs_6_, ...), custom_call_target="tpu_custom_call" | custom-call | flops 536870912 | bytes 524288 | tf_op jit(solution)/shard_map/pallas_call | solution.py:344
  16.1 0.1 collective-permute-start.5
  16.2 0.1 collective-permute-done.6.refs_10_
  16.3 27.6 %shard_map.96 = (f32[16,128]{1,0:T(8,128)S(1)}, f32[8,1,128]{2,1,0:T(1,128)S(1)}) custom-call(f32[8,512,256]{2,1,0:T(8,128)S(1)} %get-tuple-element.37.refs_0_, f32[8,256,256]{2,1,0:T(8,128)S(1)} %get-tuple-element.39.refs_1_, f32[8,256,256]{2,1,0:T(8,128)S(1)} %get-tuple-element.56.refs_2_, bf16[512,512]{1,0:T(8,128)(2,1)S(1)} %get-tuple-element.42.refs_3_, ...), custom_call_target="tpu_custom_call" | custom-call | flops 1000000000 | bytes 524288 | tf_op jit(solution)/shard_map/pallas_call | solution.py:391
  43.9 0.0 collective-permute-done.5.refs_10_
  43.9 8.3 %all_to_all.5.values_ref = f32[8,1,128]{2,1,0:T(1,128)S(1)} all-to-all(f32[8,1,128]{2,1,0:T(1,128)S(1)} %get-tuple-element.61), channel_id=1, replica_groups={{14,12,10,8,6,4,2,0},{15,13,11,9,7,5,3,1},{30,28,26,24,22,20,18,16},{31..., dimensions={0} | all-to-all | bytes 8192 | tf_op jit(solution)/shard_map/all_to_all | solution.py:408
  52.2 0.6 %shard_map.98 = (f32[1,128]{1,0:T(1,128)}, f32[16,128]{1,0:T(8,128)}) custom-call(f32[8,1,128]{2,1,0:T(1,128)S(1)} %all_to_all.5.values_ref, f32[1,128]{1,0:T(1,128)S(1)} %get-tuple-element.62.weight_ref, f32[16,128]{1,0:T(8,128)S(1)} %get-tuple-element.63.poten_ref), custom_call_target="tpu_custom_call" | custom-call | tf_op jit(solution)/shard_map/pallas_call | solution.py:410
  (6 shorter events, 0.1 us)
Async XLA Ops:
  1.5 7.2 %collective-permute-start = (f32[1,65,1,128]{3,2,1,0:T(1,128)S(1)}, f32[1,65,1,128]{3,2,1,0:T(1,128)S(1)}, u32[]{:S(2)}, u32[]{:S(2)}) collective-permute-start(f32[1,65,1,128]{3,2,1,0:T(1,128)S(1)} %get-tuple-element.34.refs_0_), channel_id=1, source_target_pairs={{0,8},{2,10},{4,12},{6,14},{8,4},{10,6},{12,0},{14,2},{1,9},{3,11}... | collective-permute-start | bytes 99848 | tf_op jit(solution)/shard_map/ppermute | solution.py:361
  5.6 4.8 %collective-permute-start.1 = (f32[1,65,1,128]{3,2,1,0:T(1,128)S(1)}, f32[1,65,1,128]{3,2,1,0:T(1,128)S(1)}, u32[]{:S(2)}, u32[]{:S(2)}) collective-permute-start(f32[1,65,1,128]{3,2,1,0:T(1,128)S(1)} %get-tuple-element.34.refs_0_), channel_id=1, source_target_pairs={{0,12},{2,14},{4,8},{6,10},{8,0},{10,2},{12,4},{14,6},{1,13},{3,15... | collective-permute-start | bytes 99848 | tf_op jit(solution)/shard_map/ppermute | solution.py:361
  6.6 4.1 %collective-permute-start.2 = (f32[1,65,1,128]{3,2,1,0:T(1,128)S(1)}, f32[1,65,1,128]{3,2,1,0:T(1,128)S(1)}, u32[]{:S(2)}, u32[]{:S(2)}) collective-permute-start(f32[1,65,1,128]{3,2,1,0:T(1,128)S(1)} %get-tuple-element.34.refs_0_), channel_id=1, source_target_pairs={{0,4},{2,6},{4,0},{6,2},{8,12},{10,14},{12,8},{14,10},{1,5},{3,7},... | collective-permute-start | bytes 99848 | tf_op jit(solution)/shard_map/ppermute | solution.py:361
  8.7 5.2 %collective-permute-start.3 = (f32[2,65,1,128]{3,2,1,0:T(1,128)S(1)}, f32[2,65,1,128]{3,2,1,0:T(1,128)S(1)}, u32[]{:S(2)}, u32[]{:S(2)}) collective-permute-start(f32[2,65,1,128]{3,2,1,0:T(1,128)S(1)} %shard_map.88.refs_2_), channel_id=1, source_target_pairs={{0,2},{2,0},{4,6},{6,4},{8,10},{10,8},{12,14},{14,12},{1,3},{3,1},... | collective-permute-start | bytes 199688 | tf_op jit(solution)/shard_map/ppermute | solution.py:357
  10.7 4.3 %collective-permute-start.4 = (f32[2,65,1,128]{3,2,1,0:T(1,128)S(1)}, f32[2,65,1,128]{3,2,1,0:T(1,128)S(1)}, u32[]{:S(2)}, u32[]{:S(2)}) collective-permute-start(f32[2,65,1,128]{3,2,1,0:T(1,128)S(1)} %shard_map.89.refs_5_), channel_id=1, source_target_pairs={{0,2},{2,0},{4,6},{6,4},{8,10},{10,8},{12,14},{14,12},{1,3},{3,1},... | collective-permute-start | bytes 199688 | tf_op jit(solution)/shard_map/ppermute | solution.py:357
  15.1 1.2 %collective-permute-start.6 = (f32[16,128]{1,0:T(8,128)S(1)}, f32[16,128]{1,0:T(8,128)S(1)}, u32[]{:S(2)}, u32[]{:S(2)}) collective-permute-start(f32[16,128]{1,0:T(8,128)S(1)} %get-tuple-element.51.refs_2_.refs_9_), channel_id=1, source_target_pairs={{0,1},{1,0},{2,3},{3,2},{4,5},{5,4},{6,7},{7,6},{8,9},{9,8},{10,11... | collective-permute-start | bytes 24584 | tf_op jit(solution)/shard_map/ppermute | solution.py:402
  16.1 27.8 %collective-permute-start.5 = (f32[16,128]{1,0:T(8,128)S(1)}, f32[16,128]{1,0:T(8,128)S(1)}, u32[]{:S(2)}, u32[]{:S(2)}) collective-permute-start(f32[16,128]{1,0:T(8,128)S(1)} %get-tuple-element.54.refs_9_), channel_id=1, source_target_pairs={{0,1},{1,0},{2,3},{3,2},{4,5},{5,4},{6,7},{7,6},{8,9},{9,8},{10,11... | collective-permute-start | bytes 24584 | tf_op jit(solution)/shard_map/ppermute | solution.py:405

commit v23 on v19

--- a/solution.py
+++ b/solution.py
@@ -229,6 +229,7 @@
         for index in range(ref.shape[0] // cells)
     ]
     used = [jnp.max(mask_ref[place], axis=0, keepdims=True) > 0.5 * very_low for place in range(shards)]
+    tile = sums_ref.shape[1:]
     ranks = [shards - 1 - block for block in blocks_at(shards)]
     sums = []
     for place, (group, rows) in enumerate(spots):
@@ -241,7 +242,7 @@
     worst = jnp.min(whole_sums)
     logs = jnp.log2(whole_sums)
     for place in range(shards):
-        sums_ref[ranks[place]] = jnp.where(used[place], logs[place : place + 1, :], very_low)
+        sums_ref[ranks[place]] = jnp.broadcast_to(jnp.where(used[place], logs[place : place + 1, :], very_low), tile)
 
     @pl.when(worst < least_sum)
     def _():
@@ -265,12 +266,12 @@
 
             sums = lax.fori_loop(0, pairs, add_up, jnp.zeros((cells, cells), jnp.float32))
             logs = across(peak) + jnp.log2(across(jnp.sum(sums, axis=1, keepdims=True)))
-            sums_ref[ranks[place]] = jnp.where(used[place], logs, very_low)
+            sums_ref[ranks[place]] = jnp.broadcast_to(jnp.where(used[place], logs, very_low), tile)
 
 
 def merge_kernel(values_ref, weight_ref, poten_ref, out_ref, poten_out_ref):
     poten_out_ref[...] = poten_ref[...]
-    values = values_ref[...]
+    values = values_ref[:, 0:1, :]
     top = jnp.max(values, axis=0)
     whole = top + jnp.log2(jnp.sum(jnp.exp2(values - top), axis=0))
     out_ref[...] = -(entropic * ln2) * (whole - weight_ref[...])
@@ -382,7 +383,7 @@
         return call(
             functools.partial(column_kernel, groups, core),
             [VM] * (2 * groups + 7 + len(given)),
-            [in_vmem((rows, cells), jnp.float32), in_vmem((shards, 1, cells), jnp.float32)],
+            [in_vmem((rows, cells), jnp.float32), in_vmem((shards, 8, cells), jnp.float32)],
             [pltpu.VMEM((shards, rows, cells), jnp.float32), pltpu.VMEM((rows, cells), jnp.float32)],
             cost_of(10**9),
         )(*exps, *tall, wide_feat, peaks, mask, own, other, mass, norm, *given)

time: 53 us -> 53.6 us (1.011)
  blocking collectives: 8.28 us -> 35.4 us
  Pallas kernels: 33.9 us -> 7.02 us
    all_to_all x1, blocking collectives: 8.28 us -> 35.4 us  [dense_device(): lax.all_to_all(columns, 'src', 0, 0, axis_index_groups=[list(range(shards...]
    pallas_call x2, Pallas kernels: 27.6 us -> 0.81 us  [columns_of(): call(functools.partial(column_kernel, groups, core), [VM] * (2 * groups +...]
  transfers between devices with their start and end apart: 7 -> 7, of which waited for: 4 -> 5; matrix products, arithmetic and copies ran while one was open for 0% -> 0% of each run, Pallas kernels for 61% -> 10%
where the time goes in v23:
time: 53.6 us; the launch traced here: 53.3 us
  blocking collectives  35.4 us (66%)
  starting transfers between devices  8.96 us (17%)
  Pallas kernels  7.02 us (13%)
  waiting for transfers between devices  1.2 us (2%)
  between operations  0.72 us (1%)
    all_to_all x1, blocking collectives, dense_device(): lax.all_to_all(columns, 'src', 0, 0, axis_index_groups=[list(range(shards...  35.4 us
    ppermute x3, starting transfers between devices, moved(): return lax.ppermute(array, 'src', moves)  5.67 us
    pallas_call x4, Pallas kernels, tiles(): call(functools.partial(tile_kernel, len(packs), core), [VM] * (len(packs)...  3.35 us
    ppermute x2, starting transfers between devices, swapped(): return lax.ppermute(array, 'src', [(i, i ^ 1) for i in range(shards)])  3.15 us
    pallas_call x2, Pallas kernels, reading(): call(kernel, [pl.BlockSpec(memory_space=pltpu.HBM)] * len(args), out_shap...  2.18 us
  transfers between devices with their start and end apart: 7, of which 5 were waited for; matrix products, arithmetic and copies ran while one was open for 0% of the time, Pallas kernels for 10%

profile of v23, /device:TPU:0, one launch (start us, length us, event | category | flops | bytes accessed | tf_op | source)
XLA Modules:
  0.0 53.3 jit_solution(9048011012419438340)
XLA Ops:
  0.6 0.8 %shard_map.86 = (f32[1,65,1,128]{3,2,1,0:T(1,128)S(1)}, f32[1,128]{1,0:T(1,128)S(1)}) custom-call(f32[1,64,128]{2,1,0:T(8,128)} %refs_0_.2, f32[1,128]{1,0:T(1,128)} %refs_1_.1, f32[1,128]{1,0:T(1,128)} %refs_2_.1), custom_call_target="tpu_custom_call" | custom-call | tf_op jit(solution)/shard_map/pallas_call | solution.py:304
  1.5 4.1 %collective-permute-start = (f32[1,65,1,128]{3,2,1,0:T(1,128)S(1)}, f32[1,65,1,128]{3,2,1,0:T(1,128)S(1)}, u32[]{:S(2)}, u32[]{:S(2)}) collective-permute-start(f32[1,65,1,128]{3,2,1,0:T(1,128)S(1)} %get-tuple-element.34.refs_0_), channel_id=1, source_target_pairs={{0,8},{2,10},{4,12},{6,14},{8,4},{10,6},{12,0},{14,2},{1,9},{3,11}... | collective-permute-start | bytes 99848 | tf_op jit(solution)/shard_map/ppermute | solution.py:353
  5.5 1.1 %collective-permute-start.1 = (f32[1,65,1,128]{3,2,1,0:T(1,128)S(1)}, f32[1,65,1,128]{3,2,1,0:T(1,128)S(1)}, u32[]{:S(2)}, u32[]{:S(2)}) collective-permute-start(f32[1,65,1,128]{3,2,1,0:T(1,128)S(1)} %get-tuple-element.34.refs_0_), channel_id=1, source_target_pairs={{0,12},{2,14},{4,8},{6,10},{8,0},{10,2},{12,4},{14,6},{1,13},{3,15... | collective-permute-start | bytes 99848 | tf_op jit(solution)/shard_map/ppermute | solution.py:353
  6.6 0.5 collective-permute-start.2
  7.1 1.4 %shard_map.87 = (bf16[8,512,256]{2,1,0:T(8,128)(2,1)S(1)}, f32[16,128]{1,0:T(8,128)S(1)}, f32[8,16,128]{2,1,0:T(8,128)S(1)}, f32[16,128]{1,0:T(8,128)S(1)}) custom-call(f32[16,128]{1,0:T(8,128)} %refs_0_.3, s32[8,16]{1,0:T(8,128)} %bitcast.4, s32[1,16]{1,0:T(1,128)} %bitcast.5, f32[16,64,128]{2,1,0:T(8,128)} %refs_3_.1), custom_call_target="tpu_custom_call" | custom-call | flops 100000000 | bytes 524288 | tf_op jit(solution)/shard_map/pallas_call | solution.py:304
  8.5 0.0 collective-permute-done.refs_1_
  8.5 1.7 %collective-permute-start.3 = (f32[2,65,1,128]{3,2,1,0:T(1,128)S(1)}, f32[2,65,1,128]{3,2,1,0:T(1,128)S(1)}, u32[]{:S(2)}, u32[]{:S(2)}) collective-permute-start(f32[2,65,1,128]{3,2,1,0:T(1,128)S(1)} %shard_map.88.refs_2_), channel_id=1, source_target_pairs={{0,2},{2,0},{4,6},{6,4},{8,10},{10,8},{12,14},{14,12},{1,3},{3,1},... | collective-permute-start | bytes 199688 | tf_op jit(solution)/shard_map/ppermute | solution.py:349
  10.2 0.2 collective-permute-done.1.refs_0_.refs_2_
  10.4 0.3 collective-permute-done.2.refs_1_.refs_3_
  10.7 1.5 %collective-permute-start.4 = (f32[2,65,1,128]{3,2,1,0:T(1,128)S(1)}, f32[2,65,1,128]{3,2,1,0:T(1,128)S(1)}, u32[]{:S(2)}, u32[]{:S(2)}) collective-permute-start(f32[2,65,1,128]{3,2,1,0:T(1,128)S(1)} %shard_map.89.refs_5_), channel_id=1, source_target_pairs={{0,2},{2,0},{4,6},{6,4},{8,10},{10,8},{12,14},{14,12},{1,3},{3,1},... | collective-permute-start | bytes 199688 | tf_op jit(solution)/shard_map/ppermute | solution.py:349
  12.2 1.6 %shard_map.90 = (f32[8,512,256]{2,1,0:T(8,128)S(1)}, bf16[512,512]{1,0:T(8,128)(2,1)S(1)}, f32[4,16,128]{2,1,0:T(8,128)S(1)}, f32[4,16,128]{2,1,0:T(8,128)S(1)}) custom-call(f32[1,65,1,128]{3,2,1,0:T(1,128)S(1)} %get-tuple-element.34.refs_0_, f32[1,65,1,128]{3,2,1,0:T(1,128)S(1)} %collective-permute-done.refs_1_, ...), custom_call_target="tpu_custom_call" | custom-call | flops 1073741824 | bytes 524288 | tf_op jit(solution)/shard_map/pallas_call | solution.py:336
  13.8 0.0 collective-permute-done.3.refs_0_
  13.8 0.9 %shard_map.91 = (f32[8,256,256]{2,1,0:T(8,128)S(1)}, bf16[256,512]{1,0:T(8,128)(2,1)S(1)}, f32[2,16,128]{2,1,0:T(8,128)S(1)}, f32[2,16,128]{2,1,0:T(8,128)S(1)}) custom-call(f32[2,65,1,128]{3,2,1,0:T(1,128)S(1)} %collective-permute-done.3.refs_0_, bf16[8,512,256]{2,1,0:T(8,128)(2,1)S(1)} %get-tuple-element.35.refs_4_.refs_1_.refs_6_, ...), custom_call_target="tpu_custom_call" | custom-call | flops 536870912 | bytes 524288 | tf_op jit(solution)/shard_map/pallas_call | solution.py:336
  14.7 0.3 collective-permute-done.4.refs_0_
  15.0 0.1 collective-permute-start.6
  15.1 0.9 %shard_map.94 = (f32[8,256,256]{2,1,0:T(8,128)S(1)}, bf16[256,512]{1,0:T(8,128)(2,1)S(1)}, f32[2,16,128]{2,1,0:T(8,128)S(1)}, f32[2,16,128]{2,1,0:T(8,128)S(1)}) custom-call(f32[2,65,1,128]{3,2,1,0:T(1,128)S(1)} %collective-permute-done.4.refs_0_, bf16[8,512,256]{2,1,0:T(8,128)(2,1)S(1)} %get-tuple-element.35.refs_4_.refs_1_.refs_6_, ...), custom_call_target="tpu_custom_call" | custom-call | flops 536870912 | bytes 524288 | tf_op jit(solution)/shard_map/pallas_call | solution.py:336
  16.0 0.1 collective-permute-start.5
  16.1 0.2 collective-permute-done.6.refs_10_
  16.3 0.8 %shard_map.96 = (f32[16,128]{1,0:T(8,128)S(1)}, f32[8,8,128]{2,1,0:T(8,128)S(1)}) custom-call(f32[8,512,256]{2,1,0:T(8,128)S(1)} %get-tuple-element.37.refs_0_, f32[8,256,256]{2,1,0:T(8,128)S(1)} %get-tuple-element.39.refs_1_, f32[8,256,256]{2,1,0:T(8,128)S(1)} %get-tuple-element.56.refs_2_, bf16[512,512]{1,0:T(8,128)(2,1)S(1)} %get-tuple-element.42.refs_3_, ...), custom_call_target="tpu_custom_call" | custom-call | flops 1000000000 | bytes 524288 | tf_op jit(solution)/shard_map/pallas_call | solution.py:383
  17.1 0.2 collective-permute-done.5.refs_10_
  17.3 35.4 %all_to_all.5.values_ref = f32[8,8,128]{2,1,0:T(8,128)S(1)} all-to-all(f32[8,8,128]{2,1,0:T(8,128)S(1)} %get-tuple-element.61), channel_id=1, replica_groups={{14,12,10,8,6,4,2,0},{15,13,11,9,7,5,3,1},{30,28,26,24,22,20,18,16},{31..., dimensions={0} | all-to-all | bytes 65536 | tf_op jit(solution)/shard_map/all_to_all | solution.py:400
  52.7 0.6 %shard_map.98 = (f32[1,128]{1,0:T(1,128)}, f32[16,128]{1,0:T(8,128)}) custom-call(f32[8,8,128]{2,1,0:T(8,128)S(1)} %all_to_all.5.values_ref, f32[1,128]{1,0:T(1,128)S(1)} %get-tuple-element.62.weight_ref, f32[16,128]{1,0:T(8,128)S(1)} %get-tuple-element.63.poten_ref), custom_call_target="tpu_custom_call" | custom-call | tf_op jit(solution)/shard_map/pallas_call | solution.py:402
  (6 shorter events, 0.1 us)
Async XLA Ops:
  1.5 7.0 %collective-permute-start = (f32[1,65,1,128]{3,2,1,0:T(1,128)S(1)}, f32[1,65,1,128]{3,2,1,0:T(1,128)S(1)}, u32[]{:S(2)}, u32[]{:S(2)}) collective-permute-start(f32[1,65,1,128]{3,2,1,0:T(1,128)S(1)} %get-tuple-element.34.refs_0_), channel_id=1, source_target_pairs={{0,8},{2,10},{4,12},{6,14},{8,4},{10,6},{12,0},{14,2},{1,9},{3,11}... | collective-permute-start | bytes 99848 | tf_op jit(solution)/shard_map/ppermute | solution.py:353
  5.5 4.8 %collective-permute-start.1 = (f32[1,65,1,128]{3,2,1,0:T(1,128)S(1)}, f32[1,65,1,128]{3,2,1,0:T(1,128)S(1)}, u32[]{:S(2)}, u32[]{:S(2)}) collective-permute-start(f32[1,65,1,128]{3,2,1,0:T(1,128)S(1)} %get-tuple-element.34.refs_0_), channel_id=1, source_target_pairs={{0,12},{2,14},{4,8},{6,10},{8,0},{10,2},{12,4},{14,6},{1,13},{3,15... | collective-permute-start | bytes 99848 | tf_op jit(solution)/shard_map/ppermute | solution.py:353
  6.6 4.1 %collective-permute-start.2 = (f32[1,65,1,128]{3,2,1,0:T(1,128)S(1)}, f32[1,65,1,128]{3,2,1,0:T(1,128)S(1)}, u32[]{:S(2)}, u32[]{:S(2)}) collective-permute-start(f32[1,65,1,128]{3,2,1,0:T(1,128)S(1)} %get-tuple-element.34.refs_0_), channel_id=1, source_target_pairs={{0,4},{2,6},{4,0},{6,2},{8,12},{10,14},{12,8},{14,10},{1,5},{3,7},... | collective-permute-start | bytes 99848 | tf_op jit(solution)/shard_map/ppermute | solution.py:353
  8.5 5.3 %collective-permute-start.3 = (f32[2,65,1,128]{3,2,1,0:T(1,128)S(1)}, f32[2,65,1,128]{3,2,1,0:T(1,128)S(1)}, u32[]{:S(2)}, u32[]{:S(2)}) collective-permute-start(f32[2,65,1,128]{3,2,1,0:T(1,128)S(1)} %shard_map.88.refs_2_), channel_id=1, source_target_pairs={{0,2},{2,0},{4,6},{6,4},{8,10},{10,8},{12,14},{14,12},{1,3},{3,1},... | collective-permute-start | bytes 199688 | tf_op jit(solution)/shard_map/ppermute | solution.py:349
  10.7 4.3 %collective-permute-start.4 = (f32[2,65,1,128]{3,2,1,0:T(1,128)S(1)}, f32[2,65,1,128]{3,2,1,0:T(1,128)S(1)}, u32[]{:S(2)}, u32[]{:S(2)}) collective-permute-start(f32[2,65,1,128]{3,2,1,0:T(1,128)S(1)} %shard_map.89.refs_5_), channel_id=1, source_target_pairs={{0,2},{2,0},{4,6},{6,4},{8,10},{10,8},{12,14},{14,12},{1,3},{3,1},... | collective-permute-start | bytes 199688 | tf_op jit(solution)/shard_map/ppermute | solution.py:349
  15.0 1.2 %collective-permute-start.6 = (f32[16,128]{1,0:T(8,128)S(1)}, f32[16,128]{1,0:T(8,128)S(1)}, u32[]{:S(2)}, u32[]{:S(2)}) collective-permute-start(f32[16,128]{1,0:T(8,128)S(1)} %get-tuple-element.51.refs_2_.refs_9_), channel_id=1, source_target_pairs={{0,1},{1,0},{2,3},{3,2},{4,5},{5,4},{6,7},{7,6},{8,9},{9,8},{10,11... | collective-permute-start | bytes 24584 | tf_op jit(solution)/shard_map/ppermute | solution.py:394
  16.0 1.2 %collective-permute-start.5 = (f32[16,128]{1,0:T(8,128)S(1)}, f32[16,128]{1,0:T(8,128)S(1)}, u32[]{:S(2)}, u32[]{:S(2)}) collective-permute-start(f32[16,128]{1,0:T(8,128)S(1)} %get-tuple-element.54.refs_9_), channel_id=1, source_target_pairs={{0,1},{1,0},{2,3},{3,2},{4,5},{5,4},{6,7},{7,6},{8,9},{9,8},{10,11... | collective-permute-start | bytes 24584 | tf_op jit(solution)/shard_map/ppermute | solution.py:397

commit v24 on v19

--- a/solution.py
+++ b/solution.py
@@ -229,7 +229,7 @@
         for index in range(ref.shape[0] // cells)
     ]
     used = [jnp.max(mask_ref[place], axis=0, keepdims=True) > 0.5 * very_low for place in range(shards)]
-    ranks = [shards - 1 - block for block in blocks_at(shards)]
+    ranks = [shards - 1 - jnp.where(block > 1, block ^ 1, block) for block in blocks_at(shards)]
     sums = []
     for place, (group, rows) in enumerate(spots):
         acc = jnp.zeros((cells, cells), jnp.float32)
@@ -396,7 +396,8 @@
     other_one = lax.ppermute(own_zero, "tgt", between)
     given = columns_of(0, last_zero, peaks_zero, own_zero, other_zero, [])
     potential_src, columns = columns_of(1, last_one, peaks_one, own_one, other_one, given)
-    arrived = lax.all_to_all(columns, "src", 0, 0, axis_index_groups=[list(range(shards))[::-1]])
+    members = [block ^ (block > 1) for block in reversed(range(shards))]
+    arrived = lax.all_to_all(columns, "src", 0, 0, axis_index_groups=[members])
     outs = [f32(1, cells), f32(rows, cells)]
     potential_new, potential_src = call(merge_kernel, [VM] * 3, outs)(arrived, weight, potential_src)
     return potential_src, potential_new

time: 53 us -> 53.8 us (1.015)
  blocking collectives: 8.28 us -> 9.04 us
    all_to_all x1, blocking collectives: 8.28 us -> 9.04 us  [dense_device(): arrived = lax.all_to_all(columns, 'src', 0, 0, axis_index_groups=[members])]
where the time goes in v24:
time: 53.8 us; the launch traced here: 53.5 us
  Pallas kernels  33.9 us (63%)
  blocking collectives  9.04 us (17%)
  starting transfers between devices  8.96 us (17%)
  waiting for transfers between devices  0.94 us (2%)
  between operations  0.73 us (1%)
    pallas_call x2, Pallas kernels, columns_of(): call(functools.partial(column_kernel, groups, core), [VM] * (2 * groups +...  27.6 us
    all_to_all x1, blocking collectives, dense_device(): arrived = lax.all_to_all(columns, 'src', 0, 0, axis_index_groups=[members])  9.04 us
    ppermute x3, starting transfers between devices, moved(): return lax.ppermute(array, 'src', moves)  5.67 us
    pallas_call x4, Pallas kernels, tiles(): call(functools.partial(tile_kernel, len(packs), core), [VM] * (len(packs)...  3.42 us
    ppermute x2, starting transfers between devices, swapped(): return lax.ppermute(array, 'src', [(i, i ^ 1) for i in range(shards)])  3.15 us
    pallas_call x2, Pallas kernels, reading(): call(kernel, [pl.BlockSpec(memory_space=pltpu.HBM)] * len(args), out_shap...  2.18 us
  transfers between devices with their start and end apart: 7, of which 4 were waited for; matrix products, arithmetic and copies ran while one was open for 0% of the time, Pallas kernels for 61%

profile of v24, /device:TPU:0, one launch (start us, length us, event | category | flops | bytes accessed | tf_op | source)
XLA Modules:
  0.0 53.5 jit_solution(18105833794346234336)
XLA Ops:
  0.6 0.8 %shard_map.86 = (f32[1,65,1,128]{3,2,1,0:T(1,128)S(1)}, f32[1,128]{1,0:T(1,128)S(1)}) custom-call(f32[1,64,128]{2,1,0:T(8,128)} %refs_0_.2, f32[1,128]{1,0:T(1,128)} %refs_1_.1, f32[1,128]{1,0:T(1,128)} %refs_2_.1), custom_call_target="tpu_custom_call" | custom-call | tf_op jit(solution)/shard_map/pallas_call | solution.py:303
  1.5 4.1 %collective-permute-start = (f32[1,65,1,128]{3,2,1,0:T(1,128)S(1)}, f32[1,65,1,128]{3,2,1,0:T(1,128)S(1)}, u32[]{:S(2)}, u32[]{:S(2)}) collective-permute-start(f32[1,65,1,128]{3,2,1,0:T(1,128)S(1)} %get-tuple-element.34.refs_0_), channel_id=1, source_target_pairs={{0,8},{2,10},{4,12},{6,14},{8,4},{10,6},{12,0},{14,2},{1,9},{3,11}... | collective-permute-start | bytes 99848 | tf_op jit(solution)/shard_map/ppermute | solution.py:352
  5.5 1.1 %collective-permute-start.1 = (f32[1,65,1,128]{3,2,1,0:T(1,128)S(1)}, f32[1,65,1,128]{3,2,1,0:T(1,128)S(1)}, u32[]{:S(2)}, u32[]{:S(2)}) collective-permute-start(f32[1,65,1,128]{3,2,1,0:T(1,128)S(1)} %get-tuple-element.34.refs_0_), channel_id=1, source_target_pairs={{0,12},{2,14},{4,8},{6,10},{8,0},{10,2},{12,4},{14,6},{1,13},{3,15... | collective-permute-start | bytes 99848 | tf_op jit(solution)/shard_map/ppermute | solution.py:352
  6.6 0.5 collective-permute-start.2
  7.1 1.4 %shard_map.87 = (bf16[8,512,256]{2,1,0:T(8,128)(2,1)S(1)}, f32[16,128]{1,0:T(8,128)S(1)}, f32[8,16,128]{2,1,0:T(8,128)S(1)}, f32[16,128]{1,0:T(8,128)S(1)}) custom-call(f32[16,128]{1,0:T(8,128)} %refs_0_.3, s32[8,16]{1,0:T(8,128)} %bitcast.4, s32[1,16]{1,0:T(1,128)} %bitcast.5, f32[16,64,128]{2,1,0:T(8,128)} %refs_3_.1), custom_call_target="tpu_custom_call" | custom-call | flops 100000000 | bytes 524288 | tf_op jit(solution)/shard_map/pallas_call | solution.py:303
  8.5 0.0 collective-permute-done.refs_1_
  8.5 1.7 %collective-permute-start.3 = (f32[2,65,1,128]{3,2,1,0:T(1,128)S(1)}, f32[2,65,1,128]{3,2,1,0:T(1,128)S(1)}, u32[]{:S(2)}, u32[]{:S(2)}) collective-permute-start(f32[2,65,1,128]{3,2,1,0:T(1,128)S(1)} %shard_map.88.refs_2_), channel_id=1, source_target_pairs={{0,2},{2,0},{4,6},{6,4},{8,10},{10,8},{12,14},{14,12},{1,3},{3,1},... | collective-permute-start | bytes 199688 | tf_op jit(solution)/shard_map/ppermute | solution.py:348
  10.2 0.2 collective-permute-done.1.refs_0_.refs_2_
  10.4 0.3 collective-permute-done.2.refs_1_.refs_3_
  10.7 1.5 %collective-permute-start.4 = (f32[2,65,1,128]{3,2,1,0:T(1,128)S(1)}, f32[2,65,1,128]{3,2,1,0:T(1,128)S(1)}, u32[]{:S(2)}, u32[]{:S(2)}) collective-permute-start(f32[2,65,1,128]{3,2,1,0:T(1,128)S(1)} %shard_map.89.refs_5_), channel_id=1, source_target_pairs={{0,2},{2,0},{4,6},{6,4},{8,10},{10,8},{12,14},{14,12},{1,3},{3,1},... | collective-permute-start | bytes 199688 | tf_op jit(solution)/shard_map/ppermute | solution.py:348
  12.2 1.6 %shard_map.90 = (f32[8,512,256]{2,1,0:T(8,128)S(1)}, bf16[512,512]{1,0:T(8,128)(2,1)S(1)}, f32[4,16,128]{2,1,0:T(8,128)S(1)}, f32[4,16,128]{2,1,0:T(8,128)S(1)}) custom-call(f32[1,65,1,128]{3,2,1,0:T(1,128)S(1)} %get-tuple-element.34.refs_0_, f32[1,65,1,128]{3,2,1,0:T(1,128)S(1)} %collective-permute-done.refs_1_, ...), custom_call_target="tpu_custom_call" | custom-call | flops 1073741824 | bytes 524288 | tf_op jit(solution)/shard_map/pallas_call | solution.py:335
  13.8 0.0 collective-permute-done.3.refs_0_
  13.9 0.9 %shard_map.91 = (f32[8,256,256]{2,1,0:T(8,128)S(1)}, bf16[256,512]{1,0:T(8,128)(2,1)S(1)}, f32[2,16,128]{2,1,0:T(8,128)S(1)}, f32[2,16,128]{2,1,0:T(8,128)S(1)}) custom-call(f32[2,65,1,128]{3,2,1,0:T(1,128)S(1)} %collective-permute-done.3.refs_0_, bf16[8,512,256]{2,1,0:T(8,128)(2,1)S(1)} %get-tuple-element.35.refs_4_.refs_1_.refs_6_, ...), custom_call_target="tpu_custom_call" | custom-call | flops 536870912 | bytes 524288 | tf_op jit(solution)/shard_map/pallas_call | solution.py:335
  14.7 0.3 collective-permute-done.4.refs_0_
  15.0 0.1 collective-permute-start.6
  15.1 0.9 %shard_map.94 = (f32[8,256,256]{2,1,0:T(8,128)S(1)}, bf16[256,512]{1,0:T(8,128)(2,1)S(1)}, f32[2,16,128]{2,1,0:T(8,128)S(1)}, f32[2,16,128]{2,1,0:T(8,128)S(1)}) custom-call(f32[2,65,1,128]{3,2,1,0:T(1,128)S(1)} %collective-permute-done.4.refs_0_, bf16[8,512,256]{2,1,0:T(8,128)(2,1)S(1)} %get-tuple-element.35.refs_4_.refs_1_.refs_6_, ...), custom_call_target="tpu_custom_call" | custom-call | flops 536870912 | bytes 524288 | tf_op jit(solution)/shard_map/pallas_call | solution.py:335
  16.1 0.1 collective-permute-start.5
  16.2 0.1 collective-permute-done.6.refs_10_
  16.3 27.5 %shard_map.96 = (f32[16,128]{1,0:T(8,128)S(1)}, f32[8,1,128]{2,1,0:T(1,128)S(1)}) custom-call(f32[8,512,256]{2,1,0:T(8,128)S(1)} %get-tuple-element.37.refs_0_, f32[8,256,256]{2,1,0:T(8,128)S(1)} %get-tuple-element.39.refs_1_, f32[8,256,256]{2,1,0:T(8,128)S(1)} %get-tuple-element.56.refs_2_, bf16[512,512]{1,0:T(8,128)(2,1)S(1)} %get-tuple-element.42.refs_3_, ...), custom_call_target="tpu_custom_call" | custom-call | flops 1000000000 | bytes 524288 | tf_op jit(solution)/shard_map/pallas_call | solution.py:382
  43.8 0.0 collective-permute-done.5.refs_10_
  43.9 9.0 %all_to_all.5.values_ref = f32[8,1,128]{2,1,0:T(1,128)S(1)} all-to-all(f32[8,1,128]{2,1,0:T(1,128)S(1)} %get-tuple-element.61), channel_id=1, replica_groups={{12,14,8,10,4,6,2,0},{13,15,9,11,5,7,3,1},{28,30,24,26,20,22,18,16},{29..., dimensions={0} | all-to-all | bytes 8192 | tf_op jit(solution)/shard_map/all_to_all | solution.py:400
  52.9 0.6 %shard_map.98 = (f32[1,128]{1,0:T(1,128)}, f32[16,128]{1,0:T(8,128)}) custom-call(f32[8,1,128]{2,1,0:T(1,128)S(1)} %all_to_all.5.values_ref, f32[1,128]{1,0:T(1,128)S(1)} %get-tuple-element.62.weight_ref, f32[16,128]{1,0:T(8,128)S(1)} %get-tuple-element.63.poten_ref), custom_call_target="tpu_custom_call" | custom-call | tf_op jit(solution)/shard_map/pallas_call | solution.py:402
  (6 shorter events, 0.1 us)
Async XLA Ops:
  1.5 7.0 %collective-permute-start = (f32[1,65,1,128]{3,2,1,0:T(1,128)S(1)}, f32[1,65,1,128]{3,2,1,0:T(1,128)S(1)}, u32[]{:S(2)}, u32[]{:S(2)}) collective-permute-start(f32[1,65,1,128]{3,2,1,0:T(1,128)S(1)} %get-tuple-element.34.refs_0_), channel_id=1, source_target_pairs={{0,8},{2,10},{4,12},{6,14},{8,4},{10,6},{12,0},{14,2},{1,9},{3,11}... | collective-permute-start | bytes 99848 | tf_op jit(solution)/shard_map/ppermute | solution.py:352
  5.5 4.8 %collective-permute-start.1 = (f32[1,65,1,128]{3,2,1,0:T(1,128)S(1)}, f32[1,65,1,128]{3,2,1,0:T(1,128)S(1)}, u32[]{:S(2)}, u32[]{:S(2)}) collective-permute-start(f32[1,65,1,128]{3,2,1,0:T(1,128)S(1)} %get-tuple-element.34.refs_0_), channel_id=1, source_target_pairs={{0,12},{2,14},{4,8},{6,10},{8,0},{10,2},{12,4},{14,6},{1,13},{3,15... | collective-permute-start | bytes 99848 | tf_op jit(solution)/shard_map/ppermute | solution.py:352
  6.6 4.1 %collective-permute-start.2 = (f32[1,65,1,128]{3,2,1,0:T(1,128)S(1)}, f32[1,65,1,128]{3,2,1,0:T(1,128)S(1)}, u32[]{:S(2)}, u32[]{:S(2)}) collective-permute-start(f32[1,65,1,128]{3,2,1,0:T(1,128)S(1)} %get-tuple-element.34.refs_0_), channel_id=1, source_target_pairs={{0,4},{2,6},{4,0},{6,2},{8,12},{10,14},{12,8},{14,10},{1,5},{3,7},... | collective-permute-start | bytes 99848 | tf_op jit(solution)/shard_map/ppermute | solution.py:352
  8.5 5.3 %collective-permute-start.3 = (f32[2,65,1,128]{3,2,1,0:T(1,128)S(1)}, f32[2,65,1,128]{3,2,1,0:T(1,128)S(1)}, u32[]{:S(2)}, u32[]{:S(2)}) collective-permute-start(f32[2,65,1,128]{3,2,1,0:T(1,128)S(1)} %shard_map.88.refs_2_), channel_id=1, source_target_pairs={{0,2},{2,0},{4,6},{6,4},{8,10},{10,8},{12,14},{14,12},{1,3},{3,1},... | collective-permute-start | bytes 199688 | tf_op jit(solution)/shard_map/ppermute | solution.py:348
  10.7 4.3 %collective-permute-start.4 = (f32[2,65,1,128]{3,2,1,0:T(1,128)S(1)}, f32[2,65,1,128]{3,2,1,0:T(1,128)S(1)}, u32[]{:S(2)}, u32[]{:S(2)}) collective-permute-start(f32[2,65,1,128]{3,2,1,0:T(1,128)S(1)} %shard_map.89.refs_5_), channel_id=1, source_target_pairs={{0,2},{2,0},{4,6},{6,4},{8,10},{10,8},{12,14},{14,12},{1,3},{3,1},... | collective-permute-start | bytes 199688 | tf_op jit(solution)/shard_map/ppermute | solution.py:348
  15.0 1.2 %collective-permute-start.6 = (f32[16,128]{1,0:T(8,128)S(1)}, f32[16,128]{1,0:T(8,128)S(1)}, u32[]{:S(2)}, u32[]{:S(2)}) collective-permute-start(f32[16,128]{1,0:T(8,128)S(1)} %get-tuple-element.51.refs_2_.refs_9_), channel_id=1, source_target_pairs={{0,1},{1,0},{2,3},{3,2},{4,5},{5,4},{6,7},{7,6},{8,9},{9,8},{10,11... | collective-permute-start | bytes 24584 | tf_op jit(solution)/shard_map/ppermute | solution.py:393
  16.1 27.8 %collective-permute-start.5 = (f32[16,128]{1,0:T(8,128)S(1)}, f32[16,128]{1,0:T(8,128)S(1)}, u32[]{:S(2)}, u32[]{:S(2)}) collective-permute-start(f32[16,128]{1,0:T(8,128)S(1)} %get-tuple-element.54.refs_9_), channel_id=1, source_target_pairs={{0,1},{1,0},{2,3},{3,2},{4,5},{5,4},{6,7},{7,6},{8,9},{9,8},{10,11... | collective-permute-start | bytes 24584 | tf_op jit(solution)/shard_map/ppermute | solution.py:396

commit v25 on v19

--- a/solution.py
+++ b/solution.py
@@ -51,6 +51,10 @@
         senders = [receivers.index(there) for there in range(shards // 2)]
         near.append(2 * sum(jnp.where(at == there, sender, 0) for there, sender in enumerate(senders)) + odd)
     return near + [block ^ 1 for block in near]
+
+
+def members_of(shards):
+    return sorted(range(shards), key=lambda at: (-(at // 2 + at % 2), -(at % 2)))
 
 
 def read_all(hbm, held, sems):
@@ -229,7 +233,8 @@
         for index in range(ref.shape[0] // cells)
     ]
     used = [jnp.max(mask_ref[place], axis=0, keepdims=True) > 0.5 * very_low for place in range(shards)]
-    ranks = [shards - 1 - block for block in blocks_at(shards)]
+    places = [members_of(shards).index(block) for block in range(shards)]
+    ranks = [sum(jnp.where(block == at, rank, 0) for at, rank in enumerate(places)) for block in blocks_at(shards)]
     sums = []
     for place, (group, rows) in enumerate(spots):
         acc = jnp.zeros((cells, cells), jnp.float32)
@@ -396,7 +401,7 @@
     other_one = lax.ppermute(own_zero, "tgt", between)
     given = columns_of(0, last_zero, peaks_zero, own_zero, other_zero, [])
     potential_src, columns = columns_of(1, last_one, peaks_one, own_one, other_one, given)
-    arrived = lax.all_to_all(columns, "src", 0, 0, axis_index_groups=[list(range(shards))[::-1]])
+    arrived = lax.all_to_all(columns, "src", 0, 0, axis_index_groups=[members_of(shards)])
     outs = [f32(1, cells), f32(rows, cells)]
     potential_new, potential_src = call(merge_kernel, [VM] * 3, outs)(arrived, weight, potential_src)
     return potential_src, potential_new

time: 53 us -> 53 us (level)
  no operation moved by 1% of the time
where the time goes in v25:
time: 53 us; the launch traced here: 52.8 us
  Pallas kernels  33.9 us (64%)
  starting transfers between devices  8.96 us (17%)
  blocking collectives  8.27 us (16%)
  waiting for transfers between devices  0.94 us (2%)
  between operations  0.73 us (1%)
    pallas_call x2, Pallas kernels, columns_of(): call(functools.partial(column_kernel, groups, core), [VM] * (2 * groups +...  27.6 us
    all_to_all x1, blocking collectives, dense_device(): lax.all_to_all(columns, 'src', 0, 0, axis_index_groups=[members_of(shards)])  8.27 us
    ppermute x3, starting transfers between devices, moved(): return lax.ppermute(array, 'src', moves)  5.67 us
    pallas_call x4, Pallas kernels, tiles(): call(functools.partial(tile_kernel, len(packs), core), [VM] * (len(packs)...  3.42 us
    ppermute x2, starting transfers between devices, swapped(): return lax.ppermute(array, 'src', [(i, i ^ 1) for i in range(shards)])  3.15 us
    pallas_call x2, Pallas kernels, reading(): call(kernel, [pl.BlockSpec(memory_space=pltpu.HBM)] * len(args), out_shap...  2.18 us
  transfers between devices with their start and end apart: 7, of which 4 were waited for; matrix products, arithmetic and copies ran while one was open for 0% of the time, Pallas kernels for 61%

profile of v25, /device:TPU:0, one launch (start us, length us, event | category | flops | bytes accessed | tf_op | source)
XLA Modules:
  0.0 52.8 jit_solution(16246352330694294388)
XLA Ops:
  0.6 0.8 %shard_map.86 = (f32[1,65,1,128]{3,2,1,0:T(1,128)S(1)}, f32[1,128]{1,0:T(1,128)S(1)}) custom-call(f32[1,64,128]{2,1,0:T(8,128)} %refs_0_.2, f32[1,128]{1,0:T(1,128)} %refs_1_.1, f32[1,128]{1,0:T(1,128)} %refs_2_.1), custom_call_target="tpu_custom_call" | custom-call | tf_op jit(solution)/shard_map/pallas_call | solution.py:308
  1.5 4.1 %collective-permute-start = (f32[1,65,1,128]{3,2,1,0:T(1,128)S(1)}, f32[1,65,1,128]{3,2,1,0:T(1,128)S(1)}, u32[]{:S(2)}, u32[]{:S(2)}) collective-permute-start(f32[1,65,1,128]{3,2,1,0:T(1,128)S(1)} %get-tuple-element.34.refs_0_), channel_id=1, source_target_pairs={{0,8},{2,10},{4,12},{6,14},{8,4},{10,6},{12,0},{14,2},{1,9},{3,11}... | collective-permute-start | bytes 99848 | tf_op jit(solution)/shard_map/ppermute | solution.py:357
  5.5 1.1 %collective-permute-start.1 = (f32[1,65,1,128]{3,2,1,0:T(1,128)S(1)}, f32[1,65,1,128]{3,2,1,0:T(1,128)S(1)}, u32[]{:S(2)}, u32[]{:S(2)}) collective-permute-start(f32[1,65,1,128]{3,2,1,0:T(1,128)S(1)} %get-tuple-element.34.refs_0_), channel_id=1, source_target_pairs={{0,12},{2,14},{4,8},{6,10},{8,0},{10,2},{12,4},{14,6},{1,13},{3,15... | collective-permute-start | bytes 99848 | tf_op jit(solution)/shard_map/ppermute | solution.py:357
  6.6 0.5 collective-permute-start.2
  7.1 1.4 %shard_map.87 = (bf16[8,512,256]{2,1,0:T(8,128)(2,1)S(1)}, f32[16,128]{1,0:T(8,128)S(1)}, f32[8,16,128]{2,1,0:T(8,128)S(1)}, f32[16,128]{1,0:T(8,128)S(1)}) custom-call(f32[16,128]{1,0:T(8,128)} %refs_0_.3, s32[8,16]{1,0:T(8,128)} %bitcast.4, s32[1,16]{1,0:T(1,128)} %bitcast.5, f32[16,64,128]{2,1,0:T(8,128)} %refs_3_.1), custom_call_target="tpu_custom_call" | custom-call | flops 100000000 | bytes 524288 | tf_op jit(solution)/shard_map/pallas_call | solution.py:308
  8.5 0.0 collective-permute-done.refs_1_
  8.5 1.7 %collective-permute-start.3 = (f32[2,65,1,128]{3,2,1,0:T(1,128)S(1)}, f32[2,65,1,128]{3,2,1,0:T(1,128)S(1)}, u32[]{:S(2)}, u32[]{:S(2)}) collective-permute-start(f32[2,65,1,128]{3,2,1,0:T(1,128)S(1)} %shard_map.88.refs_2_), channel_id=1, source_target_pairs={{0,2},{2,0},{4,6},{6,4},{8,10},{10,8},{12,14},{14,12},{1,3},{3,1},... | collective-permute-start | bytes 199688 | tf_op jit(solution)/shard_map/ppermute | solution.py:353
  10.2 0.2 collective-permute-done.1.refs_0_.refs_2_
  10.4 0.3 collective-permute-done.2.refs_1_.refs_3_
  10.7 1.5 %collective-permute-start.4 = (f32[2,65,1,128]{3,2,1,0:T(1,128)S(1)}, f32[2,65,1,128]{3,2,1,0:T(1,128)S(1)}, u32[]{:S(2)}, u32[]{:S(2)}) collective-permute-start(f32[2,65,1,128]{3,2,1,0:T(1,128)S(1)} %shard_map.89.refs_5_), channel_id=1, source_target_pairs={{0,2},{2,0},{4,6},{6,4},{8,10},{10,8},{12,14},{14,12},{1,3},{3,1},... | collective-permute-start | bytes 199688 | tf_op jit(solution)/shard_map/ppermute | solution.py:353
  12.2 1.6 %shard_map.90 = (f32[8,512,256]{2,1,0:T(8,128)S(1)}, bf16[512,512]{1,0:T(8,128)(2,1)S(1)}, f32[4,16,128]{2,1,0:T(8,128)S(1)}, f32[4,16,128]{2,1,0:T(8,128)S(1)}) custom-call(f32[1,65,1,128]{3,2,1,0:T(1,128)S(1)} %get-tuple-element.34.refs_0_, f32[1,65,1,128]{3,2,1,0:T(1,128)S(1)} %collective-permute-done.refs_1_, ...), custom_call_target="tpu_custom_call" | custom-call | flops 1073741824 | bytes 524288 | tf_op jit(solution)/shard_map/pallas_call | solution.py:340
  13.8 0.0 collective-permute-done.3.refs_0_
  13.9 0.9 %shard_map.91 = (f32[8,256,256]{2,1,0:T(8,128)S(1)}, bf16[256,512]{1,0:T(8,128)(2,1)S(1)}, f32[2,16,128]{2,1,0:T(8,128)S(1)}, f32[2,16,128]{2,1,0:T(8,128)S(1)}) custom-call(f32[2,65,1,128]{3,2,1,0:T(1,128)S(1)} %collective-permute-done.3.refs_0_, bf16[8,512,256]{2,1,0:T(8,128)(2,1)S(1)} %get-tuple-element.35.refs_4_.refs_1_.refs_6_, ...), custom_call_target="tpu_custom_call" | custom-call | flops 536870912 | bytes 524288 | tf_op jit(solution)/shard_map/pallas_call | solution.py:340
  14.7 0.3 collective-permute-done.4.refs_0_
  15.0 0.1 collective-permute-start.6
  15.1 0.9 %shard_map.94 = (f32[8,256,256]{2,1,0:T(8,128)S(1)}, bf16[256,512]{1,0:T(8,128)(2,1)S(1)}, f32[2,16,128]{2,1,0:T(8,128)S(1)}, f32[2,16,128]{2,1,0:T(8,128)S(1)}) custom-call(f32[2,65,1,128]{3,2,1,0:T(1,128)S(1)} %collective-permute-done.4.refs_0_, bf16[8,512,256]{2,1,0:T(8,128)(2,1)S(1)} %get-tuple-element.35.refs_4_.refs_1_.refs_6_, ...), custom_call_target="tpu_custom_call" | custom-call | flops 536870912 | bytes 524288 | tf_op jit(solution)/shard_map/pallas_call | solution.py:340
  16.1 0.1 collective-permute-start.5
  16.2 0.1 collective-permute-done.6.refs_10_
  16.3 27.6 %shard_map.96 = (f32[16,128]{1,0:T(8,128)S(1)}, f32[8,1,128]{2,1,0:T(1,128)S(1)}) custom-call(f32[8,512,256]{2,1,0:T(8,128)S(1)} %get-tuple-element.37.refs_0_, f32[8,256,256]{2,1,0:T(8,128)S(1)} %get-tuple-element.39.refs_1_, f32[8,256,256]{2,1,0:T(8,128)S(1)} %get-tuple-element.56.refs_2_, bf16[512,512]{1,0:T(8,128)(2,1)S(1)} %get-tuple-element.42.refs_3_, ...), custom_call_target="tpu_custom_call" | custom-call | flops 1000000000 | bytes 524288 | tf_op jit(solution)/shard_map/pallas_call | solution.py:387
  43.8 0.0 collective-permute-done.5.refs_10_
  43.9 8.3 %all_to_all.5.values_ref = f32[8,1,128]{2,1,0:T(1,128)S(1)} all-to-all(f32[8,1,128]{2,1,0:T(1,128)S(1)} %get-tuple-element.61), channel_id=1, replica_groups={{14,10,12,6,8,2,4,0},{15,11,13,7,9,3,5,1},{30,26,28,22,24,18,20,16},{31..., dimensions={0} | all-to-all | bytes 8192 | tf_op jit(solution)/shard_map/all_to_all | solution.py:404
  52.2 0.6 %shard_map.98 = (f32[1,128]{1,0:T(1,128)}, f32[16,128]{1,0:T(8,128)}) custom-call(f32[8,1,128]{2,1,0:T(1,128)S(1)} %all_to_all.5.values_ref, f32[1,128]{1,0:T(1,128)S(1)} %get-tuple-element.62.weight_ref, f32[16,128]{1,0:T(8,128)S(1)} %get-tuple-element.63.poten_ref), custom_call_target="tpu_custom_call" | custom-call | tf_op jit(solution)/shard_map/pallas_call | solution.py:406
  (6 shorter events, 0.1 us)
Async XLA Ops:
  1.5 7.0 %collective-permute-start = (f32[1,65,1,128]{3,2,1,0:T(1,128)S(1)}, f32[1,65,1,128]{3,2,1,0:T(1,128)S(1)}, u32[]{:S(2)}, u32[]{:S(2)}) collective-permute-start(f32[1,65,1,128]{3,2,1,0:T(1,128)S(1)} %get-tuple-element.34.refs_0_), channel_id=1, source_target_pairs={{0,8},{2,10},{4,12},{6,14},{8,4},{10,6},{12,0},{14,2},{1,9},{3,11}... | collective-permute-start | bytes 99848 | tf_op jit(solution)/shard_map/ppermute | solution.py:357
  5.5 4.8 %collective-permute-start.1 = (f32[1,65,1,128]{3,2,1,0:T(1,128)S(1)}, f32[1,65,1,128]{3,2,1,0:T(1,128)S(1)}, u32[]{:S(2)}, u32[]{:S(2)}) collective-permute-start(f32[1,65,1,128]{3,2,1,0:T(1,128)S(1)} %get-tuple-element.34.refs_0_), channel_id=1, source_target_pairs={{0,12},{2,14},{4,8},{6,10},{8,0},{10,2},{12,4},{14,6},{1,13},{3,15... | collective-permute-start | bytes 99848 | tf_op jit(solution)/shard_map/ppermute | solution.py:357
  6.6 4.1 %collective-permute-start.2 = (f32[1,65,1,128]{3,2,1,0:T(1,128)S(1)}, f32[1,65,1,128]{3,2,1,0:T(1,128)S(1)}, u32[]{:S(2)}, u32[]{:S(2)}) collective-permute-start(f32[1,65,1,128]{3,2,1,0:T(1,128)S(1)} %get-tuple-element.34.refs_0_), channel_id=1, source_target_pairs={{0,4},{2,6},{4,0},{6,2},{8,12},{10,14},{12,8},{14,10},{1,5},{3,7},... | collective-permute-start | bytes 99848 | tf_op jit(solution)/shard_map/ppermute | solution.py:357
  8.5 5.3 %collective-permute-start.3 = (f32[2,65,1,128]{3,2,1,0:T(1,128)S(1)}, f32[2,65,1,128]{3,2,1,0:T(1,128)S(1)}, u32[]{:S(2)}, u32[]{:S(2)}) collective-permute-start(f32[2,65,1,128]{3,2,1,0:T(1,128)S(1)} %shard_map.88.refs_2_), channel_id=1, source_target_pairs={{0,2},{2,0},{4,6},{6,4},{8,10},{10,8},{12,14},{14,12},{1,3},{3,1},... | collective-permute-start | bytes 199688 | tf_op jit(solution)/shard_map/ppermute | solution.py:353
  10.7 4.3 %collective-permute-start.4 = (f32[2,65,1,128]{3,2,1,0:T(1,128)S(1)}, f32[2,65,1,128]{3,2,1,0:T(1,128)S(1)}, u32[]{:S(2)}, u32[]{:S(2)}) collective-permute-start(f32[2,65,1,128]{3,2,1,0:T(1,128)S(1)} %shard_map.89.refs_5_), channel_id=1, source_target_pairs={{0,2},{2,0},{4,6},{6,4},{8,10},{10,8},{12,14},{14,12},{1,3},{3,1},... | collective-permute-start | bytes 199688 | tf_op jit(solution)/shard_map/ppermute | solution.py:353
  15.0 1.2 %collective-permute-start.6 = (f32[16,128]{1,0:T(8,128)S(1)}, f32[16,128]{1,0:T(8,128)S(1)}, u32[]{:S(2)}, u32[]{:S(2)}) collective-permute-start(f32[16,128]{1,0:T(8,128)S(1)} %get-tuple-element.51.refs_2_.refs_9_), channel_id=1, source_target_pairs={{0,1},{1,0},{2,3},{3,2},{4,5},{5,4},{6,7},{7,6},{8,9},{9,8},{10,11... | collective-permute-start | bytes 24584 | tf_op jit(solution)/shard_map/ppermute | solution.py:398
  16.1 27.8 %collective-permute-start.5 = (f32[16,128]{1,0:T(8,128)S(1)}, f32[16,128]{1,0:T(8,128)S(1)}, u32[]{:S(2)}, u32[]{:S(2)}) collective-permute-start(f32[16,128]{1,0:T(8,128)S(1)} %get-tuple-element.54.refs_9_), channel_id=1, source_target_pairs={{0,1},{1,0},{2,3},{3,2},{4,5},{5,4},{6,7},{7,6},{8,9},{9,8},{10,11... | collective-permute-start | bytes 24584 | tf_op jit(solution)/shard_map/ppermute | solution.py:401

commit v26 on v21

--- a/solution.py
+++ b/solution.py
@@ -51,6 +51,10 @@
         senders = [receivers.index(there) for there in range(shards // 2)]
         near.append(2 * sum(jnp.where(at == there, sender, 0) for there, sender in enumerate(senders)) + odd)
     return near + [block ^ 1 for block in near]
+
+
+def members_of(shards):
+    return sorted(range(shards), key=lambda at: (-(at // 2 + at % 2), -(at % 2)))
 
 
 def read_all(hbm, held, sems):
@@ -236,7 +240,8 @@
         for index in range(ref.shape[0] // cells)
     ]
     used = [jnp.max(mask_ref[place], axis=0, keepdims=True) > 0.5 * very_low for place in range(shards)]
-    ranks = [shards - 1 - block for block in blocks_at(shards)]
+    places = [members_of(shards).index(block) for block in range(shards)]
+    ranks = [sum(jnp.where(block == at, rank, 0) for at, rank in enumerate(places)) for block in blocks_at(shards)]
     sums = []
     for place, (group, rows) in enumerate(spots):
         acc = jnp.zeros((cells, cells), jnp.float32)
@@ -408,7 +413,7 @@
     other_one = lax.ppermute(own_zero, "tgt", between)
     given = columns_of(0, last_zero, peaks_zero, own_zero, other_zero, [])
     potential_src, columns = columns_of(1, last_one, peaks_one, own_one, other_one, given)
-    arrived = lax.all_to_all(columns, "src", 0, 0, axis_index_groups=[list(range(shards))[::-1]])
+    arrived = lax.all_to_all(columns, "src", 0, 0, axis_index_groups=[members_of(shards)])
     outs = [f32(1, cells), f32(rows, cells)]
     potential_new, potential_src = call(merge_kernel, [VM] * 3, outs)(arrived, weight, potential_src)
     return potential_src, potential_new

time: 53 us -> 53 us (level)
  no operation moved by 1% of the time
where the time goes in v26:
time: 53 us; the launch traced here: 52.8 us
  Pallas kernels  33.9 us (64%)
  starting transfers between devices  8.96 us (17%)
  blocking collectives  8.27 us (16%)
  waiting for transfers between devices  0.94 us (2%)
  between operations  0.73 us (1%)
    pallas_call x2, Pallas kernels, columns_of(): call(functools.partial(column_kernel, groups, core), [VM] * (2 * groups +...  27.6 us
    all_to_all x1, blocking collectives, dense_device(): lax.all_to_all(columns, 'src', 0, 0, axis_index_groups=[members_of(shards)])  8.27 us
    ppermute x3, starting transfers between devices, moved(): return lax.ppermute(array, 'src', moves)  5.67 us
    ppermute x2, starting transfers between devices, swapped(): return lax.ppermute(array, 'src', [(i, i ^ 1) for i in range(shards)])  3.15 us
    pallas_call x2, Pallas kernels, tiles(): call(functools.partial(tile_kernel, len(packs)), [VM] * (len(packs) + 1)...  2.52 us
    pallas_call x2, Pallas kernels, reading(): call(kernel, [pl.BlockSpec(memory_space=pltpu.HBM)] * len(args), out_shap...  2.18 us
  transfers between devices with their start and end apart: 7, of which 4 were waited for; matrix products, arithmetic and copies ran while one was open for 0% of the time, Pallas kernels for 61%

profile of v26, /device:TPU:0, one launch (start us, length us, event | category | flops | bytes accessed | tf_op | source)
XLA Modules:
  0.0 52.8 jit_solution(14385738120115906800)
XLA Ops:
  0.6 0.8 %shard_map.86 = (f32[1,65,1,128]{3,2,1,0:T(1,128)S(1)}, f32[1,128]{1,0:T(1,128)S(1)}) custom-call(f32[1,64,128]{2,1,0:T(8,128)} %refs_0_.2, f32[1,128]{1,0:T(1,128)} %refs_1_.1, f32[1,128]{1,0:T(1,128)} %refs_2_.1), custom_call_target="tpu_custom_call" | custom-call | tf_op jit(solution)/shard_map/pallas_call | solution.py:315
  1.5 4.1 %collective-permute-start = (f32[1,65,1,128]{3,2,1,0:T(1,128)S(1)}, f32[1,65,1,128]{3,2,1,0:T(1,128)S(1)}, u32[]{:S(2)}, u32[]{:S(2)}) collective-permute-start(f32[1,65,1,128]{3,2,1,0:T(1,128)S(1)} %get-tuple-element.30.refs_0_), channel_id=1, source_target_pairs={{0,8},{2,10},{4,12},{6,14},{8,4},{10,6},{12,0},{14,2},{1,9},{3,11}... | collective-permute-start | bytes 99848 | tf_op jit(solution)/shard_map/ppermute | solution.py:366
  5.5 1.1 %collective-permute-start.1 = (f32[1,65,1,128]{3,2,1,0:T(1,128)S(1)}, f32[1,65,1,128]{3,2,1,0:T(1,128)S(1)}, u32[]{:S(2)}, u32[]{:S(2)}) collective-permute-start(f32[1,65,1,128]{3,2,1,0:T(1,128)S(1)} %get-tuple-element.30.refs_0_), channel_id=1, source_target_pairs={{0,12},{2,14},{4,8},{6,10},{8,0},{10,2},{12,4},{14,6},{1,13},{3,15... | collective-permute-start | bytes 99848 | tf_op jit(solution)/shard_map/ppermute | solution.py:366
  6.6 0.5 collective-permute-start.2
  7.1 1.4 %shard_map.87 = (bf16[8,512,256]{2,1,0:T(8,128)(2,1)S(1)}, f32[16,128]{1,0:T(8,128)S(1)}, f32[8,16,128]{2,1,0:T(8,128)S(1)}, f32[16,128]{1,0:T(8,128)S(1)}) custom-call(f32[16,128]{1,0:T(8,128)} %refs_0_.3, s32[8,16]{1,0:T(8,128)} %bitcast.4, s32[1,16]{1,0:T(1,128)} %bitcast.5, f32[16,64,128]{2,1,0:T(8,128)} %refs_3_.1), custom_call_target="tpu_custom_call" | custom-call | flops 100000000 | bytes 524288 | tf_op jit(solution)/shard_map/pallas_call | solution.py:315
  8.5 0.0 collective-permute-done.refs_1_
  8.5 1.7 %collective-permute-start.3 = (f32[2,65,1,128]{3,2,1,0:T(1,128)S(1)}, f32[2,65,1,128]{3,2,1,0:T(1,128)S(1)}, u32[]{:S(2)}, u32[]{:S(2)}) collective-permute-start(f32[2,65,1,128]{3,2,1,0:T(1,128)S(1)} %shard_map.88.refs_2_), channel_id=1, source_target_pairs={{0,2},{2,0},{4,6},{6,4},{8,10},{10,8},{12,14},{14,12},{1,3},{3,1},... | collective-permute-start | bytes 199688 | tf_op jit(solution)/shard_map/ppermute | solution.py:362
  10.2 0.2 collective-permute-done.1.refs_0_.refs_2_
  10.4 0.3 collective-permute-done.2.refs_1_.refs_3_
  10.7 1.5 %collective-permute-start.4 = (f32[2,65,1,128]{3,2,1,0:T(1,128)S(1)}, f32[2,65,1,128]{3,2,1,0:T(1,128)S(1)}, u32[]{:S(2)}, u32[]{:S(2)}) collective-permute-start(f32[2,65,1,128]{3,2,1,0:T(1,128)S(1)} %shard_map.89.refs_5_), channel_id=1, source_target_pairs={{0,2},{2,0},{4,6},{6,4},{8,10},{10,8},{12,14},{14,12},{1,3},{3,1},... | collective-permute-start | bytes 199688 | tf_op jit(solution)/shard_map/ppermute | solution.py:362
  12.2 1.6 %shard_map.90 = (f32[8,512,256]{2,1,0:T(8,128)S(1)}, bf16[512,512]{1,0:T(8,128)(2,1)S(1)}, f32[4,16,128]{2,1,0:T(8,128)S(1)}, f32[4,16,128]{2,1,0:T(8,128)S(1)}) custom-call(f32[1,65,1,128]{3,2,1,0:T(1,128)S(1)} %get-tuple-element.30.refs_0_, f32[1,65,1,128]{3,2,1,0:T(1,128)S(1)} %collective-permute-done.refs_1_, ...), custom_call_target="tpu_custom_call" | custom-call | flops 1073741824 | bytes 524288 | tf_op jit(solution)/shard_map/pallas_call | solution.py:354
  13.8 0.0 collective-permute-done.3.refs_0_
  13.9 0.9 %shard_map.91 = (f32[8,256,256]{2,1,0:T(8,128)S(1)}, bf16[256,512]{1,0:T(8,128)(2,1)S(1)}, f32[2,16,128]{2,1,0:T(8,128)S(1)}, f32[2,16,128]{2,1,0:T(8,128)S(1)}) custom-call(f32[2,65,1,128]{3,2,1,0:T(1,128)S(1)} %collective-permute-done.3.refs_0_, bf16[8,512,256]{2,1,0:T(8,128)(2,1)S(1)} %get-tuple-element.31.refs_4_.refs_1_.refs_6_, ...), custom_call_target="tpu_custom_call" | custom-call | flops 536870912 | bytes 524288 | tf_op jit(solution)/shard_map/pallas_call | solution.py:354
  14.7 0.3 collective-permute-done.4.refs_0_
  15.0 0.1 collective-permute-start.6
  15.1 0.9 %shard_map.93 = (f32[8,256,256]{2,1,0:T(8,128)S(1)}, bf16[256,512]{1,0:T(8,128)(2,1)S(1)}, f32[8,16,128]{2,1,0:T(8,128)S(1)}, f32[16,128]{1,0:T(8,128)S(1)}) custom-call(f32[2,65,1,128]{3,2,1,0:T(1,128)S(1)} %collective-permute-done.4.refs_0_, bf16[8,512,256]{2,1,0:T(8,128)(2,1)S(1)} %get-tuple-element.31.refs_4_.refs_1_.refs_6_, ...), custom_call_target="tpu_custom_call" | custom-call | flops 536870912 | bytes 524288 | tf_op jit(solution)/shard_map/pallas_call | solution.py:390
  16.1 0.1 collective-permute-start.5
  16.1 0.1 collective-permute-done.6.refs_10_
  16.3 27.6 %shard_map.94 = (f32[16,128]{1,0:T(8,128)S(1)}, f32[8,1,128]{2,1,0:T(1,128)S(1)}) custom-call(f32[8,512,256]{2,1,0:T(8,128)S(1)} %get-tuple-element.33.refs_0_, f32[8,256,256]{2,1,0:T(8,128)S(1)} %get-tuple-element.35.refs_1_, f32[8,256,256]{2,1,0:T(8,128)S(1)} %get-tuple-element.48.refs_2_, bf16[512,512]{1,0:T(8,128)(2,1)S(1)} %get-tuple-element.41.refs_3_, ...), custom_call_target="tpu_custom_call" | custom-call | flops 1000000000 | bytes 524288 | tf_op jit(solution)/shard_map/pallas_call | solution.py:401
  43.8 0.0 collective-permute-done.5.refs_10_
  43.9 8.3 %all_to_all.5.values_ref = f32[8,1,128]{2,1,0:T(1,128)S(1)} all-to-all(f32[8,1,128]{2,1,0:T(1,128)S(1)} %get-tuple-element.53), channel_id=1, replica_groups={{14,10,12,6,8,2,4,0},{15,11,13,7,9,3,5,1},{30,26,28,22,24,18,20,16},{31..., dimensions={0} | all-to-all | bytes 8192 | tf_op jit(solution)/shard_map/all_to_all | solution.py:416
  52.2 0.6 %shard_map.96 = (f32[1,128]{1,0:T(1,128)}, f32[16,128]{1,0:T(8,128)}) custom-call(f32[8,1,128]{2,1,0:T(1,128)S(1)} %all_to_all.5.values_ref, f32[1,128]{1,0:T(1,128)S(1)} %get-tuple-element.54.weight_ref, f32[16,128]{1,0:T(8,128)S(1)} %get-tuple-element.55.poten_ref), custom_call_target="tpu_custom_call" | custom-call | tf_op jit(solution)/shard_map/pallas_call | solution.py:418
  (4 shorter events, 0.1 us)
Async XLA Ops:
  1.5 7.0 %collective-permute-start = (f32[1,65,1,128]{3,2,1,0:T(1,128)S(1)}, f32[1,65,1,128]{3,2,1,0:T(1,128)S(1)}, u32[]{:S(2)}, u32[]{:S(2)}) collective-permute-start(f32[1,65,1,128]{3,2,1,0:T(1,128)S(1)} %get-tuple-element.30.refs_0_), channel_id=1, source_target_pairs={{0,8},{2,10},{4,12},{6,14},{8,4},{10,6},{12,0},{14,2},{1,9},{3,11}... | collective-permute-start | bytes 99848 | tf_op jit(solution)/shard_map/ppermute | solution.py:366
  5.5 4.8 %collective-permute-start.1 = (f32[1,65,1,128]{3,2,1,0:T(1,128)S(1)}, f32[1,65,1,128]{3,2,1,0:T(1,128)S(1)}, u32[]{:S(2)}, u32[]{:S(2)}) collective-permute-start(f32[1,65,1,128]{3,2,1,0:T(1,128)S(1)} %get-tuple-element.30.refs_0_), channel_id=1, source_target_pairs={{0,12},{2,14},{4,8},{6,10},{8,0},{10,2},{12,4},{14,6},{1,13},{3,15... | collective-permute-start | bytes 99848 | tf_op jit(solution)/shard_map/ppermute | solution.py:366
  6.6 4.1 %collective-permute-start.2 = (f32[1,65,1,128]{3,2,1,0:T(1,128)S(1)}, f32[1,65,1,128]{3,2,1,0:T(1,128)S(1)}, u32[]{:S(2)}, u32[]{:S(2)}) collective-permute-start(f32[1,65,1,128]{3,2,1,0:T(1,128)S(1)} %get-tuple-element.30.refs_0_), channel_id=1, source_target_pairs={{0,4},{2,6},{4,0},{6,2},{8,12},{10,14},{12,8},{14,10},{1,5},{3,7},... | collective-permute-start | bytes 99848 | tf_op jit(solution)/shard_map/ppermute | solution.py:366
  8.5 5.3 %collective-permute-start.3 = (f32[2,65,1,128]{3,2,1,0:T(1,128)S(1)}, f32[2,65,1,128]{3,2,1,0:T(1,128)S(1)}, u32[]{:S(2)}, u32[]{:S(2)}) collective-permute-start(f32[2,65,1,128]{3,2,1,0:T(1,128)S(1)} %shard_map.88.refs_2_), channel_id=1, source_target_pairs={{0,2},{2,0},{4,6},{6,4},{8,10},{10,8},{12,14},{14,12},{1,3},{3,1},... | collective-permute-start | bytes 199688 | tf_op jit(solution)/shard_map/ppermute | solution.py:362
  10.7 4.3 %collective-permute-start.4 = (f32[2,65,1,128]{3,2,1,0:T(1,128)S(1)}, f32[2,65,1,128]{3,2,1,0:T(1,128)S(1)}, u32[]{:S(2)}, u32[]{:S(2)}) collective-permute-start(f32[2,65,1,128]{3,2,1,0:T(1,128)S(1)} %shard_map.89.refs_5_), channel_id=1, source_target_pairs={{0,2},{2,0},{4,6},{6,4},{8,10},{10,8},{12,14},{14,12},{1,3},{3,1},... | collective-permute-start | bytes 199688 | tf_op jit(solution)/shard_map/ppermute | solution.py:362
  15.0 1.2 %collective-permute-start.6 = (f32[16,128]{1,0:T(8,128)S(1)}, f32[16,128]{1,0:T(8,128)S(1)}, u32[]{:S(2)}, u32[]{:S(2)}) collective-permute-start(f32[16,128]{1,0:T(8,128)S(1)} %get-tuple-element.45.refs_2_.refs_9_), channel_id=1, source_target_pairs={{0,1},{1,0},{2,3},{3,2},{4,5},{5,4},{6,7},{7,6},{8,9},{9,8},{10,11... | collective-permute-start | bytes 24584 | tf_op jit(solution)/shard_map/ppermute | solution.py:411
  16.1 27.8 %collective-permute-start.5 = (f32[16,128]{1,0:T(8,128)S(1)}, f32[16,128]{1,0:T(8,128)S(1)}, u32[]{:S(2)}, u32[]{:S(2)}) collective-permute-start(f32[16,128]{1,0:T(8,128)S(1)} %get-tuple-element.46.refs_9_), channel_id=1, source_target_pairs={{0,1},{1,0},{2,3},{3,2},{4,5},{5,4},{6,7},{7,6},{8,9},{9,8},{10,11... | collective-permute-start | bytes 24584 | tf_op jit(solution)/shard_map/ppermute | solution.py:413
